TPU v7x, 32 devices: a whole 2x2x4 slice. The times are simulated.
32 devices in a mesh: ctx: 16 (over z, y, x), ch: 2 (over core).
Axes of the slice: x: 2, y: 2, z: 4, core: 2. Of those that a mesh axis runs over, the one named last changes fastest.
Arguments:
- query_input: bfloat16 [2048, 1024], P('ctx', 'ch'), may hold values from -6 to 6
- key_input: bfloat16 [2048, 1024], P('ctx', 'ch'), may hold values from -6 to 6
- value_input: bfloat16 [2048, 1024], P('ctx', 'ch'), may hold values from -6 to 6
- implicit_filter: float32 [2048, 1024], P('ctx', 'ch'), may hold values from -1.1 to 1.1
- explicit_taps: float32 [128, 1024], P(None, 'ch'), may hold values from -0.5 to 0.5
- skip_gain: float32 [1024], P('ch'), may hold values from -3 to 3
- out_grad: bfloat16 [2048, 1024], P('ctx', 'ch'), may hold values from -6 to 6
Outputs:
- mixed_output: float32 [2048, 1024], P('ctx', 'ch')
- query_grad: float32 [2048, 1024], P('ctx', 'ch')
- key_grad: float32 [2048, 1024], P('ctx', 'ch')
- value_grad: float32 [2048, 1024], P('ctx', 'ch')
- filter_grad: float32 [2048, 1024], P('ctx', 'ch')
- taps_grad: float32 [128, 1024], P(None, 'ch')
- skip_grad: float32 [1024], P('ch')
All inputs are finite; a program needn't handle non-finite values.
Results may differ from a plain program's by a relative error of at most 0.0005.
Values sent between devices are 32-bit elements; how exact they have to be, the bound alone decides.
No kernel may reach another device: no remote copies, remote signals or barrier semaphores. Data moves between devices by JAX's collectives and lax.ppermute only.
A program may use at most 64 MiB of HBM per device.

v0:
```python
import math

import jax
import jax.numpy as jnp
from jax import lax
from jax.sharding import PartitionSpec as P


def from_partner(value, axis, stride):
    mask = 2**stride
    pairs = [(source, source ^ mask) for source in range(lax.axis_size(axis))]
    return lax.ppermute(value, axis, pairs)


def from_behind(value, axis, by):
    length = lax.axis_size(axis)
    pairs = [(i, i + by) for i in range(length) if 0 <= i + by < length]
    return lax.ppermute(value, axis, pairs)


def reversed_bits(values, section_count):
    flipped = jnp.zeros_like(values)
    for section_level in range(section_count):
        flipped = flipped + values // 2**section_level % 2 * 2 ** (
            section_count - 1 - section_level
        )
    return flipped


def rotate_parts(real_part, imag_part, phase_angle):
    cosine = jnp.cos(phase_angle)
    sine_value = jnp.sin(phase_angle)
    return (
        real_part * cosine - imag_part * sine_value,
        real_part * sine_value + imag_part * cosine,
    )


def rotate_spectra(spectra, phase_angle):
    real_part, imag_part = rotate_parts(spectra[:, :, 0], spectra[:, :, 1], phase_angle)
    return jnp.stack([real_part, imag_part], axis=2)


def half_shift(real_fields, shard_pos, shard_count):
    phase_angle = -math.pi * shard_pos.astype(jnp.float32) / shard_count
    empty_part = jnp.zeros_like(real_fields)
    plain_pair = jnp.stack([real_fields, empty_part], axis=1)
    turned_pair = jnp.stack(
        [real_fields * jnp.cos(phase_angle), real_fields * jnp.sin(phase_angle)], axis=1
    )
    return jnp.stack([plain_pair, turned_pair], axis=1)


def butterfly_down(own_data, partner_data, upper_half, offset, half_span):
    phase_angle = -math.pi * offset.astype(jnp.float32) / half_span
    summed = own_data + partner_data
    turned = rotate_spectra(partner_data - own_data, phase_angle)
    return jnp.where(upper_half == 1, turned, summed)


def butterfly_up(own_data, partner_data, upper_half, offset, half_span):
    phase_angle = math.pi * offset.astype(jnp.float32) / half_span
    summed = own_data + rotate_spectra(partner_data, phase_angle)
    turned = partner_data - rotate_spectra(own_data, phase_angle)
    return jnp.where(upper_half == 1, turned, summed)


def pair_forward(real_fields, shard_count, shard_index):
    section_count = shard_count.bit_length() - 1
    top_level = section_count - 1
    half_span = 2**top_level
    upper_half = shard_index // half_span % 2
    partner_index = shard_index + half_span - 2 * half_span * upper_half
    partner_real = from_partner(real_fields, "ctx", top_level)
    spectra = butterfly_down(
        half_shift(real_fields, shard_index, shard_count),
        half_shift(partner_real, partner_index, shard_count),
        upper_half,
        shard_index % half_span,
        half_span,
    )
    for section_level in range(top_level - 1, -1, -1):
        half_span = 2**section_level
        upper_half = shard_index // half_span % 2
        partner_data = from_partner(spectra, "ctx", section_level)
        spectra = butterfly_down(
            spectra, partner_data, upper_half, shard_index % half_span, half_span
        )
    return spectra


def pair_inverse(spectra, shard_count, shard_index, extent):
    section_count = shard_count.bit_length() - 1
    top_level = section_count - 1
    for section_level in range(top_level):
        half_span = 2**section_level
        upper_half = shard_index // half_span % 2
        partner_data = from_partner(spectra, "ctx", section_level)
        spectra = butterfly_up(
            spectra, partner_data, upper_half, shard_index % half_span, half_span
        )
    half_span = 2**top_level
    upper_half = shard_index // half_span % 2
    partner_index = shard_index + half_span - 2 * half_span * upper_half
    twist_angle = math.pi * (shard_index % half_span).astype(jnp.float32) / half_span

    def folded(target_index):
        shift_angle = math.pi * target_index.astype(jnp.float32) / shard_count
        sum_real, sum_imag = rotate_parts(spectra[:, 1, 0], spectra[:, 1, 1], shift_angle)
        sum_real = sum_real + spectra[:, 0, 0]
        sum_imag = sum_imag + spectra[:, 0, 1]
        twisted_real, twisted_imag = rotate_parts(sum_real, sum_imag, twist_angle)
        return jnp.where(upper_half == 1, twisted_real, sum_real)

    sent_part = folded(partner_index)
    kept_part = folded(shard_index)
    received = from_partner(sent_part, "ctx", top_level)
    sign_value = (1 - 2 * upper_half).astype(jnp.float32)
    return (sign_value * kept_part + received) / extent


def local_tables(shard_count, shard_index, local_rows):
    section_count = shard_count.bit_length() - 1
    flipped = reversed_bits(shard_index, section_count)
    extent_count = 2 * shard_count * local_rows
    positions = jnp.arange(local_rows, dtype=jnp.int32)
    coarse = (positions[:, None] * positions[None, :] % local_rows).astype(jnp.float32) / local_rows
    first_freq = jnp.stack([2 * flipped, 2 * flipped + 1])
    fine = (positions[None, None, :] * first_freq[:, None, None]).astype(jnp.float32) / extent_count
    phase_angle = -2.0 * math.pi * (coarse[None] + fine)
    cosine = jnp.cos(phase_angle)
    sine_value = jnp.sin(phase_angle)
    forward_table = jnp.stack(
        [jnp.stack([cosine, -sine_value], 1), jnp.stack([sine_value, cosine], 1)], 1
    )
    cosine_turned = jnp.swapaxes(cosine, 1, 2)
    sine_turned = jnp.swapaxes(sine_value, 1, 2)
    inverse_table = jnp.stack(
        [jnp.stack([cosine_turned, sine_turned], 1), jnp.stack([-sine_turned, cosine_turned], 1)], 1
    )
    return (forward_table, inverse_table)


def spectral_products(spectra):
    prod_real, prod_imag = (spectra[0, :, 0], spectra[0, :, 1])
    kern_real, kern_imag = (spectra[1, :, 0], spectra[1, :, 1])
    grad_real, grad_imag = (spectra[2, :, 0], spectra[2, :, 1])
    out_real = kern_real * prod_real - kern_imag * prod_imag
    out_imag = kern_real * prod_imag + kern_imag * prod_real
    back_real = kern_real * grad_real + kern_imag * grad_imag
    back_imag = kern_real * grad_imag - kern_imag * grad_real
    lag_real = prod_real * grad_real + prod_imag * grad_imag
    lag_imag = prod_real * grad_imag - prod_imag * grad_real
    return jnp.stack(
        [
            jnp.stack([out_real, out_imag], 1),
            jnp.stack([back_real, back_imag], 1),
            jnp.stack([lag_real, lag_imag], 1),
        ]
    )


def body(query_input, key_input, value_input, implicit_filter, explicit_taps, skip_gain, out_grad):
    local_rows = query_input.shape[0]
    shard_count = lax.axis_size("ctx")
    shard_index = lax.axis_index("ctx")
    tap_count = explicit_taps.shape[0]
    extent = 2.0 * shard_count * local_rows
    grad_scale = 1.0 / math.sqrt(shard_count * local_rows)
    query_full = query_input.astype(jnp.float32)
    key_full = key_input.astype(jnp.float32)
    value_full = value_input.astype(jnp.float32)
    grad_full = out_grad.astype(jnp.float32)
    product = key_full * value_full
    mix_grad = grad_full * query_full
    earlier = from_behind(product[local_rows - (tap_count - 1) :], "ctx", 1)
    later = from_behind(mix_grad[: tap_count - 1], "ctx", -1)
    before_rows = jnp.concatenate([earlier, product], axis=0)
    after_rows = jnp.concatenate([mix_grad, later], axis=0)
    explicit_part = jnp.zeros_like(product)
    explicit_grad = jnp.zeros_like(product)
    for tap_lag in range(tap_count):
        lagged_rows = before_rows[tap_count - 1 - tap_lag : tap_count - 1 - tap_lag + local_rows]
        explicit_part = explicit_part + explicit_taps[tap_lag] * lagged_rows
        explicit_grad = (
            explicit_grad + explicit_taps[tap_lag] * after_rows[tap_lag : tap_lag + local_rows]
        )
    real_fields = jnp.stack([product, implicit_filter, mix_grad])
    spectra = pair_forward(real_fields, shard_count, shard_index)
    forward_table, inverse_table = local_tables(shard_count, shard_index, local_rows)
    spectra = jnp.einsum(
        "roixy,friyc->froxc", forward_table, spectra, precision=lax.Precision.HIGHEST
    )
    products = spectral_products(spectra)
    products = jnp.einsum(
        "roixy,friyc->froxc", inverse_table, products, precision=lax.Precision.HIGHEST
    )
    results = pair_inverse(products, shard_count, shard_index, extent)
    implicit_part = results[0]
    implicit_grad = results[1]
    lag_grad = results[2]
    tap_local = jnp.where(shard_index == 0, lag_grad, 0.0)
    skip_local = jnp.sum(mix_grad * product, axis=0)
    tap_total, skip_total = lax.psum((tap_local, skip_local), "ctx")
    mixer = implicit_part + explicit_part + skip_gain * product
    mixed_output = query_full * mixer
    query_grad = grad_full * mixer
    product_grad = implicit_grad + explicit_grad + skip_gain * mix_grad
    key_grad = product_grad * value_full
    value_grad = product_grad * key_full
    return (
        mixed_output,
        query_grad,
        key_grad,
        value_grad,
        lag_grad * grad_scale,
        tap_total * grad_scale,
        skip_total * grad_scale,
    )


def solution(mesh):
    in_specs = (
        P("ctx", "ch"),
        P("ctx", "ch"),
        P("ctx", "ch"),
        P("ctx", "ch"),
        P(None, "ch"),
        P("ch"),
        P("ctx", "ch"),
    )
    out_specs = (
        P("ctx", "ch"),
        P("ctx", "ch"),
        P("ctx", "ch"),
        P("ctx", "ch"),
        P("ctx", "ch"),
        P(None, "ch"),
        P("ch"),
    )
    return jax.shard_map(body, mesh=mesh, in_specs=in_specs, out_specs=out_specs, check_vma=False)
```

profile of v0, /device:TPU:0, one launch (start us, length us, event | category | flops | bytes accessed | tf_op | source)
XLA Modules:
  0.0 723.5 jit_solution(3059548028778054508)
XLA Ops:
  7.2 1.0 copy.14
  8.2 1.0 copy.15
  9.3 1.1 copy.16
  10.4 1.1 copy.18
  11.5 1.1 copy.17
  12.6 1.1 multiply_reduce_fusion
  13.7 1.0 pad_maximum_fusion.2
  14.7 4.0 collective-permute-start
  19.3 1.1 fusion.26
  20.4 32.9 %collective-permute-done = f32[3,128,512]{1,2,0:T(8,128)S(1)} collective-permute-done((f32[3,128,512]{1,2,0:T(8,128)}, f32[3,128,512]{1,2,0:T(8,128)S(1)}, u32[]{:S(2)}, u32[]{:S(2)}) %collective-permute-start) | collective-permute-done | bytes 786464 | tf_op jit(solution)/shard_map/ppermute | solution.py:12
  53.4 0.8 copy-done.6
  54.4 0.9 copy-done.7
  56.2 2.6 maximum_select_fusion
  58.8 0.8 collective-permute-start.1
  59.8 68.6 %collective-permute-done.1 = f32[3,2,2,128,512]{3,4,2,0,1:T(8,128)} collective-permute-done((f32[3,2,2,128,512]{3,4,2,0,1:T(8,128)}, f32[3,2,2,128,512]{3,4,2,0,1:T(8,128)}, u32[]{:S(2)}, u32[]{:S(2)}) %collective-permute-start.1) | collective-permute-done | bytes 3145760 | tf_op jit(solution)/shard_map/ppermute | solution.py:12
  128.4 3.8 fusion.832
  132.6 1.0 copy-done.1
  133.6 1.6 copy-done.3
  135.8 3.6 maximum_select_fusion.1
  139.4 1.3 collective-permute-start.2
  140.9 67.2 %collective-permute-done.2 = f32[3,2,2,128,512]{3,4,2,0,1:T(8,128)} collective-permute-done((f32[3,2,2,128,512]{3,4,2,0,1:T(8,128)}, f32[3,2,2,128,512]{3,4,2,0,1:T(8,128)}, u32[]{:S(2)}, u32[]{:S(2)}) %collective-permute-start.2) | collective-permute-done | bytes 3145760 | tf_op jit(solution)/shard_map/ppermute | solution.py:12
  208.1 6.1 fusion.833
  214.6 3.5 maximum_select_fusion.2
  218.1 1.5 collective-permute-start.3
  219.7 1.0 fusion.805
  220.8 64.9 %collective-permute-done.3 = f32[3,2,2,128,512]{3,4,2,0,1:T(8,128)} collective-permute-done((f32[3,2,2,128,512]{3,4,2,0,1:T(8,128)S(1)}, f32[3,2,2,128,512]{3,4,2,0,1:T(8,128)}, u32[]{:S(2)}, u32[]{:S(2)}) %collective-permute-start.3) | collective-permute-done | bytes 3145760 | tf_op jit(solution)/shard_map/ppermute | solution.py:12
  285.7 2.2 sub.151
  288.2 5.1 fusion.12
  294.0 2.8 fusion.15
  296.9 1.5 collective-permute-start.4
  298.7 64.8 %collective-permute-done.4 = f32[3,2,2,128,512]{3,4,2,0,1:T(8,128)S(1)} collective-permute-done((f32[3,2,2,128,512]{3,4,2,0,1:T(8,128)S(1)}, f32[3,2,2,128,512]{3,4,2,0,1:T(8,128)S(1)}, u32[]{:S(2)}, u32[]{:S(2)}) %collective-permute-start.4) | collective-permute-done | bytes 3145760 | tf_op jit(solution)/shard_map/ppermute | solution.py:12
  363.8 0.8 fusion.5
  364.5 1.6 collective-permute-start.5
  366.7 63.6 %collective-permute-done.5 = f32[3,2,2,128,512]{3,4,2,0,1:T(8,128)} collective-permute-done((f32[3,2,2,128,512]{3,4,2,0,1:T(8,128)S(1)}, f32[3,2,2,128,512]{3,4,2,0,1:T(8,128)}, u32[]{:S(2)}, u32[]{:S(2)}) %collective-permute-start.5) | collective-permute-done | bytes 3145760 | tf_op jit(solution)/shard_map/ppermute | solution.py:12
  430.3 2.4 multiply_subtract_fusion.2
  433.2 2.9 fusion.6
  436.1 4.9 collective-permute-start.6
  441.0 1.3 collective-permute-start.9
  442.3 0.8 slice.1831
  443.1 5.3 collective-permute-start.8
  448.8 91.6 %psum.15 = f32[512]{0:T(512)} all-reduce(f32[512]{0:T(512)S(1)} %get-tuple-element.50), channel_id=1, replica_groups=mesh['ctx'=16,'ch'=2] {'ctx'}, use_global_device_ids=true, to_apply=%region_2.3 | all-reduce | flops 512 | bytes 4096 | tf_op jit(solution)/shard_map/psum | solution.py:204
  540.4 1.7 fusion.831
  542.1 1.8 fusion.829
  543.9 1.9 fusion.828
  545.8 1.9 fusion.827
  548.2 2.3 multiply_subtract_fusion
  550.4 2.7 fusion.7
  553.4 1.3 copy-done.9
  554.7 0.6 broadcast_multiply_fusion.1
  555.5 1.2 fusion.826
  556.7 1.2 fusion.825
  557.9 1.2 fusion.830
  559.4 20.4 %collective-permute-done.7 = f32[3,128,512]{1,2,0:T(8,128)S(1)} collective-permute-done((f32[3,128,512]{1,2,0:T(8,128)S(1)}, f32[3,128,512]{1,2,0:T(8,128)S(1)}, u32[]{:S(2)}, u32[]{:S(2)}) %collective-permute-start.7) | collective-permute-done | bytes 786464 | tf_op jit(solution)/shard_map/ppermute | solution.py:12
  579.8 2.2 fusion.23
  582.0 0.7 select_bitcast_fusion
  583.2 71.5 %convert_multiply_fusion.4 = (f32[128,512]{0,1:T(8,128)S(1)}, f32[128,512]{0,1:T(8,128)S(1)}) fusion(bf16[128,512]{0,1:T(8,128)(2,1)S(1)} %copy-done.20, f32[128,512]{0,1:T(8,128)} %get-tuple-element.53, f32[512]{0:T(512)} %param.12, f32[127,512]{0,1:T(8,128)} %collective-permute-done.9, f32[512]{0:T(512)S(1)} %bitcast.405, f32[512]{0:T(512)S(1)} %bitcast.407, ...), kind=kLoop, calls=%fused_computation.611 | loop fusion | flops 25362432 | bytes 1703936 | tf_op jit(solution)/shard_map/mul | solution.py:210
  654.8 55.8 %convert_multiply_fusion = (f32[128,512]{0,1:T(8,128)S(1)}, f32[128,512]{0,1:T(8,128)S(1)}) fusion(bf16[128,512]{0,1:T(8,128)(2,1)S(1)} %copy-done.18, f32[128,512]{0,1:T(8,128)S(1)} %copy-done.14, f32[512]{0:T(512)} %param.12, f32[127,512]{0,1:T(8,128)} %collective-permute-done.8, f32[512]{0:T(512)S(1)} %bitcast.406, f32[512]{0:T(512)S(1)} %bitcast.408, ...), kind=kLoop, calls=%fused_computation.607 | loop fusion | flops 25362432 | bytes 1703936 | tf_op jit(solution)/shard_map/mul | solution.py:207
  710.6 0.8 copy.44
  711.5 0.8 copy.45
  712.3 0.8 copy.42
  713.2 0.8 copy.46
  714.0 0.8 copy.43
  714.9 1.0 broadcast_multiply_fusion
  715.8 0.8 copy.47
  (146 shorter events, 6.2 us)
Async XLA Ops:
  7.2 707.7 %all-reduce.4.cloned.1.call-start = ((), (), s32[]{:S(2)}) async-start(), calls=%async_computation | async-start | bytes 524288 | tf_op jit(solution)/shard_map/psum | solution.py:204
  9.3 4.4 copy-start.19
  10.4 4.3 copy-start.15
  11.4 3.2 copy-start.17
  14.7 38.6 %collective-permute-start = (f32[3,128,512]{1,2,0:T(8,128)}, f32[3,128,512]{1,2,0:T(8,128)S(1)}, u32[]{:S(2)}, u32[]{:S(2)}) collective-permute-start(f32[3,128,512]{1,2,0:T(8,128)} %get-tuple-element.46), channel_id=1, source_target_pairs={{0,16},{2,18},{4,20},{6,22},{8,24},{10,26},{12,28},{14,30},{16,0},... | collective-permute-start | bytes 2359304 | tf_op jit(solution)/shard_map/ppermute | solution.py:12
  54.4 1.7 copy-start
  56.1 2.6 copy-start.2
  56.1 2.6 copy-start.4
  58.8 69.6 %collective-permute-start.1 = (f32[3,2,2,128,512]{3,4,2,0,1:T(8,128)}, f32[3,2,2,128,512]{3,4,2,0,1:T(8,128)}, u32[]{:S(2)}, u32[]{:S(2)}) collective-permute-start(f32[3,2,2,128,512]{3,4,2,0,1:T(8,128)} %maximum_select_fusion), channel_id=1, source_target_pairs={{0,8},{2,10},{4,12},{6,14},{8,0},{10,2},{12,4},{14,6},{16,24},{18,... | collective-permute-start | bytes 9437192 | tf_op jit(solution)/shard_map/ppermute | solution.py:12
  132.1 3.0 copy-start.3
  132.1 3.5 copy-start.5
  132.1 3.7 copy-start.8
  132.6 6.9 copy-start.12
  132.6 6.9 copy-start.13
  139.4 68.7 %collective-permute-start.2 = (f32[3,2,2,128,512]{3,4,2,0,1:T(8,128)}, f32[3,2,2,128,512]{3,4,2,0,1:T(8,128)}, u32[]{:S(2)}, u32[]{:S(2)}) collective-permute-start(f32[3,2,2,128,512]{3,4,2,0,1:T(8,128)} %maximum_select_fusion.1), channel_id=1, source_target_pairs={{0,4},{2,6},{4,0},{6,2},{8,12},{10,14},{12,8},{14,10},{16,20},{18,... | collective-permute-start | bytes 9437192 | tf_op jit(solution)/shard_map/ppermute | solution.py:12
  218.1 67.6 %collective-permute-start.3 = (f32[3,2,2,128,512]{3,4,2,0,1:T(8,128)S(1)}, f32[3,2,2,128,512]{3,4,2,0,1:T(8,128)}, u32[]{:S(2)}, u32[]{:S(2)}) collective-permute-start(f32[3,2,2,128,512]{3,4,2,0,1:T(8,128)S(1)} %maximum_select_fusion.2), channel_id=1, source_target_pairs={{0,2},{2,0},{4,6},{6,4},{8,10},{10,8},{12,14},{14,12},{16,18},{18,... | collective-permute-start | bytes 9437192 | tf_op jit(solution)/shard_map/ppermute | solution.py:12
  296.9 66.6 %collective-permute-start.4 = (f32[3,2,2,128,512]{3,4,2,0,1:T(8,128)S(1)}, f32[3,2,2,128,512]{3,4,2,0,1:T(8,128)S(1)}, u32[]{:S(2)}, u32[]{:S(2)}) collective-permute-start(f32[3,2,2,128,512]{3,4,2,0,1:T(8,128)S(1)} %fusion.15), channel_id=1, source_target_pairs={{0,2},{2,0},{4,6},{6,4},{8,10},{10,8},{12,14},{14,12},{16,18},{18,... | collective-permute-start | bytes 9437192 | tf_op jit(solution)/shard_map/ppermute | solution.py:12
  364.5 2.2 copy-start.10
  364.5 65.8 %collective-permute-start.5 = (f32[3,2,2,128,512]{3,4,2,0,1:T(8,128)S(1)}, f32[3,2,2,128,512]{3,4,2,0,1:T(8,128)}, u32[]{:S(2)}, u32[]{:S(2)}) collective-permute-start(f32[3,2,2,128,512]{3,4,2,0,1:T(8,128)S(1)} %fusion.5), channel_id=1, source_target_pairs={{0,4},{2,6},{4,0},{6,2},{8,12},{10,14},{12,8},{14,10},{16,20},{18,... | collective-permute-start | bytes 9437192 | tf_op jit(solution)/shard_map/ppermute | solution.py:12
  430.3 2.8 copy-start.11
  433.2 9.1 %copy-start.14 = (f32[128,512]{0,1:T(8,128)S(1)}, f32[128,512]{0,1:T(8,128)}, u32[]{:S(2)}) copy-start(f32[128,512]{0,1:T(8,128)} %get-tuple-element.56) | copy-start | bytes 786436
  436.1 112.1 %collective-permute-start.6 = (f32[3,2,2,128,512]{3,4,2,0,1:T(8,128)S(1)}, f32[3,2,2,128,512]{3,4,2,0,1:T(8,128)}, u32[]{:S(2)}, u32[]{:S(2)}) collective-permute-start(f32[3,2,2,128,512]{3,4,2,0,1:T(8,128)S(1)} %fusion.6), channel_id=1, source_target_pairs={{0,8},{2,10},{4,12},{6,14},{8,0},{10,2},{12,4},{14,6},{16,24},{18,... | collective-permute-start | bytes 9437192 | tf_op jit(solution)/shard_map/ppermute | solution.py:12
  441.0 141.9 %collective-permute-start.9 = (f32[127,512]{0,1:T(8,128)}, f32[127,512]{0,1:T(8,128)}, u32[]{:S(2)}, u32[]{:S(2)}) collective-permute-start(f32[127,512]{0,1:T(8,128)} %bitcast.373), channel_id=1, source_target_pairs={{2,0},{4,2},{6,4},{8,6},{10,8},{12,10},{14,12},{16,14},{18,16},{20... | collective-permute-start | bytes 780296 | tf_op jit(solution)/shard_map/ppermute | solution.py:18
  443.1 211.6 %collective-permute-start.8 = (f32[127,512]{0,1:T(8,128)}, f32[127,512]{0,1:T(8,128)}, u32[]{:S(2)}, u32[]{:S(2)}) collective-permute-start(f32[127,512]{0,1:T(8,128)} %slice.1831), channel_id=1, source_target_pairs={{0,2},{2,4},{4,6},{6,8},{8,10},{10,12},{12,14},{14,16},{16,18},{18... | collective-permute-start | bytes 780296 | tf_op jit(solution)/shard_map/ppermute | solution.py:18
  554.7 25.0 %collective-permute-start.7 = (f32[3,128,512]{1,2,0:T(8,128)S(1)}, f32[3,128,512]{1,2,0:T(8,128)S(1)}, u32[]{:S(2)}, u32[]{:S(2)}) collective-permute-start(f32[3,128,512]{1,2,0:T(8,128)S(1)} %fusion.19), channel_id=1, source_target_pairs={{0,16},{2,18},{4,20},{6,22},{8,24},{10,26},{12,28},{14,30},{16,0},... | collective-permute-start | bytes 2359304 | tf_op jit(solution)/shard_map/ppermute | solution.py:12
  559.0 23.8 %copy-start.21 = (f32[1,512]{1,0:T(1,128)S(1)}, f32[1,512]{1,0:T(1,128)}, u32[]{:S(2)}) copy-start(f32[1,512]{1,0:T(1,128)} %get-tuple-element.175) | copy-start | bytes 6148
  559.0 23.8 %copy-start.22 = (f32[1,512]{1,0:T(1,128)S(1)}, f32[1,512]{1,0:T(1,128)}, u32[]{:S(2)}) copy-start(f32[1,512]{1,0:T(1,128)} %get-tuple-element.176) | copy-start | bytes 6148
  559.1 23.8 %copy-start.23 = (f32[1,512]{1,0:T(1,128)S(1)}, f32[1,512]{1,0:T(1,128)}, u32[]{:S(2)}) copy-start(f32[1,512]{1,0:T(1,128)} %get-tuple-element.177) | copy-start | bytes 6148
  559.1 23.8 %copy-start.24 = (f32[1,512]{1,0:T(1,128)S(1)}, f32[1,512]{1,0:T(1,128)}, u32[]{:S(2)}) copy-start(f32[1,512]{1,0:T(1,128)} %get-tuple-element.178) | copy-start | bytes 6148
  559.1 23.8 %copy-start.25 = (f32[1,512]{1,0:T(1,128)S(1)}, f32[1,512]{1,0:T(1,128)}, u32[]{:S(2)}) copy-start(f32[1,512]{1,0:T(1,128)} %get-tuple-element.179) | copy-start | bytes 6148
  559.1 23.8 %copy-start.26 = (f32[1,512]{1,0:T(1,128)S(1)}, f32[1,512]{1,0:T(1,128)}, u32[]{:S(2)}) copy-start(f32[1,512]{1,0:T(1,128)} %get-tuple-element.180) | copy-start | bytes 6148
  559.1 23.8 %copy-start.27 = (f32[1,512]{1,0:T(1,128)S(1)}, f32[1,512]{1,0:T(1,128)}, u32[]{:S(2)}) copy-start(f32[1,512]{1,0:T(1,128)} %get-tuple-element.181) | copy-start | bytes 6148
  559.1 23.8 %copy-start.28 = (f32[1,512]{1,0:T(1,128)S(1)}, f32[1,512]{1,0:T(1,128)}, u32[]{:S(2)}) copy-start(f32[1,512]{1,0:T(1,128)} %get-tuple-element.182) | copy-start | bytes 6148
  559.1 23.8 %copy-start.29 = (f32[1,512]{1,0:T(1,128)S(1)}, f32[1,512]{1,0:T(1,128)}, u32[]{:S(2)}) copy-start(f32[1,512]{1,0:T(1,128)} %get-tuple-element.183) | copy-start | bytes 6148
  559.1 23.8 %copy-start.30 = (f32[1,512]{1,0:T(1,128)S(1)}, f32[1,512]{1,0:T(1,128)}, u32[]{:S(2)}) copy-start(f32[1,512]{1,0:T(1,128)} %get-tuple-element.184) | copy-start | bytes 6148
  559.1 23.8 %copy-start.31 = (f32[1,512]{1,0:T(1,128)S(1)}, f32[1,512]{1,0:T(1,128)}, u32[]{:S(2)}) copy-start(f32[1,512]{1,0:T(1,128)} %get-tuple-element.133) | copy-start | bytes 6148
  559.2 23.8 %copy-start.32 = (f32[1,512]{1,0:T(1,128)S(1)}, f32[1,512]{1,0:T(1,128)}, u32[]{:S(2)}) copy-start(f32[1,512]{1,0:T(1,128)} %get-tuple-element.134) | copy-start | bytes 6148
  559.2 23.8 %copy-start.33 = (f32[1,512]{1,0:T(1,128)S(1)}, f32[1,512]{1,0:T(1,128)}, u32[]{:S(2)}) copy-start(f32[1,512]{1,0:T(1,128)} %get-tuple-element.135) | copy-start | bytes 6148
  559.2 23.8 %copy-start.34 = (f32[1,512]{1,0:T(1,128)S(1)}, f32[1,512]{1,0:T(1,128)}, u32[]{:S(2)}) copy-start(f32[1,512]{1,0:T(1,128)} %get-tuple-element.136) | copy-start | bytes 6148
  559.2 23.8 %copy-start.35 = (f32[1,512]{1,0:T(1,128)S(1)}, f32[1,512]{1,0:T(1,128)}, u32[]{:S(2)}) copy-start(f32[1,512]{1,0:T(1,128)} %get-tuple-element.137) | copy-start | bytes 6148
  559.2 23.8 %copy-start.36 = (f32[1,512]{1,0:T(1,128)S(1)}, f32[1,512]{1,0:T(1,128)}, u32[]{:S(2)}) copy-start(f32[1,512]{1,0:T(1,128)} %get-tuple-element.138) | copy-start | bytes 6148
  559.2 23.8 %copy-start.37 = (f32[1,512]{1,0:T(1,128)S(1)}, f32[1,512]{1,0:T(1,128)}, u32[]{:S(2)}) copy-start(f32[1,512]{1,0:T(1,128)} %get-tuple-element.139) | copy-start | bytes 6148
  559.2 23.8 %copy-start.38 = (f32[1,512]{1,0:T(1,128)S(1)}, f32[1,512]{1,0:T(1,128)}, u32[]{:S(2)}) copy-start(f32[1,512]{1,0:T(1,128)} %get-tuple-element.140) | copy-start | bytes 6148
  559.2 23.8 %copy-start.39 = (f32[1,512]{1,0:T(1,128)S(1)}, f32[1,512]{1,0:T(1,128)}, u32[]{:S(2)}) copy-start(f32[1,512]{1,0:T(1,128)} %get-tuple-element.141) | copy-start | bytes 6148
  559.2 23.8 %copy-start.40 = (f32[1,512]{1,0:T(1,128)S(1)}, f32[1,512]{1,0:T(1,128)}, u32[]{:S(2)}) copy-start(f32[1,512]{1,0:T(1,128)} %get-tuple-element.142) | copy-start | bytes 6148
  559.2 23.8 %copy-start.41 = (f32[1,512]{1,0:T(1,128)S(1)}, f32[1,512]{1,0:T(1,128)}, u32[]{:S(2)}) copy-start(f32[1,512]{1,0:T(1,128)} %get-tuple-element.143) | copy-start | bytes 6148
  559.3 23.8 %copy-start.42 = (f32[1,512]{1,0:T(1,128)S(1)}, f32[1,512]{1,0:T(1,128)}, u32[]{:S(2)}) copy-start(f32[1,512]{1,0:T(1,128)} %get-tuple-element.144) | copy-start | bytes 6148
  559.3 23.8 %copy-start.43 = (f32[1,512]{1,0:T(1,128)S(1)}, f32[1,512]{1,0:T(1,128)}, u32[]{:S(2)}) copy-start(f32[1,512]{1,0:T(1,128)} %get-tuple-element.145) | copy-start | bytes 6148
  559.3 23.8 %copy-start.44 = (f32[1,512]{1,0:T(1,128)S(1)}, f32[1,512]{1,0:T(1,128)}, u32[]{:S(2)}) copy-start(f32[1,512]{1,0:T(1,128)} %get-tuple-element.146) | copy-start | bytes 6148
  559.3 23.8 %copy-start.45 = (f32[1,512]{1,0:T(1,128)S(1)}, f32[1,512]{1,0:T(1,128)}, u32[]{:S(2)}) copy-start(f32[1,512]{1,0:T(1,128)} %get-tuple-element.147) | copy-start | bytes 6148
  559.3 23.8 %copy-start.46 = (f32[1,512]{1,0:T(1,128)S(1)}, f32[1,512]{1,0:T(1,128)}, u32[]{:S(2)}) copy-start(f32[1,512]{1,0:T(1,128)} %get-tuple-element.148) | copy-start | bytes 6148
  559.3 23.8 %copy-start.47 = (f32[1,512]{1,0:T(1,128)S(1)}, f32[1,512]{1,0:T(1,128)}, u32[]{:S(2)}) copy-start(f32[1,512]{1,0:T(1,128)} %get-tuple-element.149) | copy-start | bytes 6148
  559.3 23.8 %copy-start.48 = (f32[1,512]{1,0:T(1,128)S(1)}, f32[1,512]{1,0:T(1,128)}, u32[]{:S(2)}) copy-start(f32[1,512]{1,0:T(1,128)} %get-tuple-element.150) | copy-start | bytes 6148
  559.3 23.8 %copy-start.49 = (f32[1,512]{1,0:T(1,128)S(1)}, f32[1,512]{1,0:T(1,128)}, u32[]{:S(2)}) copy-start(f32[1,512]{1,0:T(1,128)} %get-tuple-element.151) | copy-start | bytes 6148
  559.3 23.8 %copy-start.50 = (f32[1,512]{1,0:T(1,128)S(1)}, f32[1,512]{1,0:T(1,128)}, u32[]{:S(2)}) copy-start(f32[1,512]{1,0:T(1,128)} %get-tuple-element.114) | copy-start | bytes 6148
  559.3 23.8 %copy-start.51 = (f32[1,512]{1,0:T(1,128)S(1)}, f32[1,512]{1,0:T(1,128)}, u32[]{:S(2)}) copy-start(f32[1,512]{1,0:T(1,128)} %get-tuple-element.115) | copy-start | bytes 6148
  559.4 23.8 %copy-start.52 = (f32[1,512]{1,0:T(1,128)S(1)}, f32[1,512]{1,0:T(1,128)}, u32[]{:S(2)}) copy-start(f32[1,512]{1,0:T(1,128)} %get-tuple-element.116) | copy-start | bytes 6148
  559.4 23.8 %copy-start.53 = (f32[1,512]{1,0:T(1,128)S(1)}, f32[1,512]{1,0:T(1,128)}, u32[]{:S(2)}) copy-start(f32[1,512]{1,0:T(1,128)} %get-tuple-element.117) | copy-start | bytes 6148
  559.4 23.8 %copy-start.54 = (f32[1,512]{1,0:T(1,128)S(1)}, f32[1,512]{1,0:T(1,128)}, u32[]{:S(2)}) copy-start(f32[1,512]{1,0:T(1,128)} %get-tuple-element.118) | copy-start | bytes 6148
  559.4 23.8 %copy-start.55 = (f32[1,512]{1,0:T(1,128)S(1)}, f32[1,512]{1,0:T(1,128)}, u32[]{:S(2)}) copy-start(f32[1,512]{1,0:T(1,128)} %get-tuple-element.119) | copy-start | bytes 6148
  559.4 23.8 %copy-start.56 = (f32[1,512]{1,0:T(1,128)S(1)}, f32[1,512]{1,0:T(1,128)}, u32[]{:S(2)}) copy-start(f32[1,512]{1,0:T(1,128)} %get-tuple-element.120) | copy-start | bytes 6148
  559.4 23.8 %copy-start.57 = (f32[1,512]{1,0:T(1,128)S(1)}, f32[1,512]{1,0:T(1,128)}, u32[]{:S(2)}) copy-start(f32[1,512]{1,0:T(1,128)} %get-tuple-element.121) | copy-start | bytes 6148
  582.0 72.7 %copy-start.18 = (bf16[128,512]{0,1:T(8,128)(2,1)S(1)}, bf16[128,512]{0,1:T(8,128)(2,1)}, u32[]{:S(2)}) copy-start(bf16[128,512]{0,1:T(8,128)(2,1)} %copy-done.17) | copy-start | bytes 393220
  583.2 127.4 %copy-start.16 = (bf16[128,512]{0,1:T(8,128)(2,1)S(1)}, bf16[128,512]{0,1:T(8,128)(2,1)}, u32[]{:S(2)}) copy-start(bf16[128,512]{0,1:T(8,128)(2,1)} %copy-done.15) | copy-start | bytes 393220
  (6 other events, 8.0 us)
Sparse Core Ops, SparseCore 0:
  582.9 104.7 all-reduce.3
where the time goes:
time: 725 us; the launch traced here: 724 us
  waiting for transfers between devices  382 us (53%)
  other arithmetic  174 us (24%)
  blocking collectives  91.6 us (13%)
  local copies, waits for them, and re-layouts  29.1 us (4%)
  starting transfers between devices  22.3 us (3%)
  between operations  16.8 us (2%)
  matrix products  7.97 us (1%)
    ppermute x8, waiting for transfers between devices, from_partner(): return lax.ppermute(value, axis, pairs)  382 us
    psum x1, blocking collectives, body(): tap_total, skip_total = lax.psum((tap_local, skip_local), 'ctx')  91.6 us
    mul x1, other arithmetic, body(): value_grad = product_grad * key_full  71.5 us
    mul x1, other arithmetic, body(): query_grad = grad_full * mixer  55.8 us
    unnamed x129, local copies, waits for them, and re-layouts  17.2 us
    ppermute x8, starting transfers between devices, from_partner(): return lax.ppermute(value, axis, pairs)  15.7 us
  transfers between devices with their start and end apart: 11, of which 7 were waited for; matrix products, arithmetic and copies ran while one was open for 22% of the time, Pallas kernels for 0%

commit v1 on v0

v1 whole, which is shorter than its diff:
```python
import functools
import math

import jax
import jax.numpy as jnp
import numpy as np
from jax import lax
from jax.experimental import pallas as pl
from jax.experimental.pallas import tpu as pltpu
from jax.sharding import PartitionSpec as P

VMEM_LIMIT = 48 * 1024 * 1024


def turn(value, turns):
    turns = turns % 1.0
    real, imag = value
    if turns == 0.0:
        return value
    if turns == 0.5:
        return (-real, -imag)
    if turns == 0.25:
        return (-imag, real)
    if turns == 0.75:
        return (imag, -real)
    cosine, sine = math.cos(2 * math.pi * turns), math.sin(2 * math.pi * turns)
    if abs(abs(cosine) - abs(sine)) < 1e-12:
        scale = abs(cosine)
        one, two = math.copysign(1.0, cosine), math.copysign(1.0, sine)
        new_real = (real if one > 0 else -real) - (imag if two > 0 else -imag)
        new_imag = (real if two > 0 else -real) + (imag if one > 0 else -imag)
        return (new_real * scale, new_imag * scale)
    return (real * cosine - imag * sine, real * sine + imag * cosine)


def plus(a, b):
    return (a[0] + b[0], a[1] + b[1])


def minus(a, b):
    return (a[0] - b[0], a[1] - b[1])


def complex_transform(values, sign):
    count = len(values)
    if count == 1:
        return values
    even = complex_transform(values[0::2], sign)
    odd = complex_transform(values[1::2], sign)
    odd = [turn(odd[k], sign * k / count) for k in range(count // 2)]
    return [plus(e, o) for e, o in zip(even, odd)] + [minus(e, o) for e, o in zip(even, odd)]


def odd_bins(values):
    length = len(values)
    half = length // 2
    turned = [turn((values[j], -values[j + half]), -j / (2 * length)) for j in range(half)]
    bins = {}
    for m, (real, imag) in enumerate(complex_transform(turned, -1)):
        p = 4 * m + 1
        if p < length:
            bins[p] = (real, imag)
        else:
            bins[2 * length - p] = (real, -imag)
    return bins


def real_bins(values):
    length = len(values)
    if length == 2:
        return {0: (values[0] + values[1], None), 1: (values[0] - values[1], None)}
    half = length // 2
    bins = {}
    for s, value in real_bins([values[j] + values[j + half] for j in range(half)]).items():
        bins[2 * s] = value
    bins.update(odd_bins([values[j] - values[j + half] for j in range(half)]))
    return bins


def padded_bins(values):
    bins = {2 * s: value for s, value in real_bins(values).items()}
    bins.update(odd_bins(values))
    return bins


def odd_bins_back(bins, length):
    half = length // 2
    spectrum = []
    for m in range(half):
        p = 4 * m + 1
        if p < length:
            spectrum.append(bins[p])
        else:
            real, imag = bins[2 * length - p]
            spectrum.append((real, -imag))
    values = complex_transform(spectrum, 1)
    values = [turn(value, j / (2 * length)) for j, value in enumerate(values)]
    return [value[0] for value in values] + [-value[1] for value in values]


def real_bins_back(bins, length):
    if length == 2:
        return [bins[0][0] + bins[1][0], bins[0][0] - bins[1][0]]
    half = length // 2
    even = real_bins_back({s: bins[2 * s] for s in range(half // 2 + 1)}, half)
    odd = odd_bins_back(bins, half)
    return [e + o for e, o in zip(even, odd)] + [e - o for e, o in zip(even, odd)]


def padded_bins_back(bins, length):
    even = real_bins_back({s: bins[2 * s] for s in range(length // 2 + 1)}, length)
    odd = odd_bins_back(bins, length)
    return [e + o for e, o in zip(even, odd)]


def tables(blocks, rows):
    extent = 2 * blocks * rows
    positions = np.arange(rows)
    angle = 2 * np.pi * (np.outer(positions, positions) % rows) / rows
    cosine, sine = np.cos(angle), np.sin(angle)
    forward = np.block([[cosine, -sine], [sine, cosine]])
    matrices = []
    for matrix in (forward, forward.T):
        high = matrix.astype(jnp.bfloat16)
        low = (matrix - high.astype(np.float64)).astype(jnp.bfloat16)
        matrices += [high, low]
    phase = 2 * np.pi * np.outer(np.arange(blocks + 1), positions) / extent
    weight = np.where(np.arange(blocks + 1) % blocks == 0, 1.0, 2.0)[:, None] / extent
    twists = np.stack(
        [np.cos(phase), -np.sin(phase), weight * np.cos(phase), weight * np.sin(phase)], 1
    )
    return np.stack(matrices), twists.astype(np.float32)


def multiply(values, high, low):
    values_high = values.astype(jnp.bfloat16)
    values_low = (values - values_high.astype(jnp.float32)).astype(jnp.bfloat16)
    dot = functools.partial(jnp.dot, preferred_element_type=jnp.float32)
    return dot(values_high, high) + (dot(values_low, high) + dot(values_high, low))


def pack_kernel(first, query, key, value, filt, taps, skip, grad, out):
    rows, channels = query.shape
    product = key[...].astype(jnp.float32) * value[...].astype(jnp.float32)
    mix_grad = grad[...].astype(jnp.float32) * query[...].astype(jnp.float32)
    row = lax.broadcasted_iota(jnp.int32, (rows, channels), 0)
    extra = taps[...] + jnp.where(row == 0, skip[...], 0.0)
    combined = filt[...] + jnp.where(first[0] == 1, extra, 0.0)
    for a, array in enumerate((product, combined, mix_grad)):
        turned = array.T
        if len(out.shape) == 4:
            out[:, a] = turned.reshape(out.shape[0], out.shape[2], rows)
        else:
            out[a] = turned


def mix_kernel(matrices, twists, arrays, out, taps, spectra, results, *, grad_scale):
    blocks, _, channels, rows = arrays.shape
    for a in range(3):
        for low in range(0, channels, 8):
            part = pl.ds(low, 8)
            bins = padded_bins([arrays[j, a, part, :] for j in range(blocks)])
            for p in range(blocks + 1):
                real, imag = bins[p]
                cosine, sine = twists[p, 0:1, :], twists[p, 1:2, :]
                place = pl.ds(p * channels + low, 8)
                if imag is None:
                    spectra[a, place, :rows] = real * cosine
                    spectra[a, place, rows:] = real * sine
                else:
                    spectra[a, place, :rows] = real * cosine - imag * sine
                    spectra[a, place, rows:] = real * sine + imag * cosine
    forward_high, forward_low = matrices[0], matrices[1]
    back_high, back_low = matrices[2], matrices[3]
    product, filt, mix_grad = [multiply(spectra[a], forward_high, forward_low) for a in range(3)]
    pr, pi = product[:, :rows], product[:, rows:]
    fr, fi = filt[:, :rows], filt[:, rows:]
    gr, gi = mix_grad[:, :rows], mix_grad[:, rows:]
    spectra[0, :, :rows] = fr * pr - fi * pi
    spectra[0, :, rows:] = fr * pi + fi * pr
    spectra[1, :, :rows] = fr * gr + fi * gi
    spectra[1, :, rows:] = fr * gi - fi * gr
    spectra[2, :, :rows] = pr * gr + pi * gi
    spectra[2, :, rows:] = pr * gi - pi * gr
    for a in range(3):
        results[a] = multiply(spectra[a], back_high, back_low)
        for low in range(0, channels, 8):
            bins = {}
            for p in range(blocks + 1):
                cosine, sine = twists[p, 2:3, :], twists[p, 3:4, :]
                place = pl.ds(p * channels + low, 8)
                real, imag = results[a, place, :rows], results[a, place, rows:]
                new_real = real * cosine - imag * sine
                if p % blocks == 0:
                    bins[p] = (new_real, None)
                else:
                    bins[p] = (new_real, real * sine + imag * cosine)
            values = padded_bins_back(bins, blocks)
            for j in range(blocks):
                value = values[j] * grad_scale if a == 2 else values[j]
                out[j, a, pl.ds(low, 8), :] = value
                if a == 2 and j == 0:
                    taps[pl.ds(low, 8), :] = value


def unpack_kernel(query, key, value, grad, parts, first_lags, mixed, dquery, dkey, dvalue, dfilter, dtaps, dskip):
    rows, channels = query.shape

    def whole(a):
        return parts[:, a].reshape(channels, rows).T

    mixer = whole(0)
    mixed[...] = query[...].astype(jnp.float32) * mixer
    dquery[...] = grad[...].astype(jnp.float32) * mixer
    product_grad = whole(1)
    dkey[...] = product_grad * value[...].astype(jnp.float32)
    dvalue[...] = product_grad * key[...].astype(jnp.float32)
    dfilter[...] = whole(2)
    turned = first_lags[...].T
    dtaps[...] = turned
    dskip[...] = turned[0:1, :]


def call(kernel, name, out_shape, in_count, scratch=(), smem=0, flops=0, size=0):
    vmem = pl.BlockSpec(memory_space=pltpu.VMEM)
    return pl.pallas_call(
        kernel,
        name=name,
        out_shape=out_shape,
        in_specs=[pl.BlockSpec(memory_space=pltpu.SMEM)] * smem + [vmem] * in_count,
        out_specs=jax.tree.map(lambda _: vmem, out_shape),
        scratch_shapes=list(scratch),
        compiler_params=pltpu.CompilerParams(vmem_limit_bytes=VMEM_LIMIT),
        cost_estimate=pl.CostEstimate(flops=flops, bytes_accessed=size, transcendentals=0),
    )


def body(query, key, value, implicit_filter, explicit_taps, skip_gain, out_grad):
    rows, channels = query.shape
    blocks = lax.axis_size("ctx")
    share = channels // blocks
    padded = -(-share // 8) * 8
    f32 = jnp.float32
    shape = functools.partial(jax.ShapeDtypeStruct, dtype=f32)
    grad_scale = 1.0 / math.sqrt(blocks * rows)
    first = (lax.axis_index("ctx") == 0).astype(jnp.int32).reshape(1)
    direct = share == padded

    packed_shape = (blocks, 3, share, rows) if direct else (3, channels, rows)
    packed = call(pack_kernel, "pack", shape(packed_shape), 7, smem=1, size=16 * rows * channels)(
        first, query, key, value, implicit_filter, explicit_taps, skip_gain.reshape(1, channels), out_grad
    )
    if not direct:
        packed = packed.reshape(3, blocks, share, rows).swapaxes(0, 1)
    arrays = lax.all_to_all(packed, "ctx", 0, 0, tiled=True)
    if not direct:
        arrays = jnp.pad(arrays, ((0, 0), (0, 0), (0, padded - share), (0, 0)))
    matrices, twists = tables(blocks, rows)
    height = (blocks + 1) * padded
    scratch = pltpu.VMEM((3, height, 2 * rows), f32)
    results, first_lags = call(
        functools.partial(mix_kernel, grad_scale=grad_scale),
        "mix",
        (shape((blocks, 3, padded, rows)), shape((padded, rows))),
        3,
        scratch=(scratch, scratch),
        flops=36 * height * (2 * rows) ** 2,
        size=24 * blocks * padded * rows,
    )(jnp.asarray(matrices), jnp.asarray(twists), arrays)
    if not direct:
        results, first_lags = results[:, :, :share], first_lags[:share]
    first_lags = lax.all_gather(first_lags, "ctx", axis=0, tiled=True)
    parts = lax.all_to_all(results, "ctx", 0, 0, tiled=True)
    full = shape((rows, channels))
    outs = call(
        unpack_kernel,
        "unpack",
        (full,) * 6 + (shape((1, channels)),),
        6,
        size=48 * rows * channels,
    )(query, key, value, out_grad, parts, first_lags)
    return (*outs[:6], outs[6].reshape(channels))


def solution(mesh):
    in_specs = (
        P("ctx", "ch"),
        P("ctx", "ch"),
        P("ctx", "ch"),
        P("ctx", "ch"),
        P(None, "ch"),
        P("ch"),
        P("ctx", "ch"),
    )
    out_specs = (
        P("ctx", "ch"),
        P("ctx", "ch"),
        P("ctx", "ch"),
        P("ctx", "ch"),
        P("ctx", "ch"),
        P(None, "ch"),
        P("ch"),
    )
    return jax.shard_map(body, mesh=mesh, in_specs=in_specs, out_specs=out_specs, check_vma=False)
```

time: 725 us -> 92.7 us (0.13)
  waiting for transfers between devices: 382 us -> 0.01 us
  other arithmetic: 174 us -> 0 us
  local copies, waits for them, and re-layouts: 29.1 us -> 6.22 us
  starting transfers between devices: 22.3 us -> 3.74 us
  between operations: 16.8 us -> 0.72 us
  blocking collectives: 91.6 us -> 76.9 us
  matrix products: 7.97 us -> 0 us
    ppermute x10 -> x0, waiting for transfers between devices: 382 us -> none  [the longest x8 382 us: from_partner(): return lax.ppermute(value, axis, pairs)]
    mul x7 -> x0, other arithmetic: 130 us -> none  [the longest x1 71.5 us: body(): value_grad = product_grad * key_full]
    psum x1 -> x0, blocking collectives: 91.6 us -> none  [body(): tap_total, skip_total = lax.psum((tap_local, skip_local), 'ctx')]
    all_gather x0 -> x1, blocking collectives: none -> 47.3 us  [body(): first_lags = lax.all_gather(first_lags, 'ctx', axis=0, tiled=True)]
    all_to_all x0 -> x1, blocking collectives: none -> 29.5 us  [body(): arrays = lax.all_to_all(packed, 'ctx', 0, 0, tiled=True)]
    ppermute x10 -> x0, starting transfers between devices: 22.2 us -> none  [the longest x8 15.7 us: from_partner(): return lax.ppermute(value, axis, pairs)]
    sub x16 -> x0, other arithmetic: 20.3 us -> none  [the longest x4 12.4 us: butterfly_down(): turned = rotate_spectra(partner_data - own_data, phase_angle)]
    select_n x8 -> x0, other arithmetic: 17 us -> none  [the longest x3 9.65 us: butterfly_down(): return jnp.where(upper_half == 1, turned, summed)]
  transfers between devices with their start and end apart: 11 -> 1, of which waited for: 7 -> 0; matrix products, arithmetic and copies ran while one was open for 22% -> 0% of each run, Pallas kernels for 0% -> 0%
where the time goes in v1:
time: 92.7 us; the launch traced here: 92.3 us
  blocking collectives  76.9 us (83%)
  local copies, waits for them, and re-layouts  6.22 us (7%)
  Pallas kernels  4.74 us (5%)
  starting transfers between devices  3.74 us (4%)
    all_gather x1, blocking collectives, body(): first_lags = lax.all_gather(first_lags, 'ctx', axis=0, tiled=True)  47.3 us
    all_to_all x1, blocking collectives, body(): arrays = lax.all_to_all(packed, 'ctx', 0, 0, tiled=True)  29.5 us
    unnamed x26, local copies, waits for them, and re-layouts  6.22 us
    all_to_all x1, starting transfers between devices, body(): parts = lax.all_to_all(results, 'ctx', 0, 0, tiled=True)  3.74 us
    pallas_call x1, Pallas kernels, body(): call(functools.partial(mix_kernel, grad_scale=grad_scale), 'mix', (shape(...  3.2 us
  transfers between devices with their start and end apart: 1, of which 0 were waited for; matrix products, arithmetic and copies ran while one was open for 0% of the time, Pallas kernels for 0%

profile of v1, /device:TPU:0, one launch (start us, length us, event | category | flops | bytes accessed | tf_op | source)
XLA Modules:
  0.0 92.3 jit_solution(11142069209493397602)
XLA Ops:
  0.6 0.0 copy-start.10
  0.6 0.7 copy-done.10
  1.3 0.0 copy-start
  1.3 0.9 copy-done
  2.2 0.0 copy-start.2
  2.2 0.9 copy-done.2
  3.1 0.0 copy-start.4
  3.1 0.9 copy-done.4
  4.0 0.0 copy-start.6
  4.0 0.9 copy-done.6
  4.9 0.0 copy-start.8
  4.9 0.9 %copy-done.8 = f32[128,512]{1,0:T(8,128)S(1)} copy-done((f32[128,512]{1,0:T(8,128)S(1)}, f32[128,512]{1,0:T(8,128)}, u32[]{:S(2)}) %copy-start.8) | copy-done | bytes 262168
  5.9 0.0 copy-start.9
  5.9 0.9 %copy-done.9 = f32[128,512]{1,0:T(8,128)S(1)} copy-done((f32[128,512]{1,0:T(8,128)S(1)}, f32[128,512]{1,0:T(8,128)}, u32[]{:S(2)}) %copy-start.9) | copy-done | bytes 262168
  6.8 0.3 pack.1
  7.1 0.0 copy-start.11
  7.1 0.0 copy-start.12
  7.1 29.5 %all_to_all.10.arrays = f32[16,3,32,128]{3,2,1,0:T(8,128)S(1)} all-to-all(f32[16,3,32,128]{3,2,1,0:T(8,128)S(1)} %pack.1), channel_id=1, replica_groups=mesh['ctx'=16,'ch'=2] {'ctx'}, dimensions={0} | all-to-all | bytes 1572864 | tf_op jit(solution)/shard_map/all_to_all | solution.py:255
  36.7 0.0 copy-done.11
  36.7 0.0 copy-done.12
  36.7 3.2 %mix.1 = (f32[16,3,32,128]{3,2,1,0:T(8,128)}, f32[32,128]{1,0:T(8,128)S(1)}) custom-call(bf16[4,256,256]{2,1,0:T(8,128)(2,1)S(1)} %copy-done.11, f32[17,4,128]{2,1,0:T(4,128)S(1)} %copy-done.12, f32[16,3,32,128]{3,2,1,0:T(8,128)S(1)} %all_to_all.10.arrays), custom_call_target="tpu_custom_call" | custom-call | flops 1283457024 | bytes 1572864 | tf_op jit(solution)/shard_map/mix/pallas_call | solution.py:261
  39.9 0.0 copy-start.5
  39.9 0.0 copy-start.7
  39.9 3.7 %all-to-all-start.1 = ((f32[16,3,32,128]{3,2,1,0:T(8,128)}), f32[16,3,32,128]{3,2,1,0:T(8,128)S(1)}, u32[]{:S(2)}, u32[]{:S(2)}) async-start(f32[16,3,32,128]{3,2,1,0:T(8,128)} %get-tuple-element.16), calls=%async_computation.1 | async-start | bytes 1572864 | tf_op jit(solution)/shard_map/all_to_all | solution.py:273
  43.6 0.0 copy-start.1
  43.6 0.0 copy-start.3
  43.7 47.3 %all_gather.3.first_lags = f32[512,128]{1,0:T(8,128)S(1)} all-gather(f32[32,128]{1,0:T(8,128)S(1)} %get-tuple-element.17), channel_id=1, replica_groups=mesh['ctx'=16,'ch'=2] {'ctx'}, dimensions={0}, use_global_device_ids=true | all-gather | bytes 278528 | tf_op jit(solution)/shard_map/all_gather | solution.py:272
  91.0 0.0 all-to-all-done.1.parts
  91.0 0.0 copy-done.5
  91.0 0.0 copy-done.7
  91.0 0.0 copy-done.1
  91.0 0.0 copy-done.3
  91.0 1.3 %unpack.1 = (f32[128,512]{1,0:T(8,128)}, f32[128,512]{1,0:T(8,128)}, f32[128,512]{1,0:T(8,128)}, f32[128,512]{1,0:T(8,128)}, f32[128,512]{1,0:T(8,128)}, /*index=5*/f32[128,512]{1,0:T(8,128)}, f32[1,512]{1,0:T(1,128)}) custom-call(bf16[128,512]{1,0:T(8,128)(2,1)S(1)} %copy-done.1, bf16[128,512]{1,0:T(8,128)(2,1)S(1)} %copy-done.3, ...), custom_call_target="tpu_custom_call" | custom-call | bytes 3145728 | tf_op jit(solution)/shard_map/unpack/pallas_call | solution.py:275
Async XLA Ops:
  0.6 0.7 copy-start.10
  1.3 0.9 copy-start
  2.2 0.9 copy-start.2
  3.1 0.9 copy-start.4
  4.0 0.9 copy-start.6
  4.9 0.9 %copy-start.8 = (f32[128,512]{1,0:T(8,128)S(1)}, f32[128,512]{1,0:T(8,128)}, u32[]{:S(2)}) copy-start(f32[128,512]{1,0:T(8,128)} %filt.1) | copy-start | bytes 786436
  5.9 0.9 %copy-start.9 = (f32[128,512]{1,0:T(8,128)S(1)}, f32[128,512]{1,0:T(8,128)}, u32[]{:S(2)}) copy-start(f32[128,512]{1,0:T(8,128)} %taps.1) | copy-start | bytes 786436
  7.1 29.6 %copy-start.11 = (bf16[4,256,256]{2,1,0:T(8,128)(2,1)S(1)}, bf16[4,256,256]{2,1,0:T(8,128)(2,1)}, u32[]{:S(2)}) copy-start(bf16[4,256,256]{2,1,0:T(8,128)(2,1)} %constant.12.clone.matrices) | copy-start | bytes 1572868
  7.1 29.5 %copy-start.12 = (f32[17,4,128]{2,1,0:T(4,128)S(1)}, f32[17,4,128]{2,1,0:T(4,128)}, u32[]{:S(2)}) copy-start(f32[17,4,128]{2,1,0:T(4,128)} %constant.13.clone.twists) | copy-start | bytes 104452
  39.9 51.1 %copy-start.5 = (bf16[128,512]{1,0:T(8,128)(2,1)S(1)}, bf16[128,512]{1,0:T(8,128)(2,1)}, u32[]{:S(2)}) copy-start(bf16[128,512]{1,0:T(8,128)(2,1)} %value.3) | copy-start | bytes 393220
  39.9 51.1 %copy-start.7 = (bf16[128,512]{1,0:T(8,128)(2,1)S(1)}, bf16[128,512]{1,0:T(8,128)(2,1)}, u32[]{:S(2)}) copy-start(bf16[128,512]{1,0:T(8,128)(2,1)} %grad.3) | copy-start | bytes 393220
  39.9 51.1 %all-to-all-start.1 = ((f32[16,3,32,128]{3,2,1,0:T(8,128)}), f32[16,3,32,128]{3,2,1,0:T(8,128)S(1)}, u32[]{:S(2)}, u32[]{:S(2)}) async-start(f32[16,3,32,128]{3,2,1,0:T(8,128)} %get-tuple-element.16), calls=%async_computation.1 | async-start | bytes 1572864 | tf_op jit(solution)/shard_map/all_to_all | solution.py:273
  43.6 47.4 %copy-start.1 = (bf16[128,512]{1,0:T(8,128)(2,1)S(1)}, bf16[128,512]{1,0:T(8,128)(2,1)}, u32[]{:S(2)}) copy-start(bf16[128,512]{1,0:T(8,128)(2,1)} %query.3) | copy-start | bytes 393220
  43.6 47.4 %copy-start.3 = (bf16[128,512]{1,0:T(8,128)(2,1)S(1)}, bf16[128,512]{1,0:T(8,128)(2,1)}, u32[]{:S(2)}) copy-start(bf16[128,512]{1,0:T(8,128)(2,1)} %key.3) | copy-start | bytes 393220

commit v2 on v1

--- a/solution.py
+++ b/solution.py
@@ -139,19 +139,35 @@
     return dot(values_high, high) + (dot(values_low, high) + dot(values_high, low))
 
 
-def pack_kernel(first, query, key, value, filt, taps, skip, grad, out):
+def pack_kernel(first, skip, query, key, value, filt, taps, grad, out, *scratch):
+    *held, arrived = scratch
+    copies = [
+        pltpu.make_async_copy(source, target, arrived.at[i])
+        for i, (source, target) in enumerate(zip((key, value, query, grad, filt, taps), held))
+    ]
+    for copy in copies:
+        copy.start()
+    key, value, query, grad, filt, taps = held
     rows, channels = query.shape
-    product = key[...].astype(jnp.float32) * value[...].astype(jnp.float32)
-    mix_grad = grad[...].astype(jnp.float32) * query[...].astype(jnp.float32)
-    row = lax.broadcasted_iota(jnp.int32, (rows, channels), 0)
-    extra = taps[...] + jnp.where(row == 0, skip[...], 0.0)
-    combined = filt[...] + jnp.where(first[0] == 1, extra, 0.0)
-    for a, array in enumerate((product, combined, mix_grad)):
+
+    def put(a, array):
         turned = array.T
         if len(out.shape) == 4:
             out[:, a] = turned.reshape(out.shape[0], out.shape[2], rows)
         else:
             out[a] = turned
+
+    copies[0].wait()
+    copies[1].wait()
+    put(0, key[...].astype(jnp.float32) * value[...].astype(jnp.float32))
+    copies[2].wait()
+    copies[3].wait()
+    put(2, grad[...].astype(jnp.float32) * query[...].astype(jnp.float32))
+    copies[4].wait()
+    copies[5].wait()
+    row = lax.broadcasted_iota(jnp.int32, (rows, channels), 0)
+    extra = taps[...] + jnp.where(row == 0, skip[...], 0.0)
+    put(1, filt[...] + jnp.where(first[0] == 1, extra, 0.0))
 
 
 def mix_kernel(matrices, twists, arrays, out, taps, spectra, results, *, grad_scale):
@@ -203,8 +219,9 @@
                     taps[pl.ds(low, 8), :] = value
 
 
-def unpack_kernel(query, key, value, grad, parts, first_lags, mixed, dquery, dkey, dvalue, dfilter, dtaps, dskip):
+def unpack_kernel(me, query, key, value, grad, parts, first_lags, mixed, dquery, dkey, dvalue, dfilter, dtaps, dskip, ordered, *, flips):
     rows, channels = query.shape
+    blocks, share = first_lags.shape[:2]
 
     def whole(a):
         return parts[:, a].reshape(channels, rows).T
@@ -216,23 +233,38 @@
     dkey[...] = product_grad * value[...].astype(jnp.float32)
     dvalue[...] = product_grad * key[...].astype(jnp.float32)
     dfilter[...] = whole(2)
-    turned = first_lags[...].T
+    own = sum(((me[0] >> bit) & 1) * flipped for bit, flipped in enumerate(flips))
+    for source in range(blocks):
+        place = sum(flipped for bit, flipped in enumerate(flips) if source >> bit & 1)
+        ordered[source * share : (source + 1) * share, :] = first_lags[own ^ place]
+    turned = ordered[...].T
     dtaps[...] = turned
     dskip[...] = turned[0:1, :]
 
 
-def call(kernel, name, out_shape, in_count, scratch=(), smem=0, flops=0, size=0):
+def call(kernel, name, out_shape, places, scratch=(), flops=0, size=0):
     vmem = pl.BlockSpec(memory_space=pltpu.VMEM)
     return pl.pallas_call(
         kernel,
         name=name,
         out_shape=out_shape,
-        in_specs=[pl.BlockSpec(memory_space=pltpu.SMEM)] * smem + [vmem] * in_count,
+        in_specs=[pl.BlockSpec(memory_space=place) for place in places],
         out_specs=jax.tree.map(lambda _: vmem, out_shape),
         scratch_shapes=list(scratch),
         compiler_params=pltpu.CompilerParams(vmem_limit_bytes=VMEM_LIMIT),
         cost_estimate=pl.CostEstimate(flops=flops, bytes_accessed=size, transcendentals=0),
     )
+
+
+def gather_by_distance(value, axis):
+    count = lax.axis_size(axis)
+    gathered = value[None]
+    flips = {}
+    for bit in range(count.bit_length() - 2, -1, -1):
+        flips[bit] = gathered.shape[0]
+        pairs = [(i, i ^ (1 << bit)) for i in range(count)]
+        gathered = jnp.concatenate([gathered, lax.ppermute(gathered, axis, pairs)], axis=0)
+    return gathered, [flips[bit] for bit in range(len(flips))]
 
 
 def body(query, key, value, implicit_filter, explicit_taps, skip_gain, out_grad):
@@ -243,13 +275,21 @@
     f32 = jnp.float32
     shape = functools.partial(jax.ShapeDtypeStruct, dtype=f32)
     grad_scale = 1.0 / math.sqrt(blocks * rows)
-    first = (lax.axis_index("ctx") == 0).astype(jnp.int32).reshape(1)
+    me = lax.axis_index("ctx").astype(jnp.int32).reshape(1)
+    first = (me == 0).astype(jnp.int32)
     direct = share == padded
 
     packed_shape = (blocks, 3, share, rows) if direct else (3, channels, rows)
-    packed = call(pack_kernel, "pack", shape(packed_shape), 7, smem=1, size=16 * rows * channels)(
-        first, query, key, value, implicit_filter, explicit_taps, skip_gain.reshape(1, channels), out_grad
-    )
+    half = pltpu.VMEM((rows, channels), jnp.bfloat16)
+    full = pltpu.VMEM((rows, channels), f32)
+    packed = call(
+        pack_kernel,
+        "pack",
+        shape(packed_shape),
+        (pltpu.SMEM, pltpu.VMEM) + (pltpu.HBM,) * 6,
+        scratch=(half,) * 4 + (full,) * 2 + (pltpu.SemaphoreType.DMA((6,)),),
+        size=16 * rows * channels,
+    )(first, skip_gain.reshape(1, channels), query, key, value, implicit_filter, explicit_taps, out_grad)
     if not direct:
         packed = packed.reshape(3, blocks, share, rows).swapaxes(0, 1)
     arrays = lax.all_to_all(packed, "ctx", 0, 0, tiled=True)
@@ -262,23 +302,24 @@
         functools.partial(mix_kernel, grad_scale=grad_scale),
         "mix",
         (shape((blocks, 3, padded, rows)), shape((padded, rows))),
-        3,
+        (pltpu.VMEM,) * 3,
         scratch=(scratch, scratch),
         flops=36 * height * (2 * rows) ** 2,
         size=24 * blocks * padded * rows,
     )(jnp.asarray(matrices), jnp.asarray(twists), arrays)
     if not direct:
         results, first_lags = results[:, :, :share], first_lags[:share]
-    first_lags = lax.all_gather(first_lags, "ctx", axis=0, tiled=True)
     parts = lax.all_to_all(results, "ctx", 0, 0, tiled=True)
+    first_lags, flips = gather_by_distance(first_lags, "ctx")
     full = shape((rows, channels))
     outs = call(
-        unpack_kernel,
+        functools.partial(unpack_kernel, flips=flips),
         "unpack",
         (full,) * 6 + (shape((1, channels)),),
-        6,
+        (pltpu.SMEM,) + (pltpu.VMEM,) * 6,
+        scratch=(pltpu.VMEM((channels, rows), f32),),
         size=48 * rows * channels,
-    )(query, key, value, out_grad, parts, first_lags)
+    )(me, query, key, value, out_grad, parts, first_lags)
     return (*outs[:6], outs[6].reshape(channels))
 
 

time: 92.7 us -> 79.4 us (0.86)
  blocking collectives: 76.9 us -> 29.5 us
  waiting for transfers between devices: 0.01 us -> 27.4 us
  starting transfers between devices: 3.74 us -> 9.36 us
  Pallas kernels: 4.74 us -> 5.69 us
    all_gather x1 -> x0, blocking collectives: 47.3 us -> none  [body(): first_lags = lax.all_gather(first_lags, 'ctx', axis=0, tiled=True)]
    ppermute x0 -> x4, waiting for transfers between devices: none -> 27.4 us  [gather_by_distance(): lax.ppermute(gathered, axis, pairs)]
    ppermute x0 -> x4, starting transfers between devices: none -> 5.75 us  [gather_by_distance(): lax.ppermute(gathered, axis, pairs)]
    pallas_call x2, Pallas kernels: 1.54 us -> 2.51 us  [the longest x1 1.36 us: body(): call(functools.partial(unpack_kernel, flips=flips), 'unpack', (full,) * 6...]
    unnamed x26 -> x30, local copies, waits for them, and re-layouts: 6.22 us -> 6.24 us
  transfers between devices with their start and end apart: 1 -> 5, of which waited for: 0 -> 4; matrix products, arithmetic and copies ran while one was open for 0% -> 0% of each run, Pallas kernels for 0% -> 0%
where the time goes in v2:
time: 79.4 us; the launch traced here: 79 us
  blocking collectives  29.5 us (37%)
  waiting for transfers between devices  27.4 us (35%)
  starting transfers between devices  9.36 us (12%)
  local copies, waits for them, and re-layouts  6.25 us (8%)
  Pallas kernels  5.69 us (7%)
    all_to_all x1, blocking collectives, body(): arrays = lax.all_to_all(packed, 'ctx', 0, 0, tiled=True)  29.5 us
    ppermute x4, waiting for transfers between devices, gather_by_distance(): lax.ppermute(gathered, axis, pairs)  27.4 us
    unnamed x30, local copies, waits for them, and re-layouts  6.24 us
    ppermute x4, starting transfers between devices, gather_by_distance(): lax.ppermute(gathered, axis, pairs)  5.75 us
    all_to_all x1, starting transfers between devices, body(): parts = lax.all_to_all(results, 'ctx', 0, 0, tiled=True)  3.61 us
    pallas_call x1, Pallas kernels, body(): call(functools.partial(mix_kernel, grad_scale=grad_scale), 'mix', (shape(...  3.18 us
  transfers between devices with their start and end apart: 5, of which 4 were waited for; matrix products, arithmetic and copies ran while one was open for 0% of the time, Pallas kernels for 0%

profile of v2, /device:TPU:0, one launch (start us, length us, event | category | flops | bytes accessed | tf_op | source)
XLA Modules:
  0.0 79.0 jit_solution(4561486347174919363)
XLA Ops:
  0.6 0.0 copy-start.10
  0.7 0.7 copy-done.10
  1.3 0.0 copy-start
  1.3 0.9 %copy-done = bf16[128,512]{1,0:T(8,128)(2,1)S(1)} copy-done((bf16[128,512]{1,0:T(8,128)(2,1)S(1)}, bf16[128,512]{1,0:T(8,128)(2,1)}, u32[]{:S(2)}) %copy-start) | copy-done | bytes 131096
  2.2 0.0 copy-start.2
  2.2 0.9 %copy-done.2 = bf16[128,512]{1,0:T(8,128)(2,1)S(1)} copy-done((bf16[128,512]{1,0:T(8,128)(2,1)S(1)}, bf16[128,512]{1,0:T(8,128)(2,1)}, u32[]{:S(2)}) %copy-start.2) | copy-done | bytes 131096
  3.1 0.0 copy-start.4
  3.1 0.9 %copy-done.4 = bf16[128,512]{1,0:T(8,128)(2,1)S(1)} copy-done((bf16[128,512]{1,0:T(8,128)(2,1)S(1)}, bf16[128,512]{1,0:T(8,128)(2,1)}, u32[]{:S(2)}) %copy-start.4) | copy-done | bytes 131096
  4.0 0.0 copy-start.6
  4.0 0.9 %copy-done.6 = bf16[128,512]{1,0:T(8,128)(2,1)S(1)} copy-done((bf16[128,512]{1,0:T(8,128)(2,1)S(1)}, bf16[128,512]{1,0:T(8,128)(2,1)}, u32[]{:S(2)}) %copy-start.6) | copy-done | bytes 131096
  4.9 0.0 copy-start.8
  4.9 0.9 %copy-done.8 = f32[128,512]{1,0:T(8,128)S(1)} copy-done((f32[128,512]{1,0:T(8,128)S(1)}, f32[128,512]{1,0:T(8,128)}, u32[]{:S(2)}) %copy-start.8) | copy-done | bytes 262168
  5.9 0.0 copy-start.9
  5.9 0.9 %copy-done.9 = f32[128,512]{1,0:T(8,128)S(1)} copy-done((f32[128,512]{1,0:T(8,128)S(1)}, f32[128,512]{1,0:T(8,128)}, u32[]{:S(2)}) %copy-start.9) | copy-done | bytes 262168
  6.8 1.2 %pack.1 = f32[16,3,32,128]{3,2,1,0:T(8,128)S(1)} custom-call(s32[1]{0:T(128)S(6)} %convert_element_type.3.first, f32[1,512]{1,0:T(1,128)S(1)} %bitcast.9, bf16[128,512]{1,0:T(8,128)(2,1)S(1)} %copy-done, bf16[128,512]{1,0:T(8,128)(2,1)S(1)} %copy-done.2, bf16[128,512]{1,0:T(8,128)(2,1)S(1)} %copy-done.4, f32[128,512]{1,0:T(8,128)S(1)} %copy-done.8, ...), custom_call_target="tpu_custom_call" | custom-call | bytes 1048576 | tf_op jit(solution)/shard_map/pack/pallas_call | solution.py:285
  8.0 0.0 copy-start.11
  8.0 0.0 copy-start.12
  8.0 29.5 %all_to_all.10.arrays = f32[16,3,32,128]{3,2,1,0:T(8,128)S(1)} all-to-all(f32[16,3,32,128]{3,2,1,0:T(8,128)S(1)} %pack.1), channel_id=1, replica_groups=mesh['ctx'=16,'ch'=2] {'ctx'}, dimensions={0} | all-to-all | bytes 1572864 | tf_op jit(solution)/shard_map/all_to_all | solution.py:295
  37.6 0.0 copy-done.11
  37.6 0.0 copy-done.12
  37.6 3.2 %mix.1 = (f32[16,3,32,128]{3,2,1,0:T(8,128)}, f32[32,128]{1,0:T(8,128)S(1)}) custom-call(bf16[4,256,256]{2,1,0:T(8,128)(2,1)S(1)} %copy-done.11, f32[17,4,128]{2,1,0:T(4,128)S(1)} %copy-done.12, f32[16,3,32,128]{3,2,1,0:T(8,128)S(1)} %all_to_all.10.arrays), custom_call_target="tpu_custom_call" | custom-call | flops 1283457024 | bytes 1572864 | tf_op jit(solution)/shard_map/mix/pallas_call | solution.py:301
  40.7 3.6 %all-to-all-start.1 = ((f32[16,3,32,128]{3,2,1,0:T(8,128)}), f32[16,3,32,128]{3,2,1,0:T(8,128)S(1)}, u32[]{:S(2)}, u32[]{:S(2)}) async-start(f32[16,3,32,128]{3,2,1,0:T(8,128)} %get-tuple-element.16), calls=%async_computation.1 | async-start | bytes 1572864 | tf_op jit(solution)/shard_map/all_to_all | solution.py:312
  44.4 2.8 %collective-permute-start = (f32[1,32,128]{2,1,0:T(8,128)S(1)}, f32[1,32,128]{2,1,0:T(8,128)S(1)}, u32[]{:S(2)}, u32[]{:S(2)}) collective-permute-start(f32[1,32,128]{2,1,0:T(8,128)S(1)} %bitcast.5), channel_id=1, source_target_pairs={{0,16},{2,18},{4,20},{6,22},{8,24},{10,26},{12,28},{14,30},{16,0},... | collective-permute-start | bytes 49160 | tf_op jit(solution)/shard_map/ppermute | solution.py:266
  47.1 17.2 %collective-permute-done = f32[1,32,128]{2,1,0:T(8,128)S(1)} collective-permute-done((f32[1,32,128]{2,1,0:T(8,128)S(1)}, f32[1,32,128]{2,1,0:T(8,128)S(1)}, u32[]{:S(2)}, u32[]{:S(2)}) %collective-permute-start) | collective-permute-done | bytes 16416 | tf_op jit(solution)/shard_map/ppermute | solution.py:266
  64.3 0.0 collective-permute-start.1
  64.3 3.9 %collective-permute-done.1 = f32[2,32,128]{2,1,0:T(8,128)S(1)} collective-permute-done((f32[2,32,128]{2,1,0:T(8,128)S(1)}, f32[2,32,128]{2,1,0:T(8,128)S(1)}, u32[]{:S(2)}, u32[]{:S(2)}) %collective-permute-start.1) | collective-permute-done | bytes 32800 | tf_op jit(solution)/shard_map/ppermute | solution.py:266
  68.2 1.5 %collective-permute-start.2 = (f32[4,32,128]{2,1,0:T(8,128)S(1)}, f32[4,32,128]{2,1,0:T(8,128)S(1)}, u32[]{:S(2)}, u32[]{:S(2)}) collective-permute-start(f32[4,32,128]{2,1,0:T(8,128)S(1)} %pad_maximum_fusion.1), channel_id=1, source_target_pairs={{0,4},{2,6},{4,0},{6,2},{8,12},{10,14},{12,8},{14,10},{16,20},{18,... | collective-permute-start | bytes 196616 | tf_op jit(solution)/shard_map/ppermute | solution.py:266
  69.7 2.8 %collective-permute-done.2 = f32[4,32,128]{2,1,0:T(8,128)S(1)} collective-permute-done((f32[4,32,128]{2,1,0:T(8,128)S(1)}, f32[4,32,128]{2,1,0:T(8,128)S(1)}, u32[]{:S(2)}, u32[]{:S(2)}) %collective-permute-start.2) | collective-permute-done | bytes 65568 | tf_op jit(solution)/shard_map/ppermute | solution.py:266
  72.5 0.0 copy-start.7
  72.5 1.5 %collective-permute-start.3 = (f32[8,32,128]{2,1,0:T(8,128)S(1)}, f32[8,32,128]{2,1,0:T(8,128)S(1)}, u32[]{:S(2)}, u32[]{:S(2)}) collective-permute-start(f32[8,32,128]{2,1,0:T(8,128)S(1)} %pad_maximum_fusion), channel_id=1, source_target_pairs={{0,2},{2,0},{4,6},{6,4},{8,10},{10,8},{12,14},{14,12},{16,18},{18,... | collective-permute-start | bytes 393224 | tf_op jit(solution)/shard_map/ppermute | solution.py:266
  74.0 0.0 copy-start.5
  74.1 0.0 copy-start.1
  74.1 0.0 copy-start.3
  74.1 3.5 %collective-permute-done.3 = f32[8,32,128]{2,1,0:T(8,128)S(1)} collective-permute-done((f32[8,32,128]{2,1,0:T(8,128)S(1)}, f32[8,32,128]{2,1,0:T(8,128)S(1)}, u32[]{:S(2)}, u32[]{:S(2)}) %collective-permute-start.3) | collective-permute-done | bytes 131104 | tf_op jit(solution)/shard_map/ppermute | solution.py:266
  77.6 0.0 all-to-all-done.1.parts
  77.6 0.0 copy-done.7
  77.6 0.0 copy-done.5
  77.6 0.0 copy-done.1
  77.6 0.0 copy-done.3
  77.6 1.4 %unpack.1 = (f32[128,512]{1,0:T(8,128)}, f32[128,512]{1,0:T(8,128)}, f32[128,512]{1,0:T(8,128)}, f32[128,512]{1,0:T(8,128)}, f32[128,512]{1,0:T(8,128)}, /*index=5*/f32[128,512]{1,0:T(8,128)}, f32[1,512]{1,0:T(1,128)}) custom-call(s32[1]{0:T(128)} %bitcast.me, bf16[128,512]{1,0:T(8,128)(2,1)S(1)} %copy-done.1, bf16[128,512]{1,0:T(8,128)(2,1)S(1)} %copy-done.3, ...), custom_call_target="tpu_custom_call" | custom-call | bytes 3145728 | tf_op jit(solution)/shard_map/unpack/pallas_call | solution.py:315
  (8 shorter events, 0.0 us)
Async XLA Ops:
  0.6 0.7 copy-start.10
  1.3 0.9 %copy-start = (bf16[128,512]{1,0:T(8,128)(2,1)S(1)}, bf16[128,512]{1,0:T(8,128)(2,1)}, u32[]{:S(2)}) copy-start(bf16[128,512]{1,0:T(8,128)(2,1)} %query.3) | copy-start | bytes 393220
  2.2 0.9 %copy-start.2 = (bf16[128,512]{1,0:T(8,128)(2,1)S(1)}, bf16[128,512]{1,0:T(8,128)(2,1)}, u32[]{:S(2)}) copy-start(bf16[128,512]{1,0:T(8,128)(2,1)} %key.3) | copy-start | bytes 393220
  3.1 0.9 %copy-start.4 = (bf16[128,512]{1,0:T(8,128)(2,1)S(1)}, bf16[128,512]{1,0:T(8,128)(2,1)}, u32[]{:S(2)}) copy-start(bf16[128,512]{1,0:T(8,128)(2,1)} %value.3) | copy-start | bytes 393220
  4.0 0.9 %copy-start.6 = (bf16[128,512]{1,0:T(8,128)(2,1)S(1)}, bf16[128,512]{1,0:T(8,128)(2,1)}, u32[]{:S(2)}) copy-start(bf16[128,512]{1,0:T(8,128)(2,1)} %grad.3) | copy-start | bytes 393220
  4.9 0.9 %copy-start.8 = (f32[128,512]{1,0:T(8,128)S(1)}, f32[128,512]{1,0:T(8,128)}, u32[]{:S(2)}) copy-start(f32[128,512]{1,0:T(8,128)} %filt.1) | copy-start | bytes 786436
  5.9 0.9 %copy-start.9 = (f32[128,512]{1,0:T(8,128)S(1)}, f32[128,512]{1,0:T(8,128)}, u32[]{:S(2)}) copy-start(f32[128,512]{1,0:T(8,128)} %taps.1) | copy-start | bytes 786436
  8.0 29.6 %copy-start.11 = (bf16[4,256,256]{2,1,0:T(8,128)(2,1)S(1)}, bf16[4,256,256]{2,1,0:T(8,128)(2,1)}, u32[]{:S(2)}) copy-start(bf16[4,256,256]{2,1,0:T(8,128)(2,1)} %constant.12.clone.matrices) | copy-start | bytes 1572868
  8.0 29.5 %copy-start.12 = (f32[17,4,128]{2,1,0:T(4,128)S(1)}, f32[17,4,128]{2,1,0:T(4,128)}, u32[]{:S(2)}) copy-start(f32[17,4,128]{2,1,0:T(4,128)} %constant.13.clone.twists) | copy-start | bytes 104452
  40.7 36.8 %all-to-all-start.1 = ((f32[16,3,32,128]{3,2,1,0:T(8,128)}), f32[16,3,32,128]{3,2,1,0:T(8,128)S(1)}, u32[]{:S(2)}, u32[]{:S(2)}) async-start(f32[16,3,32,128]{3,2,1,0:T(8,128)} %get-tuple-element.16), calls=%async_computation.1 | async-start | bytes 1572864 | tf_op jit(solution)/shard_map/all_to_all | solution.py:312
  44.4 19.9 %collective-permute-start = (f32[1,32,128]{2,1,0:T(8,128)S(1)}, f32[1,32,128]{2,1,0:T(8,128)S(1)}, u32[]{:S(2)}, u32[]{:S(2)}) collective-permute-start(f32[1,32,128]{2,1,0:T(8,128)S(1)} %bitcast.5), channel_id=1, source_target_pairs={{0,16},{2,18},{4,20},{6,22},{8,24},{10,26},{12,28},{14,30},{16,0},... | collective-permute-start | bytes 49160 | tf_op jit(solution)/shard_map/ppermute | solution.py:266
  64.3 3.9 %collective-permute-start.1 = (f32[2,32,128]{2,1,0:T(8,128)S(1)}, f32[2,32,128]{2,1,0:T(8,128)S(1)}, u32[]{:S(2)}, u32[]{:S(2)}) collective-permute-start(f32[2,32,128]{2,1,0:T(8,128)S(1)} %pad_maximum_fusion.2), channel_id=1, source_target_pairs={{0,8},{2,10},{4,12},{6,14},{8,0},{10,2},{12,4},{14,6},{16,24},{18,... | collective-permute-start | bytes 98312 | tf_op jit(solution)/shard_map/ppermute | solution.py:266
  68.2 4.3 %collective-permute-start.2 = (f32[4,32,128]{2,1,0:T(8,128)S(1)}, f32[4,32,128]{2,1,0:T(8,128)S(1)}, u32[]{:S(2)}, u32[]{:S(2)}) collective-permute-start(f32[4,32,128]{2,1,0:T(8,128)S(1)} %pad_maximum_fusion.1), channel_id=1, source_target_pairs={{0,4},{2,6},{4,0},{6,2},{8,12},{10,14},{12,8},{14,10},{16,20},{18,... | collective-permute-start | bytes 196616 | tf_op jit(solution)/shard_map/ppermute | solution.py:266
  72.5 5.1 %copy-start.7 = (bf16[128,512]{1,0:T(8,128)(2,1)S(1)}, bf16[128,512]{1,0:T(8,128)(2,1)}, u32[]{:S(2)}) copy-start(bf16[128,512]{1,0:T(8,128)(2,1)} %grad.3) | copy-start | bytes 393220
  72.5 5.0 %collective-permute-start.3 = (f32[8,32,128]{2,1,0:T(8,128)S(1)}, f32[8,32,128]{2,1,0:T(8,128)S(1)}, u32[]{:S(2)}, u32[]{:S(2)}) collective-permute-start(f32[8,32,128]{2,1,0:T(8,128)S(1)} %pad_maximum_fusion), channel_id=1, source_target_pairs={{0,2},{2,0},{4,6},{6,4},{8,10},{10,8},{12,14},{14,12},{16,18},{18,... | collective-permute-start | bytes 393224 | tf_op jit(solution)/shard_map/ppermute | solution.py:266
  74.0 3.5 %copy-start.5 = (bf16[128,512]{1,0:T(8,128)(2,1)S(1)}, bf16[128,512]{1,0:T(8,128)(2,1)}, u32[]{:S(2)}) copy-start(bf16[128,512]{1,0:T(8,128)(2,1)} %value.3) | copy-start | bytes 393220
  74.1 3.5 %copy-start.1 = (bf16[128,512]{1,0:T(8,128)(2,1)S(1)}, bf16[128,512]{1,0:T(8,128)(2,1)}, u32[]{:S(2)}) copy-start(bf16[128,512]{1,0:T(8,128)(2,1)} %query.3) | copy-start | bytes 393220
  74.1 3.5 %copy-start.3 = (bf16[128,512]{1,0:T(8,128)(2,1)S(1)}, bf16[128,512]{1,0:T(8,128)(2,1)}, u32[]{:S(2)}) copy-start(bf16[128,512]{1,0:T(8,128)(2,1)} %key.3) | copy-start | bytes 393220

commit v3 on v2

--- a/solution.py
+++ b/solution.py
@@ -10,6 +10,7 @@
 from jax.sharding import PartitionSpec as P
 
 VMEM_LIMIT = 48 * 1024 * 1024
+CHUNKS = 2
 
 
 def turn(value, turns):
@@ -139,8 +140,8 @@
     return dot(values_high, high) + (dot(values_low, high) + dot(values_high, low))
 
 
-def pack_kernel(first, skip, query, key, value, filt, taps, grad, out, *scratch):
-    *held, arrived = scratch
+def pack_kernel(first, skip, query, key, value, filt, taps, grad, *rest, chunks):
+    outs, held, arrived = rest[:chunks], rest[chunks:-1], rest[-1]
     copies = [
         pltpu.make_async_copy(source, target, arrived.at[i])
         for i, (source, target) in enumerate(zip((key, value, query, grad, filt, taps), held))
@@ -152,10 +153,13 @@
 
     def put(a, array):
         turned = array.T
-        if len(out.shape) == 4:
-            out[:, a] = turned.reshape(out.shape[0], out.shape[2], rows)
-        else:
-            out[a] = turned
+        if len(outs[0].shape) == 3:
+            outs[0][a] = turned
+            return
+        blocks, _, part, _ = outs[0].shape
+        turned = turned.reshape(blocks, chunks * part, rows)
+        for k, out in enumerate(outs):
+            out[:, a] = turned[:, k * part : (k + 1) * part]
 
     copies[0].wait()
     copies[1].wait()
@@ -219,12 +223,13 @@
                     taps[pl.ds(low, 8), :] = value
 
 
-def unpack_kernel(me, query, key, value, grad, parts, first_lags, mixed, dquery, dkey, dvalue, dfilter, dtaps, dskip, ordered, *, flips):
+def unpack_kernel(me, query, key, value, grad, *rest, chunks, high):
+    parts, rest = rest[:chunks], rest[chunks:]
+    *lags, mixed, dquery, dkey, dvalue, dfilter, dtaps, dskip, ordered = rest
     rows, channels = query.shape
-    blocks, share = first_lags.shape[:2]
 
     def whole(a):
-        return parts[:, a].reshape(channels, rows).T
+        return jnp.concatenate([part[:, a] for part in parts], axis=1).reshape(channels, rows).T
 
     mixer = whole(0)
     mixed[...] = query[...].astype(jnp.float32) * mixer
@@ -233,16 +238,21 @@
     dkey[...] = product_grad * value[...].astype(jnp.float32)
     dvalue[...] = product_grad * key[...].astype(jnp.float32)
     dfilter[...] = whole(2)
-    own = sum(((me[0] >> bit) & 1) * flipped for bit, flipped in enumerate(flips))
-    for source in range(blocks):
-        place = sum(flipped for bit, flipped in enumerate(flips) if source >> bit & 1)
-        ordered[source * share : (source + 1) * share, :] = first_lags[own ^ place]
-    turned = ordered[...].T
+    if high == 0:
+        turned = lags[0][...].T
+    else:
+        low, share = len(lags), lags[0].shape[1]
+        for near in range(low):
+            for far in range(high):
+                source = me[0] ^ (far * low + near)
+                place = pl.ds(pl.multiple_of(source * share, share), share)
+                ordered[place, :] = lags[near][far]
+        turned = ordered[...].T
     dtaps[...] = turned
     dskip[...] = turned[0:1, :]
 
 
-def call(kernel, name, out_shape, places, scratch=(), flops=0, size=0):
+def call(kernel, name, out_shape, places, scratch=(), flops=0, size=0, limit=VMEM_LIMIT):
     vmem = pl.BlockSpec(memory_space=pltpu.VMEM)
     return pl.pallas_call(
         kernel,
@@ -251,54 +261,54 @@
         in_specs=[pl.BlockSpec(memory_space=place) for place in places],
         out_specs=jax.tree.map(lambda _: vmem, out_shape),
         scratch_shapes=list(scratch),
-        compiler_params=pltpu.CompilerParams(vmem_limit_bytes=VMEM_LIMIT),
+        compiler_params=pltpu.CompilerParams(vmem_limit_bytes=limit),
         cost_estimate=pl.CostEstimate(flops=flops, bytes_accessed=size, transcendentals=0),
     )
+
+
+def exchange(value, axis, distance):
+    return lax.ppermute(value, axis, [(i, i ^ distance) for i in range(lax.axis_size(axis))])
 
 
 def gather_by_distance(value, axis):
     count = lax.axis_size(axis)
-    gathered = value[None]
-    flips = {}
-    for bit in range(count.bit_length() - 2, -1, -1):
-        flips[bit] = gathered.shape[0]
-        pairs = [(i, i ^ (1 << bit)) for i in range(count)]
-        gathered = jnp.concatenate([gathered, lax.ppermute(gathered, axis, pairs)], axis=0)
-    return gathered, [flips[bit] for bit in range(len(flips))]
+    low = 1 << (count.bit_length() - 1) // 2
+    stack = jnp.stack([value] + [exchange(value, axis, far * low) for far in range(1, count // low)])
+    return [stack] + [exchange(stack, axis, near) for near in range(1, low)]
 
 
 def body(query, key, value, implicit_filter, explicit_taps, skip_gain, out_grad):
     rows, channels = query.shape
     blocks = lax.axis_size("ctx")
     share = channels // blocks
-    padded = -(-share // 8) * 8
+    direct = share % (8 * CHUNKS) == 0
+    chunks = CHUNKS if direct else 1
+    part = share // chunks
+    padded = -(-part // 8) * 8
     f32 = jnp.float32
     shape = functools.partial(jax.ShapeDtypeStruct, dtype=f32)
     grad_scale = 1.0 / math.sqrt(blocks * rows)
     me = lax.axis_index("ctx").astype(jnp.int32).reshape(1)
     first = (me == 0).astype(jnp.int32)
-    direct = share == padded
-
-    packed_shape = (blocks, 3, share, rows) if direct else (3, channels, rows)
+
+    packed_shape = (blocks, 3, part, rows) if direct else (3, channels, rows)
     half = pltpu.VMEM((rows, channels), jnp.bfloat16)
     full = pltpu.VMEM((rows, channels), f32)
     packed = call(
-        pack_kernel,
+        functools.partial(pack_kernel, chunks=chunks),
         "pack",
-        shape(packed_shape),
+        (shape(packed_shape),) * chunks,
         (pltpu.SMEM, pltpu.VMEM) + (pltpu.HBM,) * 6,
         scratch=(half,) * 4 + (full,) * 2 + (pltpu.SemaphoreType.DMA((6,)),),
         size=16 * rows * channels,
+        limit=None,
     )(first, skip_gain.reshape(1, channels), query, key, value, implicit_filter, explicit_taps, out_grad)
     if not direct:
-        packed = packed.reshape(3, blocks, share, rows).swapaxes(0, 1)
-    arrays = lax.all_to_all(packed, "ctx", 0, 0, tiled=True)
-    if not direct:
-        arrays = jnp.pad(arrays, ((0, 0), (0, 0), (0, padded - share), (0, 0)))
+        packed = [packed[0].reshape(3, blocks, share, rows).swapaxes(0, 1)]
     matrices, twists = tables(blocks, rows)
     height = (blocks + 1) * padded
     scratch = pltpu.VMEM((3, height, 2 * rows), f32)
-    results, first_lags = call(
+    mix = call(
         functools.partial(mix_kernel, grad_scale=grad_scale),
         "mix",
         (shape((blocks, 3, padded, rows)), shape((padded, rows))),
@@ -306,20 +316,33 @@
         scratch=(scratch, scratch),
         flops=36 * height * (2 * rows) ** 2,
         size=24 * blocks * padded * rows,
-    )(jnp.asarray(matrices), jnp.asarray(twists), arrays)
-    if not direct:
-        results, first_lags = results[:, :, :share], first_lags[:share]
-    parts = lax.all_to_all(results, "ctx", 0, 0, tiled=True)
-    first_lags, flips = gather_by_distance(first_lags, "ctx")
+    )
+    parts, lags = [], []
+    for chunk in packed:
+        arrays = lax.all_to_all(chunk, "ctx", 0, 0, tiled=True)
+        if not direct:
+            arrays = jnp.pad(arrays, ((0, 0), (0, 0), (0, padded - part), (0, 0)))
+        results, first_lags = mix(jnp.asarray(matrices), jnp.asarray(twists), arrays)
+        if not direct:
+            results, first_lags = results[:, :, :part], first_lags[:part]
+        parts.append(lax.all_to_all(results, "ctx", 0, 0, tiled=True))
+        lags.append(first_lags)
+    first_lags = jnp.concatenate(lags, axis=0)
+    if direct:
+        gathered = gather_by_distance(first_lags, "ctx")
+        high = gathered[0].shape[0]
+    else:
+        gathered = [lax.all_gather(first_lags, "ctx", axis=0, tiled=True)]
+        high = 0
     full = shape((rows, channels))
     outs = call(
-        functools.partial(unpack_kernel, flips=flips),
+        functools.partial(unpack_kernel, chunks=chunks, high=high),
         "unpack",
         (full,) * 6 + (shape((1, channels)),),
-        (pltpu.SMEM,) + (pltpu.VMEM,) * 6,
+        (pltpu.SMEM,) + (pltpu.VMEM,) * (4 + chunks + len(gathered)),
         scratch=(pltpu.VMEM((channels, rows), f32),),
         size=48 * rows * channels,
-    )(me, query, key, value, out_grad, parts, first_lags)
+    )(me, query, key, value, out_grad, *parts, *gathered)
     return (*outs[:6], outs[6].reshape(channels))
 
 

time: 79.4 us -> 80.5 us (1.014)
  starting transfers between devices: 9.36 us -> 19.1 us
  blocking collectives: 29.5 us -> 21 us
  local copies, waits for them, and re-layouts: 6.25 us -> 0.03 us
  waiting for transfers between devices: 27.4 us -> 30.8 us
  Pallas kernels: 5.69 us -> 8.24 us
    all_to_all x1 -> x3, waiting for transfers between devices: 0.01 us -> 19.7 us  [the longest x1 10.1 us: body(): arrays = lax.all_to_all(chunk, 'ctx', 0, 0, tiled=True)]
    ppermute x4 -> x6, waiting for transfers between devices: 27.4 us -> 11.2 us  [exchange(): lax.ppermute(value, axis, [(i, i ^ distance) for i in range(lax.axis_size...]
    all_to_all x1, blocking collectives: 29.5 us -> 21 us  [body(): arrays = lax.all_to_all(chunk, 'ctx', 0, 0, tiled=True)]
    all_to_all x1 -> x3, starting transfers between devices: 3.61 us -> 11.1 us  [the longest x2 7.39 us: body(): parts.append(lax.all_to_all(results, 'ctx', 0, 0, tiled=True))]
    unnamed x30 -> x13, local copies, waits for them, and re-layouts: 6.24 us -> 0.03 us
    pallas_call x3 -> x4, Pallas kernels: 5.69 us -> 8.24 us  [the longest x2 3.86 us: body(): mix(jnp.asarray(matrices), jnp.asarray(twists), arrays)]
    ppermute x4 -> x6, starting transfers between devices: 5.75 us -> 8.01 us  [exchange(): lax.ppermute(value, axis, [(i, i ^ distance) for i in range(lax.axis_size...]
  transfers between devices with their start and end apart: 5 -> 9, of which waited for: 4 -> 7; matrix products, arithmetic and copies ran while one was open for 0% -> 0% of each run, Pallas kernels for 0% -> 5%
where the time goes in v3:
time: 80.5 us; the launch traced here: 79.9 us
  waiting for transfers between devices  30.8 us (38%)
  blocking collectives  21 us (26%)
  starting transfers between devices  19.1 us (24%)
  Pallas kernels  8.24 us (10%)
    all_to_all x1, blocking collectives, body(): arrays = lax.all_to_all(chunk, 'ctx', 0, 0, tiled=True)  21 us
    ppermute x6, waiting for transfers between devices, exchange(): lax.ppermute(value, axis, [(i, i ^ distance) for i in range(lax.axis_size...  11.2 us
    all_to_all x1, waiting for transfers between devices, body(): arrays = lax.all_to_all(chunk, 'ctx', 0, 0, tiled=True)  10.1 us
    all_to_all x2, waiting for transfers between devices, body(): parts.append(lax.all_to_all(results, 'ctx', 0, 0, tiled=True))  9.62 us
    ppermute x6, starting transfers between devices, exchange(): lax.ppermute(value, axis, [(i, i ^ distance) for i in range(lax.axis_size...  8.01 us
    all_to_all x2, starting transfers between devices, body(): parts.append(lax.all_to_all(results, 'ctx', 0, 0, tiled=True))  7.39 us
    pallas_call x2, Pallas kernels, body(): mix(jnp.asarray(matrices), jnp.asarray(twists), arrays)  3.86 us
    all_to_all x1, starting transfers between devices, body(): arrays = lax.all_to_all(chunk, 'ctx', 0, 0, tiled=True)  3.71 us
  transfers between devices with their start and end apart: 9, of which 7 were waited for; matrix products, arithmetic and copies ran while one was open for 0% of the time, Pallas kernels for 5%

profile of v3, /device:TPU:0, one launch (start us, length us, event | category | flops | bytes accessed | tf_op | source)
XLA Modules:
  0.0 79.9 jit_solution(13848538787478839074)
XLA Ops:
  0.6 3.0 %pack.1 = (f32[16,3,16,128]{3,2,1,0:T(8,128)}, f32[16,3,16,128]{3,2,1,0:T(8,128)}) custom-call(s32[1]{0:T(128)S(6)} %convert_element_type.3.first, f32[1,512]{1,0:T(1,128)} %bitcast.11, bf16[128,512]{1,0:T(8,128)(2,1)} %query.3, bf16[128,512]{1,0:T(8,128)(2,1)} %key.3, bf16[128,512]{1,0:T(8,128)(2,1)} %value.3, f32[128,512]{1,0:T(8,128)} %filt.1, ...), custom_call_target="tpu_custom_call" | custom-call | bytes 1048576 | tf_op jit(solution)/shard_map/pack/pallas_call | solution.py:297
  3.7 21.0 %all_to_all.20.arrays = f32[16,3,16,128]{3,2,1,0:T(8,128)S(1)} all-to-all(f32[16,3,16,128]{3,2,1,0:T(8,128)} %get-tuple-element.20), channel_id=1, replica_groups=mesh['ctx'=16,'ch'=2] {'ctx'}, dimensions={0} | all-to-all | bytes 786432 | tf_op jit(solution)/shard_map/all_to_all | solution.py:322
  24.6 0.0 copy-start.4
  24.6 0.0 copy-start.5
  24.6 3.7 %all-to-all-start.2 = ((f32[16,3,16,128]{3,2,1,0:T(8,128)}), f32[16,3,16,128]{3,2,1,0:T(8,128)S(1)}, u32[]{:S(2)}, u32[]{:S(2)}) async-start(f32[16,3,16,128]{3,2,1,0:T(8,128)} %get-tuple-element.22), calls=%async_computation.2 | async-start | bytes 786432 | tf_op jit(solution)/shard_map/all_to_all | solution.py:322
  28.4 0.0 copy-done.4
  28.4 0.0 copy-done.5
  28.4 1.9 %mix.2 = (f32[16,3,16,128]{3,2,1,0:T(8,128)}, f32[16,128]{1,0:T(8,128)S(1)}) custom-call(bf16[4,256,256]{2,1,0:T(8,128)(2,1)S(1)} %copy-done.4, f32[17,4,128]{2,1,0:T(4,128)S(1)} %copy-done.5, f32[16,3,16,128]{3,2,1,0:T(8,128)S(1)} %all_to_all.20.arrays), custom_call_target="tpu_custom_call" | custom-call | flops 641728512 | bytes 786432 | tf_op jit(solution)/shard_map/mix/pallas_call | solution.py:325
  30.3 10.1 %all-to-all-done.2.arrays = f32[16,3,16,128]{3,2,1,0:T(8,128)S(1)} async-done(((f32[16,3,16,128]{3,2,1,0:T(8,128)}), f32[16,3,16,128]{3,2,1,0:T(8,128)S(1)}, u32[]{:S(2)}, u32[]{:S(2)}) %all-to-all-start.2) | async-done | bytes 393248 | tf_op jit(solution)/shard_map/all_to_all | solution.py:322
  40.4 3.6 %all-to-all-start.1 = ((f32[16,3,16,128]{3,2,1,0:T(8,128)}), f32[16,3,16,128]{3,2,1,0:T(8,128)S(1)}, u32[]{:S(2)}, u32[]{:S(2)}) async-start(f32[16,3,16,128]{3,2,1,0:T(8,128)} %get-tuple-element.21), calls=%async_computation.1 | async-start | bytes 786432 | tf_op jit(solution)/shard_map/all_to_all | solution.py:328
  44.0 1.9 %mix.3 = (f32[16,3,16,128]{3,2,1,0:T(8,128)}, f32[16,128]{1,0:T(8,128)S(1)}) custom-call(bf16[4,256,256]{2,1,0:T(8,128)(2,1)S(1)} %copy-done.4, f32[17,4,128]{2,1,0:T(4,128)S(1)} %copy-done.5, f32[16,3,16,128]{3,2,1,0:T(8,128)S(1)} %all-to-all-done.2.arrays), custom_call_target="tpu_custom_call" | custom-call | flops 641728512 | bytes 786432 | tf_op jit(solution)/shard_map/mix/pallas_call | solution.py:325
  45.9 9.6 %all-to-all-done.1.rest_0_ = f32[16,3,16,128]{3,2,1,0:T(8,128)S(1)} async-done(((f32[16,3,16,128]{3,2,1,0:T(8,128)}), f32[16,3,16,128]{3,2,1,0:T(8,128)S(1)}, u32[]{:S(2)}, u32[]{:S(2)}) %all-to-all-start.1) | async-done | bytes 393248 | tf_op jit(solution)/shard_map/all_to_all | solution.py:328
  55.6 0.0 copy-start.1
  55.6 0.0 copy-start.2
  55.6 0.0 copy-start.3
  55.6 3.8 %all-to-all-start.3 = ((f32[16,3,16,128]{3,2,1,0:T(8,128)}), f32[16,3,16,128]{3,2,1,0:T(8,128)S(1)}, u32[]{:S(2)}, u32[]{:S(2)}) async-start(f32[16,3,16,128]{3,2,1,0:T(8,128)} %get-tuple-element.23), calls=%async_computation.3 | async-start | bytes 786432 | tf_op jit(solution)/shard_map/all_to_all | solution.py:328
  59.3 0.0 copy-start
  59.4 3.8 %collective-permute-start.2 = (f32[32,128]{1,0:T(8,128)S(1)}, f32[32,128]{1,0:T(8,128)S(1)}, u32[]{:S(2)}, u32[]{:S(2)}) collective-permute-start(f32[32,128]{1,0:T(8,128)S(1)} %constant_dynamic-update-slice_fusion), channel_id=1, source_target_pairs={{0,24},{2,26},{4,28},{6,30},{8,16},{10,18},{12,20},{14,22},{16,8},... | collective-permute-start | bytes 49160 | tf_op jit(solution)/shard_map/ppermute | solution.py:270
  63.2 0.0 collective-permute-start.1
  63.2 0.7 collective-permute-start
  63.8 5.7 %collective-permute-done.2 = f32[32,128]{1,0:T(8,128)S(1)} collective-permute-done((f32[32,128]{1,0:T(8,128)S(1)}, f32[32,128]{1,0:T(8,128)S(1)}, u32[]{:S(2)}, u32[]{:S(2)}) %collective-permute-start.2) | collective-permute-done | bytes 16416 | tf_op jit(solution)/shard_map/ppermute | solution.py:270
  69.6 1.7 %collective-permute-done.1 = f32[32,128]{1,0:T(8,128)S(1)} collective-permute-done((f32[32,128]{1,0:T(8,128)S(1)}, f32[32,128]{1,0:T(8,128)S(1)}, u32[]{:S(2)}, u32[]{:S(2)}) %collective-permute-start.1) | collective-permute-done | bytes 16416 | tf_op jit(solution)/shard_map/ppermute | solution.py:270
  71.3 0.0 collective-permute-done
  71.3 2.4 %collective-permute-start.5 = (f32[4,32,128]{2,1,0:T(8,128)S(1)}, f32[4,32,128]{2,1,0:T(8,128)S(1)}, u32[]{:S(2)}, u32[]{:S(2)}) collective-permute-start(f32[4,32,128]{2,1,0:T(8,128)S(1)} %pad_maximum_fusion.rest_2_), channel_id=1, source_target_pairs={{0,6},{2,4},{4,2},{6,0},{8,14},{10,12},{12,10},{14,8},{16,22},{18,... | collective-permute-start | bytes 196616 | tf_op jit(solution)/shard_map/ppermute | solution.py:270
  73.7 0.6 collective-permute-start.4
  74.3 0.6 collective-permute-start.3
  74.8 2.3 %collective-permute-done.5.rest_5_ = f32[4,32,128]{2,1,0:T(8,128)S(1)} collective-permute-done((f32[4,32,128]{2,1,0:T(8,128)S(1)}, f32[4,32,128]{2,1,0:T(8,128)S(1)}, u32[]{:S(2)}, u32[]{:S(2)}) %collective-permute-start.5) | collective-permute-done | bytes 65568 | tf_op jit(solution)/shard_map/ppermute | solution.py:270
  77.2 0.7 collective-permute-done.4.rest_4_
  77.9 0.6 collective-permute-done.3.rest_3_
  78.6 0.0 all-to-all-done.3.rest_1_
  78.6 0.0 copy-done.1
  78.6 0.0 copy-done.2
  78.6 0.0 copy-done.3
  78.6 0.0 copy-done
  78.6 1.3 %unpack.1 = (f32[128,512]{1,0:T(8,128)}, f32[128,512]{1,0:T(8,128)}, f32[128,512]{1,0:T(8,128)}, f32[128,512]{1,0:T(8,128)}, f32[128,512]{1,0:T(8,128)}, /*index=5*/f32[128,512]{1,0:T(8,128)}, f32[1,512]{1,0:T(1,128)}) custom-call(s32[1]{0:T(128)} %bitcast.me, bf16[128,512]{1,0:T(8,128)(2,1)S(1)} %copy-done, bf16[128,512]{1,0:T(8,128)(2,1)S(1)} %copy-done.1, ...), custom_call_target="tpu_custom_call" | custom-call | bytes 3145728 | tf_op jit(solution)/shard_map/unpack/pallas_call | solution.py:338
  (3 shorter events, 0.0 us)
Async XLA Ops:
  24.6 3.7 %copy-start.4 = (bf16[4,256,256]{2,1,0:T(8,128)(2,1)S(1)}, bf16[4,256,256]{2,1,0:T(8,128)(2,1)}, u32[]{:S(2)}) copy-start(bf16[4,256,256]{2,1,0:T(8,128)(2,1)} %constant.12.clone.matrices) | copy-start | bytes 1572868
  24.6 3.7 %copy-start.5 = (f32[17,4,128]{2,1,0:T(4,128)S(1)}, f32[17,4,128]{2,1,0:T(4,128)}, u32[]{:S(2)}) copy-start(f32[17,4,128]{2,1,0:T(4,128)} %constant.13.clone.twists) | copy-start | bytes 104452
  24.6 15.7 %all-to-all-start.2 = ((f32[16,3,16,128]{3,2,1,0:T(8,128)}), f32[16,3,16,128]{3,2,1,0:T(8,128)S(1)}, u32[]{:S(2)}, u32[]{:S(2)}) async-start(f32[16,3,16,128]{3,2,1,0:T(8,128)} %get-tuple-element.22), calls=%async_computation.2 | async-start | bytes 786432 | tf_op jit(solution)/shard_map/all_to_all | solution.py:322
  40.4 15.2 %all-to-all-start.1 = ((f32[16,3,16,128]{3,2,1,0:T(8,128)}), f32[16,3,16,128]{3,2,1,0:T(8,128)S(1)}, u32[]{:S(2)}, u32[]{:S(2)}) async-start(f32[16,3,16,128]{3,2,1,0:T(8,128)} %get-tuple-element.21), calls=%async_computation.1 | async-start | bytes 786432 | tf_op jit(solution)/shard_map/all_to_all | solution.py:328
  55.6 23.0 %copy-start.1 = (bf16[128,512]{1,0:T(8,128)(2,1)S(1)}, bf16[128,512]{1,0:T(8,128)(2,1)}, u32[]{:S(2)}) copy-start(bf16[128,512]{1,0:T(8,128)(2,1)} %key.3) | copy-start | bytes 393220
  55.6 23.0 %copy-start.2 = (bf16[128,512]{1,0:T(8,128)(2,1)S(1)}, bf16[128,512]{1,0:T(8,128)(2,1)}, u32[]{:S(2)}) copy-start(bf16[128,512]{1,0:T(8,128)(2,1)} %value.3) | copy-start | bytes 393220
  55.6 23.0 %copy-start.3 = (bf16[128,512]{1,0:T(8,128)(2,1)S(1)}, bf16[128,512]{1,0:T(8,128)(2,1)}, u32[]{:S(2)}) copy-start(bf16[128,512]{1,0:T(8,128)(2,1)} %grad.3) | copy-start | bytes 393220
  55.6 23.0 %all-to-all-start.3 = ((f32[16,3,16,128]{3,2,1,0:T(8,128)}), f32[16,3,16,128]{3,2,1,0:T(8,128)S(1)}, u32[]{:S(2)}, u32[]{:S(2)}) async-start(f32[16,3,16,128]{3,2,1,0:T(8,128)} %get-tuple-element.23), calls=%async_computation.3 | async-start | bytes 786432 | tf_op jit(solution)/shard_map/all_to_all | solution.py:328
  59.3 19.2 %copy-start = (bf16[128,512]{1,0:T(8,128)(2,1)S(1)}, bf16[128,512]{1,0:T(8,128)(2,1)}, u32[]{:S(2)}) copy-start(bf16[128,512]{1,0:T(8,128)(2,1)} %query.3) | copy-start | bytes 393220
  59.4 10.2 %collective-permute-start.2 = (f32[32,128]{1,0:T(8,128)S(1)}, f32[32,128]{1,0:T(8,128)S(1)}, u32[]{:S(2)}, u32[]{:S(2)}) collective-permute-start(f32[32,128]{1,0:T(8,128)S(1)} %constant_dynamic-update-slice_fusion), channel_id=1, source_target_pairs={{0,24},{2,26},{4,28},{6,30},{8,16},{10,18},{12,20},{14,22},{16,8},... | collective-permute-start | bytes 49160 | tf_op jit(solution)/shard_map/ppermute | solution.py:270
  63.2 8.1 %collective-permute-start.1 = (f32[32,128]{1,0:T(8,128)S(1)}, f32[32,128]{1,0:T(8,128)S(1)}, u32[]{:S(2)}, u32[]{:S(2)}) collective-permute-start(f32[32,128]{1,0:T(8,128)S(1)} %constant_dynamic-update-slice_fusion), channel_id=1, source_target_pairs={{0,16},{2,18},{4,20},{6,22},{8,24},{10,26},{12,28},{14,30},{16,0},... | collective-permute-start | bytes 49160 | tf_op jit(solution)/shard_map/ppermute | solution.py:270
  63.2 8.1 %collective-permute-start = (f32[32,128]{1,0:T(8,128)S(1)}, f32[32,128]{1,0:T(8,128)S(1)}, u32[]{:S(2)}, u32[]{:S(2)}) collective-permute-start(f32[32,128]{1,0:T(8,128)S(1)} %constant_dynamic-update-slice_fusion), channel_id=1, source_target_pairs={{0,8},{2,10},{4,12},{6,14},{8,0},{10,2},{12,4},{14,6},{16,24},{18,... | collective-permute-start | bytes 49160 | tf_op jit(solution)/shard_map/ppermute | solution.py:270
  71.3 5.9 %collective-permute-start.5 = (f32[4,32,128]{2,1,0:T(8,128)S(1)}, f32[4,32,128]{2,1,0:T(8,128)S(1)}, u32[]{:S(2)}, u32[]{:S(2)}) collective-permute-start(f32[4,32,128]{2,1,0:T(8,128)S(1)} %pad_maximum_fusion.rest_2_), channel_id=1, source_target_pairs={{0,6},{2,4},{4,2},{6,0},{8,14},{10,12},{12,10},{14,8},{16,22},{18,... | collective-permute-start | bytes 196616 | tf_op jit(solution)/shard_map/ppermute | solution.py:270
  73.7 4.3 %collective-permute-start.4 = (f32[4,32,128]{2,1,0:T(8,128)S(1)}, f32[4,32,128]{2,1,0:T(8,128)S(1)}, u32[]{:S(2)}, u32[]{:S(2)}) collective-permute-start(f32[4,32,128]{2,1,0:T(8,128)S(1)} %pad_maximum_fusion.rest_2_), channel_id=1, source_target_pairs={{0,4},{2,6},{4,0},{6,2},{8,12},{10,14},{12,8},{14,10},{16,20},{18,... | collective-permute-start | bytes 196616 | tf_op jit(solution)/shard_map/ppermute | solution.py:270
  74.3 4.3 %collective-permute-start.3 = (f32[4,32,128]{2,1,0:T(8,128)S(1)}, f32[4,32,128]{2,1,0:T(8,128)S(1)}, u32[]{:S(2)}, u32[]{:S(2)}) collective-permute-start(f32[4,32,128]{2,1,0:T(8,128)S(1)} %pad_maximum_fusion.rest_2_), channel_id=1, source_target_pairs={{0,2},{2,0},{4,6},{6,4},{8,10},{10,8},{12,14},{14,12},{16,18},{18,... | collective-permute-start | bytes 196616 | tf_op jit(solution)/shard_map/ppermute | solution.py:270

commit v4 on v2

--- a/solution.py
+++ b/solution.py
@@ -139,8 +139,8 @@
     return dot(values_high, high) + (dot(values_low, high) + dot(values_high, low))
 
 
-def pack_kernel(first, skip, query, key, value, filt, taps, grad, out, *scratch):
-    *held, arrived = scratch
+def pack_kernel(me, first, skip, query, key, value, filt, taps, grad, *rest):
+    outs, held, packed, arrived = rest[:-8], rest[-8:-2], rest[-2], rest[-1]
     copies = [
         pltpu.make_async_copy(source, target, arrived.at[i])
         for i, (source, target) in enumerate(zip((key, value, query, grad, filt, taps), held))
@@ -149,13 +149,10 @@
         copy.start()
     key, value, query, grad, filt, taps = held
     rows, channels = query.shape
+    blocks, _, share, _ = packed.shape
 
     def put(a, array):
-        turned = array.T
-        if len(out.shape) == 4:
-            out[:, a] = turned.reshape(out.shape[0], out.shape[2], rows)
-        else:
-            out[a] = turned
+        packed[:, a] = array.T.reshape(blocks, share, rows)
 
     copies[0].wait()
     copies[1].wait()
@@ -168,10 +165,16 @@
     row = lax.broadcasted_iota(jnp.int32, (rows, channels), 0)
     extra = taps[...] + jnp.where(row == 0, skip[...], 0.0)
     put(1, filt[...] + jnp.where(first[0] == 1, extra, 0.0))
-
-
-def mix_kernel(matrices, twists, arrays, out, taps, spectra, results, *, grad_scale):
-    blocks, _, channels, rows = arrays.shape
+    for distance, out in enumerate(outs):
+        out[...] = packed[me[0] ^ distance]
+
+
+def mix_kernel(me, matrices, twists, *rest, blocks, grad_scale):
+    parts, outs = rest[:blocks], rest[blocks : 2 * blocks]
+    arrays, spectra, results = rest[2 * blocks :]
+    _, _, channels, rows = arrays.shape
+    for distance, part in enumerate(parts):
+        arrays[me[0] ^ distance] = part[...]
     for a in range(3):
         for low in range(0, channels, 8):
             part = pl.ds(low, 8)
@@ -214,17 +217,26 @@
             values = padded_bins_back(bins, blocks)
             for j in range(blocks):
                 value = values[j] * grad_scale if a == 2 else values[j]
-                out[j, a, pl.ds(low, 8), :] = value
-                if a == 2 and j == 0:
-                    taps[pl.ds(low, 8), :] = value
-
-
-def unpack_kernel(me, query, key, value, grad, parts, first_lags, mixed, dquery, dkey, dvalue, dfilter, dtaps, dskip, ordered, *, flips):
+                arrays[j, a, pl.ds(low, 8), :] = value
+    for distance, out in enumerate(outs):
+        out[:3] = arrays[me[0] ^ distance]
+        if out.shape[0] == 4:
+            out[3] = arrays[0, 2]
+
+
+def unpack_kernel(me, query, key, value, grad, *rest, blocks, low, lag_place):
+    parts, rest = rest[:blocks], rest[blocks:]
+    mixed, dquery, dkey, dvalue, dfilter, dtaps, dskip, arrays, first_lags = rest
     rows, channels = query.shape
-    blocks, share = first_lags.shape[:2]
+    for distance, part in enumerate(parts):
+        arrays[me[0] ^ distance] = part[:3]
+        if distance < low:
+            for far in range(blocks // low):
+                holder, place = lag_place(distance, far)
+                first_lags[me[0] ^ (far * low + distance)] = parts[holder][place]
 
     def whole(a):
-        return parts[:, a].reshape(channels, rows).T
+        return arrays[:, a].reshape(channels, rows).T
 
     mixer = whole(0)
     mixed[...] = query[...].astype(jnp.float32) * mixer
@@ -233,16 +245,12 @@
     dkey[...] = product_grad * value[...].astype(jnp.float32)
     dvalue[...] = product_grad * key[...].astype(jnp.float32)
     dfilter[...] = whole(2)
-    own = sum(((me[0] >> bit) & 1) * flipped for bit, flipped in enumerate(flips))
-    for source in range(blocks):
-        place = sum(flipped for bit, flipped in enumerate(flips) if source >> bit & 1)
-        ordered[source * share : (source + 1) * share, :] = first_lags[own ^ place]
-    turned = ordered[...].T
+    turned = first_lags[...].reshape(channels, rows).T
     dtaps[...] = turned
     dskip[...] = turned[0:1, :]
 
 
-def call(kernel, name, out_shape, places, scratch=(), flops=0, size=0):
+def call(kernel, name, out_shape, places, scratch=(), flops=0, size=0, limit=VMEM_LIMIT):
     vmem = pl.BlockSpec(memory_space=pltpu.VMEM)
     return pl.pallas_call(
         kernel,
@@ -251,75 +259,96 @@
         in_specs=[pl.BlockSpec(memory_space=place) for place in places],
         out_specs=jax.tree.map(lambda _: vmem, out_shape),
         scratch_shapes=list(scratch),
-        compiler_params=pltpu.CompilerParams(vmem_limit_bytes=VMEM_LIMIT),
+        compiler_params=pltpu.CompilerParams(vmem_limit_bytes=limit),
         cost_estimate=pl.CostEstimate(flops=flops, bytes_accessed=size, transcendentals=0),
     )
 
 
-def gather_by_distance(value, axis):
-    count = lax.axis_size(axis)
-    gathered = value[None]
-    flips = {}
-    for bit in range(count.bit_length() - 2, -1, -1):
-        flips[bit] = gathered.shape[0]
-        pairs = [(i, i ^ (1 << bit)) for i in range(count)]
-        gathered = jnp.concatenate([gathered, lax.ppermute(gathered, axis, pairs)], axis=0)
-    return gathered, [flips[bit] for bit in range(len(flips))]
+def exchange(value, axis, distance):
+    return lax.ppermute(value, axis, [(i, i ^ distance) for i in range(lax.axis_size(axis))])
+
+
+def send_all(parts, axis):
+    received = list(parts)
+    for distance in range(len(parts) - 1, 0, -1):
+        received[distance] = exchange(parts[distance], axis, distance)
+    return received
+
+
+def send_all_with_lags(parts, axis, low):
+    received = list(parts)
+    for distance in range(len(parts) - 1, low - 1, -1):
+        received[distance] = exchange(parts[distance], axis, distance)
+    lags = [received[far][3:4] for far in range(0, len(parts), low)]
+    for distance in range(low - 1, 0, -1):
+        payload = jnp.concatenate([parts[distance]] + lags, axis=0)
+        received[distance] = exchange(payload, axis, distance)
+    return received
 
 
 def body(query, key, value, implicit_filter, explicit_taps, skip_gain, out_grad):
     rows, channels = query.shape
     blocks = lax.axis_size("ctx")
     share = channels // blocks
+    direct = share % 8 == 0
     padded = -(-share // 8) * 8
+    low = 1 << (blocks.bit_length() - 1) // 2 if direct else 1
     f32 = jnp.float32
     shape = functools.partial(jax.ShapeDtypeStruct, dtype=f32)
     grad_scale = 1.0 / math.sqrt(blocks * rows)
-    me = lax.axis_index("ctx").astype(jnp.int32).reshape(1)
-    first = (me == 0).astype(jnp.int32)
-    direct = share == padded
-
-    packed_shape = (blocks, 3, share, rows) if direct else (3, channels, rows)
+    index = lax.axis_index("ctx").astype(jnp.int32).reshape(1)
+    first = (index == 0).astype(jnp.int32)
+    me = index if direct else jnp.zeros_like(index)
+
     half = pltpu.VMEM((rows, channels), jnp.bfloat16)
     full = pltpu.VMEM((rows, channels), f32)
-    packed = call(
+    parts = call(
         pack_kernel,
         "pack",
-        shape(packed_shape),
-        (pltpu.SMEM, pltpu.VMEM) + (pltpu.HBM,) * 6,
-        scratch=(half,) * 4 + (full,) * 2 + (pltpu.SemaphoreType.DMA((6,)),),
+        (shape((3, share, rows)),) * blocks,
+        (pltpu.SMEM, pltpu.SMEM, pltpu.VMEM) + (pltpu.HBM,) * 6,
+        scratch=(half,) * 4 + (full,) * 2 + (pltpu.VMEM((blocks, 3, share, rows), f32), pltpu.SemaphoreType.DMA((6,))),
         size=16 * rows * channels,
-    )(first, skip_gain.reshape(1, channels), query, key, value, implicit_filter, explicit_taps, out_grad)
-    if not direct:
-        packed = packed.reshape(3, blocks, share, rows).swapaxes(0, 1)
-    arrays = lax.all_to_all(packed, "ctx", 0, 0, tiled=True)
-    if not direct:
-        arrays = jnp.pad(arrays, ((0, 0), (0, 0), (0, padded - share), (0, 0)))
+        limit=None,
+    )(me, first, skip_gain.reshape(1, channels), query, key, value, implicit_filter, explicit_taps, out_grad)
+    if direct:
+        parts = send_all(parts, "ctx")
+    else:
+        arrays = lax.all_to_all(jnp.stack(parts), "ctx", 0, 0, tiled=True)
+        parts = list(jnp.pad(arrays, ((0, 0), (0, 0), (0, padded - share), (0, 0))))
+
     matrices, twists = tables(blocks, rows)
     height = (blocks + 1) * padded
     scratch = pltpu.VMEM((3, height, 2 * rows), f32)
-    results, first_lags = call(
-        functools.partial(mix_kernel, grad_scale=grad_scale),
+    depth = [4 if distance % low == 0 else 3 for distance in range(blocks)]
+    parts = call(
+        functools.partial(mix_kernel, blocks=blocks, grad_scale=grad_scale),
         "mix",
-        (shape((blocks, 3, padded, rows)), shape((padded, rows))),
-        (pltpu.VMEM,) * 3,
-        scratch=(scratch, scratch),
+        tuple(shape((count, padded, rows)) for count in depth),
+        (pltpu.SMEM,) + (pltpu.VMEM,) * (2 + blocks),
+        scratch=(pltpu.VMEM((blocks, 3, padded, rows), f32), scratch, scratch),
         flops=36 * height * (2 * rows) ** 2,
         size=24 * blocks * padded * rows,
-    )(jnp.asarray(matrices), jnp.asarray(twists), arrays)
-    if not direct:
-        results, first_lags = results[:, :, :share], first_lags[:share]
-    parts = lax.all_to_all(results, "ctx", 0, 0, tiled=True)
-    first_lags, flips = gather_by_distance(first_lags, "ctx")
+    )(me, jnp.asarray(matrices), jnp.asarray(twists), *parts)
+    if direct:
+        parts = send_all_with_lags(parts, "ctx", low)
+    else:
+        parts = list(lax.all_to_all(jnp.stack(parts)[:, :, :share], "ctx", 0, 0, tiled=True))
+
+    def lag_place(near, far):
+        if near == 0:
+            return far * low, 3
+        return near, 3 + far
+
     full = shape((rows, channels))
     outs = call(
-        functools.partial(unpack_kernel, flips=flips),
+        functools.partial(unpack_kernel, blocks=blocks, low=low, lag_place=lag_place),
         "unpack",
         (full,) * 6 + (shape((1, channels)),),
-        (pltpu.SMEM,) + (pltpu.VMEM,) * 6,
-        scratch=(pltpu.VMEM((channels, rows), f32),),
+        (pltpu.SMEM,) + (pltpu.VMEM,) * (4 + blocks),
+        scratch=(pltpu.VMEM((blocks, 3, share, rows), f32), pltpu.VMEM((blocks, share, rows), f32)),
         size=48 * rows * channels,
-    )(me, query, key, value, out_grad, parts, first_lags)
+    )(me, query, key, value, out_grad, *parts)
     return (*outs[:6], outs[6].reshape(channels))
 
 

time: 79.4 us -> 88.7 us (1.12)
  starting transfers between devices: 9.36 us -> 57.1 us
  blocking collectives: 29.5 us -> 0 us
  local copies, waits for them, and re-layouts: 6.25 us -> 0.87 us
  waiting for transfers between devices: 27.4 us -> 22.9 us
  Pallas kernels: 5.69 us -> 6.84 us
    ppermute x4 -> x30, starting transfers between devices: 5.75 us -> 57.1 us  [exchange(): lax.ppermute(value, axis, [(i, i ^ distance) for i in range(lax.axis_size...]
    all_to_all x1 -> x0, blocking collectives: 29.5 us -> none  [body(): arrays = lax.all_to_all(packed, 'ctx', 0, 0, tiled=True)]
    unnamed x30 -> x19, local copies, waits for them, and re-layouts: 6.24 us -> 0.86 us
    ppermute x4 -> x30, waiting for transfers between devices: 27.4 us -> 22.9 us  [exchange(): lax.ppermute(value, axis, [(i, i ^ distance) for i in range(lax.axis_size...]
    all_to_all x1 -> x0, starting transfers between devices: 3.61 us -> none  [body(): parts = lax.all_to_all(results, 'ctx', 0, 0, tiled=True)]
    pallas_call x3, Pallas kernels: 5.69 us -> 6.84 us  [the longest x1 3.09 us: body(): call(pack_kernel, 'pack', (shape((3, share, rows)),) * blocks, (pltpu.SME...]
  transfers between devices with their start and end apart: 5 -> 30, of which waited for: 4 -> 8; matrix products, arithmetic and copies ran while one was open for 0% -> 0% of each run, Pallas kernels for 0% -> 0%
where the time goes in v4:
time: 88.7 us; the launch traced here: 88.5 us
  starting transfers between devices  57.1 us (64%)
  waiting for transfers between devices  22.9 us (26%)
  Pallas kernels  6.84 us (8%)
    ppermute x30, starting transfers between devices, exchange(): lax.ppermute(value, axis, [(i, i ^ distance) for i in range(lax.axis_size...  57.1 us
    ppermute x30, waiting for transfers between devices, exchange(): lax.ppermute(value, axis, [(i, i ^ distance) for i in range(lax.axis_size...  22.9 us
    pallas_call x1, Pallas kernels, body(): call(pack_kernel, 'pack', (shape((3, share, rows)),) * blocks, (pltpu.SME...  3.09 us
    pallas_call x1, Pallas kernels, body(): call(functools.partial(mix_kernel, blocks=blocks, grad_scale=grad_scale),...  2.38 us
  transfers between devices with their start and end apart: 30, of which 8 were waited for; matrix products, arithmetic and copies ran while one was open for 0% of the time, Pallas kernels for 0%

profile of v4, /device:TPU:0, one launch (start us, length us, event | category | flops | bytes accessed | tf_op | source)
XLA Modules:
  0.0 88.5 jit_solution(8204121415257460707)
XLA Ops:
  0.6 0.0 copy-start.5
  0.7 0.0 copy-start.6
  0.7 3.1 %pack.1 = (f32[3,32,128]{2,1,0:T(8,128)}, f32[3,32,128]{2,1,0:T(8,128)}, f32[3,32,128]{2,1,0:T(8,128)}, f32[3,32,128]{2,1,0:T(8,128)}, f32[3,32,128]{2,1,0:T(8,1...) custom-call(s32[1]{0:T(128)} %bitcast.me, ...), custom_call_target="tpu_custom_call" | custom-call | bytes 1048576 | tf_op jit(solution)/shard_map/pack/pallas_call | solution.py:305
  3.8 3.0 %collective-permute-start = (f32[3,32,128]{2,1,0:T(8,128)}, f32[3,32,128]{2,1,0:T(8,128)S(1)}, u32[]{:S(2)}, u32[]{:S(2)}) collective-permute-start(f32[3,32,128]{2,1,0:T(8,128)} %get-tuple-element.47), channel_id=1, source_target_pairs={{0,2},{2,0},{4,6},{6,4},{8,10},{10,8},{12,14},{14,12},{16,18},{18,... | collective-permute-start | bytes 147464 | tf_op jit(solution)/shard_map/ppermute | solution.py:268
  6.8 1.5 %collective-permute-start.1 = (f32[3,32,128]{2,1,0:T(8,128)}, f32[3,32,128]{2,1,0:T(8,128)S(1)}, u32[]{:S(2)}, u32[]{:S(2)}) collective-permute-start(f32[3,32,128]{2,1,0:T(8,128)} %get-tuple-element.48), channel_id=1, source_target_pairs={{0,4},{2,6},{4,0},{6,2},{8,12},{10,14},{12,8},{14,10},{16,20},{18,... | collective-permute-start | bytes 147464 | tf_op jit(solution)/shard_map/ppermute | solution.py:268
  8.3 0.0 collective-permute-start.2
  8.3 2.0 %collective-permute-start.3 = (f32[3,32,128]{2,1,0:T(8,128)}, f32[3,32,128]{2,1,0:T(8,128)S(1)}, u32[]{:S(2)}, u32[]{:S(2)}) collective-permute-start(f32[3,32,128]{2,1,0:T(8,128)} %get-tuple-element.50), channel_id=1, source_target_pairs={{0,8},{2,10},{4,12},{6,14},{8,0},{10,2},{12,4},{14,6},{16,24},{18,... | collective-permute-start | bytes 147464 | tf_op jit(solution)/shard_map/ppermute | solution.py:268
  10.3 1.4 %collective-permute-start.4 = (f32[3,32,128]{2,1,0:T(8,128)}, f32[3,32,128]{2,1,0:T(8,128)S(1)}, u32[]{:S(2)}, u32[]{:S(2)}) collective-permute-start(f32[3,32,128]{2,1,0:T(8,128)} %get-tuple-element.51), channel_id=1, source_target_pairs={{0,10},{2,8},{4,14},{6,12},{8,2},{10,0},{12,6},{14,4},{16,26},{18,... | collective-permute-start | bytes 147464 | tf_op jit(solution)/shard_map/ppermute | solution.py:268
  11.7 0.0 collective-permute-done.rest_1_
  11.7 2.5 %collective-permute-start.5 = (f32[3,32,128]{2,1,0:T(8,128)}, f32[3,32,128]{2,1,0:T(8,128)S(1)}, u32[]{:S(2)}, u32[]{:S(2)}) collective-permute-start(f32[3,32,128]{2,1,0:T(8,128)} %get-tuple-element.52), channel_id=1, source_target_pairs={{0,12},{2,14},{4,8},{6,10},{8,4},{10,6},{12,0},{14,2},{16,28},{18,... | collective-permute-start | bytes 147464 | tf_op jit(solution)/shard_map/ppermute | solution.py:268
  14.3 0.0 collective-permute-done.1.rest_2_
  14.3 0.0 collective-permute-start.6
  14.3 0.0 collective-permute-done.2.rest_3_
  14.3 2.9 %collective-permute-start.7 = (f32[3,32,128]{2,1,0:T(8,128)}, f32[3,32,128]{2,1,0:T(8,128)S(1)}, u32[]{:S(2)}, u32[]{:S(2)}) collective-permute-start(f32[3,32,128]{2,1,0:T(8,128)} %get-tuple-element.54), channel_id=1, source_target_pairs={{0,16},{2,18},{4,20},{6,22},{8,24},{10,26},{12,28},{14,30},{16,0},... | collective-permute-start | bytes 147464 | tf_op jit(solution)/shard_map/ppermute | solution.py:268
  17.2 0.0 collective-permute-done.3.rest_4_
  17.2 1.3 %collective-permute-start.8 = (f32[3,32,128]{2,1,0:T(8,128)}, f32[3,32,128]{2,1,0:T(8,128)S(1)}, u32[]{:S(2)}, u32[]{:S(2)}) collective-permute-start(f32[3,32,128]{2,1,0:T(8,128)} %get-tuple-element.55), channel_id=1, source_target_pairs={{0,18},{2,16},{4,22},{6,20},{8,26},{10,24},{12,30},{14,28},{16,2},... | collective-permute-start | bytes 147464 | tf_op jit(solution)/shard_map/ppermute | solution.py:268
  18.5 0.0 collective-permute-done.4.rest_5_
  18.5 3.5 %collective-permute-start.9 = (f32[3,32,128]{2,1,0:T(8,128)}, f32[3,32,128]{2,1,0:T(8,128)S(1)}, u32[]{:S(2)}, u32[]{:S(2)}) collective-permute-start(f32[3,32,128]{2,1,0:T(8,128)} %get-tuple-element.56), channel_id=1, source_target_pairs={{0,20},{2,22},{4,16},{6,18},{8,28},{10,30},{12,24},{14,26},{16,4},... | collective-permute-start | bytes 147464 | tf_op jit(solution)/shard_map/ppermute | solution.py:268
  22.0 0.0 collective-permute-done.5.rest_6_
  22.0 0.0 collective-permute-start.10
  22.1 0.0 collective-permute-done.6.rest_7_
  22.1 3.8 %collective-permute-start.11 = (f32[3,32,128]{2,1,0:T(8,128)}, f32[3,32,128]{2,1,0:T(8,128)S(1)}, u32[]{:S(2)}, u32[]{:S(2)}) collective-permute-start(f32[3,32,128]{2,1,0:T(8,128)} %get-tuple-element.58), channel_id=1, source_target_pairs={{0,24},{2,26},{4,28},{6,30},{8,16},{10,18},{12,20},{14,22},{16,8},... | collective-permute-start | bytes 147464 | tf_op jit(solution)/shard_map/ppermute | solution.py:268
  25.9 0.0 collective-permute-done.7.rest_8_
  25.9 1.2 %collective-permute-start.12 = (f32[3,32,128]{2,1,0:T(8,128)}, f32[3,32,128]{2,1,0:T(8,128)S(1)}, u32[]{:S(2)}, u32[]{:S(2)}) collective-permute-start(f32[3,32,128]{2,1,0:T(8,128)} %get-tuple-element.59), channel_id=1, source_target_pairs={{0,26},{2,24},{4,30},{6,28},{8,18},{10,16},{12,22},{14,20},{16,10}... | collective-permute-start | bytes 147464 | tf_op jit(solution)/shard_map/ppermute | solution.py:268
  27.1 0.0 collective-permute-done.8.rest_9_
  27.1 4.6 %collective-permute-start.13 = (f32[3,32,128]{2,1,0:T(8,128)}, f32[3,32,128]{2,1,0:T(8,128)S(1)}, u32[]{:S(2)}, u32[]{:S(2)}) collective-permute-start(f32[3,32,128]{2,1,0:T(8,128)} %get-tuple-element.60), channel_id=1, source_target_pairs={{0,28},{2,30},{4,24},{6,26},{8,20},{10,22},{12,16},{14,18},{16,12}... | collective-permute-start | bytes 147464 | tf_op jit(solution)/shard_map/ppermute | solution.py:268
  31.6 0.0 collective-permute-done.9.rest_10_
  31.6 0.4 collective-permute-start.14
  32.0 0.0 collective-permute-done.10.rest_11_
  32.0 0.0 collective-permute-done.11.rest_12_
  32.0 1.0 %collective-permute-done.12.rest_13_ = f32[3,32,128]{2,1,0:T(8,128)S(1)} collective-permute-done((f32[3,32,128]{2,1,0:T(8,128)}, f32[3,32,128]{2,1,0:T(8,128)S(1)}, u32[]{:S(2)}, u32[]{:S(2)}) %collective-permute-start.12) | collective-permute-done | bytes 49184 | tf_op jit(solution)/shard_map/ppermute | solution.py:268
  33.0 2.0 %collective-permute-done.13.rest_14_ = f32[3,32,128]{2,1,0:T(8,128)S(1)} collective-permute-done((f32[3,32,128]{2,1,0:T(8,128)}, f32[3,32,128]{2,1,0:T(8,128)S(1)}, u32[]{:S(2)}, u32[]{:S(2)}) %collective-permute-start.13) | collective-permute-done | bytes 49184 | tf_op jit(solution)/shard_map/ppermute | solution.py:268
  35.0 4.6 %collective-permute-done.14.rest_15_ = f32[3,32,128]{2,1,0:T(8,128)S(1)} collective-permute-done((f32[3,32,128]{2,1,0:T(8,128)}, f32[3,32,128]{2,1,0:T(8,128)S(1)}, u32[]{:S(2)}, u32[]{:S(2)}) %collective-permute-start.14) | collective-permute-done | bytes 49184 | tf_op jit(solution)/shard_map/ppermute | solution.py:268
  39.5 0.8 copy-done.4
  40.3 2.4 %mix.1 = (f32[4,32,128]{2,1,0:T(8,128)S(1)}, f32[3,32,128]{2,1,0:T(8,128)S(1)}, f32[3,32,128]{2,1,0:T(8,128)S(1)}, f32[3,32,128]{2,1,0:T(8,128)S(1)}, f32[4,32,1...) custom-call(s32[1]{0:T(128)} %bitcast.me, ...), custom_call_target="tpu_custom_call" | custom-call | flops 1283457024 | bytes 1572864 | tf_op jit(solution)/shard_map/mix/pallas_call | solution.py:324
  42.7 0.1 collective-permute-start.21
  42.8 1.9 %collective-permute-start.22 = (f32[3,32,128]{2,1,0:T(8,128)S(1)}, f32[3,32,128]{2,1,0:T(8,128)S(1)}, u32[]{:S(2)}, u32[]{:S(2)}) collective-permute-start(f32[3,32,128]{2,1,0:T(8,128)S(1)} %get-tuple-element.70), channel_id=1, source_target_pairs={{0,12},{2,14},{4,8},{6,10},{8,4},{10,6},{12,0},{14,2},{16,28},{18,... | collective-permute-start | bytes 147464 | tf_op jit(solution)/shard_map/ppermute | solution.py:268
  44.7 1.0 %collective-permute-start.23 = (f32[3,32,128]{2,1,0:T(8,128)S(1)}, f32[3,32,128]{2,1,0:T(8,128)S(1)}, u32[]{:S(2)}, u32[]{:S(2)}) collective-permute-start(f32[3,32,128]{2,1,0:T(8,128)S(1)} %get-tuple-element.71), channel_id=1, source_target_pairs={{0,14},{2,12},{4,10},{6,8},{8,6},{10,4},{12,2},{14,0},{16,30},{18,... | collective-permute-start | bytes 147464 | tf_op jit(solution)/shard_map/ppermute | solution.py:268
  45.8 1.6 %collective-permute-start.24 = (f32[3,32,128]{2,1,0:T(8,128)S(1)}, f32[3,32,128]{2,1,0:T(8,128)S(1)}, u32[]{:S(2)}, u32[]{:S(2)}) collective-permute-start(f32[3,32,128]{2,1,0:T(8,128)S(1)} %get-tuple-element.72), channel_id=1, source_target_pairs={{0,18},{2,16},{4,22},{6,20},{8,26},{10,24},{12,30},{14,28},{16,2},... | collective-permute-start | bytes 147464 | tf_op jit(solution)/shard_map/ppermute | solution.py:268
  47.4 1.3 %collective-permute-start.15 = (f32[4,32,128]{2,1,0:T(8,128)S(1)}, f32[4,32,128]{2,1,0:T(8,128)S(1)}, u32[]{:S(2)}, u32[]{:S(2)}) collective-permute-start(f32[4,32,128]{2,1,0:T(8,128)S(1)} %get-tuple-element.64), channel_id=1, source_target_pairs={{0,8},{2,10},{4,12},{6,14},{8,0},{10,2},{12,4},{14,6},{16,24},{18,... | collective-permute-start | bytes 196616 | tf_op jit(solution)/shard_map/ppermute | solution.py:268
  48.7 0.0 copy-start.1
  48.7 0.0 copy-start
  48.7 3.5 %collective-permute-done.15.rest_4_ = f32[4,32,128]{2,1,0:T(8,128)S(1)} collective-permute-done((f32[4,32,128]{2,1,0:T(8,128)S(1)}, f32[4,32,128]{2,1,0:T(8,128)S(1)}, u32[]{:S(2)}, u32[]{:S(2)}) %collective-permute-start.15) | collective-permute-done | bytes 65568 | tf_op jit(solution)/shard_map/ppermute | solution.py:268
  52.2 2.1 %collective-permute-start.16 = (f32[4,32,128]{2,1,0:T(8,128)S(1)}, f32[4,32,128]{2,1,0:T(8,128)S(1)}, u32[]{:S(2)}, u32[]{:S(2)}) collective-permute-start(f32[4,32,128]{2,1,0:T(8,128)S(1)} %get-tuple-element.65), channel_id=1, source_target_pairs={{0,16},{2,18},{4,20},{6,22},{8,24},{10,26},{12,28},{14,30},{16,0},... | collective-permute-start | bytes 196616 | tf_op jit(solution)/shard_map/ppermute | solution.py:268
  54.3 3.7 %collective-permute-done.16.rest_8_ = f32[4,32,128]{2,1,0:T(8,128)S(1)} collective-permute-done((f32[4,32,128]{2,1,0:T(8,128)S(1)}, f32[4,32,128]{2,1,0:T(8,128)S(1)}, u32[]{:S(2)}, u32[]{:S(2)}) %collective-permute-start.16) | collective-permute-done | bytes 65568 | tf_op jit(solution)/shard_map/ppermute | solution.py:268
  58.0 3.6 %collective-permute-start.17 = (f32[4,32,128]{2,1,0:T(8,128)S(1)}, f32[4,32,128]{2,1,0:T(8,128)S(1)}, u32[]{:S(2)}, u32[]{:S(2)}) collective-permute-start(f32[4,32,128]{2,1,0:T(8,128)S(1)} %get-tuple-element.66), channel_id=1, source_target_pairs={{0,24},{2,26},{4,28},{6,30},{8,16},{10,18},{12,20},{14,22},{16,8},... | collective-permute-start | bytes 196616 | tf_op jit(solution)/shard_map/ppermute | solution.py:268
  61.6 2.5 %collective-permute-done.17.rest_12_ = f32[4,32,128]{2,1,0:T(8,128)S(1)} collective-permute-done((f32[4,32,128]{2,1,0:T(8,128)S(1)}, f32[4,32,128]{2,1,0:T(8,128)S(1)}, u32[]{:S(2)}, u32[]{:S(2)}) %collective-permute-start.17) | collective-permute-done | bytes 65568 | tf_op jit(solution)/shard_map/ppermute | solution.py:268
  64.1 0.0 collective-permute-start.25
  64.1 0.0 collective-permute-done.21.rest_5_
  64.1 2.1 %collective-permute-start.20 = (f32[7,32,128]{2,1,0:T(8,128)S(1)}, f32[7,32,128]{2,1,0:T(8,128)S(1)}, u32[]{:S(2)}, u32[]{:S(2)}) collective-permute-start(f32[7,32,128]{2,1,0:T(8,128)S(1)} %get-tuple-element.85), channel_id=1, source_target_pairs={{0,6},{2,4},{4,2},{6,0},{8,14},{10,12},{12,10},{14,8},{16,22},{18,... | collective-permute-start | bytes 344072 | tf_op jit(solution)/shard_map/ppermute | solution.py:268
  66.3 0.0 collective-permute-done.22.rest_6_
  66.3 1.1 %collective-permute-start.19 = (f32[7,32,128]{2,1,0:T(8,128)S(1)}, f32[7,32,128]{2,1,0:T(8,128)S(1)}, u32[]{:S(2)}, u32[]{:S(2)}) collective-permute-start(f32[7,32,128]{2,1,0:T(8,128)S(1)} %get-tuple-element.86), channel_id=1, source_target_pairs={{0,4},{2,6},{4,0},{6,2},{8,12},{10,14},{12,8},{14,10},{16,20},{18,... | collective-permute-start | bytes 344072 | tf_op jit(solution)/shard_map/ppermute | solution.py:268
  67.4 0.0 collective-permute-done.23.rest_7_
  67.4 0.3 collective-permute-start.18
  67.7 4.9 %collective-permute-start.26 = (f32[3,32,128]{2,1,0:T(8,128)S(1)}, f32[3,32,128]{2,1,0:T(8,128)S(1)}, u32[]{:S(2)}, u32[]{:S(2)}) collective-permute-start(f32[3,32,128]{2,1,0:T(8,128)S(1)} %get-tuple-element.74), channel_id=1, source_target_pairs={{0,22},{2,20},{4,18},{6,16},{8,30},{10,28},{12,26},{14,24},{16,6},... | collective-permute-start | bytes 147464 | tf_op jit(solution)/shard_map/ppermute | solution.py:268
  72.6 0.0 collective-permute-done.25.rest_10_
  72.6 3.3 %collective-permute-start.27 = (f32[3,32,128]{2,1,0:T(8,128)S(1)}, f32[3,32,128]{2,1,0:T(8,128)S(1)}, u32[]{:S(2)}, u32[]{:S(2)}) collective-permute-start(f32[3,32,128]{2,1,0:T(8,128)S(1)} %get-tuple-element.75), channel_id=1, source_target_pairs={{0,26},{2,24},{4,30},{6,28},{8,18},{10,16},{12,22},{14,20},{16,10}... | collective-permute-start | bytes 147464 | tf_op jit(solution)/shard_map/ppermute | solution.py:268
  76.0 0.0 collective-permute-done.26.rest_11_
  76.0 2.1 %collective-permute-start.28 = (f32[3,32,128]{2,1,0:T(8,128)S(1)}, f32[3,32,128]{2,1,0:T(8,128)S(1)}, u32[]{:S(2)}, u32[]{:S(2)}) collective-permute-start(f32[3,32,128]{2,1,0:T(8,128)S(1)} %get-tuple-element.76), channel_id=1, source_target_pairs={{0,28},{2,30},{4,24},{6,26},{8,20},{10,22},{12,16},{14,18},{16,12}... | collective-permute-start | bytes 147464 | tf_op jit(solution)/shard_map/ppermute | solution.py:268
  78.1 1.3 %collective-permute-done.27.rest_13_ = f32[3,32,128]{2,1,0:T(8,128)S(1)} collective-permute-done((f32[3,32,128]{2,1,0:T(8,128)S(1)}, f32[3,32,128]{2,1,0:T(8,128)S(1)}, u32[]{:S(2)}, u32[]{:S(2)}) %collective-permute-start.27) | collective-permute-done | bytes 49184 | tf_op jit(solution)/shard_map/ppermute | solution.py:268
  79.4 3.4 %collective-permute-start.29 = (f32[3,32,128]{2,1,0:T(8,128)S(1)}, f32[3,32,128]{2,1,0:T(8,128)S(1)}, u32[]{:S(2)}, u32[]{:S(2)}) collective-permute-start(f32[3,32,128]{2,1,0:T(8,128)S(1)} %get-tuple-element.77), channel_id=1, source_target_pairs={{0,30},{2,28},{4,26},{6,24},{8,22},{10,20},{12,18},{14,16},{16,14}... | collective-permute-start | bytes 147464 | tf_op jit(solution)/shard_map/ppermute | solution.py:268
  82.8 0.0 collective-permute-done.28.rest_14_
  82.8 4.3 %collective-permute-done.29.rest_15_ = f32[3,32,128]{2,1,0:T(8,128)S(1)} collective-permute-done((f32[3,32,128]{2,1,0:T(8,128)S(1)}, f32[3,32,128]{2,1,0:T(8,128)S(1)}, u32[]{:S(2)}, u32[]{:S(2)}) %collective-permute-start.29) | collective-permute-done | bytes 49184 | tf_op jit(solution)/shard_map/ppermute | solution.py:268
  87.2 1.4 %unpack.1 = (f32[128,512]{1,0:T(8,128)}, f32[128,512]{1,0:T(8,128)}, f32[128,512]{1,0:T(8,128)}, f32[128,512]{1,0:T(8,128)}, f32[128,512]{1,0:T(8,128)}, /*index=5*/f32[128,512]{1,0:T(8,128)}, f32[1,512]{1,0:T(1,128)}) custom-call(s32[1]{0:T(128)} %bitcast.me, bf16[128,512]{1,0:T(8,128)(2,1)S(1)} %copy-done, bf16[128,512]{1,0:T(8,128)(2,1)S(1)} %copy-done.1, ...), custom_call_target="tpu_custom_call" | custom-call | bytes 3145728 | tf_op jit(solution)/shard_map/unpack/pallas_call | solution.py:344
  (19 shorter events, 0.1 us)
Async XLA Ops:
  0.6 38.9 %copy-start.5 = (bf16[4,256,256]{2,1,0:T(8,128)(2,1)S(1)}, bf16[4,256,256]{2,1,0:T(8,128)(2,1)}, u32[]{:S(2)}) copy-start(bf16[4,256,256]{2,1,0:T(8,128)(2,1)} %constant.12.clone.matrices) | copy-start | bytes 1572868
  0.7 38.9 %copy-start.6 = (f32[17,4,128]{2,1,0:T(4,128)S(1)}, f32[17,4,128]{2,1,0:T(4,128)}, u32[]{:S(2)}) copy-start(f32[17,4,128]{2,1,0:T(4,128)} %constant.13.clone.twists) | copy-start | bytes 104452
  3.8 8.0 %collective-permute-start = (f32[3,32,128]{2,1,0:T(8,128)}, f32[3,32,128]{2,1,0:T(8,128)S(1)}, u32[]{:S(2)}, u32[]{:S(2)}) collective-permute-start(f32[3,32,128]{2,1,0:T(8,128)} %get-tuple-element.47), channel_id=1, source_target_pairs={{0,2},{2,0},{4,6},{6,4},{8,10},{10,8},{12,14},{14,12},{16,18},{18,... | collective-permute-start | bytes 147464 | tf_op jit(solution)/shard_map/ppermute | solution.py:268
  6.8 7.5 %collective-permute-start.1 = (f32[3,32,128]{2,1,0:T(8,128)}, f32[3,32,128]{2,1,0:T(8,128)S(1)}, u32[]{:S(2)}, u32[]{:S(2)}) collective-permute-start(f32[3,32,128]{2,1,0:T(8,128)} %get-tuple-element.48), channel_id=1, source_target_pairs={{0,4},{2,6},{4,0},{6,2},{8,12},{10,14},{12,8},{14,10},{16,20},{18,... | collective-permute-start | bytes 147464 | tf_op jit(solution)/shard_map/ppermute | solution.py:268
  8.3 6.0 %collective-permute-start.2 = (f32[3,32,128]{2,1,0:T(8,128)}, f32[3,32,128]{2,1,0:T(8,128)S(1)}, u32[]{:S(2)}, u32[]{:S(2)}) collective-permute-start(f32[3,32,128]{2,1,0:T(8,128)} %get-tuple-element.49), channel_id=1, source_target_pairs={{0,6},{2,4},{4,2},{6,0},{8,14},{10,12},{12,10},{14,8},{16,22},{18,... | collective-permute-start | bytes 147464 | tf_op jit(solution)/shard_map/ppermute | solution.py:268
  8.3 8.9 %collective-permute-start.3 = (f32[3,32,128]{2,1,0:T(8,128)}, f32[3,32,128]{2,1,0:T(8,128)S(1)}, u32[]{:S(2)}, u32[]{:S(2)}) collective-permute-start(f32[3,32,128]{2,1,0:T(8,128)} %get-tuple-element.50), channel_id=1, source_target_pairs={{0,8},{2,10},{4,12},{6,14},{8,0},{10,2},{12,4},{14,6},{16,24},{18,... | collective-permute-start | bytes 147464 | tf_op jit(solution)/shard_map/ppermute | solution.py:268
  10.3 8.1 %collective-permute-start.4 = (f32[3,32,128]{2,1,0:T(8,128)}, f32[3,32,128]{2,1,0:T(8,128)S(1)}, u32[]{:S(2)}, u32[]{:S(2)}) collective-permute-start(f32[3,32,128]{2,1,0:T(8,128)} %get-tuple-element.51), channel_id=1, source_target_pairs={{0,10},{2,8},{4,14},{6,12},{8,2},{10,0},{12,6},{14,4},{16,26},{18,... | collective-permute-start | bytes 147464 | tf_op jit(solution)/shard_map/ppermute | solution.py:268
  11.7 10.3 %collective-permute-start.5 = (f32[3,32,128]{2,1,0:T(8,128)}, f32[3,32,128]{2,1,0:T(8,128)S(1)}, u32[]{:S(2)}, u32[]{:S(2)}) collective-permute-start(f32[3,32,128]{2,1,0:T(8,128)} %get-tuple-element.52), channel_id=1, source_target_pairs={{0,12},{2,14},{4,8},{6,10},{8,4},{10,6},{12,0},{14,2},{16,28},{18,... | collective-permute-start | bytes 147464 | tf_op jit(solution)/shard_map/ppermute | solution.py:268
  14.3 7.8 %collective-permute-start.6 = (f32[3,32,128]{2,1,0:T(8,128)}, f32[3,32,128]{2,1,0:T(8,128)S(1)}, u32[]{:S(2)}, u32[]{:S(2)}) collective-permute-start(f32[3,32,128]{2,1,0:T(8,128)} %get-tuple-element.53), channel_id=1, source_target_pairs={{0,14},{2,12},{4,10},{6,8},{8,6},{10,4},{12,2},{14,0},{16,30},{18,... | collective-permute-start | bytes 147464 | tf_op jit(solution)/shard_map/ppermute | solution.py:268
  14.3 11.6 %collective-permute-start.7 = (f32[3,32,128]{2,1,0:T(8,128)}, f32[3,32,128]{2,1,0:T(8,128)S(1)}, u32[]{:S(2)}, u32[]{:S(2)}) collective-permute-start(f32[3,32,128]{2,1,0:T(8,128)} %get-tuple-element.54), channel_id=1, source_target_pairs={{0,16},{2,18},{4,20},{6,22},{8,24},{10,26},{12,28},{14,30},{16,0},... | collective-permute-start | bytes 147464 | tf_op jit(solution)/shard_map/ppermute | solution.py:268
  17.2 9.8 %collective-permute-start.8 = (f32[3,32,128]{2,1,0:T(8,128)}, f32[3,32,128]{2,1,0:T(8,128)S(1)}, u32[]{:S(2)}, u32[]{:S(2)}) collective-permute-start(f32[3,32,128]{2,1,0:T(8,128)} %get-tuple-element.55), channel_id=1, source_target_pairs={{0,18},{2,16},{4,22},{6,20},{8,26},{10,24},{12,30},{14,28},{16,2},... | collective-permute-start | bytes 147464 | tf_op jit(solution)/shard_map/ppermute | solution.py:268
  18.5 13.1 %collective-permute-start.9 = (f32[3,32,128]{2,1,0:T(8,128)}, f32[3,32,128]{2,1,0:T(8,128)S(1)}, u32[]{:S(2)}, u32[]{:S(2)}) collective-permute-start(f32[3,32,128]{2,1,0:T(8,128)} %get-tuple-element.56), channel_id=1, source_target_pairs={{0,20},{2,22},{4,16},{6,18},{8,28},{10,30},{12,24},{14,26},{16,4},... | collective-permute-start | bytes 147464 | tf_op jit(solution)/shard_map/ppermute | solution.py:268
  22.0 9.9 %collective-permute-start.10 = (f32[3,32,128]{2,1,0:T(8,128)}, f32[3,32,128]{2,1,0:T(8,128)S(1)}, u32[]{:S(2)}, u32[]{:S(2)}) collective-permute-start(f32[3,32,128]{2,1,0:T(8,128)} %get-tuple-element.57), channel_id=1, source_target_pairs={{0,22},{2,20},{4,18},{6,16},{8,30},{10,28},{12,26},{14,24},{16,6},... | collective-permute-start | bytes 147464 | tf_op jit(solution)/shard_map/ppermute | solution.py:268
  22.1 9.9 %collective-permute-start.11 = (f32[3,32,128]{2,1,0:T(8,128)}, f32[3,32,128]{2,1,0:T(8,128)S(1)}, u32[]{:S(2)}, u32[]{:S(2)}) collective-permute-start(f32[3,32,128]{2,1,0:T(8,128)} %get-tuple-element.58), channel_id=1, source_target_pairs={{0,24},{2,26},{4,28},{6,30},{8,16},{10,18},{12,20},{14,22},{16,8},... | collective-permute-start | bytes 147464 | tf_op jit(solution)/shard_map/ppermute | solution.py:268
  25.9 7.1 %collective-permute-start.12 = (f32[3,32,128]{2,1,0:T(8,128)}, f32[3,32,128]{2,1,0:T(8,128)S(1)}, u32[]{:S(2)}, u32[]{:S(2)}) collective-permute-start(f32[3,32,128]{2,1,0:T(8,128)} %get-tuple-element.59), channel_id=1, source_target_pairs={{0,26},{2,24},{4,30},{6,28},{8,18},{10,16},{12,22},{14,20},{16,10}... | collective-permute-start | bytes 147464 | tf_op jit(solution)/shard_map/ppermute | solution.py:268
  27.1 7.9 %collective-permute-start.13 = (f32[3,32,128]{2,1,0:T(8,128)}, f32[3,32,128]{2,1,0:T(8,128)S(1)}, u32[]{:S(2)}, u32[]{:S(2)}) collective-permute-start(f32[3,32,128]{2,1,0:T(8,128)} %get-tuple-element.60), channel_id=1, source_target_pairs={{0,28},{2,30},{4,24},{6,26},{8,20},{10,22},{12,16},{14,18},{16,12}... | collective-permute-start | bytes 147464 | tf_op jit(solution)/shard_map/ppermute | solution.py:268
  31.6 7.9 %collective-permute-start.14 = (f32[3,32,128]{2,1,0:T(8,128)}, f32[3,32,128]{2,1,0:T(8,128)S(1)}, u32[]{:S(2)}, u32[]{:S(2)}) collective-permute-start(f32[3,32,128]{2,1,0:T(8,128)} %get-tuple-element.61), channel_id=1, source_target_pairs={{0,30},{2,28},{4,26},{6,24},{8,22},{10,20},{12,18},{14,16},{16,14}... | collective-permute-start | bytes 147464 | tf_op jit(solution)/shard_map/ppermute | solution.py:268
  39.5 0.8 copy-start.4
  42.7 21.4 %collective-permute-start.21 = (f32[3,32,128]{2,1,0:T(8,128)S(1)}, f32[3,32,128]{2,1,0:T(8,128)S(1)}, u32[]{:S(2)}, u32[]{:S(2)}) collective-permute-start(f32[3,32,128]{2,1,0:T(8,128)S(1)} %get-tuple-element.69), channel_id=1, source_target_pairs={{0,10},{2,8},{4,14},{6,12},{8,2},{10,0},{12,6},{14,4},{16,26},{18,... | collective-permute-start | bytes 147464 | tf_op jit(solution)/shard_map/ppermute | solution.py:268
  42.8 23.5 %collective-permute-start.22 = (f32[3,32,128]{2,1,0:T(8,128)S(1)}, f32[3,32,128]{2,1,0:T(8,128)S(1)}, u32[]{:S(2)}, u32[]{:S(2)}) collective-permute-start(f32[3,32,128]{2,1,0:T(8,128)S(1)} %get-tuple-element.70), channel_id=1, source_target_pairs={{0,12},{2,14},{4,8},{6,10},{8,4},{10,6},{12,0},{14,2},{16,28},{18,... | collective-permute-start | bytes 147464 | tf_op jit(solution)/shard_map/ppermute | solution.py:268
  44.7 22.6 %collective-permute-start.23 = (f32[3,32,128]{2,1,0:T(8,128)S(1)}, f32[3,32,128]{2,1,0:T(8,128)S(1)}, u32[]{:S(2)}, u32[]{:S(2)}) collective-permute-start(f32[3,32,128]{2,1,0:T(8,128)S(1)} %get-tuple-element.71), channel_id=1, source_target_pairs={{0,14},{2,12},{4,10},{6,8},{8,6},{10,4},{12,2},{14,0},{16,30},{18,... | collective-permute-start | bytes 147464 | tf_op jit(solution)/shard_map/ppermute | solution.py:268
  45.8 21.9 %collective-permute-start.24 = (f32[3,32,128]{2,1,0:T(8,128)S(1)}, f32[3,32,128]{2,1,0:T(8,128)S(1)}, u32[]{:S(2)}, u32[]{:S(2)}) collective-permute-start(f32[3,32,128]{2,1,0:T(8,128)S(1)} %get-tuple-element.72), channel_id=1, source_target_pairs={{0,18},{2,16},{4,22},{6,20},{8,26},{10,24},{12,30},{14,28},{16,2},... | collective-permute-start | bytes 147464 | tf_op jit(solution)/shard_map/ppermute | solution.py:268
  47.4 4.8 %collective-permute-start.15 = (f32[4,32,128]{2,1,0:T(8,128)S(1)}, f32[4,32,128]{2,1,0:T(8,128)S(1)}, u32[]{:S(2)}, u32[]{:S(2)}) collective-permute-start(f32[4,32,128]{2,1,0:T(8,128)S(1)} %get-tuple-element.64), channel_id=1, source_target_pairs={{0,8},{2,10},{4,12},{6,14},{8,0},{10,2},{12,4},{14,6},{16,24},{18,... | collective-permute-start | bytes 196616 | tf_op jit(solution)/shard_map/ppermute | solution.py:268
  48.6 38.5 %copy-start.3 = (bf16[128,512]{1,0:T(8,128)(2,1)S(1)}, bf16[128,512]{1,0:T(8,128)(2,1)}, u32[]{:S(2)}) copy-start(bf16[128,512]{1,0:T(8,128)(2,1)} %grad.3) | copy-start | bytes 393220
  48.6 38.5 %copy-start.2 = (bf16[128,512]{1,0:T(8,128)(2,1)S(1)}, bf16[128,512]{1,0:T(8,128)(2,1)}, u32[]{:S(2)}) copy-start(bf16[128,512]{1,0:T(8,128)(2,1)} %value.3) | copy-start | bytes 393220
  48.7 38.5 %copy-start.1 = (bf16[128,512]{1,0:T(8,128)(2,1)S(1)}, bf16[128,512]{1,0:T(8,128)(2,1)}, u32[]{:S(2)}) copy-start(bf16[128,512]{1,0:T(8,128)(2,1)} %key.3) | copy-start | bytes 393220
  48.7 38.5 %copy-start = (bf16[128,512]{1,0:T(8,128)(2,1)S(1)}, bf16[128,512]{1,0:T(8,128)(2,1)}, u32[]{:S(2)}) copy-start(bf16[128,512]{1,0:T(8,128)(2,1)} %query.3) | copy-start | bytes 393220
  52.2 5.9 %collective-permute-start.16 = (f32[4,32,128]{2,1,0:T(8,128)S(1)}, f32[4,32,128]{2,1,0:T(8,128)S(1)}, u32[]{:S(2)}, u32[]{:S(2)}) collective-permute-start(f32[4,32,128]{2,1,0:T(8,128)S(1)} %get-tuple-element.65), channel_id=1, source_target_pairs={{0,16},{2,18},{4,20},{6,22},{8,24},{10,26},{12,28},{14,30},{16,0},... | collective-permute-start | bytes 196616 | tf_op jit(solution)/shard_map/ppermute | solution.py:268
  58.0 6.1 %collective-permute-start.17 = (f32[4,32,128]{2,1,0:T(8,128)S(1)}, f32[4,32,128]{2,1,0:T(8,128)S(1)}, u32[]{:S(2)}, u32[]{:S(2)}) collective-permute-start(f32[4,32,128]{2,1,0:T(8,128)S(1)} %get-tuple-element.66), channel_id=1, source_target_pairs={{0,24},{2,26},{4,28},{6,30},{8,16},{10,18},{12,20},{14,22},{16,8},... | collective-permute-start | bytes 196616 | tf_op jit(solution)/shard_map/ppermute | solution.py:268
  64.1 8.5 %collective-permute-start.25 = (f32[3,32,128]{2,1,0:T(8,128)S(1)}, f32[3,32,128]{2,1,0:T(8,128)S(1)}, u32[]{:S(2)}, u32[]{:S(2)}) collective-permute-start(f32[3,32,128]{2,1,0:T(8,128)S(1)} %get-tuple-element.73), channel_id=1, source_target_pairs={{0,20},{2,22},{4,16},{6,18},{8,28},{10,30},{12,24},{14,26},{16,4},... | collective-permute-start | bytes 147464 | tf_op jit(solution)/shard_map/ppermute | solution.py:268
  64.1 23.0 %collective-permute-start.20 = (f32[7,32,128]{2,1,0:T(8,128)S(1)}, f32[7,32,128]{2,1,0:T(8,128)S(1)}, u32[]{:S(2)}, u32[]{:S(2)}) collective-permute-start(f32[7,32,128]{2,1,0:T(8,128)S(1)} %get-tuple-element.85), channel_id=1, source_target_pairs={{0,6},{2,4},{4,2},{6,0},{8,14},{10,12},{12,10},{14,8},{16,22},{18,... | collective-permute-start | bytes 344072 | tf_op jit(solution)/shard_map/ppermute | solution.py:268
  66.3 20.9 %collective-permute-start.19 = (f32[7,32,128]{2,1,0:T(8,128)S(1)}, f32[7,32,128]{2,1,0:T(8,128)S(1)}, u32[]{:S(2)}, u32[]{:S(2)}) collective-permute-start(f32[7,32,128]{2,1,0:T(8,128)S(1)} %get-tuple-element.86), channel_id=1, source_target_pairs={{0,4},{2,6},{4,0},{6,2},{8,12},{10,14},{12,8},{14,10},{16,20},{18,... | collective-permute-start | bytes 344072 | tf_op jit(solution)/shard_map/ppermute | solution.py:268
  67.4 19.8 %collective-permute-start.18 = (f32[7,32,128]{2,1,0:T(8,128)S(1)}, f32[7,32,128]{2,1,0:T(8,128)S(1)}, u32[]{:S(2)}, u32[]{:S(2)}) collective-permute-start(f32[7,32,128]{2,1,0:T(8,128)S(1)} %get-tuple-element.87), channel_id=1, source_target_pairs={{0,2},{2,0},{4,6},{6,4},{8,10},{10,8},{12,14},{14,12},{16,18},{18,... | collective-permute-start | bytes 344072 | tf_op jit(solution)/shard_map/ppermute | solution.py:268
  67.7 8.3 %collective-permute-start.26 = (f32[3,32,128]{2,1,0:T(8,128)S(1)}, f32[3,32,128]{2,1,0:T(8,128)S(1)}, u32[]{:S(2)}, u32[]{:S(2)}) collective-permute-start(f32[3,32,128]{2,1,0:T(8,128)S(1)} %get-tuple-element.74), channel_id=1, source_target_pairs={{0,22},{2,20},{4,18},{6,16},{8,30},{10,28},{12,26},{14,24},{16,6},... | collective-permute-start | bytes 147464 | tf_op jit(solution)/shard_map/ppermute | solution.py:268
  72.6 6.8 %collective-permute-start.27 = (f32[3,32,128]{2,1,0:T(8,128)S(1)}, f32[3,32,128]{2,1,0:T(8,128)S(1)}, u32[]{:S(2)}, u32[]{:S(2)}) collective-permute-start(f32[3,32,128]{2,1,0:T(8,128)S(1)} %get-tuple-element.75), channel_id=1, source_target_pairs={{0,26},{2,24},{4,30},{6,28},{8,18},{10,16},{12,22},{14,20},{16,10}... | collective-permute-start | bytes 147464 | tf_op jit(solution)/shard_map/ppermute | solution.py:268
  76.0 6.8 %collective-permute-start.28 = (f32[3,32,128]{2,1,0:T(8,128)S(1)}, f32[3,32,128]{2,1,0:T(8,128)S(1)}, u32[]{:S(2)}, u32[]{:S(2)}) collective-permute-start(f32[3,32,128]{2,1,0:T(8,128)S(1)} %get-tuple-element.76), channel_id=1, source_target_pairs={{0,28},{2,30},{4,24},{6,26},{8,20},{10,22},{12,16},{14,18},{16,12}... | collective-permute-start | bytes 147464 | tf_op jit(solution)/shard_map/ppermute | solution.py:268
  79.4 7.7 %collective-permute-start.29 = (f32[3,32,128]{2,1,0:T(8,128)S(1)}, f32[3,32,128]{2,1,0:T(8,128)S(1)}, u32[]{:S(2)}, u32[]{:S(2)}) collective-permute-start(f32[3,32,128]{2,1,0:T(8,128)S(1)} %get-tuple-element.77), channel_id=1, source_target_pairs={{0,30},{2,28},{4,26},{6,24},{8,22},{10,20},{12,18},{14,16},{16,14}... | collective-permute-start | bytes 147464 | tf_op jit(solution)/shard_map/ppermute | solution.py:268

commit v5 on v4

--- a/solution.py
+++ b/solution.py
@@ -10,6 +10,7 @@
 from jax.sharding import PartitionSpec as P
 
 VMEM_LIMIT = 48 * 1024 * 1024
+IN_FLIGHT = 5
 
 
 def turn(value, turns):
@@ -169,11 +170,12 @@
         out[...] = packed[me[0] ^ distance]
 
 
-def mix_kernel(me, matrices, twists, *rest, blocks, grad_scale):
+def mix_kernel(me, matrices, twists, *rest, order, grad_scale):
+    blocks = len(order)
     parts, outs = rest[:blocks], rest[blocks : 2 * blocks]
     arrays, spectra, results = rest[2 * blocks :]
     _, _, channels, rows = arrays.shape
-    for distance, part in enumerate(parts):
+    for distance, part in zip(order, parts):
         arrays[me[0] ^ distance] = part[...]
     for a in range(3):
         for low in range(0, channels, 8):
@@ -224,11 +226,12 @@
             out[3] = arrays[0, 2]
 
 
-def unpack_kernel(me, query, key, value, grad, *rest, blocks, low, lag_place):
-    parts, rest = rest[:blocks], rest[blocks:]
+def unpack_kernel(me, query, key, value, grad, *rest, order, low, lag_place):
+    blocks = len(order)
+    parts, rest = dict(zip(order, rest[:blocks])), rest[blocks:]
     mixed, dquery, dkey, dvalue, dfilter, dtaps, dskip, arrays, first_lags = rest
     rows, channels = query.shape
-    for distance, part in enumerate(parts):
+    for distance, part in parts.items():
         arrays[me[0] ^ distance] = part[:3]
         if distance < low:
             for far in range(blocks // low):
@@ -268,22 +271,28 @@
     return lax.ppermute(value, axis, [(i, i ^ distance) for i in range(lax.axis_size(axis))])
 
 
-def send_all(parts, axis):
-    received = list(parts)
-    for distance in range(len(parts) - 1, 0, -1):
-        received[distance] = exchange(parts[distance], axis, distance)
+def send_all(parts, axis, order, low=0):
+    received, started = {0: parts[0]}, []
+    for distance in order[1:]:
+        payload = parts[distance]
+        if distance < low:
+            lags = [received[far][3:4] for far in range(0, len(parts), low)]
+            payload = jnp.concatenate([payload] + lags, axis=0)
+        if len(started) >= IN_FLIGHT:
+            earlier = started[-IN_FLIGHT]
+            payload, received[earlier] = lax.optimization_barrier((payload, received[earlier]))
+        received[distance] = exchange(payload, axis, distance)
+        started.append(distance)
     return received
 
 
-def send_all_with_lags(parts, axis, low):
-    received = list(parts)
-    for distance in range(len(parts) - 1, low - 1, -1):
-        received[distance] = exchange(parts[distance], axis, distance)
-    lags = [received[far][3:4] for far in range(0, len(parts), low)]
-    for distance in range(low - 1, 0, -1):
-        payload = jnp.concatenate([parts[distance]] + lags, axis=0)
-        received[distance] = exchange(payload, axis, distance)
-    return received
+def send_order(count, early):
+    crossing = [d for d in range(count // 2, count) if d not in early]
+    others = [d for d in range(count // 2 - 1, 0, -1) if d not in early]
+    order = sorted(early, reverse=True)
+    while crossing or others:
+        order += [group.pop(0) for group in (crossing, others) if group]
+    return [0] + order
 
 
 def body(query, key, value, implicit_filter, explicit_taps, skip_gain, out_grad):
@@ -300,6 +309,9 @@
     first = (index == 0).astype(jnp.int32)
     me = index if direct else jnp.zeros_like(index)
 
+    order_in = send_order(blocks, [])
+    order_out = send_order(blocks, range(low, blocks, low))
+
     half = pltpu.VMEM((rows, channels), jnp.bfloat16)
     full = pltpu.VMEM((rows, channels), f32)
     parts = call(
@@ -312,7 +324,7 @@
         limit=None,
     )(me, first, skip_gain.reshape(1, channels), query, key, value, implicit_filter, explicit_taps, out_grad)
     if direct:
-        parts = send_all(parts, "ctx")
+        parts = send_all(parts, "ctx", order_in)
     else:
         arrays = lax.all_to_all(jnp.stack(parts), "ctx", 0, 0, tiled=True)
         parts = list(jnp.pad(arrays, ((0, 0), (0, 0), (0, padded - share), (0, 0))))
@@ -322,16 +334,16 @@
     scratch = pltpu.VMEM((3, height, 2 * rows), f32)
     depth = [4 if distance % low == 0 else 3 for distance in range(blocks)]
     parts = call(
-        functools.partial(mix_kernel, blocks=blocks, grad_scale=grad_scale),
+        functools.partial(mix_kernel, order=order_in, grad_scale=grad_scale),
         "mix",
         tuple(shape((count, padded, rows)) for count in depth),
         (pltpu.SMEM,) + (pltpu.VMEM,) * (2 + blocks),
         scratch=(pltpu.VMEM((blocks, 3, padded, rows), f32), scratch, scratch),
         flops=36 * height * (2 * rows) ** 2,
         size=24 * blocks * padded * rows,
-    )(me, jnp.asarray(matrices), jnp.asarray(twists), *parts)
+    )(me, jnp.asarray(matrices), jnp.asarray(twists), *[parts[distance] for distance in order_in])
     if direct:
-        parts = send_all_with_lags(parts, "ctx", low)
+        parts = send_all(parts, "ctx", order_out, low)
     else:
         parts = list(lax.all_to_all(jnp.stack(parts)[:, :, :share], "ctx", 0, 0, tiled=True))
 
@@ -342,13 +354,13 @@
 
     full = shape((rows, channels))
     outs = call(
-        functools.partial(unpack_kernel, blocks=blocks, low=low, lag_place=lag_place),
+        functools.partial(unpack_kernel, order=order_out, low=low, lag_place=lag_place),
         "unpack",
         (full,) * 6 + (shape((1, channels)),),
         (pltpu.SMEM,) + (pltpu.VMEM,) * (4 + blocks),
         scratch=(pltpu.VMEM((blocks, 3, share, rows), f32), pltpu.VMEM((blocks, share, rows), f32)),
         size=48 * rows * channels,
-    )(me, query, key, value, out_grad, *parts)
+    )(me, query, key, value, out_grad, *[parts[distance] for distance in order_out])
     return (*outs[:6], outs[6].reshape(channels))
 
 

time: 88.7 us -> 81.1 us (0.914)
  starting transfers between devices: 57.1 us -> 51.7 us
  waiting for transfers between devices: 22.9 us -> 20.7 us
    ppermute x30, starting transfers between devices: 57.1 us -> 51.7 us  [exchange(): lax.ppermute(value, axis, [(i, i ^ distance) for i in range(lax.axis_size...]
    ppermute x30, waiting for transfers between devices: 22.9 us -> 20.7 us  [exchange(): lax.ppermute(value, axis, [(i, i ^ distance) for i in range(lax.axis_size...]
  transfers between devices with their start and end apart: 30 -> 30, of which waited for: 8 -> 11; matrix products, arithmetic and copies ran while one was open for 0% -> 0% of each run, Pallas kernels for 0% -> 0%
where the time goes in v5:
time: 81.1 us; the launch traced here: 80.9 us
  starting transfers between devices  51.7 us (64%)
  waiting for transfers between devices  20.7 us (26%)
  Pallas kernels  6.9 us (9%)
  local copies, waits for them, and re-layouts  0.87 us (1%)
    ppermute x30, starting transfers between devices, exchange(): lax.ppermute(value, axis, [(i, i ^ distance) for i in range(lax.axis_size...  51.7 us
    ppermute x30, waiting for transfers between devices, exchange(): lax.ppermute(value, axis, [(i, i ^ distance) for i in range(lax.axis_size...  20.7 us
    pallas_call x1, Pallas kernels, body(): call(pack_kernel, 'pack', (shape((3, share, rows)),) * blocks, (pltpu.SME...  3.09 us
    pallas_call x1, Pallas kernels, body(): call(functools.partial(mix_kernel, order=order_in, grad_scale=grad_scale)...  2.39 us
  transfers between devices with their start and end apart: 30, of which 11 were waited for; matrix products, arithmetic and copies ran while one was open for 0% of the time, Pallas kernels for 0%

profile of v5, /device:TPU:0, one launch (start us, length us, event | category | flops | bytes accessed | tf_op | source)
XLA Modules:
  0.0 80.9 jit_solution(5052156218203209343)
XLA Ops:
  0.6 0.0 copy-start.5
  0.7 0.0 copy-start.6
  0.7 3.1 %pack.1 = (f32[3,32,128]{2,1,0:T(8,128)}, f32[3,32,128]{2,1,0:T(8,128)}, f32[3,32,128]{2,1,0:T(8,128)}, f32[3,32,128]{2,1,0:T(8,128)}, f32[3,32,128]{2,1,0:T(8,1...) custom-call(s32[1]{0:T(128)} %bitcast.me, ...), custom_call_target="tpu_custom_call" | custom-call | bytes 1048576 | tf_op jit(solution)/shard_map/pack/pallas_call | solution.py:317
  3.8 4.1 %collective-permute-start = (f32[3,32,128]{2,1,0:T(8,128)}, f32[3,32,128]{2,1,0:T(8,128)S(1)}, u32[]{:S(2)}, u32[]{:S(2)}) collective-permute-start(f32[3,32,128]{2,1,0:T(8,128)} %get-tuple-element.88), channel_id=1, source_target_pairs={{0,16},{2,18},{4,20},{6,22},{8,24},{10,26},{12,28},{14,30},{16,0},... | collective-permute-start | bytes 147464 | tf_op jit(solution)/shard_map/ppermute | solution.py:271
  7.9 3.5 %collective-permute-start.1 = (f32[3,32,128]{2,1,0:T(8,128)}, f32[3,32,128]{2,1,0:T(8,128)S(1)}, u32[]{:S(2)}, u32[]{:S(2)}) collective-permute-start(f32[3,32,128]{2,1,0:T(8,128)} %get-tuple-element.91), channel_id=1, source_target_pairs={{0,14},{2,12},{4,10},{6,8},{8,6},{10,4},{12,2},{14,0},{16,30},{18,... | collective-permute-start | bytes 147464 | tf_op jit(solution)/shard_map/ppermute | solution.py:271
  11.3 0.3 collective-permute-start.2
  11.6 0.1 collective-permute-start.3
  11.8 3.8 %collective-permute-start.4 = (f32[3,32,128]{2,1,0:T(8,128)}, f32[3,32,128]{2,1,0:T(8,128)S(1)}, u32[]{:S(2)}, u32[]{:S(2)}) collective-permute-start(f32[3,32,128]{2,1,0:T(8,128)} %get-tuple-element.100), channel_id=1, source_target_pairs={{0,20},{2,22},{4,16},{6,18},{8,28},{10,30},{12,24},{14,26},{16,4},... | collective-permute-start | bytes 147464 | tf_op jit(solution)/shard_map/ppermute | solution.py:271
  15.6 0.0 collective-permute-done.rest_1_
  15.6 2.5 %collective-permute-start.5 = (f32[3,32,128]{2,1,0:T(8,128)}, f32[3,32,128]{2,1,0:T(8,128)S(1)}, u32[]{:S(2)}, u32[]{:S(2)}) collective-permute-start(f32[3,32,128]{2,1,0:T(8,128)} %get-tuple-element.103), channel_id=1, source_target_pairs={{0,10},{2,8},{4,14},{6,12},{8,2},{10,0},{12,6},{14,4},{16,26},{18,... | collective-permute-start | bytes 147464 | tf_op jit(solution)/shard_map/ppermute | solution.py:271
  18.1 0.0 collective-permute-done.1.rest_2_
  18.1 0.3 collective-permute-start.6
  18.3 0.2 collective-permute-done.2.rest_3_
  18.6 0.0 collective-permute-start.7
  18.6 0.0 collective-permute-done.3.rest_4_
  18.6 3.8 %collective-permute-start.8 = (f32[3,32,128]{2,1,0:T(8,128)}, f32[3,32,128]{2,1,0:T(8,128)S(1)}, u32[]{:S(2)}, u32[]{:S(2)}) collective-permute-start(f32[3,32,128]{2,1,0:T(8,128)} %get-tuple-element.112), channel_id=1, source_target_pairs={{0,24},{2,26},{4,28},{6,30},{8,16},{10,18},{12,20},{14,22},{16,8},... | collective-permute-start | bytes 147464 | tf_op jit(solution)/shard_map/ppermute | solution.py:271
  22.4 0.0 collective-permute-done.4.rest_5_
  22.4 2.4 %collective-permute-start.9 = (f32[3,32,128]{2,1,0:T(8,128)}, f32[3,32,128]{2,1,0:T(8,128)S(1)}, u32[]{:S(2)}, u32[]{:S(2)}) collective-permute-start(f32[3,32,128]{2,1,0:T(8,128)} %get-tuple-element.115), channel_id=1, source_target_pairs={{0,6},{2,4},{4,2},{6,0},{8,14},{10,12},{12,10},{14,8},{16,22},{18,... | collective-permute-start | bytes 147464 | tf_op jit(solution)/shard_map/ppermute | solution.py:271
  24.8 0.0 collective-permute-done.5.rest_6_
  24.9 0.2 collective-permute-start.10
  25.0 1.0 %collective-permute-done.6.rest_7_ = f32[3,32,128]{2,1,0:T(8,128)S(1)} collective-permute-done((f32[3,32,128]{2,1,0:T(8,128)}, f32[3,32,128]{2,1,0:T(8,128)S(1)}, u32[]{:S(2)}, u32[]{:S(2)}) %collective-permute-start.6) | collective-permute-done | bytes 49184 | tf_op jit(solution)/shard_map/ppermute | solution.py:271
  26.0 0.2 collective-permute-start.11
  26.2 0.0 collective-permute-done.7.rest_8_
  26.2 3.9 %collective-permute-start.12 = (f32[3,32,128]{2,1,0:T(8,128)}, f32[3,32,128]{2,1,0:T(8,128)S(1)}, u32[]{:S(2)}, u32[]{:S(2)}) collective-permute-start(f32[3,32,128]{2,1,0:T(8,128)} %get-tuple-element.119), channel_id=1, source_target_pairs={{0,28},{2,30},{4,24},{6,26},{8,20},{10,22},{12,16},{14,18},{16,12}... | collective-permute-start | bytes 147464 | tf_op jit(solution)/shard_map/ppermute | solution.py:271
  30.1 0.0 collective-permute-done.8.rest_9_
  30.1 1.5 %collective-permute-start.13 = (f32[3,32,128]{2,1,0:T(8,128)}, f32[3,32,128]{2,1,0:T(8,128)S(1)}, u32[]{:S(2)}, u32[]{:S(2)}) collective-permute-start(f32[3,32,128]{2,1,0:T(8,128)} %get-tuple-element.120), channel_id=1, source_target_pairs={{0,2},{2,0},{4,6},{6,4},{8,10},{10,8},{12,14},{14,12},{16,18},{18,... | collective-permute-start | bytes 147464 | tf_op jit(solution)/shard_map/ppermute | solution.py:271
  31.6 0.0 collective-permute-done.9.rest_10_
  31.6 0.8 collective-permute-start.14
  32.4 0.0 collective-permute-done.10.rest_11_
  32.4 0.0 collective-permute-done.11.rest_12_
  32.4 1.0 %collective-permute-done.12.rest_13_ = f32[3,32,128]{2,1,0:T(8,128)S(1)} collective-permute-done((f32[3,32,128]{2,1,0:T(8,128)}, f32[3,32,128]{2,1,0:T(8,128)S(1)}, u32[]{:S(2)}, u32[]{:S(2)}) %collective-permute-start.12) | collective-permute-done | bytes 49184 | tf_op jit(solution)/shard_map/ppermute | solution.py:271
  33.4 1.1 %collective-permute-done.13.rest_14_ = f32[3,32,128]{2,1,0:T(8,128)S(1)} collective-permute-done((f32[3,32,128]{2,1,0:T(8,128)}, f32[3,32,128]{2,1,0:T(8,128)S(1)}, u32[]{:S(2)}, u32[]{:S(2)}) %collective-permute-start.13) | collective-permute-done | bytes 49184 | tf_op jit(solution)/shard_map/ppermute | solution.py:271
  34.5 5.3 %collective-permute-done.14.rest_15_ = f32[3,32,128]{2,1,0:T(8,128)S(1)} collective-permute-done((f32[3,32,128]{2,1,0:T(8,128)}, f32[3,32,128]{2,1,0:T(8,128)S(1)}, u32[]{:S(2)}, u32[]{:S(2)}) %collective-permute-start.14) | collective-permute-done | bytes 49184 | tf_op jit(solution)/shard_map/ppermute | solution.py:271
  39.8 0.8 copy-done.4
  40.6 2.4 %mix.1 = (f32[4,32,128]{2,1,0:T(8,128)S(1)}, f32[3,32,128]{2,1,0:T(8,128)S(1)}, f32[3,32,128]{2,1,0:T(8,128)S(1)}, f32[3,32,128]{2,1,0:T(8,128)S(1)}, f32[4,32,1...) custom-call(s32[1]{0:T(128)} %bitcast.me, ...), custom_call_target="tpu_custom_call" | custom-call | flops 1283457024 | bytes 1572864 | tf_op jit(solution)/shard_map/mix/pallas_call | solution.py:336
  43.0 0.1 collective-permute-start.18
  43.1 2.0 %collective-permute-start.19 = (f32[3,32,128]{2,1,0:T(8,128)S(1)}, f32[3,32,128]{2,1,0:T(8,128)S(1)}, u32[]{:S(2)}, u32[]{:S(2)}) collective-permute-start(f32[3,32,128]{2,1,0:T(8,128)S(1)} %get-tuple-element.136), channel_id=1, source_target_pairs={{0,14},{2,12},{4,10},{6,8},{8,6},{10,4},{12,2},{14,0},{16,30},{18,... | collective-permute-start | bytes 147464 | tf_op jit(solution)/shard_map/ppermute | solution.py:271
  45.1 2.9 %collective-permute-start.15 = (f32[4,32,128]{2,1,0:T(8,128)S(1)}, f32[4,32,128]{2,1,0:T(8,128)S(1)}, u32[]{:S(2)}, u32[]{:S(2)}) collective-permute-start(f32[4,32,128]{2,1,0:T(8,128)S(1)} %get-tuple-element.124), channel_id=1, source_target_pairs={{0,24},{2,26},{4,28},{6,30},{8,16},{10,18},{12,20},{14,22},{16,8},... | collective-permute-start | bytes 196616 | tf_op jit(solution)/shard_map/ppermute | solution.py:271
  48.0 0.0 collective-permute-start.16
  48.0 1.4 %collective-permute-start.17 = (f32[4,32,128]{2,1,0:T(8,128)S(1)}, f32[4,32,128]{2,1,0:T(8,128)S(1)}, u32[]{:S(2)}, u32[]{:S(2)}) collective-permute-start(f32[4,32,128]{2,1,0:T(8,128)S(1)} %get-tuple-element.130), channel_id=1, source_target_pairs={{0,8},{2,10},{4,12},{6,14},{8,0},{10,2},{12,4},{14,6},{16,24},{18,... | collective-permute-start | bytes 196616 | tf_op jit(solution)/shard_map/ppermute | solution.py:271
  49.5 0.0 copy-start.1
  49.5 0.0 copy-start
  49.5 0.3 collective-permute-done.19.rest_5_
  49.9 2.6 %collective-permute-start.24 = (f32[3,32,128]{2,1,0:T(8,128)S(1)}, f32[3,32,128]{2,1,0:T(8,128)S(1)}, u32[]{:S(2)}, u32[]{:S(2)}) collective-permute-start(f32[3,32,128]{2,1,0:T(8,128)S(1)} %get-tuple-element.151), channel_id=1, source_target_pairs={{0,26},{2,24},{4,30},{6,28},{8,18},{10,16},{12,22},{14,20},{16,10}... | collective-permute-start | bytes 147464 | tf_op jit(solution)/shard_map/ppermute | solution.py:271
  52.5 0.0 collective-permute-done.15.rest_1_
  52.5 0.4 collective-permute-start.20
  52.9 1.1 %collective-permute-done.16.rest_2_ = f32[4,32,128]{2,1,0:T(8,128)S(1)} collective-permute-done((f32[4,32,128]{2,1,0:T(8,128)S(1)}, f32[4,32,128]{2,1,0:T(8,128)S(1)}, u32[]{:S(2)}, u32[]{:S(2)}) %collective-permute-start.16) | collective-permute-done | bytes 65568 | tf_op jit(solution)/shard_map/ppermute | solution.py:271
  54.0 0.0 collective-permute-done.17.rest_3_
  54.0 3.2 %collective-permute-start.22 = (f32[3,32,128]{2,1,0:T(8,128)S(1)}, f32[3,32,128]{2,1,0:T(8,128)S(1)}, u32[]{:S(2)}, u32[]{:S(2)}) collective-permute-start(f32[3,32,128]{2,1,0:T(8,128)S(1)} %get-tuple-element.145), channel_id=1, source_target_pairs={{0,22},{2,20},{4,18},{6,16},{8,30},{10,28},{12,26},{14,24},{16,6},... | collective-permute-start | bytes 147464 | tf_op jit(solution)/shard_map/ppermute | solution.py:271
  57.3 0.7 collective-permute-start.29
  58.0 2.9 %collective-permute-done.22.rest_8_ = f32[3,32,128]{2,1,0:T(8,128)S(1)} collective-permute-done((f32[3,32,128]{2,1,0:T(8,128)S(1)}, f32[3,32,128]{2,1,0:T(8,128)S(1)}, u32[]{:S(2)}, u32[]{:S(2)}) %collective-permute-start.22) | collective-permute-done | bytes 49184 | tf_op jit(solution)/shard_map/ppermute | solution.py:271
  60.9 2.1 %collective-permute-start.25 = (f32[7,32,128]{2,1,0:T(8,128)S(1)}, f32[7,32,128]{2,1,0:T(8,128)S(1)}, u32[]{:S(2)}, u32[]{:S(2)}) collective-permute-start(f32[7,32,128]{2,1,0:T(8,128)S(1)} %get-tuple-element.153), channel_id=1, source_target_pairs={{0,6},{2,4},{4,2},{6,0},{8,14},{10,12},{12,10},{14,8},{16,22},{18,... | collective-permute-start | bytes 344072 | tf_op jit(solution)/shard_map/ppermute | solution.py:271
  63.1 0.2 collective-permute-start.27
  63.3 2.7 %collective-permute-start.23 = (f32[3,32,128]{2,1,0:T(8,128)S(1)}, f32[3,32,128]{2,1,0:T(8,128)S(1)}, u32[]{:S(2)}, u32[]{:S(2)}) collective-permute-start(f32[3,32,128]{2,1,0:T(8,128)S(1)} %get-tuple-element.148), channel_id=1, source_target_pairs={{0,10},{2,8},{4,14},{6,12},{8,2},{10,0},{12,6},{14,4},{16,26},{18,... | collective-permute-start | bytes 147464 | tf_op jit(solution)/shard_map/ppermute | solution.py:271
  66.1 0.5 collective-permute-start.21
  66.5 1.8 %collective-permute-done.23.rest_9_ = f32[3,32,128]{2,1,0:T(8,128)S(1)} collective-permute-done((f32[3,32,128]{2,1,0:T(8,128)S(1)}, f32[3,32,128]{2,1,0:T(8,128)S(1)}, u32[]{:S(2)}, u32[]{:S(2)}) %collective-permute-start.23) | collective-permute-done | bytes 49184 | tf_op jit(solution)/shard_map/ppermute | solution.py:271
  68.3 4.4 %collective-permute-start.28 = (f32[3,32,128]{2,1,0:T(8,128)S(1)}, f32[3,32,128]{2,1,0:T(8,128)S(1)}, u32[]{:S(2)}, u32[]{:S(2)}) collective-permute-start(f32[3,32,128]{2,1,0:T(8,128)S(1)} %get-tuple-element.156), channel_id=1, source_target_pairs={{0,30},{2,28},{4,26},{6,24},{8,22},{10,20},{12,18},{14,16},{16,14}... | collective-permute-start | bytes 147464 | tf_op jit(solution)/shard_map/ppermute | solution.py:271
  72.7 0.9 %collective-permute-start.26 = (f32[3,32,128]{2,1,0:T(8,128)S(1)}, f32[3,32,128]{2,1,0:T(8,128)S(1)}, u32[]{:S(2)}, u32[]{:S(2)}) collective-permute-start(f32[3,32,128]{2,1,0:T(8,128)S(1)} %get-tuple-element.154), channel_id=1, source_target_pairs={{0,28},{2,30},{4,24},{6,26},{8,20},{10,22},{12,16},{14,18},{16,12}... | collective-permute-start | bytes 147464 | tf_op jit(solution)/shard_map/ppermute | solution.py:271
  73.6 2.5 %collective-permute-done.28.rest_14_ = f32[3,32,128]{2,1,0:T(8,128)S(1)} collective-permute-done((f32[3,32,128]{2,1,0:T(8,128)S(1)}, f32[3,32,128]{2,1,0:T(8,128)S(1)}, u32[]{:S(2)}, u32[]{:S(2)}) %collective-permute-start.28) | collective-permute-done | bytes 49184 | tf_op jit(solution)/shard_map/ppermute | solution.py:271
  76.0 3.4 %collective-permute-done.26.rest_12_ = f32[3,32,128]{2,1,0:T(8,128)S(1)} collective-permute-done((f32[3,32,128]{2,1,0:T(8,128)S(1)}, f32[3,32,128]{2,1,0:T(8,128)S(1)}, u32[]{:S(2)}, u32[]{:S(2)}) %collective-permute-start.26) | collective-permute-done | bytes 49184 | tf_op jit(solution)/shard_map/ppermute | solution.py:271
  79.5 0.0 collective-permute-done.29.rest_15_
  79.5 0.0 collective-permute-done.25.rest_11_
  79.5 0.0 collective-permute-done.27.rest_13_
  79.5 1.4 %unpack.1 = (f32[128,512]{1,0:T(8,128)}, f32[128,512]{1,0:T(8,128)}, f32[128,512]{1,0:T(8,128)}, f32[128,512]{1,0:T(8,128)}, f32[128,512]{1,0:T(8,128)}, /*index=5*/f32[128,512]{1,0:T(8,128)}, f32[1,512]{1,0:T(1,128)}) custom-call(s32[1]{0:T(128)} %bitcast.me, bf16[128,512]{1,0:T(8,128)(2,1)S(1)} %copy-done, bf16[128,512]{1,0:T(8,128)(2,1)S(1)} %copy-done.1, ...), custom_call_target="tpu_custom_call" | custom-call | bytes 3145728 | tf_op jit(solution)/shard_map/unpack/pallas_call | solution.py:356
  (19 shorter events, 0.1 us)
Async XLA Ops:
  0.6 39.2 %copy-start.5 = (bf16[4,256,256]{2,1,0:T(8,128)(2,1)S(1)}, bf16[4,256,256]{2,1,0:T(8,128)(2,1)}, u32[]{:S(2)}) copy-start(bf16[4,256,256]{2,1,0:T(8,128)(2,1)} %constant.12.clone.matrices) | copy-start | bytes 1572868
  0.7 39.1 %copy-start.6 = (f32[17,4,128]{2,1,0:T(4,128)S(1)}, f32[17,4,128]{2,1,0:T(4,128)}, u32[]{:S(2)}) copy-start(f32[17,4,128]{2,1,0:T(4,128)} %constant.13.clone.twists) | copy-start | bytes 104452
  3.8 11.8 %collective-permute-start = (f32[3,32,128]{2,1,0:T(8,128)}, f32[3,32,128]{2,1,0:T(8,128)S(1)}, u32[]{:S(2)}, u32[]{:S(2)}) collective-permute-start(f32[3,32,128]{2,1,0:T(8,128)} %get-tuple-element.88), channel_id=1, source_target_pairs={{0,16},{2,18},{4,20},{6,22},{8,24},{10,26},{12,28},{14,30},{16,0},... | collective-permute-start | bytes 147464 | tf_op jit(solution)/shard_map/ppermute | solution.py:271
  7.9 10.2 %collective-permute-start.1 = (f32[3,32,128]{2,1,0:T(8,128)}, f32[3,32,128]{2,1,0:T(8,128)S(1)}, u32[]{:S(2)}, u32[]{:S(2)}) collective-permute-start(f32[3,32,128]{2,1,0:T(8,128)} %get-tuple-element.91), channel_id=1, source_target_pairs={{0,14},{2,12},{4,10},{6,8},{8,6},{10,4},{12,2},{14,0},{16,30},{18,... | collective-permute-start | bytes 147464 | tf_op jit(solution)/shard_map/ppermute | solution.py:271
  11.3 7.2 %collective-permute-start.2 = (f32[3,32,128]{2,1,0:T(8,128)}, f32[3,32,128]{2,1,0:T(8,128)S(1)}, u32[]{:S(2)}, u32[]{:S(2)}) collective-permute-start(f32[3,32,128]{2,1,0:T(8,128)} %get-tuple-element.94), channel_id=1, source_target_pairs={{0,18},{2,16},{4,22},{6,20},{8,26},{10,24},{12,30},{14,28},{16,2},... | collective-permute-start | bytes 147464 | tf_op jit(solution)/shard_map/ppermute | solution.py:271
  11.6 7.0 %collective-permute-start.3 = (f32[3,32,128]{2,1,0:T(8,128)}, f32[3,32,128]{2,1,0:T(8,128)S(1)}, u32[]{:S(2)}, u32[]{:S(2)}) collective-permute-start(f32[3,32,128]{2,1,0:T(8,128)} %get-tuple-element.97), channel_id=1, source_target_pairs={{0,12},{2,14},{4,8},{6,10},{8,4},{10,6},{12,0},{14,2},{16,28},{18,... | collective-permute-start | bytes 147464 | tf_op jit(solution)/shard_map/ppermute | solution.py:271
  11.8 10.6 %collective-permute-start.4 = (f32[3,32,128]{2,1,0:T(8,128)}, f32[3,32,128]{2,1,0:T(8,128)S(1)}, u32[]{:S(2)}, u32[]{:S(2)}) collective-permute-start(f32[3,32,128]{2,1,0:T(8,128)} %get-tuple-element.100), channel_id=1, source_target_pairs={{0,20},{2,22},{4,16},{6,18},{8,28},{10,30},{12,24},{14,26},{16,4},... | collective-permute-start | bytes 147464 | tf_op jit(solution)/shard_map/ppermute | solution.py:271
  15.6 9.3 %collective-permute-start.5 = (f32[3,32,128]{2,1,0:T(8,128)}, f32[3,32,128]{2,1,0:T(8,128)S(1)}, u32[]{:S(2)}, u32[]{:S(2)}) collective-permute-start(f32[3,32,128]{2,1,0:T(8,128)} %get-tuple-element.103), channel_id=1, source_target_pairs={{0,10},{2,8},{4,14},{6,12},{8,2},{10,0},{12,6},{14,4},{16,26},{18,... | collective-permute-start | bytes 147464 | tf_op jit(solution)/shard_map/ppermute | solution.py:271
  18.1 7.9 %collective-permute-start.6 = (f32[3,32,128]{2,1,0:T(8,128)}, f32[3,32,128]{2,1,0:T(8,128)S(1)}, u32[]{:S(2)}, u32[]{:S(2)}) collective-permute-start(f32[3,32,128]{2,1,0:T(8,128)} %get-tuple-element.106), channel_id=1, source_target_pairs={{0,22},{2,20},{4,18},{6,16},{8,30},{10,28},{12,26},{14,24},{16,6},... | collective-permute-start | bytes 147464 | tf_op jit(solution)/shard_map/ppermute | solution.py:271
  18.6 7.7 %collective-permute-start.7 = (f32[3,32,128]{2,1,0:T(8,128)}, f32[3,32,128]{2,1,0:T(8,128)S(1)}, u32[]{:S(2)}, u32[]{:S(2)}) collective-permute-start(f32[3,32,128]{2,1,0:T(8,128)} %get-tuple-element.109), channel_id=1, source_target_pairs={{0,8},{2,10},{4,12},{6,14},{8,0},{10,2},{12,4},{14,6},{16,24},{18,... | collective-permute-start | bytes 147464 | tf_op jit(solution)/shard_map/ppermute | solution.py:271
  18.6 11.5 %collective-permute-start.8 = (f32[3,32,128]{2,1,0:T(8,128)}, f32[3,32,128]{2,1,0:T(8,128)S(1)}, u32[]{:S(2)}, u32[]{:S(2)}) collective-permute-start(f32[3,32,128]{2,1,0:T(8,128)} %get-tuple-element.112), channel_id=1, source_target_pairs={{0,24},{2,26},{4,28},{6,30},{8,16},{10,18},{12,20},{14,22},{16,8},... | collective-permute-start | bytes 147464 | tf_op jit(solution)/shard_map/ppermute | solution.py:271
  22.4 9.2 %collective-permute-start.9 = (f32[3,32,128]{2,1,0:T(8,128)}, f32[3,32,128]{2,1,0:T(8,128)S(1)}, u32[]{:S(2)}, u32[]{:S(2)}) collective-permute-start(f32[3,32,128]{2,1,0:T(8,128)} %get-tuple-element.115), channel_id=1, source_target_pairs={{0,6},{2,4},{4,2},{6,0},{8,14},{10,12},{12,10},{14,8},{16,22},{18,... | collective-permute-start | bytes 147464 | tf_op jit(solution)/shard_map/ppermute | solution.py:271
  24.9 7.6 %collective-permute-start.10 = (f32[3,32,128]{2,1,0:T(8,128)}, f32[3,32,128]{2,1,0:T(8,128)S(1)}, u32[]{:S(2)}, u32[]{:S(2)}) collective-permute-start(f32[3,32,128]{2,1,0:T(8,128)} %get-tuple-element.117), channel_id=1, source_target_pairs={{0,26},{2,24},{4,30},{6,28},{8,18},{10,16},{12,22},{14,20},{16,10}... | collective-permute-start | bytes 147464 | tf_op jit(solution)/shard_map/ppermute | solution.py:271
  26.0 6.4 %collective-permute-start.11 = (f32[3,32,128]{2,1,0:T(8,128)}, f32[3,32,128]{2,1,0:T(8,128)S(1)}, u32[]{:S(2)}, u32[]{:S(2)}) collective-permute-start(f32[3,32,128]{2,1,0:T(8,128)} %get-tuple-element.118), channel_id=1, source_target_pairs={{0,4},{2,6},{4,0},{6,2},{8,12},{10,14},{12,8},{14,10},{16,20},{18,... | collective-permute-start | bytes 147464 | tf_op jit(solution)/shard_map/ppermute | solution.py:271
  26.2 7.2 %collective-permute-start.12 = (f32[3,32,128]{2,1,0:T(8,128)}, f32[3,32,128]{2,1,0:T(8,128)S(1)}, u32[]{:S(2)}, u32[]{:S(2)}) collective-permute-start(f32[3,32,128]{2,1,0:T(8,128)} %get-tuple-element.119), channel_id=1, source_target_pairs={{0,28},{2,30},{4,24},{6,26},{8,20},{10,22},{12,16},{14,18},{16,12}... | collective-permute-start | bytes 147464 | tf_op jit(solution)/shard_map/ppermute | solution.py:271
  30.1 4.4 %collective-permute-start.13 = (f32[3,32,128]{2,1,0:T(8,128)}, f32[3,32,128]{2,1,0:T(8,128)S(1)}, u32[]{:S(2)}, u32[]{:S(2)}) collective-permute-start(f32[3,32,128]{2,1,0:T(8,128)} %get-tuple-element.120), channel_id=1, source_target_pairs={{0,2},{2,0},{4,6},{6,4},{8,10},{10,8},{12,14},{14,12},{16,18},{18,... | collective-permute-start | bytes 147464 | tf_op jit(solution)/shard_map/ppermute | solution.py:271
  31.6 8.2 %collective-permute-start.14 = (f32[3,32,128]{2,1,0:T(8,128)}, f32[3,32,128]{2,1,0:T(8,128)S(1)}, u32[]{:S(2)}, u32[]{:S(2)}) collective-permute-start(f32[3,32,128]{2,1,0:T(8,128)} %get-tuple-element.121), channel_id=1, source_target_pairs={{0,30},{2,28},{4,26},{6,24},{8,22},{10,20},{12,18},{14,16},{16,14}... | collective-permute-start | bytes 147464 | tf_op jit(solution)/shard_map/ppermute | solution.py:271
  39.8 0.8 copy-start.4
  43.0 20.3 %collective-permute-start.18 = (f32[3,32,128]{2,1,0:T(8,128)S(1)}, f32[3,32,128]{2,1,0:T(8,128)S(1)}, u32[]{:S(2)}, u32[]{:S(2)}) collective-permute-start(f32[3,32,128]{2,1,0:T(8,128)S(1)} %get-tuple-element.133), channel_id=1, source_target_pairs={{0,18},{2,16},{4,22},{6,20},{8,26},{10,24},{12,30},{14,28},{16,2},... | collective-permute-start | bytes 147464 | tf_op jit(solution)/shard_map/ppermute | solution.py:271
  43.1 6.8 %collective-permute-start.19 = (f32[3,32,128]{2,1,0:T(8,128)S(1)}, f32[3,32,128]{2,1,0:T(8,128)S(1)}, u32[]{:S(2)}, u32[]{:S(2)}) collective-permute-start(f32[3,32,128]{2,1,0:T(8,128)S(1)} %get-tuple-element.136), channel_id=1, source_target_pairs={{0,14},{2,12},{4,10},{6,8},{8,6},{10,4},{12,2},{14,0},{16,30},{18,... | collective-permute-start | bytes 147464 | tf_op jit(solution)/shard_map/ppermute | solution.py:271
  45.1 7.4 %collective-permute-start.15 = (f32[4,32,128]{2,1,0:T(8,128)S(1)}, f32[4,32,128]{2,1,0:T(8,128)S(1)}, u32[]{:S(2)}, u32[]{:S(2)}) collective-permute-start(f32[4,32,128]{2,1,0:T(8,128)S(1)} %get-tuple-element.124), channel_id=1, source_target_pairs={{0,24},{2,26},{4,28},{6,30},{8,16},{10,18},{12,20},{14,22},{16,8},... | collective-permute-start | bytes 196616 | tf_op jit(solution)/shard_map/ppermute | solution.py:271
  48.0 6.0 %collective-permute-start.16 = (f32[4,32,128]{2,1,0:T(8,128)S(1)}, f32[4,32,128]{2,1,0:T(8,128)S(1)}, u32[]{:S(2)}, u32[]{:S(2)}) collective-permute-start(f32[4,32,128]{2,1,0:T(8,128)S(1)} %get-tuple-element.127), channel_id=1, source_target_pairs={{0,16},{2,18},{4,20},{6,22},{8,24},{10,26},{12,28},{14,30},{16,0},... | collective-permute-start | bytes 196616 | tf_op jit(solution)/shard_map/ppermute | solution.py:271
  48.0 6.0 %collective-permute-start.17 = (f32[4,32,128]{2,1,0:T(8,128)S(1)}, f32[4,32,128]{2,1,0:T(8,128)S(1)}, u32[]{:S(2)}, u32[]{:S(2)}) collective-permute-start(f32[4,32,128]{2,1,0:T(8,128)S(1)} %get-tuple-element.130), channel_id=1, source_target_pairs={{0,8},{2,10},{4,12},{6,14},{8,0},{10,2},{12,4},{14,6},{16,24},{18,... | collective-permute-start | bytes 196616 | tf_op jit(solution)/shard_map/ppermute | solution.py:271
  49.5 30.0 %copy-start.3 = (bf16[128,512]{1,0:T(8,128)(2,1)S(1)}, bf16[128,512]{1,0:T(8,128)(2,1)}, u32[]{:S(2)}) copy-start(bf16[128,512]{1,0:T(8,128)(2,1)} %grad.3) | copy-start | bytes 393220
  49.5 30.0 %copy-start.2 = (bf16[128,512]{1,0:T(8,128)(2,1)S(1)}, bf16[128,512]{1,0:T(8,128)(2,1)}, u32[]{:S(2)}) copy-start(bf16[128,512]{1,0:T(8,128)(2,1)} %value.3) | copy-start | bytes 393220
  49.5 30.0 %copy-start.1 = (bf16[128,512]{1,0:T(8,128)(2,1)S(1)}, bf16[128,512]{1,0:T(8,128)(2,1)}, u32[]{:S(2)}) copy-start(bf16[128,512]{1,0:T(8,128)(2,1)} %key.3) | copy-start | bytes 393220
  49.5 30.0 %copy-start = (bf16[128,512]{1,0:T(8,128)(2,1)S(1)}, bf16[128,512]{1,0:T(8,128)(2,1)}, u32[]{:S(2)}) copy-start(bf16[128,512]{1,0:T(8,128)(2,1)} %query.3) | copy-start | bytes 393220
  49.9 7.4 %collective-permute-start.24 = (f32[3,32,128]{2,1,0:T(8,128)S(1)}, f32[3,32,128]{2,1,0:T(8,128)S(1)}, u32[]{:S(2)}, u32[]{:S(2)}) collective-permute-start(f32[3,32,128]{2,1,0:T(8,128)S(1)} %get-tuple-element.151), channel_id=1, source_target_pairs={{0,26},{2,24},{4,30},{6,28},{8,18},{10,16},{12,22},{14,20},{16,10}... | collective-permute-start | bytes 147464 | tf_op jit(solution)/shard_map/ppermute | solution.py:271
  52.5 8.4 %collective-permute-start.20 = (f32[3,32,128]{2,1,0:T(8,128)S(1)}, f32[3,32,128]{2,1,0:T(8,128)S(1)}, u32[]{:S(2)}, u32[]{:S(2)}) collective-permute-start(f32[3,32,128]{2,1,0:T(8,128)S(1)} %get-tuple-element.139), channel_id=1, source_target_pairs={{0,20},{2,22},{4,16},{6,18},{8,28},{10,30},{12,24},{14,26},{16,4},... | collective-permute-start | bytes 147464 | tf_op jit(solution)/shard_map/ppermute | solution.py:271
  54.0 6.9 %collective-permute-start.22 = (f32[3,32,128]{2,1,0:T(8,128)S(1)}, f32[3,32,128]{2,1,0:T(8,128)S(1)}, u32[]{:S(2)}, u32[]{:S(2)}) collective-permute-start(f32[3,32,128]{2,1,0:T(8,128)S(1)} %get-tuple-element.145), channel_id=1, source_target_pairs={{0,22},{2,20},{4,18},{6,16},{8,30},{10,28},{12,26},{14,24},{16,6},... | collective-permute-start | bytes 147464 | tf_op jit(solution)/shard_map/ppermute | solution.py:271
  57.3 22.2 %collective-permute-start.29 = (f32[7,32,128]{2,1,0:T(8,128)S(1)}, f32[7,32,128]{2,1,0:T(8,128)S(1)}, u32[]{:S(2)}, u32[]{:S(2)}) collective-permute-start(f32[7,32,128]{2,1,0:T(8,128)S(1)} %get-tuple-element.157), channel_id=1, source_target_pairs={{0,2},{2,0},{4,6},{6,4},{8,10},{10,8},{12,14},{14,12},{16,18},{18,... | collective-permute-start | bytes 344072 | tf_op jit(solution)/shard_map/ppermute | solution.py:271
  60.9 18.5 %collective-permute-start.25 = (f32[7,32,128]{2,1,0:T(8,128)S(1)}, f32[7,32,128]{2,1,0:T(8,128)S(1)}, u32[]{:S(2)}, u32[]{:S(2)}) collective-permute-start(f32[7,32,128]{2,1,0:T(8,128)S(1)} %get-tuple-element.153), channel_id=1, source_target_pairs={{0,6},{2,4},{4,2},{6,0},{8,14},{10,12},{12,10},{14,8},{16,22},{18,... | collective-permute-start | bytes 344072 | tf_op jit(solution)/shard_map/ppermute | solution.py:271
  63.1 16.4 %collective-permute-start.27 = (f32[7,32,128]{2,1,0:T(8,128)S(1)}, f32[7,32,128]{2,1,0:T(8,128)S(1)}, u32[]{:S(2)}, u32[]{:S(2)}) collective-permute-start(f32[7,32,128]{2,1,0:T(8,128)S(1)} %get-tuple-element.155), channel_id=1, source_target_pairs={{0,4},{2,6},{4,0},{6,2},{8,12},{10,14},{12,8},{14,10},{16,20},{18,... | collective-permute-start | bytes 344072 | tf_op jit(solution)/shard_map/ppermute | solution.py:271
  63.3 5.0 %collective-permute-start.23 = (f32[3,32,128]{2,1,0:T(8,128)S(1)}, f32[3,32,128]{2,1,0:T(8,128)S(1)}, u32[]{:S(2)}, u32[]{:S(2)}) collective-permute-start(f32[3,32,128]{2,1,0:T(8,128)S(1)} %get-tuple-element.148), channel_id=1, source_target_pairs={{0,10},{2,8},{4,14},{6,12},{8,2},{10,0},{12,6},{14,4},{16,26},{18,... | collective-permute-start | bytes 147464 | tf_op jit(solution)/shard_map/ppermute | solution.py:271
  66.1 6.6 %collective-permute-start.21 = (f32[3,32,128]{2,1,0:T(8,128)S(1)}, f32[3,32,128]{2,1,0:T(8,128)S(1)}, u32[]{:S(2)}, u32[]{:S(2)}) collective-permute-start(f32[3,32,128]{2,1,0:T(8,128)S(1)} %get-tuple-element.142), channel_id=1, source_target_pairs={{0,12},{2,14},{4,8},{6,10},{8,4},{10,6},{12,0},{14,2},{16,28},{18,... | collective-permute-start | bytes 147464 | tf_op jit(solution)/shard_map/ppermute | solution.py:271
  68.3 7.8 %collective-permute-start.28 = (f32[3,32,128]{2,1,0:T(8,128)S(1)}, f32[3,32,128]{2,1,0:T(8,128)S(1)}, u32[]{:S(2)}, u32[]{:S(2)}) collective-permute-start(f32[3,32,128]{2,1,0:T(8,128)S(1)} %get-tuple-element.156), channel_id=1, source_target_pairs={{0,30},{2,28},{4,26},{6,24},{8,22},{10,20},{12,18},{14,16},{16,14}... | collective-permute-start | bytes 147464 | tf_op jit(solution)/shard_map/ppermute | solution.py:271
  72.7 6.8 %collective-permute-start.26 = (f32[3,32,128]{2,1,0:T(8,128)S(1)}, f32[3,32,128]{2,1,0:T(8,128)S(1)}, u32[]{:S(2)}, u32[]{:S(2)}) collective-permute-start(f32[3,32,128]{2,1,0:T(8,128)S(1)} %get-tuple-element.154), channel_id=1, source_target_pairs={{0,28},{2,30},{4,24},{6,26},{8,20},{10,22},{12,16},{14,18},{16,12}... | collective-permute-start | bytes 147464 | tf_op jit(solution)/shard_map/ppermute | solution.py:271

commit v6 on v2

--- a/solution.py
+++ b/solution.py
@@ -149,13 +149,10 @@
         copy.start()
     key, value, query, grad, filt, taps = held
     rows, channels = query.shape
+    blocks, _, share, _ = out.shape
 
     def put(a, array):
-        turned = array.T
-        if len(out.shape) == 4:
-            out[:, a] = turned.reshape(out.shape[0], out.shape[2], rows)
-        else:
-            out[a] = turned
+        out[:, a] = array.T.reshape(blocks, share, rows)
 
     copies[0].wait()
     copies[1].wait()
@@ -170,7 +167,7 @@
     put(1, filt[...] + jnp.where(first[0] == 1, extra, 0.0))
 
 
-def mix_kernel(matrices, twists, arrays, out, taps, spectra, results, *, grad_scale):
+def mix_kernel(matrices, twists, arrays, out, spectra, results, *, grad_scale):
     blocks, _, channels, rows = arrays.shape
     for a in range(3):
         for low in range(0, channels, 8):
@@ -215,13 +212,13 @@
             for j in range(blocks):
                 value = values[j] * grad_scale if a == 2 else values[j]
                 out[j, a, pl.ds(low, 8), :] = value
-                if a == 2 and j == 0:
-                    taps[pl.ds(low, 8), :] = value
-
-
-def unpack_kernel(me, query, key, value, grad, parts, first_lags, mixed, dquery, dkey, dvalue, dfilter, dtaps, dskip, ordered, *, flips):
+            if a == 2:
+                for j in range(blocks):
+                    out[j, 3, pl.ds(low, 8), :] = values[0] * grad_scale
+
+
+def unpack_kernel(query, key, value, grad, parts, mixed, dquery, dkey, dvalue, dfilter, dtaps, dskip):
     rows, channels = query.shape
-    blocks, share = first_lags.shape[:2]
 
     def whole(a):
         return parts[:, a].reshape(channels, rows).T
@@ -233,16 +230,12 @@
     dkey[...] = product_grad * value[...].astype(jnp.float32)
     dvalue[...] = product_grad * key[...].astype(jnp.float32)
     dfilter[...] = whole(2)
-    own = sum(((me[0] >> bit) & 1) * flipped for bit, flipped in enumerate(flips))
-    for source in range(blocks):
-        place = sum(flipped for bit, flipped in enumerate(flips) if source >> bit & 1)
-        ordered[source * share : (source + 1) * share, :] = first_lags[own ^ place]
-    turned = ordered[...].T
-    dtaps[...] = turned
-    dskip[...] = turned[0:1, :]
-
-
-def call(kernel, name, out_shape, places, scratch=(), flops=0, size=0):
+    first_lags = whole(3)
+    dtaps[...] = first_lags
+    dskip[...] = first_lags[0:1, :]
+
+
+def call(kernel, name, out_shape, places, scratch=(), flops=0, size=0, limit=VMEM_LIMIT):
     vmem = pl.BlockSpec(memory_space=pltpu.VMEM)
     return pl.pallas_call(
         kernel,
@@ -251,20 +244,9 @@
         in_specs=[pl.BlockSpec(memory_space=place) for place in places],
         out_specs=jax.tree.map(lambda _: vmem, out_shape),
         scratch_shapes=list(scratch),
-        compiler_params=pltpu.CompilerParams(vmem_limit_bytes=VMEM_LIMIT),
+        compiler_params=pltpu.CompilerParams(vmem_limit_bytes=limit),
         cost_estimate=pl.CostEstimate(flops=flops, bytes_accessed=size, transcendentals=0),
     )
-
-
-def gather_by_distance(value, axis):
-    count = lax.axis_size(axis)
-    gathered = value[None]
-    flips = {}
-    for bit in range(count.bit_length() - 2, -1, -1):
-        flips[bit] = gathered.shape[0]
-        pairs = [(i, i ^ (1 << bit)) for i in range(count)]
-        gathered = jnp.concatenate([gathered, lax.ppermute(gathered, axis, pairs)], axis=0)
-    return gathered, [flips[bit] for bit in range(len(flips))]
 
 
 def body(query, key, value, implicit_filter, explicit_taps, skip_gain, out_grad):
@@ -275,51 +257,43 @@
     f32 = jnp.float32
     shape = functools.partial(jax.ShapeDtypeStruct, dtype=f32)
     grad_scale = 1.0 / math.sqrt(blocks * rows)
-    me = lax.axis_index("ctx").astype(jnp.int32).reshape(1)
-    first = (me == 0).astype(jnp.int32)
-    direct = share == padded
-
-    packed_shape = (blocks, 3, share, rows) if direct else (3, channels, rows)
+    first = (lax.axis_index("ctx") == 0).astype(jnp.int32).reshape(1)
+
     half = pltpu.VMEM((rows, channels), jnp.bfloat16)
     full = pltpu.VMEM((rows, channels), f32)
     packed = call(
         pack_kernel,
         "pack",
-        shape(packed_shape),
+        shape((blocks, 3, share, rows)),
         (pltpu.SMEM, pltpu.VMEM) + (pltpu.HBM,) * 6,
         scratch=(half,) * 4 + (full,) * 2 + (pltpu.SemaphoreType.DMA((6,)),),
         size=16 * rows * channels,
+        limit=None,
     )(first, skip_gain.reshape(1, channels), query, key, value, implicit_filter, explicit_taps, out_grad)
-    if not direct:
-        packed = packed.reshape(3, blocks, share, rows).swapaxes(0, 1)
     arrays = lax.all_to_all(packed, "ctx", 0, 0, tiled=True)
-    if not direct:
+    if share != padded:
         arrays = jnp.pad(arrays, ((0, 0), (0, 0), (0, padded - share), (0, 0)))
     matrices, twists = tables(blocks, rows)
     height = (blocks + 1) * padded
     scratch = pltpu.VMEM((3, height, 2 * rows), f32)
-    results, first_lags = call(
+    results = call(
         functools.partial(mix_kernel, grad_scale=grad_scale),
         "mix",
-        (shape((blocks, 3, padded, rows)), shape((padded, rows))),
+        shape((blocks, 4, padded, rows)),
         (pltpu.VMEM,) * 3,
         scratch=(scratch, scratch),
         flops=36 * height * (2 * rows) ** 2,
         size=24 * blocks * padded * rows,
     )(jnp.asarray(matrices), jnp.asarray(twists), arrays)
-    if not direct:
-        results, first_lags = results[:, :, :share], first_lags[:share]
-    parts = lax.all_to_all(results, "ctx", 0, 0, tiled=True)
-    first_lags, flips = gather_by_distance(first_lags, "ctx")
+    parts = lax.all_to_all(results[:, :, :share], "ctx", 0, 0, tiled=True)
     full = shape((rows, channels))
     outs = call(
-        functools.partial(unpack_kernel, flips=flips),
+        unpack_kernel,
         "unpack",
         (full,) * 6 + (shape((1, channels)),),
-        (pltpu.SMEM,) + (pltpu.VMEM,) * 6,
-        scratch=(pltpu.VMEM((channels, rows), f32),),
+        (pltpu.VMEM,) * 5,
         size=48 * rows * channels,
-    )(me, query, key, value, out_grad, parts, first_lags)
+    )(query, key, value, out_grad, parts)
     return (*outs[:6], outs[6].reshape(channels))
 
 

time: 79.4 us -> 66.5 us (0.84)
  blocking collectives: 29.5 us -> 58.8 us
  waiting for transfers between devices: 27.4 us -> 0 us
  starting transfers between devices: 9.36 us -> 0 us
  local copies, waits for them, and re-layouts: 6.25 us -> 0.04 us
  Pallas kernels: 5.69 us -> 6.63 us
    all_to_all x0 -> x1, blocking collectives: none -> 29.1 us  [body(): parts = lax.all_to_all(results[:, :, :share], 'ctx', 0, 0, tiled=True)]
    ppermute x4 -> x0, waiting for transfers between devices: 27.4 us -> none  [gather_by_distance(): lax.ppermute(gathered, axis, pairs)]
    unnamed x30 -> x12, local copies, waits for them, and re-layouts: 6.24 us -> 0.04 us
    ppermute x4 -> x0, starting transfers between devices: 5.75 us -> none  [gather_by_distance(): lax.ppermute(gathered, axis, pairs)]
    all_to_all x1 -> x0, starting transfers between devices: 3.61 us -> none  [body(): parts = lax.all_to_all(results, 'ctx', 0, 0, tiled=True)]
    pallas_call x3, Pallas kernels: 5.69 us -> 6.63 us  [the longest x1 3.05 us: body(): call(pack_kernel, 'pack', shape((blocks, 3, share, rows)), (pltpu.SMEM, p...]
  transfers between devices with their start and end apart: 5 -> 0, of which waited for: 4 -> 0; matrix products, arithmetic and copies ran while one was open for 0% -> 0% of each run, Pallas kernels for 0% -> 0%
where the time goes in v6:
time: 66.5 us; the launch traced here: 66.2 us
  blocking collectives  58.8 us (88%)
  Pallas kernels  6.63 us (10%)
  between operations  0.72 us (1%)
    all_to_all x1, blocking collectives, body(): arrays = lax.all_to_all(packed, 'ctx', 0, 0, tiled=True)  29.7 us
    all_to_all x1, blocking collectives, body(): parts = lax.all_to_all(results[:, :, :share], 'ctx', 0, 0, tiled=True)  29.1 us
    pallas_call x1, Pallas kernels, body(): call(pack_kernel, 'pack', shape((blocks, 3, share, rows)), (pltpu.SMEM, p...  3.05 us
    pallas_call x1, Pallas kernels, body(): call(functools.partial(mix_kernel, grad_scale=grad_scale), 'mix', shape((...  2.3 us

profile of v6, /device:TPU:0, one launch (start us, length us, event | category | flops | bytes accessed | tf_op | source)
XLA Modules:
  0.0 66.2 jit_solution(3755155711550718044)
XLA Ops:
  0.6 3.1 %pack.1 = f32[16,3,32,128]{3,2,1,0:T(8,128)} custom-call(s32[1]{0:T(128)} %bitcast.first, f32[1,512]{1,0:T(1,128)} %bitcast.3, bf16[128,512]{1,0:T(8,128)(2,1)} %query.3, bf16[128,512]{1,0:T(8,128)(2,1)} %key.3, bf16[128,512]{1,0:T(8,128)(2,1)} %value.3, f32[128,512]{1,0:T(8,128)} %filt.1, f32[128,512]{1,0:T(8,128)} %taps.1, bf16[128,512]{1,0:T(8,128)(2,1)} %grad.3), custom_call_target="tpu_custom_call" | custom-call | bytes 1048576 | tf_op jit(solution)/shard_map/pack/pallas_call | solution.py:264
  3.7 0.0 copy-start.4
  3.7 0.0 copy-start.5
  3.7 29.7 %all_to_all.10.arrays = f32[16,3,32,128]{3,2,1,0:T(8,128)S(1)} all-to-all(f32[16,3,32,128]{3,2,1,0:T(8,128)} %pack.1), channel_id=1, replica_groups=mesh['ctx'=16,'ch'=2] {'ctx'}, dimensions={0} | all-to-all | bytes 1572864 | tf_op jit(solution)/shard_map/all_to_all | solution.py:273
  33.5 0.0 copy-done.4
  33.5 0.0 copy-done.5
  33.5 2.3 %mix.1 = f32[16,4,32,128]{3,2,1,0:T(8,128)S(1)} custom-call(bf16[4,256,256]{2,1,0:T(8,128)(2,1)S(1)} %copy-done.4, f32[17,4,128]{2,1,0:T(4,128)S(1)} %copy-done.5, f32[16,3,32,128]{3,2,1,0:T(8,128)S(1)} %all_to_all.10.arrays), custom_call_target="tpu_custom_call" | custom-call | flops 1283457024 | bytes 1572864 | tf_op jit(solution)/shard_map/mix/pallas_call | solution.py:279
  35.8 0.0 copy-start
  35.8 0.0 copy-start.1
  35.8 0.0 copy-start.2
  35.8 0.0 copy-start.3
  35.8 29.1 %all_to_all.11.parts = f32[16,4,32,128]{3,2,1,0:T(8,128)S(1)} all-to-all(f32[16,4,32,128]{3,2,1,0:T(8,128)S(1)} %mix.1), channel_id=1, replica_groups=mesh['ctx'=16,'ch'=2] {'ctx'}, dimensions={0} | all-to-all | bytes 2097152 | tf_op jit(solution)/shard_map/all_to_all | solution.py:288
  64.9 0.0 copy-done
  64.9 0.0 copy-done.1
  64.9 0.0 copy-done.2
  64.9 0.0 copy-done.3
  64.9 1.3 %unpack.1 = (f32[128,512]{1,0:T(8,128)}, f32[128,512]{1,0:T(8,128)}, f32[128,512]{1,0:T(8,128)}, f32[128,512]{1,0:T(8,128)}, f32[128,512]{1,0:T(8,128)}, /*index=5*/f32[128,512]{1,0:T(8,128)}, f32[1,512]{1,0:T(1,128)}) custom-call(bf16[128,512]{1,0:T(8,128)(2,1)S(1)} %copy-done, bf16[128,512]{1,0:T(8,128)(2,1)S(1)} %copy-done.1, ...), custom_call_target="tpu_custom_call" | custom-call | bytes 3145728 | tf_op jit(solution)/shard_map/unpack/pallas_call | solution.py:290
Async XLA Ops:
  3.7 29.8 %copy-start.4 = (bf16[4,256,256]{2,1,0:T(8,128)(2,1)S(1)}, bf16[4,256,256]{2,1,0:T(8,128)(2,1)}, u32[]{:S(2)}) copy-start(bf16[4,256,256]{2,1,0:T(8,128)(2,1)} %constant.12.clone.matrices) | copy-start | bytes 1572868
  3.7 29.8 %copy-start.5 = (f32[17,4,128]{2,1,0:T(4,128)S(1)}, f32[17,4,128]{2,1,0:T(4,128)}, u32[]{:S(2)}) copy-start(f32[17,4,128]{2,1,0:T(4,128)} %constant.13.clone.twists) | copy-start | bytes 104452
  35.8 29.1 %copy-start = (bf16[128,512]{1,0:T(8,128)(2,1)S(1)}, bf16[128,512]{1,0:T(8,128)(2,1)}, u32[]{:S(2)}) copy-start(bf16[128,512]{1,0:T(8,128)(2,1)} %query.3) | copy-start | bytes 393220
  35.8 29.1 %copy-start.1 = (bf16[128,512]{1,0:T(8,128)(2,1)S(1)}, bf16[128,512]{1,0:T(8,128)(2,1)}, u32[]{:S(2)}) copy-start(bf16[128,512]{1,0:T(8,128)(2,1)} %key.3) | copy-start | bytes 393220
  35.8 29.1 %copy-start.2 = (bf16[128,512]{1,0:T(8,128)(2,1)S(1)}, bf16[128,512]{1,0:T(8,128)(2,1)}, u32[]{:S(2)}) copy-start(bf16[128,512]{1,0:T(8,128)(2,1)} %value.3) | copy-start | bytes 393220
  35.8 29.1 %copy-start.3 = (bf16[128,512]{1,0:T(8,128)(2,1)S(1)}, bf16[128,512]{1,0:T(8,128)(2,1)}, u32[]{:S(2)}) copy-start(bf16[128,512]{1,0:T(8,128)(2,1)} %grad.3) | copy-start | bytes 393220

commit v7 on v6

--- a/solution.py
+++ b/solution.py
@@ -140,7 +140,7 @@
 
 
 def pack_kernel(first, skip, query, key, value, filt, taps, grad, out, *scratch):
-    *held, arrived = scratch
+    *held, packed, arrived, sent = scratch
     copies = [
         pltpu.make_async_copy(source, target, arrived.at[i])
         for i, (source, target) in enumerate(zip((key, value, query, grad, filt, taps), held))
@@ -151,8 +151,11 @@
     rows, channels = query.shape
     blocks, _, share, _ = out.shape
 
+    sends = [pltpu.make_async_copy(packed.at[:, a], out.at[:, a], sent.at[a]) for a in range(3)]
+
     def put(a, array):
-        out[:, a] = array.T.reshape(blocks, share, rows)
+        packed[:, a] = array.T.reshape(blocks, share, rows)
+        sends[a].start()
 
     copies[0].wait()
     copies[1].wait()
@@ -165,6 +168,8 @@
     row = lax.broadcasted_iota(jnp.int32, (rows, channels), 0)
     extra = taps[...] + jnp.where(row == 0, skip[...], 0.0)
     put(1, filt[...] + jnp.where(first[0] == 1, extra, 0.0))
+    for send in sends:
+        send.wait()
 
 
 def mix_kernel(matrices, twists, arrays, out, spectra, results, *, grad_scale):
@@ -217,32 +222,42 @@
                     out[j, 3, pl.ds(low, 8), :] = values[0] * grad_scale
 
 
-def unpack_kernel(query, key, value, grad, parts, mixed, dquery, dkey, dvalue, dfilter, dtaps, dskip):
+def unpack_kernel(query, key, value, grad, parts, *rest):
+    outs, held, sent = rest[:7], rest[7:14], rest[14]
     rows, channels = query.shape
+    copies = [
+        pltpu.make_async_copy(source, target, sent.at[i])
+        for i, (source, target) in enumerate(zip(held, outs))
+    ]
 
     def whole(a):
         return parts[:, a].reshape(channels, rows).T
 
+    def put(i, array):
+        held[i][...] = array
+        copies[i].start()
+
+    first_lags = whole(3)
+    put(5, first_lags)
+    put(6, first_lags[0:1, :])
+    put(4, whole(2))
     mixer = whole(0)
-    mixed[...] = query[...].astype(jnp.float32) * mixer
-    dquery[...] = grad[...].astype(jnp.float32) * mixer
+    put(0, query[...].astype(jnp.float32) * mixer)
+    put(1, grad[...].astype(jnp.float32) * mixer)
     product_grad = whole(1)
-    dkey[...] = product_grad * value[...].astype(jnp.float32)
-    dvalue[...] = product_grad * key[...].astype(jnp.float32)
-    dfilter[...] = whole(2)
-    first_lags = whole(3)
-    dtaps[...] = first_lags
-    dskip[...] = first_lags[0:1, :]
-
-
-def call(kernel, name, out_shape, places, scratch=(), flops=0, size=0, limit=VMEM_LIMIT):
-    vmem = pl.BlockSpec(memory_space=pltpu.VMEM)
+    put(2, product_grad * value[...].astype(jnp.float32))
+    put(3, product_grad * key[...].astype(jnp.float32))
+    for copy in copies:
+        copy.wait()
+
+
+def call(kernel, name, out_shape, places, scratch=(), flops=0, size=0, limit=VMEM_LIMIT, to=pltpu.VMEM):
     return pl.pallas_call(
         kernel,
         name=name,
         out_shape=out_shape,
         in_specs=[pl.BlockSpec(memory_space=place) for place in places],
-        out_specs=jax.tree.map(lambda _: vmem, out_shape),
+        out_specs=jax.tree.map(lambda _: pl.BlockSpec(memory_space=to), out_shape),
         scratch_shapes=list(scratch),
         compiler_params=pltpu.CompilerParams(vmem_limit_bytes=limit),
         cost_estimate=pl.CostEstimate(flops=flops, bytes_accessed=size, transcendentals=0),
@@ -266,9 +281,12 @@
         "pack",
         shape((blocks, 3, share, rows)),
         (pltpu.SMEM, pltpu.VMEM) + (pltpu.HBM,) * 6,
-        scratch=(half,) * 4 + (full,) * 2 + (pltpu.SemaphoreType.DMA((6,)),),
+        scratch=(half,) * 4
+        + (full,) * 2
+        + (pltpu.VMEM((blocks, 3, share, rows), f32), pltpu.SemaphoreType.DMA((6,)), pltpu.SemaphoreType.DMA((3,))),
         size=16 * rows * channels,
         limit=None,
+        to=pltpu.HBM,
     )(first, skip_gain.reshape(1, channels), query, key, value, implicit_filter, explicit_taps, out_grad)
     arrays = lax.all_to_all(packed, "ctx", 0, 0, tiled=True)
     if share != padded:
@@ -286,12 +304,14 @@
         size=24 * blocks * padded * rows,
     )(jnp.asarray(matrices), jnp.asarray(twists), arrays)
     parts = lax.all_to_all(results[:, :, :share], "ctx", 0, 0, tiled=True)
-    full = shape((rows, channels))
+    full, one = shape((rows, channels)), shape((1, channels))
     outs = call(
         unpack_kernel,
         "unpack",
-        (full,) * 6 + (shape((1, channels)),),
+        (full,) * 6 + (one,),
         (pltpu.VMEM,) * 5,
+        scratch=tuple(pltpu.VMEM(out.shape, f32) for out in (full,) * 6 + (one,)) + (pltpu.SemaphoreType.DMA((7,)),),
+        to=pltpu.HBM,
         size=48 * rows * channels,
     )(query, key, value, out_grad, parts)
     return (*outs[:6], outs[6].reshape(channels))

time: 66.5 us -> 66.4 us (level)
  no operation moved by 1% of the time
where the time goes in v7:
time: 66.4 us; the launch traced here: 66.1 us
  blocking collectives  58.8 us (89%)
  Pallas kernels  6.55 us (10%)
  between operations  0.72 us (1%)
    all_to_all x1, blocking collectives, body(): arrays = lax.all_to_all(packed, 'ctx', 0, 0, tiled=True)  29.7 us
    all_to_all x1, blocking collectives, body(): parts = lax.all_to_all(results[:, :, :share], 'ctx', 0, 0, tiled=True)  29.1 us
    pallas_call x1, Pallas kernels, body(): call(pack_kernel, 'pack', shape((blocks, 3, share, rows)), (pltpu.SMEM, p...  2.91 us
    pallas_call x1, Pallas kernels, body(): call(functools.partial(mix_kernel, grad_scale=grad_scale), 'mix', shape((...  2.3 us
    pallas_call x1, Pallas kernels, body(): call(unpack_kernel, 'unpack', (full,) * 6 + (one,), (pltpu.VMEM,) * 5, sc...  1.34 us

profile of v7, /device:TPU:0, one launch (start us, length us, event | category | flops | bytes accessed | tf_op | source)
XLA Modules:
  0.0 66.1 jit_solution(9204287269890788757)
XLA Ops:
  0.6 2.9 %pack.1 = f32[16,3,32,128]{3,2,1,0:T(8,128)} custom-call(s32[1]{0:T(128)} %bitcast.first, f32[1,512]{1,0:T(1,128)} %bitcast.3, bf16[128,512]{1,0:T(8,128)(2,1)} %query.3, bf16[128,512]{1,0:T(8,128)(2,1)} %key.3, bf16[128,512]{1,0:T(8,128)(2,1)} %value.3, f32[128,512]{1,0:T(8,128)} %filt.1, f32[128,512]{1,0:T(8,128)} %taps.1, bf16[128,512]{1,0:T(8,128)(2,1)} %grad.3), custom_call_target="tpu_custom_call" | custom-call | bytes 1048576 | tf_op jit(solution)/shard_map/pack/pallas_call | solution.py:279
  3.6 0.0 copy-start.4
  3.6 0.0 copy-start.5
  3.6 29.7 %all_to_all.10.arrays = f32[16,3,32,128]{3,2,1,0:T(8,128)S(1)} all-to-all(f32[16,3,32,128]{3,2,1,0:T(8,128)} %pack.1), channel_id=1, replica_groups=mesh['ctx'=16,'ch'=2] {'ctx'}, dimensions={0} | all-to-all | bytes 1572864 | tf_op jit(solution)/shard_map/all_to_all | solution.py:291
  33.3 0.0 copy-done.4
  33.3 0.0 copy-done.5
  33.3 2.3 %mix.1 = f32[16,4,32,128]{3,2,1,0:T(8,128)S(1)} custom-call(bf16[4,256,256]{2,1,0:T(8,128)(2,1)S(1)} %copy-done.4, f32[17,4,128]{2,1,0:T(4,128)S(1)} %copy-done.5, f32[16,3,32,128]{3,2,1,0:T(8,128)S(1)} %all_to_all.10.arrays), custom_call_target="tpu_custom_call" | custom-call | flops 1283457024 | bytes 1572864 | tf_op jit(solution)/shard_map/mix/pallas_call | solution.py:297
  35.6 0.0 copy-start
  35.6 0.0 copy-start.1
  35.7 0.0 copy-start.2
  35.7 0.0 copy-start.3
  35.7 29.1 %all_to_all.11.parts = f32[16,4,32,128]{3,2,1,0:T(8,128)S(1)} all-to-all(f32[16,4,32,128]{3,2,1,0:T(8,128)S(1)} %mix.1), channel_id=1, replica_groups=mesh['ctx'=16,'ch'=2] {'ctx'}, dimensions={0} | all-to-all | bytes 2097152 | tf_op jit(solution)/shard_map/all_to_all | solution.py:306
  64.8 0.0 copy-done
  64.8 0.0 copy-done.1
  64.8 0.0 copy-done.2
  64.8 0.0 copy-done.3
  64.8 1.3 %unpack.1 = (f32[128,512]{1,0:T(8,128)}, f32[128,512]{1,0:T(8,128)}, f32[128,512]{1,0:T(8,128)}, f32[128,512]{1,0:T(8,128)}, f32[128,512]{1,0:T(8,128)}, /*index=5*/f32[128,512]{1,0:T(8,128)}, f32[1,512]{1,0:T(1,128)}) custom-call(bf16[128,512]{1,0:T(8,128)(2,1)S(1)} %copy-done, bf16[128,512]{1,0:T(8,128)(2,1)S(1)} %copy-done.1, ...), custom_call_target="tpu_custom_call" | custom-call | bytes 3145728 | tf_op jit(solution)/shard_map/unpack/pallas_call | solution.py:308
Async XLA Ops:
  3.6 29.8 %copy-start.4 = (bf16[4,256,256]{2,1,0:T(8,128)(2,1)S(1)}, bf16[4,256,256]{2,1,0:T(8,128)(2,1)}, u32[]{:S(2)}) copy-start(bf16[4,256,256]{2,1,0:T(8,128)(2,1)} %constant.12.clone.matrices) | copy-start | bytes 1572868
  3.6 29.8 %copy-start.5 = (f32[17,4,128]{2,1,0:T(4,128)S(1)}, f32[17,4,128]{2,1,0:T(4,128)}, u32[]{:S(2)}) copy-start(f32[17,4,128]{2,1,0:T(4,128)} %constant.13.clone.twists) | copy-start | bytes 104452
  35.6 29.1 %copy-start = (bf16[128,512]{1,0:T(8,128)(2,1)S(1)}, bf16[128,512]{1,0:T(8,128)(2,1)}, u32[]{:S(2)}) copy-start(bf16[128,512]{1,0:T(8,128)(2,1)} %query.3) | copy-start | bytes 393220
  35.6 29.1 %copy-start.1 = (bf16[128,512]{1,0:T(8,128)(2,1)S(1)}, bf16[128,512]{1,0:T(8,128)(2,1)}, u32[]{:S(2)}) copy-start(bf16[128,512]{1,0:T(8,128)(2,1)} %key.3) | copy-start | bytes 393220
  35.7 29.1 %copy-start.2 = (bf16[128,512]{1,0:T(8,128)(2,1)S(1)}, bf16[128,512]{1,0:T(8,128)(2,1)}, u32[]{:S(2)}) copy-start(bf16[128,512]{1,0:T(8,128)(2,1)} %value.3) | copy-start | bytes 393220
  35.7 29.1 %copy-start.3 = (bf16[128,512]{1,0:T(8,128)(2,1)S(1)}, bf16[128,512]{1,0:T(8,128)(2,1)}, u32[]{:S(2)}) copy-start(bf16[128,512]{1,0:T(8,128)(2,1)} %grad.3) | copy-start | bytes 393220

commit v8 on v7

--- a/solution.py
+++ b/solution.py
@@ -139,37 +139,10 @@
     return dot(values_high, high) + (dot(values_low, high) + dot(values_high, low))
 
 
-def pack_kernel(first, skip, query, key, value, filt, taps, grad, out, *scratch):
-    *held, packed, arrived, sent = scratch
-    copies = [
-        pltpu.make_async_copy(source, target, arrived.at[i])
-        for i, (source, target) in enumerate(zip((key, value, query, grad, filt, taps), held))
-    ]
-    for copy in copies:
-        copy.start()
-    key, value, query, grad, filt, taps = held
-    rows, channels = query.shape
-    blocks, _, share, _ = out.shape
-
-    sends = [pltpu.make_async_copy(packed.at[:, a], out.at[:, a], sent.at[a]) for a in range(3)]
-
-    def put(a, array):
-        packed[:, a] = array.T.reshape(blocks, share, rows)
-        sends[a].start()
-
-    copies[0].wait()
-    copies[1].wait()
-    put(0, key[...].astype(jnp.float32) * value[...].astype(jnp.float32))
-    copies[2].wait()
-    copies[3].wait()
-    put(2, grad[...].astype(jnp.float32) * query[...].astype(jnp.float32))
-    copies[4].wait()
-    copies[5].wait()
-    row = lax.broadcasted_iota(jnp.int32, (rows, channels), 0)
-    extra = taps[...] + jnp.where(row == 0, skip[...], 0.0)
-    put(1, filt[...] + jnp.where(first[0] == 1, extra, 0.0))
-    for send in sends:
-        send.wait()
+def pack_kernel(product, filt, mix_grad, out):
+    blocks, _, share, rows = out.shape
+    for a, field in enumerate((product, filt, mix_grad)):
+        out[:, a] = field[...].T.reshape(blocks, share, rows)
 
 
 def mix_kernel(matrices, twists, arrays, out, spectra, results, *, grad_scale):
@@ -272,22 +245,15 @@
     f32 = jnp.float32
     shape = functools.partial(jax.ShapeDtypeStruct, dtype=f32)
     grad_scale = 1.0 / math.sqrt(blocks * rows)
-    first = (lax.axis_index("ctx") == 0).astype(jnp.int32).reshape(1)
-
-    half = pltpu.VMEM((rows, channels), jnp.bfloat16)
-    full = pltpu.VMEM((rows, channels), f32)
+    first = lax.axis_index("ctx") == 0
+
+    product = key.astype(f32) * value.astype(f32)
+    mix_grad = out_grad.astype(f32) * query.astype(f32)
+    direct = jnp.where(jnp.arange(rows)[:, None] == 0, skip_gain, 0.0)
+    combined = implicit_filter + jnp.where(first, explicit_taps + direct, 0.0)
     packed = call(
-        pack_kernel,
-        "pack",
-        shape((blocks, 3, share, rows)),
-        (pltpu.SMEM, pltpu.VMEM) + (pltpu.HBM,) * 6,
-        scratch=(half,) * 4
-        + (full,) * 2
-        + (pltpu.VMEM((blocks, 3, share, rows), f32), pltpu.SemaphoreType.DMA((6,)), pltpu.SemaphoreType.DMA((3,))),
-        size=16 * rows * channels,
-        limit=None,
-        to=pltpu.HBM,
-    )(first, skip_gain.reshape(1, channels), query, key, value, implicit_filter, explicit_taps, out_grad)
+        pack_kernel, "pack", shape((blocks, 3, share, rows)), (pltpu.VMEM,) * 3, size=24 * rows * channels
+    )(product, combined, mix_grad)
     arrays = lax.all_to_all(packed, "ctx", 0, 0, tiled=True)
     if share != padded:
         arrays = jnp.pad(arrays, ((0, 0), (0, 0), (0, padded - share), (0, 0)))

time: 66.4 us -> 65.8 us (level)
  Pallas kernels: 6.55 us -> 3.89 us
  other arithmetic: 0 us -> 2.11 us
    pallas_call x1, Pallas kernels: 2.91 us -> 0.26 us  [body(): call(pack_kernel, 'pack', shape((blocks, 3, share, rows)), (pltpu.VMEM,)...]
    mul x0 -> x2, other arithmetic: none -> 2.11 us  [the longest x1 1.06 us: body(): mix_grad = out_grad.astype(f32) * query.astype(f32)]
where the time goes in v8:
time: 65.8 us; the launch traced here: 65.5 us
  blocking collectives  58.6 us (89%)
  Pallas kernels  3.89 us (6%)
  other arithmetic  2.11 us (3%)
  between operations  0.77 us (1%)
    all_to_all x1, blocking collectives, body(): arrays = lax.all_to_all(packed, 'ctx', 0, 0, tiled=True)  29.5 us
    all_to_all x1, blocking collectives, body(): parts = lax.all_to_all(results[:, :, :share], 'ctx', 0, 0, tiled=True)  29.1 us
    pallas_call x1, Pallas kernels, body(): call(functools.partial(mix_kernel, grad_scale=grad_scale), 'mix', shape((...  2.3 us
    pallas_call x1, Pallas kernels, body(): call(unpack_kernel, 'unpack', (full,) * 6 + (one,), (pltpu.VMEM,) * 5, sc...  1.34 us

profile of v8, /device:TPU:0, one launch (start us, length us, event | category | flops | bytes accessed | tf_op | source)
XLA Modules:
  0.0 65.5 jit_solution(12138204681659433605)
XLA Ops:
  0.7 0.0 copy-start.7
  0.7 0.0 copy-start
  0.7 0.0 copy-start.1
  0.7 0.0 copy-start.6
  0.7 1.1 %convert_multiply_fusion.1.product = f32[128,512]{1,0:T(8,128)S(1)} fusion(bf16[128,512]{1,0:T(8,128)(2,1)} %value.1, bf16[128,512]{1,0:T(8,128)(2,1)} %key.1), kind=kLoop, calls=%fused_computation.2 | loop fusion | flops 196608 | bytes 524288 | tf_op jit(solution)/shard_map/mul | solution.py:250
  1.8 0.0 copy-done.7
  1.8 0.0 copy-done
  1.8 0.0 copy-done.1
  1.8 0.1 copy-done.6
  1.9 1.1 %convert_multiply_fusion = (f32[128,512]{1,0:T(8,128)S(1)}, f32[128,512]{1,0:T(8,128)S(1)}) fusion(bf16[128,512]{1,0:T(8,128)(2,1)S(1)} %copy-done, bf16[128,512]{1,0:T(8,128)(2,1)S(1)} %copy-done.1, f32[128,512]{1,0:T(8,128)S(1)} %copy-done.6, f32[128,512]{1,0:T(8,128)} %param.13, f32[512]{0:T(512)S(1)} %copy-done.7, pred[128]{0:T(512)(128)(4,1)S(1)} %iota_compare_fusion, ...), kind=kLoop, calls=%fused_computation | loop fusion | flops 458752 | bytes 1312897 | tf_op jit(solution)/shard_map/mul | solution.py:251
  2.9 0.3 pack.1
  3.2 0.0 copy-start.4
  3.2 0.0 copy-start.5
  3.2 29.5 %all_to_all.10.arrays = f32[16,3,32,128]{3,2,1,0:T(8,128)S(1)} all-to-all(f32[16,3,32,128]{3,2,1,0:T(8,128)S(1)} %pack.1), channel_id=1, replica_groups=mesh['ctx'=16,'ch'=2] {'ctx'}, dimensions={0} | all-to-all | bytes 1572864 | tf_op jit(solution)/shard_map/all_to_all | solution.py:257
  32.8 0.0 copy-done.4
  32.8 0.0 copy-done.5
  32.8 2.3 %mix.1 = f32[16,4,32,128]{3,2,1,0:T(8,128)S(1)} custom-call(bf16[4,256,256]{2,1,0:T(8,128)(2,1)S(1)} %copy-done.4, f32[17,4,128]{2,1,0:T(4,128)S(1)} %copy-done.5, f32[16,3,32,128]{3,2,1,0:T(8,128)S(1)} %all_to_all.10.arrays), custom_call_target="tpu_custom_call" | custom-call | flops 1283457024 | bytes 1572864 | tf_op jit(solution)/shard_map/mix/pallas_call | solution.py:263
  35.1 0.0 copy-start.2
  35.1 0.0 copy-start.3
  35.1 29.1 %all_to_all.11.parts = f32[16,4,32,128]{3,2,1,0:T(8,128)S(1)} all-to-all(f32[16,4,32,128]{3,2,1,0:T(8,128)S(1)} %mix.1), channel_id=1, replica_groups=mesh['ctx'=16,'ch'=2] {'ctx'}, dimensions={0} | all-to-all | bytes 2097152 | tf_op jit(solution)/shard_map/all_to_all | solution.py:272
  64.2 0.0 copy-done.2
  64.2 0.0 copy-done.3
  64.2 1.3 %unpack.1 = (f32[128,512]{1,0:T(8,128)}, f32[128,512]{1,0:T(8,128)}, f32[128,512]{1,0:T(8,128)}, f32[128,512]{1,0:T(8,128)}, f32[128,512]{1,0:T(8,128)}, /*index=5*/f32[128,512]{1,0:T(8,128)}, f32[1,512]{1,0:T(1,128)}) custom-call(bf16[128,512]{1,0:T(8,128)(2,1)S(1)} %copy-done, bf16[128,512]{1,0:T(8,128)(2,1)S(1)} %copy-done.2, ...), custom_call_target="tpu_custom_call" | custom-call | bytes 3145728 | tf_op jit(solution)/shard_map/unpack/pallas_call | solution.py:274
  (1 shorter events, 0.0 us)
Async XLA Ops:
  0.7 1.1 %copy-start.7 = (f32[512]{0:T(512)S(1)}, f32[512]{0:T(512)}, u32[]{:S(2)}) copy-start(f32[512]{0:T(512)} %param.14) | copy-start | bytes 6148
  0.7 1.1 %copy-start = (bf16[128,512]{1,0:T(8,128)(2,1)S(1)}, bf16[128,512]{1,0:T(8,128)(2,1)}, u32[]{:S(2)}) copy-start(bf16[128,512]{1,0:T(8,128)(2,1)} %query.1) | copy-start | bytes 393220
  0.7 1.1 %copy-start.1 = (bf16[128,512]{1,0:T(8,128)(2,1)S(1)}, bf16[128,512]{1,0:T(8,128)(2,1)}, u32[]{:S(2)}) copy-start(bf16[128,512]{1,0:T(8,128)(2,1)} %grad.1) | copy-start | bytes 393220
  0.7 1.2 %copy-start.6 = (f32[128,512]{1,0:T(8,128)S(1)}, f32[128,512]{1,0:T(8,128)}, u32[]{:S(2)}) copy-start(f32[128,512]{1,0:T(8,128)} %param.12) | copy-start | bytes 786436
  3.2 29.6 %copy-start.4 = (bf16[4,256,256]{2,1,0:T(8,128)(2,1)S(1)}, bf16[4,256,256]{2,1,0:T(8,128)(2,1)}, u32[]{:S(2)}) copy-start(bf16[4,256,256]{2,1,0:T(8,128)(2,1)} %constant.15.clone.matrices) | copy-start | bytes 1572868
  3.2 29.5 %copy-start.5 = (f32[17,4,128]{2,1,0:T(4,128)S(1)}, f32[17,4,128]{2,1,0:T(4,128)}, u32[]{:S(2)}) copy-start(f32[17,4,128]{2,1,0:T(4,128)} %constant.16.clone.twists) | copy-start | bytes 104452
  35.1 29.1 %copy-start.2 = (bf16[128,512]{1,0:T(8,128)(2,1)S(1)}, bf16[128,512]{1,0:T(8,128)(2,1)}, u32[]{:S(2)}) copy-start(bf16[128,512]{1,0:T(8,128)(2,1)} %key.1) | copy-start | bytes 393220
  35.1 29.1 %copy-start.3 = (bf16[128,512]{1,0:T(8,128)(2,1)S(1)}, bf16[128,512]{1,0:T(8,128)(2,1)}, u32[]{:S(2)}) copy-start(bf16[128,512]{1,0:T(8,128)(2,1)} %value.1) | copy-start | bytes 393220

commit v9 on v8

--- a/solution.py
+++ b/solution.py
@@ -139,18 +139,29 @@
     return dot(values_high, high) + (dot(values_low, high) + dot(values_high, low))
 
 
-def pack_kernel(product, filt, mix_grad, out):
+def pack_kernel(product, query, grad, filt, out):
     blocks, _, share, rows = out.shape
-    for a, field in enumerate((product, filt, mix_grad)):
-        out[:, a] = field[...].T.reshape(blocks, share, rows)
-
-
-def mix_kernel(matrices, twists, arrays, out, spectra, results, *, grad_scale):
+
+    def put(a, field):
+        out[:, a] = field.T.reshape(blocks, share, rows)
+
+    put(0, product[...])
+    put(2, grad[...].astype(jnp.float32) * query[...].astype(jnp.float32))
+    put(1, filt[...])
+
+
+def mix_kernel(taps, skip, matrices, twists, arrays, out, spectra, results, direct, *, grad_scale):
     blocks, _, channels, rows = arrays.shape
+    row = lax.broadcasted_iota(jnp.int32, taps.shape, 0)
+    direct[...] = (taps[...] + jnp.where(row == 0, skip[...], 0.0)).T
+    own = 0 if direct.shape[0] == channels else pl.multiple_of(lax.axis_index("ctx") * channels, channels)
     for a in range(3):
         for low in range(0, channels, 8):
             part = pl.ds(low, 8)
-            bins = padded_bins([arrays[j, a, part, :] for j in range(blocks)])
+            values = [arrays[j, a, part, :] for j in range(blocks)]
+            if a == 1:
+                values[0] = values[0] + direct[pl.ds(own + low, 8), :]
+            bins = padded_bins(values)
             for p in range(blocks + 1):
                 real, imag = bins[p]
                 cosine, sine = twists[p, 0:1, :], twists[p, 1:2, :]
@@ -245,18 +256,20 @@
     f32 = jnp.float32
     shape = functools.partial(jax.ShapeDtypeStruct, dtype=f32)
     grad_scale = 1.0 / math.sqrt(blocks * rows)
-    first = lax.axis_index("ctx") == 0
+    taps, skip = explicit_taps, skip_gain.reshape(1, channels)
 
     product = key.astype(f32) * value.astype(f32)
-    mix_grad = out_grad.astype(f32) * query.astype(f32)
-    direct = jnp.where(jnp.arange(rows)[:, None] == 0, skip_gain, 0.0)
-    combined = implicit_filter + jnp.where(first, explicit_taps + direct, 0.0)
     packed = call(
-        pack_kernel, "pack", shape((blocks, 3, share, rows)), (pltpu.VMEM,) * 3, size=24 * rows * channels
-    )(product, combined, mix_grad)
+        pack_kernel, "pack", shape((blocks, 3, share, rows)), (pltpu.VMEM,) * 4, size=24 * rows * channels
+    )(product, query, out_grad, implicit_filter)
     arrays = lax.all_to_all(packed, "ctx", 0, 0, tiled=True)
     if share != padded:
         arrays = jnp.pad(arrays, ((0, 0), (0, 0), (0, padded - share), (0, 0)))
+        own = lax.axis_index("ctx") * share
+        taps, skip = [
+            jnp.pad(lax.dynamic_slice_in_dim(each, own, share, 1), ((0, 0), (0, padded - share)))
+            for each in (taps, skip)
+        ]
     matrices, twists = tables(blocks, rows)
     height = (blocks + 1) * padded
     scratch = pltpu.VMEM((3, height, 2 * rows), f32)
@@ -264,11 +277,11 @@
         functools.partial(mix_kernel, grad_scale=grad_scale),
         "mix",
         shape((blocks, 4, padded, rows)),
-        (pltpu.VMEM,) * 3,
-        scratch=(scratch, scratch),
+        (pltpu.VMEM,) * 5,
+        scratch=(scratch, scratch, pltpu.VMEM(taps.shape[::-1], f32)),
         flops=36 * height * (2 * rows) ** 2,
         size=24 * blocks * padded * rows,
-    )(jnp.asarray(matrices), jnp.asarray(twists), arrays)
+    )(taps, skip, jnp.asarray(matrices), jnp.asarray(twists), arrays)
     parts = lax.all_to_all(results[:, :, :share], "ctx", 0, 0, tiled=True)
     full, one = shape((rows, channels)), shape((1, channels))
     outs = call(

time: 65.8 us -> 64.6 us (0.982)
  other arithmetic: 2.11 us -> 1.05 us
    mul x1 -> x0, other arithmetic: 1.06 us -> none  [body(): mix_grad = out_grad.astype(f32) * query.astype(f32)]
where the time goes in v9:
time: 64.6 us; the launch traced here: 64.4 us
  blocking collectives  58.6 us (91%)
  Pallas kernels  3.84 us (6%)
  other arithmetic  1.05 us (2%)
  between operations  0.76 us (1%)
    all_to_all x1, blocking collectives, body(): arrays = lax.all_to_all(packed, 'ctx', 0, 0, tiled=True)  29.5 us
    all_to_all x1, blocking collectives, body(): parts = lax.all_to_all(results[:, :, :share], 'ctx', 0, 0, tiled=True)  29.1 us
    pallas_call x1, Pallas kernels, body(): call(functools.partial(mix_kernel, grad_scale=grad_scale), 'mix', shape((...  2.24 us
    pallas_call x1, Pallas kernels, body(): call(unpack_kernel, 'unpack', (full,) * 6 + (one,), (pltpu.VMEM,) * 5, sc...  1.34 us

profile of v9, /device:TPU:0, one launch (start us, length us, event | category | flops | bytes accessed | tf_op | source)
XLA Modules:
  0.0 64.4 jit_solution(3074953882828332261)
XLA Ops:
  0.6 0.0 copy-start.1
  0.6 0.0 copy-start
  0.7 0.0 copy-start.4
  0.7 1.1 %convert_multiply_fusion.product = f32[128,512]{1,0:T(8,128)S(1)} fusion(bf16[128,512]{1,0:T(8,128)(2,1)} %value.1, bf16[128,512]{1,0:T(8,128)(2,1)} %key.1), kind=kLoop, calls=%fused_computation | loop fusion | flops 196608 | bytes 524288 | tf_op jit(solution)/shard_map/mul | solution.py:261
  1.7 0.0 copy-done.1
  1.7 0.0 copy-done
  1.7 0.1 copy-done.4
  1.8 0.3 pack.1
  2.1 0.0 copy-start.5
  2.1 0.0 copy-start.6
  2.1 0.0 copy-start.7
  2.1 0.0 copy-start.8
  2.2 29.5 %all_to_all.10.arrays = f32[16,3,32,128]{3,2,1,0:T(8,128)S(1)} all-to-all(f32[16,3,32,128]{3,2,1,0:T(8,128)S(1)} %pack.1), channel_id=1, replica_groups=mesh['ctx'=16,'ch'=2] {'ctx'}, dimensions={0} | all-to-all | bytes 1572864 | tf_op jit(solution)/shard_map/all_to_all | solution.py:265
  31.7 0.0 copy-done.5
  31.7 0.0 copy-done.6
  31.7 0.0 copy-done.7
  31.7 0.0 copy-done.8
  31.7 2.2 %mix.1 = f32[16,4,32,128]{3,2,1,0:T(8,128)S(1)} custom-call(f32[128,512]{1,0:T(8,128)S(1)} %copy-done.5, f32[1,512]{1,0:T(1,128)S(1)} %bitcast.2, bf16[4,256,256]{2,1,0:T(8,128)(2,1)S(1)} %copy-done.7, f32[17,4,128]{2,1,0:T(4,128)S(1)} %copy-done.8, f32[16,3,32,128]{3,2,1,0:T(8,128)S(1)} %all_to_all.10.arrays), custom_call_target="tpu_custom_call" | custom-call | flops 1283457024 | bytes 1572864 | tf_op jit(solution)/shard_map/mix/pallas_call | solution.py:276
  34.0 0.0 copy-start.2
  34.0 0.0 copy-start.3
  34.0 29.1 %all_to_all.11.parts = f32[16,4,32,128]{3,2,1,0:T(8,128)S(1)} all-to-all(f32[16,4,32,128]{3,2,1,0:T(8,128)S(1)} %mix.1), channel_id=1, replica_groups=mesh['ctx'=16,'ch'=2] {'ctx'}, dimensions={0} | all-to-all | bytes 2097152 | tf_op jit(solution)/shard_map/all_to_all | solution.py:285
  63.1 0.0 copy-done.2
  63.1 0.0 copy-done.3
  63.1 1.3 %unpack.1 = (f32[128,512]{1,0:T(8,128)}, f32[128,512]{1,0:T(8,128)}, f32[128,512]{1,0:T(8,128)}, f32[128,512]{1,0:T(8,128)}, f32[128,512]{1,0:T(8,128)}, /*index=5*/f32[128,512]{1,0:T(8,128)}, f32[1,512]{1,0:T(1,128)}) custom-call(bf16[128,512]{1,0:T(8,128)(2,1)S(1)} %copy-done, bf16[128,512]{1,0:T(8,128)(2,1)S(1)} %copy-done.2, ...), custom_call_target="tpu_custom_call" | custom-call | bytes 3145728 | tf_op jit(solution)/shard_map/unpack/pallas_call | solution.py:287
Async XLA Ops:
  0.6 1.1 %copy-start.1 = (bf16[128,512]{1,0:T(8,128)(2,1)S(1)}, bf16[128,512]{1,0:T(8,128)(2,1)}, u32[]{:S(2)}) copy-start(bf16[128,512]{1,0:T(8,128)(2,1)} %grad.3) | copy-start | bytes 393220
  0.6 1.1 %copy-start = (bf16[128,512]{1,0:T(8,128)(2,1)S(1)}, bf16[128,512]{1,0:T(8,128)(2,1)}, u32[]{:S(2)}) copy-start(bf16[128,512]{1,0:T(8,128)(2,1)} %query.3) | copy-start | bytes 393220
  0.7 1.2 %copy-start.4 = (f32[128,512]{1,0:T(8,128)S(1)}, f32[128,512]{1,0:T(8,128)}, u32[]{:S(2)}) copy-start(f32[128,512]{1,0:T(8,128)} %filt.1) | copy-start | bytes 786436
  2.1 29.6 %copy-start.5 = (f32[128,512]{1,0:T(8,128)S(1)}, f32[128,512]{1,0:T(8,128)}, u32[]{:S(2)}) copy-start(f32[128,512]{1,0:T(8,128)} %taps.1) | copy-start | bytes 786436
  2.1 29.6 %copy-start.6 = (f32[512]{0:T(512)S(1)}, f32[512]{0:T(512)}, u32[]{:S(2)}) copy-start(f32[512]{0:T(512)} %param.14) | copy-start | bytes 6148
  2.1 29.6 %copy-start.7 = (bf16[4,256,256]{2,1,0:T(8,128)(2,1)S(1)}, bf16[4,256,256]{2,1,0:T(8,128)(2,1)}, u32[]{:S(2)}) copy-start(bf16[4,256,256]{2,1,0:T(8,128)(2,1)} %constant.4.clone.matrices) | copy-start | bytes 1572868
  2.1 29.6 %copy-start.8 = (f32[17,4,128]{2,1,0:T(4,128)S(1)}, f32[17,4,128]{2,1,0:T(4,128)}, u32[]{:S(2)}) copy-start(f32[17,4,128]{2,1,0:T(4,128)} %constant.5.clone.twists) | copy-start | bytes 104452
  34.0 29.1 %copy-start.2 = (bf16[128,512]{1,0:T(8,128)(2,1)S(1)}, bf16[128,512]{1,0:T(8,128)(2,1)}, u32[]{:S(2)}) copy-start(bf16[128,512]{1,0:T(8,128)(2,1)} %key.1) | copy-start | bytes 393220
  34.0 29.1 %copy-start.3 = (bf16[128,512]{1,0:T(8,128)(2,1)S(1)}, bf16[128,512]{1,0:T(8,128)(2,1)}, u32[]{:S(2)}) copy-start(bf16[128,512]{1,0:T(8,128)(2,1)} %value.1) | copy-start | bytes 393220

commit v10 on v9

--- a/solution.py
+++ b/solution.py
@@ -10,6 +10,7 @@
 from jax.sharding import PartitionSpec as P
 
 VMEM_LIMIT = 48 * 1024 * 1024
+RELAY_WEIGHT = 10**11
 
 
 def turn(value, turns):
@@ -139,18 +140,19 @@
     return dot(values_high, high) + (dot(values_low, high) + dot(values_high, low))
 
 
-def pack_kernel(product, query, grad, filt, out):
+def pack_kernel(product, grad, filt, out):
     blocks, _, share, rows = out.shape
 
     def put(a, field):
         out[:, a] = field.T.reshape(blocks, share, rows)
 
     put(0, product[...])
-    put(2, grad[...].astype(jnp.float32) * query[...].astype(jnp.float32))
+    put(2, grad[...])
     put(1, filt[...])
 
 
-def mix_kernel(taps, skip, matrices, twists, arrays, out, spectra, results, direct, *, grad_scale):
+def spectra_kernel(taps, skip, matrices, twists, arrays, products, *rest, near_count, grad_scale):
+    *lag_outs, spectra, results, direct, lags = rest
     blocks, _, channels, rows = arrays.shape
     row = lax.broadcasted_iota(jnp.int32, taps.shape, 0)
     direct[...] = (taps[...] + jnp.where(row == 0, skip[...], 0.0)).T
@@ -172,65 +174,94 @@
                 else:
                     spectra[a, place, :rows] = real * cosine - imag * sine
                     spectra[a, place, rows:] = real * sine + imag * cosine
-    forward_high, forward_low = matrices[0], matrices[1]
-    back_high, back_low = matrices[2], matrices[3]
-    product, filt, mix_grad = [multiply(spectra[a], forward_high, forward_low) for a in range(3)]
+    product, filt, mix_grad = [multiply(spectra[a], matrices[0], matrices[1]) for a in range(3)]
     pr, pi = product[:, :rows], product[:, rows:]
     fr, fi = filt[:, :rows], filt[:, rows:]
     gr, gi = mix_grad[:, :rows], mix_grad[:, rows:]
-    spectra[0, :, :rows] = fr * pr - fi * pi
-    spectra[0, :, rows:] = fr * pi + fi * pr
-    spectra[1, :, :rows] = fr * gr + fi * gi
-    spectra[1, :, rows:] = fr * gi - fi * gr
-    spectra[2, :, :rows] = pr * gr + pi * gi
-    spectra[2, :, rows:] = pr * gi - pi * gr
-    for a in range(3):
-        results[a] = multiply(spectra[a], back_high, back_low)
-        for low in range(0, channels, 8):
-            bins = {}
-            for p in range(blocks + 1):
-                cosine, sine = twists[p, 2:3, :], twists[p, 3:4, :]
-                place = pl.ds(p * channels + low, 8)
-                real, imag = results[a, place, :rows], results[a, place, rows:]
-                new_real = real * cosine - imag * sine
-                if p % blocks == 0:
-                    bins[p] = (new_real, None)
-                else:
-                    bins[p] = (new_real, real * sine + imag * cosine)
-            values = padded_bins_back(bins, blocks)
-            for j in range(blocks):
-                value = values[j] * grad_scale if a == 2 else values[j]
+    spectra[0, :, :rows] = pr * gr + pi * gi
+    spectra[0, :, rows:] = pr * gi - pi * gr
+    products[0, :, :rows] = fr * pr - fi * pi
+    products[0, :, rows:] = fr * pi + fi * pr
+    products[1, :, :rows] = fr * gr + fi * gi
+    products[1, :, rows:] = fr * gi - fi * gr
+    for low, values in blocks_back(spectra.at[0], results, matrices, twists, channels):
+        for j, value in enumerate(values):
+            lags[j, pl.ds(low, 8), :] = value * grad_scale
+    me = lax.axis_index("ctx") if near_count > 1 else 0
+    for far, lag_out in enumerate(lag_outs):
+        for near in range(near_count):
+            lag_out[near] = lags[me ^ (far * near_count + near)]
+        lag_out[near_count] = lags[0]
+
+
+def blocks_back(spectrum, result, matrices, twists, channels):
+    blocks, rows = twists.shape[0] - 1, twists.shape[2]
+    result[...] = multiply(spectrum[...], matrices[2], matrices[3])
+    for low in range(0, channels, 8):
+        bins = {}
+        for p in range(blocks + 1):
+            cosine, sine = twists[p, 2:3, :], twists[p, 3:4, :]
+            place = pl.ds(p * channels + low, 8)
+            real, imag = result[place, :rows], result[place, rows:]
+            new_real = real * cosine - imag * sine
+            bins[p] = (new_real, None if p % blocks == 0 else real * sine + imag * cosine)
+        yield low, padded_bins_back(bins, blocks)
+
+
+def mix_kernel(matrices, twists, products, out, results):
+    for a in range(2):
+        for low, values in blocks_back(products.at[a], results.at[a], matrices, twists, out.shape[2]):
+            for j, value in enumerate(values):
                 out[j, a, pl.ds(low, 8), :] = value
-            if a == 2:
-                for j in range(blocks):
-                    out[j, 3, pl.ds(low, 8), :] = values[0] * grad_scale
-
-
-def unpack_kernel(query, key, value, grad, parts, *rest):
-    outs, held, sent = rest[:7], rest[7:14], rest[14]
+
+
+def relay_kernel(*refs):
+    near_count = refs[0].shape[0] - 1
+    far_count = len(refs) - near_count + 1
+    parts, outs = refs[:far_count], refs[far_count:]
+    for near, out in enumerate(outs, 1):
+        for far, part in enumerate(parts):
+            out[far] = part[near]
+            out[far_count + far] = part[near_count]
+
+
+def unpack_kernel(query, key, value, grad, parts, *rest, far_count, near_count):
+    far_parts, rest = rest[:far_count], rest[far_count:]
+    near_parts, rest = rest[: near_count - 1], rest[near_count - 1 :]
+    outs, held, sent, lags, first_lags = rest[:7], rest[7:14], rest[14], rest[15], rest[16]
     rows, channels = query.shape
     copies = [
         pltpu.make_async_copy(source, target, sent.at[i])
         for i, (source, target) in enumerate(zip(held, outs))
     ]
 
-    def whole(a):
-        return parts[:, a].reshape(channels, rows).T
+    def whole(array):
+        return array.reshape(channels, rows).T
 
     def put(i, array):
         held[i][...] = array
         copies[i].start()
 
-    first_lags = whole(3)
-    put(5, first_lags)
-    put(6, first_lags[0:1, :])
-    put(4, whole(2))
-    mixer = whole(0)
+    mixer = whole(parts[:, 0])
     put(0, query[...].astype(jnp.float32) * mixer)
     put(1, grad[...].astype(jnp.float32) * mixer)
-    product_grad = whole(1)
+    product_grad = whole(parts[:, 1])
     put(2, product_grad * value[...].astype(jnp.float32))
     put(3, product_grad * key[...].astype(jnp.float32))
+    me = lax.axis_index("ctx") if near_count > 1 else 0
+    for far, part in enumerate(far_parts):
+        source = me ^ (far * near_count)
+        lags[source] = part[0]
+        first_lags[source] = part[near_count]
+    for near, part in enumerate(near_parts, 1):
+        for far in range(far_count):
+            source = me ^ (far * near_count + near)
+            lags[source] = part[far]
+            first_lags[source] = part[far_count + far]
+    put(4, whole(lags[...]))
+    first = whole(first_lags[...])
+    put(5, first)
+    put(6, first[0:1, :])
     for copy in copies:
         copy.wait()
 
@@ -248,6 +279,22 @@
     )
 
 
+def exchange(value, axis, distance):
+    return lax.ppermute(value, axis, [(i, i ^ distance) for i in range(lax.axis_size(axis))])
+
+
+def send_lags(lag_parts, axis, near_count):
+    far_parts = list(lag_parts)
+    for far in range(len(far_parts) - 1, 0, -1):
+        far_parts[far] = exchange(lag_parts[far], axis, far * near_count)
+    payload = jax.ShapeDtypeStruct((2 * len(far_parts), *lag_parts[0].shape[1:]), jnp.float32)
+    relay = call(
+        relay_kernel, "relay", (payload,) * (near_count - 1), (pltpu.VMEM,) * len(far_parts), flops=RELAY_WEIGHT
+    )
+    near_parts = relay(*far_parts)
+    return far_parts, [exchange(part, axis, near) for near, part in enumerate(near_parts, 1)]
+
+
 def body(query, key, value, implicit_filter, explicit_taps, skip_gain, out_grad):
     rows, channels = query.shape
     blocks = lax.axis_size("ctx")
@@ -259,9 +306,10 @@
     taps, skip = explicit_taps, skip_gain.reshape(1, channels)
 
     product = key.astype(f32) * value.astype(f32)
+    mix_grad = out_grad.astype(f32) * query.astype(f32)
     packed = call(
-        pack_kernel, "pack", shape((blocks, 3, share, rows)), (pltpu.VMEM,) * 4, size=24 * rows * channels
-    )(product, query, out_grad, implicit_filter)
+        pack_kernel, "pack", shape((blocks, 3, share, rows)), (pltpu.VMEM,) * 3, size=24 * rows * channels
+    )(product, mix_grad, implicit_filter)
     arrays = lax.all_to_all(packed, "ctx", 0, 0, tiled=True)
     if share != padded:
         arrays = jnp.pad(arrays, ((0, 0), (0, 0), (0, padded - share), (0, 0)))
@@ -272,27 +320,52 @@
         ]
     matrices, twists = tables(blocks, rows)
     height = (blocks + 1) * padded
-    scratch = pltpu.VMEM((3, height, 2 * rows), f32)
+    near_count = 1 << (blocks.bit_length() - 1) // 2 if share == padded else 1
+    far_count = blocks // near_count
+    matrices, twists = jnp.asarray(matrices), jnp.asarray(twists)
+    products, *lag_parts = call(
+        functools.partial(spectra_kernel, near_count=near_count, grad_scale=grad_scale),
+        "spectra",
+        (shape((2, height, 2 * rows)),) + (shape((near_count + 1, padded, rows)),) * far_count,
+        (pltpu.VMEM,) * 5,
+        scratch=(
+            pltpu.VMEM((3, height, 2 * rows), f32),
+            pltpu.VMEM((height, 2 * rows), f32),
+            pltpu.VMEM(taps.shape[::-1], f32),
+            pltpu.VMEM((blocks, padded, rows), f32),
+        ),
+        flops=24 * height * (2 * rows) ** 2,
+        size=24 * blocks * padded * rows,
+    )(taps, skip, matrices, twists, arrays)
+    if near_count > 1:
+        far_parts, near_parts = send_lags(lag_parts, "ctx", near_count)
     results = call(
-        functools.partial(mix_kernel, grad_scale=grad_scale),
+        mix_kernel,
         "mix",
-        shape((blocks, 4, padded, rows)),
-        (pltpu.VMEM,) * 5,
-        scratch=(scratch, scratch, pltpu.VMEM(taps.shape[::-1], f32)),
-        flops=36 * height * (2 * rows) ** 2,
+        shape((blocks, 2, padded, rows)),
+        (pltpu.VMEM,) * 3,
+        scratch=(pltpu.VMEM((2, height, 2 * rows), f32),),
+        flops=12 * height * (2 * rows) ** 2,
         size=24 * blocks * padded * rows,
-    )(taps, skip, jnp.asarray(matrices), jnp.asarray(twists), arrays)
-    parts = lax.all_to_all(results[:, :, :share], "ctx", 0, 0, tiled=True)
+    )(matrices, twists, products)
+    if near_count > 1:
+        parts = lax.all_to_all(results, "ctx", 0, 0, tiled=True)
+    else:
+        together = jnp.concatenate([results, jnp.stack(lag_parts)], axis=1)[:, :, :share]
+        together = lax.all_to_all(together, "ctx", 0, 0, tiled=True)
+        parts, far_parts, near_parts = together[:, :2], list(together[:, 2:]), []
     full, one = shape((rows, channels)), shape((1, channels))
+    lags = pltpu.VMEM((blocks, share, rows), f32)
     outs = call(
-        unpack_kernel,
+        functools.partial(unpack_kernel, far_count=far_count, near_count=near_count),
         "unpack",
         (full,) * 6 + (one,),
-        (pltpu.VMEM,) * 5,
-        scratch=tuple(pltpu.VMEM(out.shape, f32) for out in (full,) * 6 + (one,)) + (pltpu.SemaphoreType.DMA((7,)),),
+        (pltpu.VMEM,) * (4 + far_count + near_count),
+        scratch=tuple(pltpu.VMEM(out.shape, f32) for out in (full,) * 6 + (one,))
+        + (pltpu.SemaphoreType.DMA((7,)), lags, lags),
         to=pltpu.HBM,
         size=48 * rows * channels,
-    )(query, key, value, out_grad, parts)
+    )(query, key, value, out_grad, parts, *far_parts, *near_parts)
     return (*outs[:6], outs[6].reshape(channels))
 
 

time: 64.6 us -> 58.6 us (0.907)
  blocking collectives: 58.6 us -> 29.5 us
  starting transfers between devices: 0 us -> 11.6 us
  waiting for transfers between devices: 0 us -> 9.9 us
  Pallas kernels: 3.84 us -> 5.21 us
    all_to_all x1 -> x0, blocking collectives: 29.1 us -> none  [body(): parts = lax.all_to_all(results[:, :, :share], 'ctx', 0, 0, tiled=True)]
    ppermute x0 -> x6, waiting for transfers between devices: none -> 8.96 us  [exchange(): lax.ppermute(value, axis, [(i, i ^ distance) for i in range(lax.axis_size...]
    ppermute x0 -> x6, starting transfers between devices: none -> 8.01 us  [exchange(): lax.ppermute(value, axis, [(i, i ^ distance) for i in range(lax.axis_size...]
    all_to_all x0 -> x1, starting transfers between devices: none -> 3.57 us  [body(): parts = lax.all_to_all(results, 'ctx', 0, 0, tiled=True)]
    pallas_call x2 -> x4, Pallas kernels: 3.58 us -> 4.95 us  [the longest x1 1.87 us: body(): call(functools.partial(spectra_kernel, near_count=near_count, grad_scale=...]
    all_to_all x0 -> x1, waiting for transfers between devices: none -> 0.94 us  [body(): parts = lax.all_to_all(results, 'ctx', 0, 0, tiled=True)]
  transfers between devices with their start and end apart: 0 -> 7, of which waited for: 0 -> 4; matrix products, arithmetic and copies ran while one was open for 0% -> 0% of each run, Pallas kernels for 0% -> 3%
where the time goes in v10:
time: 58.6 us; the launch traced here: 58.3 us
  blocking collectives  29.5 us (50%)
  starting transfers between devices  11.6 us (20%)
  waiting for transfers between devices  9.9 us (17%)
  Pallas kernels  5.21 us (9%)
  other arithmetic  1.21 us (2%)
  between operations  0.8 us (1%)
    all_to_all x1, blocking collectives, body(): arrays = lax.all_to_all(packed, 'ctx', 0, 0, tiled=True)  29.5 us
    ppermute x6, waiting for transfers between devices, exchange(): lax.ppermute(value, axis, [(i, i ^ distance) for i in range(lax.axis_size...  8.96 us
    ppermute x6, starting transfers between devices, exchange(): lax.ppermute(value, axis, [(i, i ^ distance) for i in range(lax.axis_size...  8.01 us
    all_to_all x1, starting transfers between devices, body(): parts = lax.all_to_all(results, 'ctx', 0, 0, tiled=True)  3.57 us
    pallas_call x1, Pallas kernels, body(): call(functools.partial(spectra_kernel, near_count=near_count, grad_scale=...  1.87 us
    pallas_call x1, Pallas kernels, body(): call(mix_kernel, 'mix', shape((blocks, 2, padded, rows)), (pltpu.VMEM,) *...  1.66 us
    pallas_call x1, Pallas kernels, body(): call(functools.partial(unpack_kernel, far_count=far_count, near_count=nea...  1.4 us
    mul x1, other arithmetic, body(): mix_grad = out_grad.astype(f32) * query.astype(f32)  1.21 us
  transfers between devices with their start and end apart: 7, of which 4 were waited for; matrix products, arithmetic and copies ran while one was open for 0% of the time, Pallas kernels for 3%

profile of v10, /device:TPU:0, one launch (start us, length us, event | category | flops | bytes accessed | tf_op | source)
XLA Modules:
  0.0 58.3 jit_solution(7493963898453233258)
XLA Ops:
  0.6 0.0 copy-start.5
  0.6 1.2 %convert_multiply_fusion = (f32[128,512]{1,0:T(8,128)S(1)}, f32[128,512]{1,0:T(8,128)S(1)}) fusion(bf16[128,512]{1,0:T(8,128)(2,1)} %query.1, bf16[128,512]{1,0:T(8,128)(2,1)} %grad.1, bf16[128,512]{1,0:T(8,128)(2,1)} %value.1, bf16[128,512]{1,0:T(8,128)(2,1)} %key.1), kind=kLoop, calls=%fused_computation | loop fusion | flops 393216 | bytes 1048576 | tf_op jit(solution)/shard_map/mul | solution.py:309
  1.9 0.0 copy-done.5
  1.9 0.3 pack.1
  2.1 0.0 copy-start
  2.1 0.0 copy-start.6
  2.2 0.0 copy-start.7
  2.2 0.0 copy-start.8
  2.2 29.5 %all_to_all.10.arrays = f32[16,3,32,128]{3,2,1,0:T(8,128)S(1)} all-to-all(f32[16,3,32,128]{3,2,1,0:T(8,128)S(1)} %pack.1), channel_id=1, replica_groups=mesh['ctx'=16,'ch'=2] {'ctx'}, dimensions={0} | all-to-all | bytes 1572864 | tf_op jit(solution)/shard_map/all_to_all | solution.py:313
  31.7 0.0 copy-done
  31.7 0.0 copy-done.6
  31.7 0.0 copy-done.7
  31.7 0.0 copy-done.8
  31.7 1.9 %spectra.1 = (f32[2,544,256]{2,1,0:T(8,128)S(1)}, f32[5,32,128]{2,1,0:T(8,128)S(1)}, f32[5,32,128]{2,1,0:T(8,128)S(1)}, f32[5,32,128]{2,1,0:T(8,128)S(1)}, f32[5,32,128]{2,1,0:T(8,128)S(1)}) custom-call(f32[128,512]{1,0:T(8,128)S(1)} %copy-done.7, f32[1,512]{1,0:T(1,128)S(1)} %bitcast.2, bf16[4,256,256]{2,1,0:T(8,128)(2,1)S(1)} %copy-done, ...), custom_call_target="tpu_custom_call" | custom-call | flops 855638016 | bytes 1572864 | tf_op jit(solution)/shard_map/spectra/pallas_call | solution.py:326
  33.6 1.0 %collective-permute-start = (f32[5,32,128]{2,1,0:T(8,128)S(1)}, f32[5,32,128]{2,1,0:T(8,128)S(1)}, u32[]{:S(2)}, u32[]{:S(2)}) collective-permute-start(f32[5,32,128]{2,1,0:T(8,128)S(1)} %get-tuple-element.24), channel_id=1, source_target_pairs={{0,8},{2,10},{4,12},{6,14},{8,0},{10,2},{12,4},{14,6},{16,24},{18,... | collective-permute-start | bytes 245768 | tf_op jit(solution)/shard_map/ppermute | solution.py:283
  34.6 1.3 %collective-permute-start.1 = (f32[5,32,128]{2,1,0:T(8,128)S(1)}, f32[5,32,128]{2,1,0:T(8,128)S(1)}, u32[]{:S(2)}, u32[]{:S(2)}) collective-permute-start(f32[5,32,128]{2,1,0:T(8,128)S(1)} %get-tuple-element.25), channel_id=1, source_target_pairs={{0,16},{2,18},{4,20},{6,22},{8,24},{10,26},{12,28},{14,30},{16,0},... | collective-permute-start | bytes 245768 | tf_op jit(solution)/shard_map/ppermute | solution.py:283
  35.9 2.2 %collective-permute-start.2 = (f32[5,32,128]{2,1,0:T(8,128)S(1)}, f32[5,32,128]{2,1,0:T(8,128)S(1)}, u32[]{:S(2)}, u32[]{:S(2)}) collective-permute-start(f32[5,32,128]{2,1,0:T(8,128)S(1)} %get-tuple-element.26), channel_id=1, source_target_pairs={{0,24},{2,26},{4,28},{6,30},{8,16},{10,18},{12,20},{14,22},{16,8},... | collective-permute-start | bytes 245768 | tf_op jit(solution)/shard_map/ppermute | solution.py:283
  38.1 1.7 %mix.1 = f32[16,2,32,128]{3,2,1,0:T(8,128)} custom-call(bf16[4,256,256]{2,1,0:T(8,128)(2,1)S(1)} %copy-done, f32[17,4,128]{2,1,0:T(4,128)S(1)} %copy-done.6, f32[2,544,256]{2,1,0:T(8,128)S(1)} %get-tuple-element.22.products), custom_call_target="tpu_custom_call" | custom-call | flops 427819008 | bytes 1572864 | tf_op jit(solution)/shard_map/mix/pallas_call | solution.py:342
  39.7 3.6 %all-to-all-start.1 = ((f32[16,2,32,128]{3,2,1,0:T(8,128)}), f32[16,2,32,128]{3,2,1,0:T(8,128)S(1)}, u32[]{:S(2)}, u32[]{:S(2)}) async-start(f32[16,2,32,128]{3,2,1,0:T(8,128)} %mix.1), calls=%async_computation.1 | async-start | bytes 1048576 | tf_op jit(solution)/shard_map/all_to_all | solution.py:352
  43.3 0.0 collective-permute-done.refs_1_.rest_1_
  43.3 0.0 collective-permute-done.1.refs_2_.rest_2_
  43.3 0.0 collective-permute-done.2.refs_3_.rest_3_
  43.3 0.0 copy-start.1
  43.3 0.0 copy-start.2
  43.4 0.0 copy-start.3
  43.4 0.0 copy-start.4
  43.4 1.9 %collective-permute-start.3 = (f32[8,32,128]{2,1,0:T(8,128)S(1)}, f32[8,32,128]{2,1,0:T(8,128)S(1)}, u32[]{:S(2)}, u32[]{:S(2)}) collective-permute-start(f32[8,32,128]{2,1,0:T(8,128)S(1)} %get-tuple-element.27), channel_id=1, source_target_pairs={{0,2},{2,0},{4,6},{6,4},{8,10},{10,8},{12,14},{14,12},{16,18},{18,... | collective-permute-start | bytes 393224 | tf_op jit(solution)/shard_map/ppermute | solution.py:283
  45.3 1.5 %collective-permute-start.4 = (f32[8,32,128]{2,1,0:T(8,128)S(1)}, f32[8,32,128]{2,1,0:T(8,128)S(1)}, u32[]{:S(2)}, u32[]{:S(2)}) collective-permute-start(f32[8,32,128]{2,1,0:T(8,128)S(1)} %get-tuple-element.28), channel_id=1, source_target_pairs={{0,4},{2,6},{4,0},{6,2},{8,12},{10,14},{12,8},{14,10},{16,20},{18,... | collective-permute-start | bytes 393224 | tf_op jit(solution)/shard_map/ppermute | solution.py:283
  46.8 0.2 collective-permute-start.5
  47.0 5.6 %collective-permute-done.3.rest_4_ = f32[8,32,128]{2,1,0:T(8,128)S(1)} collective-permute-done((f32[8,32,128]{2,1,0:T(8,128)S(1)}, f32[8,32,128]{2,1,0:T(8,128)S(1)}, u32[]{:S(2)}, u32[]{:S(2)}) %collective-permute-start.3) | collective-permute-done | bytes 131104 | tf_op jit(solution)/shard_map/ppermute | solution.py:283
  52.5 1.6 %collective-permute-done.4.rest_5_ = f32[8,32,128]{2,1,0:T(8,128)S(1)} collective-permute-done((f32[8,32,128]{2,1,0:T(8,128)S(1)}, f32[8,32,128]{2,1,0:T(8,128)S(1)}, u32[]{:S(2)}, u32[]{:S(2)}) %collective-permute-start.4) | collective-permute-done | bytes 131104 | tf_op jit(solution)/shard_map/ppermute | solution.py:283
  54.1 1.8 %collective-permute-done.5.rest_6_ = f32[8,32,128]{2,1,0:T(8,128)S(1)} collective-permute-done((f32[8,32,128]{2,1,0:T(8,128)S(1)}, f32[8,32,128]{2,1,0:T(8,128)S(1)}, u32[]{:S(2)}, u32[]{:S(2)}) %collective-permute-start.5) | collective-permute-done | bytes 131104 | tf_op jit(solution)/shard_map/ppermute | solution.py:283
  55.9 0.9 %all-to-all-done.1.parts = f32[16,2,32,128]{3,2,1,0:T(8,128)S(1)} async-done(((f32[16,2,32,128]{3,2,1,0:T(8,128)}), f32[16,2,32,128]{3,2,1,0:T(8,128)S(1)}, u32[]{:S(2)}, u32[]{:S(2)}) %all-to-all-start.1) | async-done | bytes 524320 | tf_op jit(solution)/shard_map/all_to_all | solution.py:352
  56.9 0.0 copy-done.1
  56.9 0.0 copy-done.2
  56.9 0.0 copy-done.3
  56.9 0.0 copy-done.4
  56.9 1.4 %unpack.1 = (f32[128,512]{1,0:T(8,128)}, f32[128,512]{1,0:T(8,128)}, f32[128,512]{1,0:T(8,128)}, f32[128,512]{1,0:T(8,128)}, f32[128,512]{1,0:T(8,128)}, /*index=5*/f32[128,512]{1,0:T(8,128)}, f32[1,512]{1,0:T(1,128)}) custom-call(bf16[128,512]{1,0:T(8,128)(2,1)S(1)} %copy-done.1, bf16[128,512]{1,0:T(8,128)(2,1)S(1)} %copy-done.2, ...), custom_call_target="tpu_custom_call" | custom-call | bytes 3145728 | tf_op jit(solution)/shard_map/unpack/pallas_call | solution.py:359
  (1 shorter events, 0.0 us)
Async XLA Ops:
  0.6 1.2 %copy-start.5 = (f32[128,512]{1,0:T(8,128)S(1)}, f32[128,512]{1,0:T(8,128)}, u32[]{:S(2)}) copy-start(f32[128,512]{1,0:T(8,128)} %filt.1) | copy-start | bytes 786436
  2.1 29.6 %copy-start = (bf16[4,256,256]{2,1,0:T(8,128)(2,1)S(1)}, bf16[4,256,256]{2,1,0:T(8,128)(2,1)}, u32[]{:S(2)}) copy-start(bf16[4,256,256]{2,1,0:T(8,128)(2,1)} %constant.4.clone.matrices) | copy-start | bytes 1572868
  2.1 29.6 %copy-start.6 = (f32[17,4,128]{2,1,0:T(4,128)S(1)}, f32[17,4,128]{2,1,0:T(4,128)}, u32[]{:S(2)}) copy-start(f32[17,4,128]{2,1,0:T(4,128)} %constant.5.clone.twists) | copy-start | bytes 104452
  2.2 29.6 %copy-start.7 = (f32[128,512]{1,0:T(8,128)S(1)}, f32[128,512]{1,0:T(8,128)}, u32[]{:S(2)}) copy-start(f32[128,512]{1,0:T(8,128)} %taps.1) | copy-start | bytes 786436
  2.2 29.6 %copy-start.8 = (f32[512]{0:T(512)S(1)}, f32[512]{0:T(512)}, u32[]{:S(2)}) copy-start(f32[512]{0:T(512)} %param.14) | copy-start | bytes 6148
  33.6 9.7 %collective-permute-start = (f32[5,32,128]{2,1,0:T(8,128)S(1)}, f32[5,32,128]{2,1,0:T(8,128)S(1)}, u32[]{:S(2)}, u32[]{:S(2)}) collective-permute-start(f32[5,32,128]{2,1,0:T(8,128)S(1)} %get-tuple-element.24), channel_id=1, source_target_pairs={{0,8},{2,10},{4,12},{6,14},{8,0},{10,2},{12,4},{14,6},{16,24},{18,... | collective-permute-start | bytes 245768 | tf_op jit(solution)/shard_map/ppermute | solution.py:283
  34.6 8.7 %collective-permute-start.1 = (f32[5,32,128]{2,1,0:T(8,128)S(1)}, f32[5,32,128]{2,1,0:T(8,128)S(1)}, u32[]{:S(2)}, u32[]{:S(2)}) collective-permute-start(f32[5,32,128]{2,1,0:T(8,128)S(1)} %get-tuple-element.25), channel_id=1, source_target_pairs={{0,16},{2,18},{4,20},{6,22},{8,24},{10,26},{12,28},{14,30},{16,0},... | collective-permute-start | bytes 245768 | tf_op jit(solution)/shard_map/ppermute | solution.py:283
  35.9 7.4 %collective-permute-start.2 = (f32[5,32,128]{2,1,0:T(8,128)S(1)}, f32[5,32,128]{2,1,0:T(8,128)S(1)}, u32[]{:S(2)}, u32[]{:S(2)}) collective-permute-start(f32[5,32,128]{2,1,0:T(8,128)S(1)} %get-tuple-element.26), channel_id=1, source_target_pairs={{0,24},{2,26},{4,28},{6,30},{8,16},{10,18},{12,20},{14,22},{16,8},... | collective-permute-start | bytes 245768 | tf_op jit(solution)/shard_map/ppermute | solution.py:283
  39.7 17.1 %all-to-all-start.1 = ((f32[16,2,32,128]{3,2,1,0:T(8,128)}), f32[16,2,32,128]{3,2,1,0:T(8,128)S(1)}, u32[]{:S(2)}, u32[]{:S(2)}) async-start(f32[16,2,32,128]{3,2,1,0:T(8,128)} %mix.1), calls=%async_computation.1 | async-start | bytes 1048576 | tf_op jit(solution)/shard_map/all_to_all | solution.py:352
  43.3 13.5 %copy-start.1 = (bf16[128,512]{1,0:T(8,128)(2,1)S(1)}, bf16[128,512]{1,0:T(8,128)(2,1)}, u32[]{:S(2)}) copy-start(bf16[128,512]{1,0:T(8,128)(2,1)} %query.1) | copy-start | bytes 393220
  43.3 13.5 %copy-start.2 = (bf16[128,512]{1,0:T(8,128)(2,1)S(1)}, bf16[128,512]{1,0:T(8,128)(2,1)}, u32[]{:S(2)}) copy-start(bf16[128,512]{1,0:T(8,128)(2,1)} %key.1) | copy-start | bytes 393220
  43.4 13.5 %copy-start.3 = (bf16[128,512]{1,0:T(8,128)(2,1)S(1)}, bf16[128,512]{1,0:T(8,128)(2,1)}, u32[]{:S(2)}) copy-start(bf16[128,512]{1,0:T(8,128)(2,1)} %value.1) | copy-start | bytes 393220
  43.4 13.5 %copy-start.4 = (bf16[128,512]{1,0:T(8,128)(2,1)S(1)}, bf16[128,512]{1,0:T(8,128)(2,1)}, u32[]{:S(2)}) copy-start(bf16[128,512]{1,0:T(8,128)(2,1)} %grad.1) | copy-start | bytes 393220
  43.4 9.1 %collective-permute-start.3 = (f32[8,32,128]{2,1,0:T(8,128)S(1)}, f32[8,32,128]{2,1,0:T(8,128)S(1)}, u32[]{:S(2)}, u32[]{:S(2)}) collective-permute-start(f32[8,32,128]{2,1,0:T(8,128)S(1)} %get-tuple-element.27), channel_id=1, source_target_pairs={{0,2},{2,0},{4,6},{6,4},{8,10},{10,8},{12,14},{14,12},{16,18},{18,... | collective-permute-start | bytes 393224 | tf_op jit(solution)/shard_map/ppermute | solution.py:283
  45.3 8.9 %collective-permute-start.4 = (f32[8,32,128]{2,1,0:T(8,128)S(1)}, f32[8,32,128]{2,1,0:T(8,128)S(1)}, u32[]{:S(2)}, u32[]{:S(2)}) collective-permute-start(f32[8,32,128]{2,1,0:T(8,128)S(1)} %get-tuple-element.28), channel_id=1, source_target_pairs={{0,4},{2,6},{4,0},{6,2},{8,12},{10,14},{12,8},{14,10},{16,20},{18,... | collective-permute-start | bytes 393224 | tf_op jit(solution)/shard_map/ppermute | solution.py:283
  46.8 9.2 %collective-permute-start.5 = (f32[8,32,128]{2,1,0:T(8,128)S(1)}, f32[8,32,128]{2,1,0:T(8,128)S(1)}, u32[]{:S(2)}, u32[]{:S(2)}) collective-permute-start(f32[8,32,128]{2,1,0:T(8,128)S(1)} %get-tuple-element.29), channel_id=1, source_target_pairs={{0,6},{2,4},{4,2},{6,0},{8,14},{10,12},{12,10},{14,8},{16,22},{18,... | collective-permute-start | bytes 393224 | tf_op jit(solution)/shard_map/ppermute | solution.py:283

commit v11 on v10

--- a/solution.py
+++ b/solution.py
@@ -140,29 +140,45 @@
     return dot(values_high, high) + (dot(values_low, high) + dot(values_high, low))
 
 
-def pack_kernel(product, grad, filt, out):
+def pack_kernel(product, mix_grad, out):
     blocks, _, share, rows = out.shape
-
-    def put(a, field):
-        out[:, a] = field.T.reshape(blocks, share, rows)
-
-    put(0, product[...])
-    put(2, grad[...])
-    put(1, filt[...])
-
-
-def spectra_kernel(taps, skip, matrices, twists, arrays, products, *rest, near_count, grad_scale):
-    *lag_outs, spectra, results, direct, lags = rest
+    for a, field in enumerate((product, mix_grad)):
+        out[:, a] = field[...].T.reshape(blocks, share, rows)
+
+
+def split_kernel(field, *rest, near_count):
+    outs, turned = rest[:-1], rest[-1]
+    share = outs[0].shape[1]
+    turned[...] = field[...].T
+    me = lax.axis_index("ctx") if near_count > 1 else 0
+    for far, out in enumerate(outs):
+        for near in range(near_count):
+            start = (me ^ (far * near_count + near)) * share
+            out[near] = turned[pl.ds(start if near_count == 1 else pl.multiple_of(start, share), share), :]
+
+
+def spectra_kernel(taps, skip, matrices, twists, arrays, *rest, near_count, grad_scale):
     blocks, _, channels, rows = arrays.shape
+    far_count = blocks // near_count
+    far_parts, rest = rest[:far_count], rest[far_count:]
+    near_parts, rest = rest[: near_count - 1], rest[near_count - 1 :]
+    products, *lag_outs, spectra, results, direct, lags, filter_blocks = rest
+    me = lax.axis_index("ctx") if near_count > 1 else 0
+    for far, part in enumerate(far_parts):
+        filter_blocks[me ^ (far * near_count)] = part[0]
+        for near, near_part in enumerate(near_parts, 1):
+            filter_blocks[me ^ (far * near_count + near)] = near_part[far]
     row = lax.broadcasted_iota(jnp.int32, taps.shape, 0)
     direct[...] = (taps[...] + jnp.where(row == 0, skip[...], 0.0)).T
     own = 0 if direct.shape[0] == channels else pl.multiple_of(lax.axis_index("ctx") * channels, channels)
     for a in range(3):
         for low in range(0, channels, 8):
             part = pl.ds(low, 8)
-            values = [arrays[j, a, part, :] for j in range(blocks)]
             if a == 1:
+                values = [filter_blocks[j, part, :] for j in range(blocks)]
                 values[0] = values[0] + direct[pl.ds(own + low, 8), :]
+            else:
+                values = [arrays[j, a // 2, part, :] for j in range(blocks)]
             bins = padded_bins(values)
             for p in range(blocks + 1):
                 real, imag = bins[p]
@@ -187,7 +203,6 @@
     for low, values in blocks_back(spectra.at[0], results, matrices, twists, channels):
         for j, value in enumerate(values):
             lags[j, pl.ds(low, 8), :] = value * grad_scale
-    me = lax.axis_index("ctx") if near_count > 1 else 0
     for far, lag_out in enumerate(lag_outs):
         for near in range(near_count):
             lag_out[near] = lags[me ^ (far * near_count + near)]
@@ -215,14 +230,15 @@
                 out[j, a, pl.ds(low, 8), :] = value
 
 
-def relay_kernel(*refs):
-    near_count = refs[0].shape[0] - 1
-    far_count = len(refs) - near_count + 1
-    parts, outs = refs[:far_count], refs[far_count:]
+def relay_kernel(*refs, far_count):
+    parts = (refs[0], *refs[1:far_count][::-1])
+    outs = refs[far_count:]
+    near_count = len(outs) + 1
     for near, out in enumerate(outs, 1):
         for far, part in enumerate(parts):
             out[far] = part[near]
-            out[far_count + far] = part[near_count]
+            if part.shape[0] > near_count:
+                out[far_count + far] = part[near_count]
 
 
 def unpack_kernel(query, key, value, grad, parts, *rest, far_count, near_count):
@@ -283,15 +299,20 @@
     return lax.ppermute(value, axis, [(i, i ^ distance) for i in range(lax.axis_size(axis))])
 
 
-def send_lags(lag_parts, axis, near_count):
-    far_parts = list(lag_parts)
-    for far in range(len(far_parts) - 1, 0, -1):
-        far_parts[far] = exchange(lag_parts[far], axis, far * near_count)
-    payload = jax.ShapeDtypeStruct((2 * len(far_parts), *lag_parts[0].shape[1:]), jnp.float32)
+def send_parts(parts, axis, near_count):
+    far_parts, far_count = list(parts), len(parts)
+    for far in range(far_count - 1, 0, -1):
+        far_parts[far] = exchange(parts[far], axis, far * near_count)
+    depth = far_count * (1 + parts[0].shape[0] - near_count)
+    payload = jax.ShapeDtypeStruct((depth, *parts[0].shape[1:]), jnp.float32)
     relay = call(
-        relay_kernel, "relay", (payload,) * (near_count - 1), (pltpu.VMEM,) * len(far_parts), flops=RELAY_WEIGHT
+        functools.partial(relay_kernel, far_count=far_count),
+        "relay",
+        (payload,) * (near_count - 1),
+        (pltpu.VMEM,) * far_count,
+        flops=RELAY_WEIGHT,
     )
-    near_parts = relay(*far_parts)
+    near_parts = relay(far_parts[0], *far_parts[:0:-1])
     return far_parts, [exchange(part, axis, near) for near, part in enumerate(near_parts, 1)]
 
 
@@ -305,14 +326,28 @@
     grad_scale = 1.0 / math.sqrt(blocks * rows)
     taps, skip = explicit_taps, skip_gain.reshape(1, channels)
 
+    near_count = 1 << (blocks.bit_length() - 1) // 2 if share == padded else 1
+    far_count = blocks // near_count
     product = key.astype(f32) * value.astype(f32)
     mix_grad = out_grad.astype(f32) * query.astype(f32)
+    filter_parts = call(
+        functools.partial(split_kernel, near_count=near_count),
+        "split",
+        (shape((near_count, share, rows)),) * far_count,
+        (pltpu.VMEM,),
+        scratch=(pltpu.VMEM((channels, rows), f32),),
+        size=8 * rows * channels,
+    )(implicit_filter)
     packed = call(
-        pack_kernel, "pack", shape((blocks, 3, share, rows)), (pltpu.VMEM,) * 3, size=24 * rows * channels
-    )(product, mix_grad, implicit_filter)
-    arrays = lax.all_to_all(packed, "ctx", 0, 0, tiled=True)
-    if share != padded:
+        pack_kernel, "pack", shape((blocks, 2, share, rows)), (pltpu.VMEM,) * 2, size=16 * rows * channels
+    )(product, mix_grad)
+    if near_count > 1:
+        filter_far, filter_near = send_parts(filter_parts, "ctx", near_count)
+        arrays = lax.all_to_all(packed, "ctx", 0, 0, tiled=True)
+    else:
+        arrays = lax.all_to_all(jnp.concatenate([packed, jnp.stack(filter_parts)], axis=1), "ctx", 0, 0, tiled=True)
         arrays = jnp.pad(arrays, ((0, 0), (0, 0), (0, padded - share), (0, 0)))
+        arrays, filter_far, filter_near = arrays[:, :2], list(arrays[:, 2:]), []
         own = lax.axis_index("ctx") * share
         taps, skip = [
             jnp.pad(lax.dynamic_slice_in_dim(each, own, share, 1), ((0, 0), (0, padded - share)))
@@ -320,25 +355,24 @@
         ]
     matrices, twists = tables(blocks, rows)
     height = (blocks + 1) * padded
-    near_count = 1 << (blocks.bit_length() - 1) // 2 if share == padded else 1
-    far_count = blocks // near_count
     matrices, twists = jnp.asarray(matrices), jnp.asarray(twists)
     products, *lag_parts = call(
         functools.partial(spectra_kernel, near_count=near_count, grad_scale=grad_scale),
         "spectra",
         (shape((2, height, 2 * rows)),) + (shape((near_count + 1, padded, rows)),) * far_count,
-        (pltpu.VMEM,) * 5,
+        (pltpu.VMEM,) * (4 + far_count + near_count),
         scratch=(
             pltpu.VMEM((3, height, 2 * rows), f32),
             pltpu.VMEM((height, 2 * rows), f32),
             pltpu.VMEM(taps.shape[::-1], f32),
             pltpu.VMEM((blocks, padded, rows), f32),
+            pltpu.VMEM((blocks, padded, rows), f32),
         ),
         flops=24 * height * (2 * rows) ** 2,
         size=24 * blocks * padded * rows,
-    )(taps, skip, matrices, twists, arrays)
+    )(taps, skip, matrices, twists, arrays, *filter_far, *filter_near)
     if near_count > 1:
-        far_parts, near_parts = send_lags(lag_parts, "ctx", near_count)
+        far_parts, near_parts = send_parts(lag_parts, "ctx", near_count)
     results = call(
         mix_kernel,
         "mix",

time: 58.6 us -> 58.1 us (level)
  blocking collectives: 29.5 us -> 0 us
  starting transfers between devices: 11.6 us -> 28.2 us
  waiting for transfers between devices: 9.9 us -> 20.4 us
  local copies, waits for them, and re-layouts: 0.06 us -> 0.99 us
  Pallas kernels: 5.21 us -> 6.12 us
    all_to_all x1 -> x0, blocking collectives: 29.5 us -> none  [body(): arrays = lax.all_to_all(packed, 'ctx', 0, 0, tiled=True)]
    ppermute x6 -> x12, starting transfers between devices: 8.01 us -> 17.2 us  [exchange(): lax.ppermute(value, axis, [(i, i ^ distance) for i in range(lax.axis_size...]
    all_to_all x0 -> x1, starting transfers between devices: none -> 7.09 us  [body(): arrays = lax.all_to_all(packed, 'ctx', 0, 0, tiled=True)]
    ppermute x6 -> x12, waiting for transfers between devices: 8.96 us -> 14.5 us  [exchange(): lax.ppermute(value, axis, [(i, i ^ distance) for i in range(lax.axis_size...]
    all_to_all x0 -> x1, waiting for transfers between devices: none -> 4.99 us  [body(): arrays = lax.all_to_all(packed, 'ctx', 0, 0, tiled=True)]
    unnamed x18, local copies, waits for them, and re-layouts: 0.06 us -> 0.99 us
    pallas_call x2 -> x4, Pallas kernels: 0.29 us -> 1.22 us  [the longest x1 1.03 us: body(): call(pack_kernel, 'pack', shape((blocks, 2, share, rows)), (pltpu.VMEM,)...]
  transfers between devices with their start and end apart: 7 -> 14, of which waited for: 4 -> 8; matrix products, arithmetic and copies ran while one was open for 0% -> 2% of each run, Pallas kernels for 3% -> 5%
where the time goes in v11:
time: 58.1 us; the launch traced here: 57.7 us
  starting transfers between devices  28.2 us (49%)
  waiting for transfers between devices  20.4 us (35%)
  Pallas kernels  6.12 us (11%)
  other arithmetic  1.16 us (2%)
  local copies, waits for them, and re-layouts  0.99 us (2%)
  between operations  0.84 us (1%)
    ppermute x12, starting transfers between devices, exchange(): lax.ppermute(value, axis, [(i, i ^ distance) for i in range(lax.axis_size...  17.2 us
    ppermute x12, waiting for transfers between devices, exchange(): lax.ppermute(value, axis, [(i, i ^ distance) for i in range(lax.axis_size...  14.5 us
    all_to_all x1, starting transfers between devices, body(): arrays = lax.all_to_all(packed, 'ctx', 0, 0, tiled=True)  7.09 us
    all_to_all x1, waiting for transfers between devices, body(): arrays = lax.all_to_all(packed, 'ctx', 0, 0, tiled=True)  4.99 us
    all_to_all x1, starting transfers between devices, body(): parts = lax.all_to_all(results, 'ctx', 0, 0, tiled=True)  3.85 us
    pallas_call x1, Pallas kernels, body(): call(functools.partial(spectra_kernel, near_count=near_count, grad_scale=...  1.8 us
    pallas_call x1, Pallas kernels, body(): call(mix_kernel, 'mix', shape((blocks, 2, padded, rows)), (pltpu.VMEM,) *...  1.7 us
    pallas_call x1, Pallas kernels, body(): call(functools.partial(unpack_kernel, far_count=far_count, near_count=nea...  1.4 us
  transfers between devices with their start and end apart: 14, of which 8 were waited for; matrix products, arithmetic and copies ran while one was open for 2% of the time, Pallas kernels for 5%

profile of v11, /device:TPU:0, one launch (start us, length us, event | category | flops | bytes accessed | tf_op | source)
XLA Modules:
  0.0 57.7 jit_solution(12783340761960006330)
XLA Ops:
  0.6 0.0 copy-start.5
  0.6 0.9 %copy-done.5 = f32[128,512]{1,0:T(8,128)S(1)} copy-done((f32[128,512]{1,0:T(8,128)S(1)}, f32[128,512]{1,0:T(8,128)}, u32[]{:S(2)}) %copy-start.5) | copy-done | bytes 262168
  1.6 0.1 split.1
  1.7 3.1 %collective-permute-start = (f32[4,32,128]{2,1,0:T(8,128)S(1)}, f32[4,32,128]{2,1,0:T(8,128)S(1)}, u32[]{:S(2)}, u32[]{:S(2)}) collective-permute-start(f32[4,32,128]{2,1,0:T(8,128)S(1)} %get-tuple-element.30), channel_id=1, source_target_pairs={{0,8},{2,10},{4,12},{6,14},{8,0},{10,2},{12,4},{14,6},{16,24},{18,... | collective-permute-start | bytes 196616 | tf_op jit(solution)/shard_map/ppermute | solution.py:299
  4.8 2.6 %collective-permute-start.1 = (f32[4,32,128]{2,1,0:T(8,128)S(1)}, f32[4,32,128]{2,1,0:T(8,128)S(1)}, u32[]{:S(2)}, u32[]{:S(2)}) collective-permute-start(f32[4,32,128]{2,1,0:T(8,128)S(1)} %get-tuple-element.31), channel_id=1, source_target_pairs={{0,16},{2,18},{4,20},{6,22},{8,24},{10,26},{12,28},{14,30},{16,0},... | collective-permute-start | bytes 196616 | tf_op jit(solution)/shard_map/ppermute | solution.py:299
  7.4 0.0 collective-permute-start.2
  7.4 1.2 %convert_multiply_fusion = (f32[128,512]{1,0:T(8,128)S(1)}, f32[128,512]{1,0:T(8,128)S(1)}) fusion(bf16[128,512]{1,0:T(8,128)(2,1)} %query.1, bf16[128,512]{1,0:T(8,128)(2,1)} %grad.1, bf16[128,512]{1,0:T(8,128)(2,1)} %value.1, bf16[128,512]{1,0:T(8,128)(2,1)} %key.1), kind=kLoop, calls=%fused_computation | loop fusion | flops 393216 | bytes 1048576 | tf_op jit(solution)/shard_map/mul | solution.py:332
  8.6 1.0 %pack.1 = f32[16,2,32,128]{3,2,1,0:T(8,128)} custom-call(f32[128,512]{1,0:T(8,128)S(1)} %get-tuple-element.52.product, f32[128,512]{1,0:T(8,128)S(1)} %get-tuple-element.51.mix_grad), custom_call_target="tpu_custom_call" | custom-call | bytes 1048576 | tf_op jit(solution)/shard_map/pack/pallas_call | solution.py:341
  9.6 7.1 %all-to-all-start = ((f32[16,2,32,128]{3,2,1,0:T(8,128)}), f32[16,2,32,128]{3,2,1,0:T(8,128)S(1)}, u32[]{:S(2)}, u32[]{:S(2)}) async-start(f32[16,2,32,128]{3,2,1,0:T(8,128)} %pack.1), calls=%async_computation | async-start | bytes 1048576 | tf_op jit(solution)/shard_map/all_to_all | solution.py:346
  16.7 0.0 collective-permute-done.refs_3_.rest_1_
  16.7 0.0 collective-permute-done.1.refs_2_.rest_2_
  16.7 0.0 collective-permute-done.2.refs_1_.rest_3_
  16.7 0.0 copy-start
  16.8 0.0 copy-start.6
  16.8 0.0 copy-start.7
  16.8 0.0 copy-start.8
  16.8 2.0 %collective-permute-start.3 = (f32[4,32,128]{2,1,0:T(8,128)S(1)}, f32[4,32,128]{2,1,0:T(8,128)S(1)}, u32[]{:S(2)}, u32[]{:S(2)}) collective-permute-start(f32[4,32,128]{2,1,0:T(8,128)S(1)} %get-tuple-element.33), channel_id=1, source_target_pairs={{0,2},{2,0},{4,6},{6,4},{8,10},{10,8},{12,14},{14,12},{16,18},{18,... | collective-permute-start | bytes 196616 | tf_op jit(solution)/shard_map/ppermute | solution.py:299
  18.8 1.5 %collective-permute-start.4 = (f32[4,32,128]{2,1,0:T(8,128)S(1)}, f32[4,32,128]{2,1,0:T(8,128)S(1)}, u32[]{:S(2)}, u32[]{:S(2)}) collective-permute-start(f32[4,32,128]{2,1,0:T(8,128)S(1)} %get-tuple-element.34), channel_id=1, source_target_pairs={{0,4},{2,6},{4,0},{6,2},{8,12},{10,14},{12,8},{14,10},{16,20},{18,... | collective-permute-start | bytes 196616 | tf_op jit(solution)/shard_map/ppermute | solution.py:299
  20.3 0.1 collective-permute-start.5
  20.4 2.7 %collective-permute-done.3.rest_4_ = f32[4,32,128]{2,1,0:T(8,128)S(1)} collective-permute-done((f32[4,32,128]{2,1,0:T(8,128)S(1)}, f32[4,32,128]{2,1,0:T(8,128)S(1)}, u32[]{:S(2)}, u32[]{:S(2)}) %collective-permute-start.3) | collective-permute-done | bytes 65568 | tf_op jit(solution)/shard_map/ppermute | solution.py:299
  23.1 1.5 %collective-permute-done.4.rest_5_ = f32[4,32,128]{2,1,0:T(8,128)S(1)} collective-permute-done((f32[4,32,128]{2,1,0:T(8,128)S(1)}, f32[4,32,128]{2,1,0:T(8,128)S(1)}, u32[]{:S(2)}, u32[]{:S(2)}) %collective-permute-start.4) | collective-permute-done | bytes 65568 | tf_op jit(solution)/shard_map/ppermute | solution.py:299
  24.6 1.5 %collective-permute-done.5.rest_6_ = f32[4,32,128]{2,1,0:T(8,128)S(1)} collective-permute-done((f32[4,32,128]{2,1,0:T(8,128)S(1)}, f32[4,32,128]{2,1,0:T(8,128)S(1)}, u32[]{:S(2)}, u32[]{:S(2)}) %collective-permute-start.5) | collective-permute-done | bytes 65568 | tf_op jit(solution)/shard_map/ppermute | solution.py:299
  26.1 5.0 %all-to-all-done.arrays = f32[16,2,32,128]{3,2,1,0:T(8,128)S(1)} async-done(((f32[16,2,32,128]{3,2,1,0:T(8,128)}), f32[16,2,32,128]{3,2,1,0:T(8,128)S(1)}, u32[]{:S(2)}, u32[]{:S(2)}) %all-to-all-start) | async-done | bytes 524320 | tf_op jit(solution)/shard_map/all_to_all | solution.py:346
  31.1 0.0 copy-done
  31.1 0.0 copy-done.6
  31.1 0.0 copy-done.7
  31.1 0.0 copy-done.8
  31.1 1.8 %spectra.1 = (f32[2,544,256]{2,1,0:T(8,128)S(1)}, f32[5,32,128]{2,1,0:T(8,128)S(1)}, f32[5,32,128]{2,1,0:T(8,128)S(1)}, f32[5,32,128]{2,1,0:T(8,128)S(1)}, f32[5,32,128]{2,1,0:T(8,128)S(1)}) custom-call(f32[128,512]{1,0:T(8,128)S(1)} %copy-done.7, f32[1,512]{1,0:T(1,128)S(1)} %bitcast.2, bf16[4,256,256]{2,1,0:T(8,128)(2,1)S(1)} %copy-done, ...), custom_call_target="tpu_custom_call" | custom-call | flops 855638016 | bytes 1572864 | tf_op jit(solution)/shard_map/spectra/pallas_call | solution.py:359
  32.9 1.3 %collective-permute-start.6 = (f32[5,32,128]{2,1,0:T(8,128)S(1)}, f32[5,32,128]{2,1,0:T(8,128)S(1)}, u32[]{:S(2)}, u32[]{:S(2)}) collective-permute-start(f32[5,32,128]{2,1,0:T(8,128)S(1)} %get-tuple-element.38), channel_id=1, source_target_pairs={{0,8},{2,10},{4,12},{6,14},{8,0},{10,2},{12,4},{14,6},{16,24},{18,... | collective-permute-start | bytes 245768 | tf_op jit(solution)/shard_map/ppermute | solution.py:299
  34.2 1.1 %collective-permute-start.7 = (f32[5,32,128]{2,1,0:T(8,128)S(1)}, f32[5,32,128]{2,1,0:T(8,128)S(1)}, u32[]{:S(2)}, u32[]{:S(2)}) collective-permute-start(f32[5,32,128]{2,1,0:T(8,128)S(1)} %get-tuple-element.39), channel_id=1, source_target_pairs={{0,16},{2,18},{4,20},{6,22},{8,24},{10,26},{12,28},{14,30},{16,0},... | collective-permute-start | bytes 245768 | tf_op jit(solution)/shard_map/ppermute | solution.py:299
  35.3 2.0 %collective-permute-start.8 = (f32[5,32,128]{2,1,0:T(8,128)S(1)}, f32[5,32,128]{2,1,0:T(8,128)S(1)}, u32[]{:S(2)}, u32[]{:S(2)}) collective-permute-start(f32[5,32,128]{2,1,0:T(8,128)S(1)} %get-tuple-element.40), channel_id=1, source_target_pairs={{0,24},{2,26},{4,28},{6,30},{8,16},{10,18},{12,20},{14,22},{16,8},... | collective-permute-start | bytes 245768 | tf_op jit(solution)/shard_map/ppermute | solution.py:299
  37.3 1.7 %mix.1 = f32[16,2,32,128]{3,2,1,0:T(8,128)} custom-call(bf16[4,256,256]{2,1,0:T(8,128)(2,1)S(1)} %copy-done, f32[17,4,128]{2,1,0:T(4,128)S(1)} %copy-done.6, f32[2,544,256]{2,1,0:T(8,128)S(1)} %get-tuple-element.36.products), custom_call_target="tpu_custom_call" | custom-call | flops 427819008 | bytes 1572864 | tf_op jit(solution)/shard_map/mix/pallas_call | solution.py:376
  39.1 3.9 %all-to-all-start.1 = ((f32[16,2,32,128]{3,2,1,0:T(8,128)}), f32[16,2,32,128]{3,2,1,0:T(8,128)S(1)}, u32[]{:S(2)}, u32[]{:S(2)}) async-start(f32[16,2,32,128]{3,2,1,0:T(8,128)} %mix.1), calls=%async_computation.1 | async-start | bytes 1048576 | tf_op jit(solution)/shard_map/all_to_all | solution.py:386
  42.9 0.0 collective-permute-done.6.refs_3_.rest_1_
  42.9 0.0 collective-permute-done.7.refs_2_.rest_2_
  42.9 0.0 collective-permute-done.8.refs_1_.rest_3_
  42.9 0.0 copy-start.1
  43.0 0.0 copy-start.2
  43.0 0.0 copy-start.3
  43.0 0.0 copy-start.4
  43.0 2.0 %collective-permute-start.9 = (f32[8,32,128]{2,1,0:T(8,128)S(1)}, f32[8,32,128]{2,1,0:T(8,128)S(1)}, u32[]{:S(2)}, u32[]{:S(2)}) collective-permute-start(f32[8,32,128]{2,1,0:T(8,128)S(1)} %get-tuple-element.41), channel_id=1, source_target_pairs={{0,2},{2,0},{4,6},{6,4},{8,10},{10,8},{12,14},{14,12},{16,18},{18,... | collective-permute-start | bytes 393224 | tf_op jit(solution)/shard_map/ppermute | solution.py:299
  45.0 1.5 %collective-permute-start.10 = (f32[8,32,128]{2,1,0:T(8,128)S(1)}, f32[8,32,128]{2,1,0:T(8,128)S(1)}, u32[]{:S(2)}, u32[]{:S(2)}) collective-permute-start(f32[8,32,128]{2,1,0:T(8,128)S(1)} %get-tuple-element.42), channel_id=1, source_target_pairs={{0,4},{2,6},{4,0},{6,2},{8,12},{10,14},{12,8},{14,10},{16,20},{18,... | collective-permute-start | bytes 393224 | tf_op jit(solution)/shard_map/ppermute | solution.py:299
  46.5 0.1 collective-permute-start.11
  46.6 5.4 %collective-permute-done.9.rest_4_ = f32[8,32,128]{2,1,0:T(8,128)S(1)} collective-permute-done((f32[8,32,128]{2,1,0:T(8,128)S(1)}, f32[8,32,128]{2,1,0:T(8,128)S(1)}, u32[]{:S(2)}, u32[]{:S(2)}) %collective-permute-start.9) | collective-permute-done | bytes 131104 | tf_op jit(solution)/shard_map/ppermute | solution.py:299
  52.0 1.6 %collective-permute-done.10.rest_5_ = f32[8,32,128]{2,1,0:T(8,128)S(1)} collective-permute-done((f32[8,32,128]{2,1,0:T(8,128)S(1)}, f32[8,32,128]{2,1,0:T(8,128)S(1)}, u32[]{:S(2)}, u32[]{:S(2)}) %collective-permute-start.10) | collective-permute-done | bytes 131104 | tf_op jit(solution)/shard_map/ppermute | solution.py:299
  53.6 1.8 %collective-permute-done.11.rest_6_ = f32[8,32,128]{2,1,0:T(8,128)S(1)} collective-permute-done((f32[8,32,128]{2,1,0:T(8,128)S(1)}, f32[8,32,128]{2,1,0:T(8,128)S(1)}, u32[]{:S(2)}, u32[]{:S(2)}) %collective-permute-start.11) | collective-permute-done | bytes 131104 | tf_op jit(solution)/shard_map/ppermute | solution.py:299
  55.4 0.9 %all-to-all-done.1.parts = f32[16,2,32,128]{3,2,1,0:T(8,128)S(1)} async-done(((f32[16,2,32,128]{3,2,1,0:T(8,128)}), f32[16,2,32,128]{3,2,1,0:T(8,128)S(1)}, u32[]{:S(2)}, u32[]{:S(2)}) %all-to-all-start.1) | async-done | bytes 524320 | tf_op jit(solution)/shard_map/all_to_all | solution.py:386
  56.3 0.0 copy-done.1
  56.3 0.0 copy-done.2
  56.3 0.0 copy-done.3
  56.3 0.0 copy-done.4
  56.3 1.4 %unpack.1 = (f32[128,512]{1,0:T(8,128)}, f32[128,512]{1,0:T(8,128)}, f32[128,512]{1,0:T(8,128)}, f32[128,512]{1,0:T(8,128)}, f32[128,512]{1,0:T(8,128)}, /*index=5*/f32[128,512]{1,0:T(8,128)}, f32[1,512]{1,0:T(1,128)}) custom-call(bf16[128,512]{1,0:T(8,128)(2,1)S(1)} %copy-done.1, bf16[128,512]{1,0:T(8,128)(2,1)S(1)} %copy-done.2, ...), custom_call_target="tpu_custom_call" | custom-call | bytes 3145728 | tf_op jit(solution)/shard_map/unpack/pallas_call | solution.py:393
  (2 shorter events, 0.0 us)
Async XLA Ops:
  0.6 1.0 %copy-start.5 = (f32[128,512]{1,0:T(8,128)S(1)}, f32[128,512]{1,0:T(8,128)}, u32[]{:S(2)}) copy-start(f32[128,512]{1,0:T(8,128)} %field.1) | copy-start | bytes 786436
  1.7 15.0 %collective-permute-start = (f32[4,32,128]{2,1,0:T(8,128)S(1)}, f32[4,32,128]{2,1,0:T(8,128)S(1)}, u32[]{:S(2)}, u32[]{:S(2)}) collective-permute-start(f32[4,32,128]{2,1,0:T(8,128)S(1)} %get-tuple-element.30), channel_id=1, source_target_pairs={{0,8},{2,10},{4,12},{6,14},{8,0},{10,2},{12,4},{14,6},{16,24},{18,... | collective-permute-start | bytes 196616 | tf_op jit(solution)/shard_map/ppermute | solution.py:299
  4.8 11.9 %collective-permute-start.1 = (f32[4,32,128]{2,1,0:T(8,128)S(1)}, f32[4,32,128]{2,1,0:T(8,128)S(1)}, u32[]{:S(2)}, u32[]{:S(2)}) collective-permute-start(f32[4,32,128]{2,1,0:T(8,128)S(1)} %get-tuple-element.31), channel_id=1, source_target_pairs={{0,16},{2,18},{4,20},{6,22},{8,24},{10,26},{12,28},{14,30},{16,0},... | collective-permute-start | bytes 196616 | tf_op jit(solution)/shard_map/ppermute | solution.py:299
  7.4 9.3 %collective-permute-start.2 = (f32[4,32,128]{2,1,0:T(8,128)S(1)}, f32[4,32,128]{2,1,0:T(8,128)S(1)}, u32[]{:S(2)}, u32[]{:S(2)}) collective-permute-start(f32[4,32,128]{2,1,0:T(8,128)S(1)} %get-tuple-element.32), channel_id=1, source_target_pairs={{0,24},{2,26},{4,28},{6,30},{8,16},{10,18},{12,20},{14,22},{16,8},... | collective-permute-start | bytes 196616 | tf_op jit(solution)/shard_map/ppermute | solution.py:299
  9.6 21.4 %all-to-all-start = ((f32[16,2,32,128]{3,2,1,0:T(8,128)}), f32[16,2,32,128]{3,2,1,0:T(8,128)S(1)}, u32[]{:S(2)}, u32[]{:S(2)}) async-start(f32[16,2,32,128]{3,2,1,0:T(8,128)} %pack.1), calls=%async_computation | async-start | bytes 1048576 | tf_op jit(solution)/shard_map/all_to_all | solution.py:346
  16.7 14.3 %copy-start = (bf16[4,256,256]{2,1,0:T(8,128)(2,1)S(1)}, bf16[4,256,256]{2,1,0:T(8,128)(2,1)}, u32[]{:S(2)}) copy-start(bf16[4,256,256]{2,1,0:T(8,128)(2,1)} %constant.4.clone.matrices) | copy-start | bytes 1572868
  16.8 14.3 %copy-start.6 = (f32[17,4,128]{2,1,0:T(4,128)S(1)}, f32[17,4,128]{2,1,0:T(4,128)}, u32[]{:S(2)}) copy-start(f32[17,4,128]{2,1,0:T(4,128)} %constant.5.clone.twists) | copy-start | bytes 104452
  16.8 14.3 %copy-start.7 = (f32[128,512]{1,0:T(8,128)S(1)}, f32[128,512]{1,0:T(8,128)}, u32[]{:S(2)}) copy-start(f32[128,512]{1,0:T(8,128)} %taps.1) | copy-start | bytes 786436
  16.8 14.3 %copy-start.8 = (f32[512]{0:T(512)S(1)}, f32[512]{0:T(512)}, u32[]{:S(2)}) copy-start(f32[512]{0:T(512)} %param.14) | copy-start | bytes 6148
  16.8 6.2 %collective-permute-start.3 = (f32[4,32,128]{2,1,0:T(8,128)S(1)}, f32[4,32,128]{2,1,0:T(8,128)S(1)}, u32[]{:S(2)}, u32[]{:S(2)}) collective-permute-start(f32[4,32,128]{2,1,0:T(8,128)S(1)} %get-tuple-element.33), channel_id=1, source_target_pairs={{0,2},{2,0},{4,6},{6,4},{8,10},{10,8},{12,14},{14,12},{16,18},{18,... | collective-permute-start | bytes 196616 | tf_op jit(solution)/shard_map/ppermute | solution.py:299
  18.8 5.8 %collective-permute-start.4 = (f32[4,32,128]{2,1,0:T(8,128)S(1)}, f32[4,32,128]{2,1,0:T(8,128)S(1)}, u32[]{:S(2)}, u32[]{:S(2)}) collective-permute-start(f32[4,32,128]{2,1,0:T(8,128)S(1)} %get-tuple-element.34), channel_id=1, source_target_pairs={{0,4},{2,6},{4,0},{6,2},{8,12},{10,14},{12,8},{14,10},{16,20},{18,... | collective-permute-start | bytes 196616 | tf_op jit(solution)/shard_map/ppermute | solution.py:299
  20.3 5.8 %collective-permute-start.5 = (f32[4,32,128]{2,1,0:T(8,128)S(1)}, f32[4,32,128]{2,1,0:T(8,128)S(1)}, u32[]{:S(2)}, u32[]{:S(2)}) collective-permute-start(f32[4,32,128]{2,1,0:T(8,128)S(1)} %get-tuple-element.35), channel_id=1, source_target_pairs={{0,6},{2,4},{4,2},{6,0},{8,14},{10,12},{12,10},{14,8},{16,22},{18,... | collective-permute-start | bytes 196616 | tf_op jit(solution)/shard_map/ppermute | solution.py:299
  32.9 10.0 %collective-permute-start.6 = (f32[5,32,128]{2,1,0:T(8,128)S(1)}, f32[5,32,128]{2,1,0:T(8,128)S(1)}, u32[]{:S(2)}, u32[]{:S(2)}) collective-permute-start(f32[5,32,128]{2,1,0:T(8,128)S(1)} %get-tuple-element.38), channel_id=1, source_target_pairs={{0,8},{2,10},{4,12},{6,14},{8,0},{10,2},{12,4},{14,6},{16,24},{18,... | collective-permute-start | bytes 245768 | tf_op jit(solution)/shard_map/ppermute | solution.py:299
  34.2 8.7 %collective-permute-start.7 = (f32[5,32,128]{2,1,0:T(8,128)S(1)}, f32[5,32,128]{2,1,0:T(8,128)S(1)}, u32[]{:S(2)}, u32[]{:S(2)}) collective-permute-start(f32[5,32,128]{2,1,0:T(8,128)S(1)} %get-tuple-element.39), channel_id=1, source_target_pairs={{0,16},{2,18},{4,20},{6,22},{8,24},{10,26},{12,28},{14,30},{16,0},... | collective-permute-start | bytes 245768 | tf_op jit(solution)/shard_map/ppermute | solution.py:299
  35.3 7.6 %collective-permute-start.8 = (f32[5,32,128]{2,1,0:T(8,128)S(1)}, f32[5,32,128]{2,1,0:T(8,128)S(1)}, u32[]{:S(2)}, u32[]{:S(2)}) collective-permute-start(f32[5,32,128]{2,1,0:T(8,128)S(1)} %get-tuple-element.40), channel_id=1, source_target_pairs={{0,24},{2,26},{4,28},{6,30},{8,16},{10,18},{12,20},{14,22},{16,8},... | collective-permute-start | bytes 245768 | tf_op jit(solution)/shard_map/ppermute | solution.py:299
  39.1 17.3 %all-to-all-start.1 = ((f32[16,2,32,128]{3,2,1,0:T(8,128)}), f32[16,2,32,128]{3,2,1,0:T(8,128)S(1)}, u32[]{:S(2)}, u32[]{:S(2)}) async-start(f32[16,2,32,128]{3,2,1,0:T(8,128)} %mix.1), calls=%async_computation.1 | async-start | bytes 1048576 | tf_op jit(solution)/shard_map/all_to_all | solution.py:386
  42.9 13.4 %copy-start.1 = (bf16[128,512]{1,0:T(8,128)(2,1)S(1)}, bf16[128,512]{1,0:T(8,128)(2,1)}, u32[]{:S(2)}) copy-start(bf16[128,512]{1,0:T(8,128)(2,1)} %query.1) | copy-start | bytes 393220
  43.0 13.4 %copy-start.2 = (bf16[128,512]{1,0:T(8,128)(2,1)S(1)}, bf16[128,512]{1,0:T(8,128)(2,1)}, u32[]{:S(2)}) copy-start(bf16[128,512]{1,0:T(8,128)(2,1)} %key.1) | copy-start | bytes 393220
  43.0 13.3 %copy-start.3 = (bf16[128,512]{1,0:T(8,128)(2,1)S(1)}, bf16[128,512]{1,0:T(8,128)(2,1)}, u32[]{:S(2)}) copy-start(bf16[128,512]{1,0:T(8,128)(2,1)} %value.1) | copy-start | bytes 393220
  43.0 13.3 %copy-start.4 = (bf16[128,512]{1,0:T(8,128)(2,1)S(1)}, bf16[128,512]{1,0:T(8,128)(2,1)}, u32[]{:S(2)}) copy-start(bf16[128,512]{1,0:T(8,128)(2,1)} %grad.1) | copy-start | bytes 393220
  43.0 9.0 %collective-permute-start.9 = (f32[8,32,128]{2,1,0:T(8,128)S(1)}, f32[8,32,128]{2,1,0:T(8,128)S(1)}, u32[]{:S(2)}, u32[]{:S(2)}) collective-permute-start(f32[8,32,128]{2,1,0:T(8,128)S(1)} %get-tuple-element.41), channel_id=1, source_target_pairs={{0,2},{2,0},{4,6},{6,4},{8,10},{10,8},{12,14},{14,12},{16,18},{18,... | collective-permute-start | bytes 393224 | tf_op jit(solution)/shard_map/ppermute | solution.py:299
  45.0 8.6 %collective-permute-start.10 = (f32[8,32,128]{2,1,0:T(8,128)S(1)}, f32[8,32,128]{2,1,0:T(8,128)S(1)}, u32[]{:S(2)}, u32[]{:S(2)}) collective-permute-start(f32[8,32,128]{2,1,0:T(8,128)S(1)} %get-tuple-element.42), channel_id=1, source_target_pairs={{0,4},{2,6},{4,0},{6,2},{8,12},{10,14},{12,8},{14,10},{16,20},{18,... | collective-permute-start | bytes 393224 | tf_op jit(solution)/shard_map/ppermute | solution.py:299
  46.5 8.9 %collective-permute-start.11 = (f32[8,32,128]{2,1,0:T(8,128)S(1)}, f32[8,32,128]{2,1,0:T(8,128)S(1)}, u32[]{:S(2)}, u32[]{:S(2)}) collective-permute-start(f32[8,32,128]{2,1,0:T(8,128)S(1)} %get-tuple-element.43), channel_id=1, source_target_pairs={{0,6},{2,4},{4,2},{6,0},{8,14},{10,12},{12,10},{14,8},{16,22},{18,... | collective-permute-start | bytes 393224 | tf_op jit(solution)/shard_map/ppermute | solution.py:299

commit v12 on v11

--- a/solution.py
+++ b/solution.py
@@ -140,45 +140,65 @@
     return dot(values_high, high) + (dot(values_low, high) + dot(values_high, low))
 
 
-def pack_kernel(product, mix_grad, out):
-    blocks, _, share, rows = out.shape
-    for a, field in enumerate((product, mix_grad)):
-        out[:, a] = field[...].T.reshape(blocks, share, rows)
-
-
-def split_kernel(field, *rest, near_count):
-    outs, turned = rest[:-1], rest[-1]
-    share = outs[0].shape[1]
-    turned[...] = field[...].T
+def pack_kernel(field, out):
+    blocks, share, rows = out.shape
+    out[...] = field[...].T.reshape(blocks, share, rows)
+
+
+def chunk(sizes, count, field, at):
+    return pl.ds(count * sum(sizes[:field]) + at * sizes[field], sizes[field])
+
+
+def split_kernel(*refs, near_count):
+    fields, outs, turned = refs[:2], refs[2:-1], refs[-1]
+    share = outs[0].shape[0] // (2 * near_count)
     me = lax.axis_index("ctx") if near_count > 1 else 0
-    for far, out in enumerate(outs):
+    for k, field in enumerate(fields):
+        turned[...] = field[...].T
+        for far, out in enumerate(outs):
+            for near in range(near_count):
+                start = (me ^ (far * near_count + near)) * share
+                start = start if near_count == 1 else pl.multiple_of(start, share)
+                out[chunk((share, share), near_count, k, near), :] = turned[pl.ds(start, share), :]
+
+
+def gather_blocks(outs, sizes, far_parts, near_parts, me):
+    far_count, near_count = len(far_parts), len(near_parts) + 1
+    for far, part in enumerate(far_parts):
         for near in range(near_count):
-            start = (me ^ (far * near_count + near)) * share
-            out[near] = turned[pl.ds(start if near_count == 1 else pl.multiple_of(start, share), share), :]
-
-
-def spectra_kernel(taps, skip, matrices, twists, arrays, *rest, near_count, grad_scale):
-    blocks, _, channels, rows = arrays.shape
+            source = me ^ (far * near_count + near)
+            for k, size in enumerate(sizes):
+                if near:
+                    rows = near_parts[near - 1][chunk(sizes, far_count, k, far), :]
+                else:
+                    rows = part[chunk(sizes, near_count, k, 0), :]
+                outs[k][source, :size, :] = rows
+            if len(outs) > len(sizes):
+                extra = outs[len(sizes)].shape[1]
+                if near:
+                    rows = near_parts[near - 1][pl.ds(far_count * sum(sizes) + far * extra, extra), :]
+                else:
+                    rows = part[pl.ds(near_count * sum(sizes), extra), :]
+                outs[len(sizes)][source] = rows
+
+
+def spectra_kernel(taps, skip, matrices, twists, mix_grads, *rest, near_count, early, grad_scale):
+    blocks, channels, rows = mix_grads.shape
     far_count = blocks // near_count
     far_parts, rest = rest[:far_count], rest[far_count:]
     near_parts, rest = rest[: near_count - 1], rest[near_count - 1 :]
-    products, *lag_outs, spectra, results, direct, lags, filter_blocks = rest
+    products, *outs, spectra, results, direct, lags, back, filters, gates = rest
     me = lax.axis_index("ctx") if near_count > 1 else 0
-    for far, part in enumerate(far_parts):
-        filter_blocks[me ^ (far * near_count)] = part[0]
-        for near, near_part in enumerate(near_parts, 1):
-            filter_blocks[me ^ (far * near_count + near)] = near_part[far]
+    gather_blocks((filters, gates), (channels, channels), far_parts, near_parts, me)
     row = lax.broadcasted_iota(jnp.int32, taps.shape, 0)
     direct[...] = (taps[...] + jnp.where(row == 0, skip[...], 0.0)).T
     own = 0 if direct.shape[0] == channels else pl.multiple_of(lax.axis_index("ctx") * channels, channels)
     for a in range(3):
         for low in range(0, channels, 8):
             part = pl.ds(low, 8)
+            values = [(gates, filters, mix_grads)[a][j, part, :] for j in range(blocks)]
             if a == 1:
-                values = [filter_blocks[j, part, :] for j in range(blocks)]
                 values[0] = values[0] + direct[pl.ds(own + low, 8), :]
-            else:
-                values = [arrays[j, a // 2, part, :] for j in range(blocks)]
             bins = padded_bins(values)
             for p in range(blocks + 1):
                 real, imag = bins[p]
@@ -200,52 +220,66 @@
     products[0, :, rows:] = fr * pi + fi * pr
     products[1, :, :rows] = fr * gr + fi * gi
     products[1, :, rows:] = fr * gi - fi * gr
-    for low, values in blocks_back(spectra.at[0], results, matrices, twists, channels):
+    for low, values in blocks_back(spectra.at[0], results, matrices, twists, channels, 0, channels):
         for j, value in enumerate(values):
             lags[j, pl.ds(low, 8), :] = value * grad_scale
-    for far, lag_out in enumerate(lag_outs):
+    for low, values in blocks_back(products.at[1], results, matrices, twists, channels, 0, early):
+        for j, value in enumerate(values):
+            back[j, pl.ds(low, 8), :] = value
+    sizes = (channels, early) if early else (channels,)
+    for far, out in enumerate(outs):
         for near in range(near_count):
-            lag_out[near] = lags[me ^ (far * near_count + near)]
-        lag_out[near_count] = lags[0]
-
-
-def blocks_back(spectrum, result, matrices, twists, channels):
+            target = me ^ (far * near_count + near)
+            for k, size in enumerate(sizes):
+                out[chunk(sizes, near_count, k, near), :] = (lags, back)[k][target]
+        out[pl.ds(near_count * sum(sizes), channels), :] = lags[0]
+
+
+def blocks_back(spectrum, result, matrices, twists, channels, first, last):
     blocks, rows = twists.shape[0] - 1, twists.shape[2]
-    result[...] = multiply(spectrum[...], matrices[2], matrices[3])
-    for low in range(0, channels, 8):
+    count = last - first
+    if count == 0:
+        return
+    height = (blocks + 1) * count
+    wanted = spectrum[...].reshape(blocks + 1, channels, 2 * rows)[:, first:last].reshape(height, 2 * rows)
+    result[:height, :] = multiply(wanted, matrices[2], matrices[3])
+    for low in range(0, count, 8):
         bins = {}
         for p in range(blocks + 1):
             cosine, sine = twists[p, 2:3, :], twists[p, 3:4, :]
-            place = pl.ds(p * channels + low, 8)
+            place = pl.ds(p * count + low, 8)
             real, imag = result[place, :rows], result[place, rows:]
             new_real = real * cosine - imag * sine
             bins[p] = (new_real, None if p % blocks == 0 else real * sine + imag * cosine)
         yield low, padded_bins_back(bins, blocks)
 
 
-def mix_kernel(matrices, twists, products, out, results):
-    for a in range(2):
-        for low, values in blocks_back(products.at[a], results.at[a], matrices, twists, out.shape[2]):
+def mix_kernel(matrices, twists, products, out, results, *, channels, early):
+    for a, first in enumerate((0, early)):
+        for low, values in blocks_back(products.at[a], results.at[a], matrices, twists, channels, first, channels):
             for j, value in enumerate(values):
-                out[j, a, pl.ds(low, 8), :] = value
-
-
-def relay_kernel(*refs, far_count):
+                out[j, pl.ds(a * channels + low, 8), :] = value
+
+
+def relay_kernel(*refs, far_count, sizes, extra):
     parts = (refs[0], *refs[1:far_count][::-1])
     outs = refs[far_count:]
     near_count = len(outs) + 1
     for near, out in enumerate(outs, 1):
         for far, part in enumerate(parts):
-            out[far] = part[near]
-            if part.shape[0] > near_count:
-                out[far_count + far] = part[near_count]
-
-
-def unpack_kernel(query, key, value, grad, parts, *rest, far_count, near_count):
+            for k in range(len(sizes)):
+                out[chunk(sizes, far_count, k, far), :] = part[chunk(sizes, near_count, k, near), :]
+            if extra:
+                place = pl.ds(far_count * sum(sizes) + far * extra, extra)
+                out[place, :] = part[pl.ds(near_count * sum(sizes), extra), :]
+
+
+def unpack_kernel(query, key, value, grad, parts, *rest, far_count, near_count, early):
     far_parts, rest = rest[:far_count], rest[far_count:]
     near_parts, rest = rest[: near_count - 1], rest[near_count - 1 :]
-    outs, held, sent, lags, first_lags = rest[:7], rest[7:14], rest[14], rest[15], rest[16]
+    outs, held, sent, lags, back, first_lags = rest[:7], rest[7:14], rest[14], rest[15], rest[16], rest[17]
     rows, channels = query.shape
+    blocks, share, _ = lags.shape
     copies = [
         pltpu.make_async_copy(source, target, sent.at[i])
         for i, (source, target) in enumerate(zip(held, outs))
@@ -258,22 +292,18 @@
         held[i][...] = array
         copies[i].start()
 
-    mixer = whole(parts[:, 0])
+    mixer = whole(parts[:, :share])
     put(0, query[...].astype(jnp.float32) * mixer)
     put(1, grad[...].astype(jnp.float32) * mixer)
-    product_grad = whole(parts[:, 1])
+    me = lax.axis_index("ctx") if near_count > 1 else 0
+    if early:
+        gather_blocks((lags, back, first_lags), (share, early), far_parts, near_parts, me)
+    else:
+        gather_blocks((lags, first_lags), (share,), far_parts, near_parts, me)
+    back[:, early:, :] = parts[:, share:]
+    product_grad = whole(back[...])
     put(2, product_grad * value[...].astype(jnp.float32))
     put(3, product_grad * key[...].astype(jnp.float32))
-    me = lax.axis_index("ctx") if near_count > 1 else 0
-    for far, part in enumerate(far_parts):
-        source = me ^ (far * near_count)
-        lags[source] = part[0]
-        first_lags[source] = part[near_count]
-    for near, part in enumerate(near_parts, 1):
-        for far in range(far_count):
-            source = me ^ (far * near_count + near)
-            lags[source] = part[far]
-            first_lags[source] = part[far_count + far]
     put(4, whole(lags[...]))
     first = whole(first_lags[...])
     put(5, first)
@@ -299,14 +329,13 @@
     return lax.ppermute(value, axis, [(i, i ^ distance) for i in range(lax.axis_size(axis))])
 
 
-def send_parts(parts, axis, near_count):
+def send_parts(parts, axis, near_count, sizes, extra=0):
     far_parts, far_count = list(parts), len(parts)
     for far in range(far_count - 1, 0, -1):
         far_parts[far] = exchange(parts[far], axis, far * near_count)
-    depth = far_count * (1 + parts[0].shape[0] - near_count)
-    payload = jax.ShapeDtypeStruct((depth, *parts[0].shape[1:]), jnp.float32)
+    payload = jax.ShapeDtypeStruct((far_count * (sum(sizes) + extra), parts[0].shape[1]), jnp.float32)
     relay = call(
-        functools.partial(relay_kernel, far_count=far_count),
+        functools.partial(relay_kernel, far_count=far_count, sizes=sizes, extra=extra),
         "relay",
         (payload,) * (near_count - 1),
         (pltpu.VMEM,) * far_count,
@@ -330,24 +359,24 @@
     far_count = blocks // near_count
     product = key.astype(f32) * value.astype(f32)
     mix_grad = out_grad.astype(f32) * query.astype(f32)
-    filter_parts = call(
+    split_parts = call(
         functools.partial(split_kernel, near_count=near_count),
         "split",
-        (shape((near_count, share, rows)),) * far_count,
-        (pltpu.VMEM,),
+        (shape((2 * near_count * share, rows)),) * far_count,
+        (pltpu.VMEM,) * 2,
         scratch=(pltpu.VMEM((channels, rows), f32),),
-        size=8 * rows * channels,
-    )(implicit_filter)
-    packed = call(
-        pack_kernel, "pack", shape((blocks, 2, share, rows)), (pltpu.VMEM,) * 2, size=16 * rows * channels
-    )(product, mix_grad)
+        size=16 * rows * channels,
+    )(implicit_filter, product)
+    packed = call(pack_kernel, "pack", shape((blocks, share, rows)), (pltpu.VMEM,), size=8 * rows * channels)(mix_grad)
     if near_count > 1:
-        filter_far, filter_near = send_parts(filter_parts, "ctx", near_count)
-        arrays = lax.all_to_all(packed, "ctx", 0, 0, tiled=True)
+        far_parts, near_parts = send_parts(split_parts, "ctx", near_count, (share, share))
+        mix_grads = lax.all_to_all(packed, "ctx", 0, 0, tiled=True)
     else:
-        arrays = lax.all_to_all(jnp.concatenate([packed, jnp.stack(filter_parts)], axis=1), "ctx", 0, 0, tiled=True)
-        arrays = jnp.pad(arrays, ((0, 0), (0, 0), (0, padded - share), (0, 0)))
-        arrays, filter_far, filter_near = arrays[:, :2], list(arrays[:, 2:]), []
+        together = jnp.concatenate([packed, jnp.stack(split_parts)], axis=1)
+        together = lax.all_to_all(together, "ctx", 0, 0, tiled=True).reshape(blocks, 3, share, rows)
+        together = jnp.pad(together, ((0, 0), (0, 0), (0, padded - share), (0, 0)))
+        mix_grads, near_parts = together[:, 0], []
+        far_parts = list(together[:, 1:].reshape(blocks, 2 * padded, rows))
         own = lax.axis_index("ctx") * share
         taps, skip = [
             jnp.pad(lax.dynamic_slice_in_dim(each, own, share, 1), ((0, 0), (0, padded - share)))
@@ -356,47 +385,52 @@
     matrices, twists = tables(blocks, rows)
     height = (blocks + 1) * padded
     matrices, twists = jnp.asarray(matrices), jnp.asarray(twists)
-    products, *lag_parts = call(
-        functools.partial(spectra_kernel, near_count=near_count, grad_scale=grad_scale),
+    early = padded // 16 * 8 if near_count > 1 else 0
+    block = pltpu.VMEM((blocks, padded, rows), f32)
+    products, *split_parts = call(
+        functools.partial(spectra_kernel, near_count=near_count, early=early, grad_scale=grad_scale),
         "spectra",
-        (shape((2, height, 2 * rows)),) + (shape((near_count + 1, padded, rows)),) * far_count,
+        (shape((2, height, 2 * rows)),) + (shape((near_count * (padded + early) + padded, rows)),) * far_count,
         (pltpu.VMEM,) * (4 + far_count + near_count),
         scratch=(
             pltpu.VMEM((3, height, 2 * rows), f32),
             pltpu.VMEM((height, 2 * rows), f32),
             pltpu.VMEM(taps.shape[::-1], f32),
-            pltpu.VMEM((blocks, padded, rows), f32),
-            pltpu.VMEM((blocks, padded, rows), f32),
+            block,
+            pltpu.VMEM((blocks, max(early, 8), rows), f32),
+            block,
+            block,
         ),
-        flops=24 * height * (2 * rows) ** 2,
+        flops=27 * height * (2 * rows) ** 2,
         size=24 * blocks * padded * rows,
-    )(taps, skip, matrices, twists, arrays, *filter_far, *filter_near)
+    )(taps, skip, matrices, twists, mix_grads, *far_parts, *near_parts)
     if near_count > 1:
-        far_parts, near_parts = send_parts(lag_parts, "ctx", near_count)
+        sizes = (share, early) if early else (share,)
+        far_parts, near_parts = send_parts(split_parts, "ctx", near_count, sizes, share)
     results = call(
-        mix_kernel,
+        functools.partial(mix_kernel, channels=padded, early=early),
         "mix",
-        shape((blocks, 2, padded, rows)),
+        shape((blocks, 2 * padded - early, rows)),
         (pltpu.VMEM,) * 3,
         scratch=(pltpu.VMEM((2, height, 2 * rows), f32),),
-        flops=12 * height * (2 * rows) ** 2,
+        flops=9 * height * (2 * rows) ** 2,
         size=24 * blocks * padded * rows,
     )(matrices, twists, products)
     if near_count > 1:
         parts = lax.all_to_all(results, "ctx", 0, 0, tiled=True)
     else:
-        together = jnp.concatenate([results, jnp.stack(lag_parts)], axis=1)[:, :, :share]
-        together = lax.all_to_all(together, "ctx", 0, 0, tiled=True)
-        parts, far_parts, near_parts = together[:, :2], list(together[:, 2:]), []
+        together = jnp.concatenate([results, jnp.stack(split_parts)], axis=1).reshape(blocks, 4, padded, rows)
+        together = lax.all_to_all(together[:, :, :share], "ctx", 0, 0, tiled=True).reshape(blocks, 4 * share, rows)
+        parts, far_parts, near_parts = together[:, : 2 * share], list(together[:, 2 * share :]), []
     full, one = shape((rows, channels)), shape((1, channels))
-    lags = pltpu.VMEM((blocks, share, rows), f32)
+    block = pltpu.VMEM((blocks, share, rows), f32)
     outs = call(
-        functools.partial(unpack_kernel, far_count=far_count, near_count=near_count),
+        functools.partial(unpack_kernel, far_count=far_count, near_count=near_count, early=early),
         "unpack",
         (full,) * 6 + (one,),
         (pltpu.VMEM,) * (4 + far_count + near_count),
         scratch=tuple(pltpu.VMEM(out.shape, f32) for out in (full,) * 6 + (one,))
-        + (pltpu.SemaphoreType.DMA((7,)), lags, lags),
+        + (pltpu.SemaphoreType.DMA((7,)), block, block, block),
         to=pltpu.HBM,
         size=48 * rows * channels,
     )(query, key, value, out_grad, parts, *far_parts, *near_parts)

time: 58.1 us -> 58.4 us (level)
  the two profiles are of different devices: /device:TPU:0 before, /device:TPU:18 now
where the time goes in v12:
time: 58.4 us; the launch traced here: 58.1 us
  starting transfers between devices  28.3 us (48%)
  waiting for transfers between devices  21.1 us (36%)
  Pallas kernels  5.81 us (10%)
  other arithmetic  1.07 us (2%)
  local copies, waits for them, and re-layouts  0.99 us (2%)
  between operations  0.8 us (1%)
    ppermute x12, waiting for transfers between devices, exchange(): lax.ppermute(value, axis, [(i, i ^ distance) for i in range(lax.axis_size...  21.1 us
    ppermute x12, starting transfers between devices, exchange(): lax.ppermute(value, axis, [(i, i ^ distance) for i in range(lax.axis_size...  14.8 us
    all_to_all x1, starting transfers between devices, body(): mix_grads = lax.all_to_all(packed, 'ctx', 0, 0, tiled=True)  7.99 us
    all_to_all x1, starting transfers between devices, body(): parts = lax.all_to_all(results, 'ctx', 0, 0, tiled=True)  5.57 us
    pallas_call x1, Pallas kernels, body(): call(functools.partial(spectra_kernel, near_count=near_count, early=early...  1.84 us
    pallas_call x1, Pallas kernels, body(): call(functools.partial(mix_kernel, channels=padded, early=early), 'mix',...  1.45 us
    pallas_call x1, Pallas kernels, body(): call(functools.partial(unpack_kernel, far_count=far_count, near_count=nea...  1.4 us
  transfers between devices with their start and end apart: 14, of which 7 were waited for; matrix products, arithmetic and copies ran while one was open for 0% of the time, Pallas kernels for 4%

profile of v12, /device:TPU:18, one launch (start us, length us, event | category | flops | bytes accessed | tf_op | source)
XLA Modules:
  0.0 58.1 jit_solution(1971490872408159836)
XLA Ops:
  0.6 0.0 copy-start.4
  0.6 0.0 copy-start
  0.7 1.0 %convert_multiply_fusion.refs_1_ = f32[128,512]{1,0:T(8,128)S(1)} fusion(bf16[128,512]{1,0:T(8,128)(2,1)} %value.1, bf16[128,512]{1,0:T(8,128)(2,1)} %key.1), kind=kLoop, calls=%fused_computation | loop fusion | flops 196608 | bytes 524288 | tf_op jit(solution)/shard_map/mul | solution.py:360
  1.7 0.0 copy-start.7
  1.7 0.9 %copy-done.7 = f32[128,512]{1,0:T(8,128)S(1)} copy-done((f32[128,512]{1,0:T(8,128)S(1)}, f32[128,512]{1,0:T(8,128)}, u32[]{:S(2)}) %copy-start.7) | copy-done | bytes 262168
  2.7 0.2 split.1
  2.9 1.6 %collective-permute-start = (f32[256,128]{1,0:T(8,128)S(1)}, f32[256,128]{1,0:T(8,128)S(1)}, u32[]{:S(2)}, u32[]{:S(2)}) collective-permute-start(f32[256,128]{1,0:T(8,128)S(1)} %get-tuple-element.30), channel_id=1, source_target_pairs={{0,8},{2,10},{4,12},{6,14},{8,0},{10,2},{12,4},{14,6},{16,24},{18,... | collective-permute-start | bytes 393224 | tf_op jit(solution)/shard_map/ppermute | solution.py:329
  4.5 0.3 collective-permute-start.1
  4.9 1.6 %collective-permute-start.2 = (f32[256,128]{1,0:T(8,128)S(1)}, f32[256,128]{1,0:T(8,128)S(1)}, u32[]{:S(2)}, u32[]{:S(2)}) collective-permute-start(f32[256,128]{1,0:T(8,128)S(1)} %get-tuple-element.32), channel_id=1, source_target_pairs={{0,24},{2,26},{4,28},{6,30},{8,16},{10,18},{12,20},{14,22},{16,8},... | collective-permute-start | bytes 393224 | tf_op jit(solution)/shard_map/ppermute | solution.py:329
  6.4 0.0 copy-done.4
  6.4 0.0 copy-done
  6.5 0.8 %pack.1 = f32[16,32,128]{2,1,0:T(8,128)} custom-call(f32[128,512]{1,0:T(8,128)S(1)} %convert_multiply_fusion.1.field), custom_call_target="tpu_custom_call" | custom-call | bytes 524288 | tf_op jit(solution)/shard_map/pack/pallas_call | solution.py:370
  7.3 8.0 %all-to-all-start = ((f32[16,32,128]{2,1,0:T(8,128)}), f32[16,32,128]{2,1,0:T(8,128)S(1)}, u32[]{:S(2)}, u32[]{:S(2)}) async-start(f32[16,32,128]{2,1,0:T(8,128)} %pack.1), calls=%async_computation | async-start | bytes 524288 | tf_op jit(solution)/shard_map/all_to_all | solution.py:373
  15.3 0.0 collective-permute-done.refs_3_.rest_1_
  15.3 0.0 collective-permute-done.1.refs_2_.rest_2_
  15.3 6.6 %collective-permute-done.2.refs_1_.rest_3_ = f32[256,128]{1,0:T(8,128)S(1)} collective-permute-done((f32[256,128]{1,0:T(8,128)S(1)}, f32[256,128]{1,0:T(8,128)S(1)}, u32[]{:S(2)}, u32[]{:S(2)}) %collective-permute-start.2) | collective-permute-done | bytes 131104 | tf_op jit(solution)/shard_map/ppermute | solution.py:329
  21.9 0.0 copy-start.6
  21.9 0.0 copy-start.8
  21.9 0.0 copy-start.9
  21.9 0.0 copy-start.10
  21.9 0.6 %collective-permute-start.3 = (f32[256,128]{1,0:T(8,128)S(1)}, f32[256,128]{1,0:T(8,128)S(1)}, u32[]{:S(2)}, u32[]{:S(2)}) collective-permute-start(f32[256,128]{1,0:T(8,128)S(1)} %get-tuple-element.33), channel_id=1, source_target_pairs={{0,2},{2,0},{4,6},{6,4},{8,10},{10,8},{12,14},{14,12},{16,18},{18,... | collective-permute-start | bytes 393224 | tf_op jit(solution)/shard_map/ppermute | solution.py:329
  22.5 1.5 %collective-permute-start.4 = (f32[256,128]{1,0:T(8,128)S(1)}, f32[256,128]{1,0:T(8,128)S(1)}, u32[]{:S(2)}, u32[]{:S(2)}) collective-permute-start(f32[256,128]{1,0:T(8,128)S(1)} %get-tuple-element.34), channel_id=1, source_target_pairs={{0,4},{2,6},{4,0},{6,2},{8,12},{10,14},{12,8},{14,10},{16,20},{18,... | collective-permute-start | bytes 393224 | tf_op jit(solution)/shard_map/ppermute | solution.py:329
  24.1 1.4 %collective-permute-start.5 = (f32[256,128]{1,0:T(8,128)S(1)}, f32[256,128]{1,0:T(8,128)S(1)}, u32[]{:S(2)}, u32[]{:S(2)}) collective-permute-start(f32[256,128]{1,0:T(8,128)S(1)} %get-tuple-element.35), channel_id=1, source_target_pairs={{0,6},{2,4},{4,2},{6,0},{8,14},{10,12},{12,10},{14,8},{16,22},{18,... | collective-permute-start | bytes 393224 | tf_op jit(solution)/shard_map/ppermute | solution.py:329
  25.5 1.5 %collective-permute-done.3.rest_4_ = f32[256,128]{1,0:T(8,128)S(1)} collective-permute-done((f32[256,128]{1,0:T(8,128)S(1)}, f32[256,128]{1,0:T(8,128)S(1)}, u32[]{:S(2)}, u32[]{:S(2)}) %collective-permute-start.3) | collective-permute-done | bytes 131104 | tf_op jit(solution)/shard_map/ppermute | solution.py:329
  27.0 0.5 collective-permute-done.4.rest_5_
  27.5 2.4 %collective-permute-done.5.rest_6_ = f32[256,128]{1,0:T(8,128)S(1)} collective-permute-done((f32[256,128]{1,0:T(8,128)S(1)}, f32[256,128]{1,0:T(8,128)S(1)}, u32[]{:S(2)}, u32[]{:S(2)}) %collective-permute-start.5) | collective-permute-done | bytes 131104 | tf_op jit(solution)/shard_map/ppermute | solution.py:329
  29.9 0.0 all-to-all-done.mix_grads
  29.9 0.0 copy-done.6
  29.9 0.0 copy-done.8
  29.9 0.0 copy-done.9
  29.9 0.0 copy-done.10
  29.9 1.8 %spectra.1 = (f32[2,544,256]{2,1,0:T(8,128)S(1)}, f32[224,128]{1,0:T(8,128)S(1)}, f32[224,128]{1,0:T(8,128)S(1)}, f32[224,128]{1,0:T(8,128)S(1)}, f32[224,128]{1,0:T(8,128)S(1)}) custom-call(f32[128,512]{1,0:T(8,128)S(1)} %copy-done.9, f32[1,512]{1,0:T(1,128)S(1)} %bitcast.2, bf16[4,256,256]{2,1,0:T(8,128)(2,1)S(1)} %copy-done.6, ...), custom_call_target="tpu_custom_call" | custom-call | flops 962592768 | bytes 1572864 | tf_op jit(solution)/shard_map/spectra/pallas_call | solution.py:390
  31.8 0.1 collective-permute-start.6
  31.9 2.1 %collective-permute-start.7 = (f32[224,128]{1,0:T(8,128)S(1)}, f32[224,128]{1,0:T(8,128)S(1)}, u32[]{:S(2)}, u32[]{:S(2)}) collective-permute-start(f32[224,128]{1,0:T(8,128)S(1)} %get-tuple-element.39), channel_id=1, source_target_pairs={{0,16},{2,18},{4,20},{6,22},{8,24},{10,26},{12,28},{14,30},{16,0},... | collective-permute-start | bytes 344072 | tf_op jit(solution)/shard_map/ppermute | solution.py:329
  33.9 1.4 %collective-permute-start.8 = (f32[224,128]{1,0:T(8,128)S(1)}, f32[224,128]{1,0:T(8,128)S(1)}, u32[]{:S(2)}, u32[]{:S(2)}) collective-permute-start(f32[224,128]{1,0:T(8,128)S(1)} %get-tuple-element.40), channel_id=1, source_target_pairs={{0,24},{2,26},{4,28},{6,30},{8,16},{10,18},{12,20},{14,22},{16,8},... | collective-permute-start | bytes 344072 | tf_op jit(solution)/shard_map/ppermute | solution.py:329
  35.4 1.4 %mix.1 = f32[16,48,128]{2,1,0:T(8,128)} custom-call(bf16[4,256,256]{2,1,0:T(8,128)(2,1)S(1)} %copy-done.6, f32[17,4,128]{2,1,0:T(4,128)S(1)} %copy-done.8, f32[2,544,256]{2,1,0:T(8,128)S(1)} %get-tuple-element.36.products), custom_call_target="tpu_custom_call" | custom-call | flops 320864256 | bytes 1572864 | tf_op jit(solution)/shard_map/mix/pallas_call | solution.py:410
  36.8 5.6 %all-to-all-start.1 = ((f32[16,48,128]{2,1,0:T(8,128)}), f32[16,48,128]{2,1,0:T(8,128)S(1)}, u32[]{:S(2)}, u32[]{:S(2)}) async-start(f32[16,48,128]{2,1,0:T(8,128)} %mix.1), calls=%async_computation.1 | async-start | bytes 786432 | tf_op jit(solution)/shard_map/all_to_all | solution.py:420
  42.4 0.0 collective-permute-done.6.refs_3_.rest_1_
  42.4 0.0 collective-permute-done.7.refs_2_.rest_2_
  42.4 4.5 %collective-permute-done.8.refs_1_.rest_3_ = f32[224,128]{1,0:T(8,128)S(1)} collective-permute-done((f32[224,128]{1,0:T(8,128)S(1)}, f32[224,128]{1,0:T(8,128)S(1)}, u32[]{:S(2)}, u32[]{:S(2)}) %collective-permute-start.8) | collective-permute-done | bytes 114720 | tf_op jit(solution)/shard_map/ppermute | solution.py:329
  46.9 0.0 copy-start.1
  46.9 0.0 copy-start.2
  46.9 0.0 copy-start.3
  46.9 0.0 copy-start.5
  47.0 2.6 %collective-permute-start.9 = (f32[320,128]{1,0:T(8,128)S(1)}, f32[320,128]{1,0:T(8,128)S(1)}, u32[]{:S(2)}, u32[]{:S(2)}) collective-permute-start(f32[320,128]{1,0:T(8,128)S(1)} %get-tuple-element.41), channel_id=1, source_target_pairs={{0,2},{2,0},{4,6},{6,4},{8,10},{10,8},{12,14},{14,12},{16,18},{18,... | collective-permute-start | bytes 491528 | tf_op jit(solution)/shard_map/ppermute | solution.py:329
  49.6 0.5 collective-permute-start.10
  50.1 1.0 %collective-permute-start.11 = (f32[320,128]{1,0:T(8,128)S(1)}, f32[320,128]{1,0:T(8,128)S(1)}, u32[]{:S(2)}, u32[]{:S(2)}) collective-permute-start(f32[320,128]{1,0:T(8,128)S(1)} %get-tuple-element.43), channel_id=1, source_target_pairs={{0,6},{2,4},{4,2},{6,0},{8,14},{10,12},{12,10},{14,8},{16,22},{18,... | collective-permute-start | bytes 491528 | tf_op jit(solution)/shard_map/ppermute | solution.py:329
  51.1 1.8 %collective-permute-done.9.rest_4_ = f32[320,128]{1,0:T(8,128)S(1)} collective-permute-done((f32[320,128]{1,0:T(8,128)S(1)}, f32[320,128]{1,0:T(8,128)S(1)}, u32[]{:S(2)}, u32[]{:S(2)}) %collective-permute-start.9) | collective-permute-done | bytes 163872 | tf_op jit(solution)/shard_map/ppermute | solution.py:329
  52.9 3.8 %collective-permute-done.10.rest_5_ = f32[320,128]{1,0:T(8,128)S(1)} collective-permute-done((f32[320,128]{1,0:T(8,128)S(1)}, f32[320,128]{1,0:T(8,128)S(1)}, u32[]{:S(2)}, u32[]{:S(2)}) %collective-permute-start.10) | collective-permute-done | bytes 163872 | tf_op jit(solution)/shard_map/ppermute | solution.py:329
  56.6 0.0 collective-permute-done.11.rest_6_
  56.6 0.0 all-to-all-done.1.parts
  56.6 0.0 copy-done.1
  56.6 0.0 copy-done.2
  56.7 0.0 copy-done.3
  56.7 0.0 copy-done.5
  56.7 1.4 %unpack.1 = (f32[128,512]{1,0:T(8,128)}, f32[128,512]{1,0:T(8,128)}, f32[128,512]{1,0:T(8,128)}, f32[128,512]{1,0:T(8,128)}, f32[128,512]{1,0:T(8,128)}, /*index=5*/f32[128,512]{1,0:T(8,128)}, f32[1,512]{1,0:T(1,128)}) custom-call(bf16[128,512]{1,0:T(8,128)(2,1)S(1)} %copy-done.1, bf16[128,512]{1,0:T(8,128)(2,1)S(1)} %copy-done.2, ...), custom_call_target="tpu_custom_call" | custom-call | bytes 3145728 | tf_op jit(solution)/shard_map/unpack/pallas_call | solution.py:427
  (3 shorter events, 0.1 us)
Async XLA Ops:
  0.6 5.8 %copy-start.4 = (bf16[128,512]{1,0:T(8,128)(2,1)S(1)}, bf16[128,512]{1,0:T(8,128)(2,1)}, u32[]{:S(2)}) copy-start(bf16[128,512]{1,0:T(8,128)(2,1)} %grad.1) | copy-start | bytes 393220
  0.6 5.8 %copy-start = (bf16[128,512]{1,0:T(8,128)(2,1)S(1)}, bf16[128,512]{1,0:T(8,128)(2,1)}, u32[]{:S(2)}) copy-start(bf16[128,512]{1,0:T(8,128)(2,1)} %query.1) | copy-start | bytes 393220
  1.7 1.0 %copy-start.7 = (f32[128,512]{1,0:T(8,128)S(1)}, f32[128,512]{1,0:T(8,128)}, u32[]{:S(2)}) copy-start(f32[128,512]{1,0:T(8,128)} %refs_0_.1) | copy-start | bytes 786436
  2.9 12.4 %collective-permute-start = (f32[256,128]{1,0:T(8,128)S(1)}, f32[256,128]{1,0:T(8,128)S(1)}, u32[]{:S(2)}, u32[]{:S(2)}) collective-permute-start(f32[256,128]{1,0:T(8,128)S(1)} %get-tuple-element.30), channel_id=1, source_target_pairs={{0,8},{2,10},{4,12},{6,14},{8,0},{10,2},{12,4},{14,6},{16,24},{18,... | collective-permute-start | bytes 393224 | tf_op jit(solution)/shard_map/ppermute | solution.py:329
  4.5 10.8 %collective-permute-start.1 = (f32[256,128]{1,0:T(8,128)S(1)}, f32[256,128]{1,0:T(8,128)S(1)}, u32[]{:S(2)}, u32[]{:S(2)}) collective-permute-start(f32[256,128]{1,0:T(8,128)S(1)} %get-tuple-element.31), channel_id=1, source_target_pairs={{0,16},{2,18},{4,20},{6,22},{8,24},{10,26},{12,28},{14,30},{16,0},... | collective-permute-start | bytes 393224 | tf_op jit(solution)/shard_map/ppermute | solution.py:329
  4.9 17.0 %collective-permute-start.2 = (f32[256,128]{1,0:T(8,128)S(1)}, f32[256,128]{1,0:T(8,128)S(1)}, u32[]{:S(2)}, u32[]{:S(2)}) collective-permute-start(f32[256,128]{1,0:T(8,128)S(1)} %get-tuple-element.32), channel_id=1, source_target_pairs={{0,24},{2,26},{4,28},{6,30},{8,16},{10,18},{12,20},{14,22},{16,8},... | collective-permute-start | bytes 393224 | tf_op jit(solution)/shard_map/ppermute | solution.py:329
  7.3 22.6 %all-to-all-start = ((f32[16,32,128]{2,1,0:T(8,128)}), f32[16,32,128]{2,1,0:T(8,128)S(1)}, u32[]{:S(2)}, u32[]{:S(2)}) async-start(f32[16,32,128]{2,1,0:T(8,128)} %pack.1), calls=%async_computation | async-start | bytes 524288 | tf_op jit(solution)/shard_map/all_to_all | solution.py:373
  21.9 8.0 %copy-start.6 = (bf16[4,256,256]{2,1,0:T(8,128)(2,1)S(1)}, bf16[4,256,256]{2,1,0:T(8,128)(2,1)}, u32[]{:S(2)}) copy-start(bf16[4,256,256]{2,1,0:T(8,128)(2,1)} %constant.4.clone.matrices) | copy-start | bytes 1572868
  21.9 8.0 %copy-start.8 = (f32[17,4,128]{2,1,0:T(4,128)S(1)}, f32[17,4,128]{2,1,0:T(4,128)}, u32[]{:S(2)}) copy-start(f32[17,4,128]{2,1,0:T(4,128)} %constant.5.clone.twists) | copy-start | bytes 104452
  21.9 8.0 %copy-start.9 = (f32[128,512]{1,0:T(8,128)S(1)}, f32[128,512]{1,0:T(8,128)}, u32[]{:S(2)}) copy-start(f32[128,512]{1,0:T(8,128)} %taps.1) | copy-start | bytes 786436
  21.9 8.1 %copy-start.10 = (f32[512]{0:T(512)S(1)}, f32[512]{0:T(512)}, u32[]{:S(2)}) copy-start(f32[512]{0:T(512)} %param.14) | copy-start | bytes 6148
  21.9 5.0 %collective-permute-start.3 = (f32[256,128]{1,0:T(8,128)S(1)}, f32[256,128]{1,0:T(8,128)S(1)}, u32[]{:S(2)}, u32[]{:S(2)}) collective-permute-start(f32[256,128]{1,0:T(8,128)S(1)} %get-tuple-element.33), channel_id=1, source_target_pairs={{0,2},{2,0},{4,6},{6,4},{8,10},{10,8},{12,14},{14,12},{16,18},{18,... | collective-permute-start | bytes 393224 | tf_op jit(solution)/shard_map/ppermute | solution.py:329
  22.5 5.0 %collective-permute-start.4 = (f32[256,128]{1,0:T(8,128)S(1)}, f32[256,128]{1,0:T(8,128)S(1)}, u32[]{:S(2)}, u32[]{:S(2)}) collective-permute-start(f32[256,128]{1,0:T(8,128)S(1)} %get-tuple-element.34), channel_id=1, source_target_pairs={{0,4},{2,6},{4,0},{6,2},{8,12},{10,14},{12,8},{14,10},{16,20},{18,... | collective-permute-start | bytes 393224 | tf_op jit(solution)/shard_map/ppermute | solution.py:329
  24.1 5.9 %collective-permute-start.5 = (f32[256,128]{1,0:T(8,128)S(1)}, f32[256,128]{1,0:T(8,128)S(1)}, u32[]{:S(2)}, u32[]{:S(2)}) collective-permute-start(f32[256,128]{1,0:T(8,128)S(1)} %get-tuple-element.35), channel_id=1, source_target_pairs={{0,6},{2,4},{4,2},{6,0},{8,14},{10,12},{12,10},{14,8},{16,22},{18,... | collective-permute-start | bytes 393224 | tf_op jit(solution)/shard_map/ppermute | solution.py:329
  31.8 10.6 %collective-permute-start.6 = (f32[224,128]{1,0:T(8,128)S(1)}, f32[224,128]{1,0:T(8,128)S(1)}, u32[]{:S(2)}, u32[]{:S(2)}) collective-permute-start(f32[224,128]{1,0:T(8,128)S(1)} %get-tuple-element.38), channel_id=1, source_target_pairs={{0,8},{2,10},{4,12},{6,14},{8,0},{10,2},{12,4},{14,6},{16,24},{18,... | collective-permute-start | bytes 344072 | tf_op jit(solution)/shard_map/ppermute | solution.py:329
  31.9 10.5 %collective-permute-start.7 = (f32[224,128]{1,0:T(8,128)S(1)}, f32[224,128]{1,0:T(8,128)S(1)}, u32[]{:S(2)}, u32[]{:S(2)}) collective-permute-start(f32[224,128]{1,0:T(8,128)S(1)} %get-tuple-element.39), channel_id=1, source_target_pairs={{0,16},{2,18},{4,20},{6,22},{8,24},{10,26},{12,28},{14,30},{16,0},... | collective-permute-start | bytes 344072 | tf_op jit(solution)/shard_map/ppermute | solution.py:329
  33.9 13.0 %collective-permute-start.8 = (f32[224,128]{1,0:T(8,128)S(1)}, f32[224,128]{1,0:T(8,128)S(1)}, u32[]{:S(2)}, u32[]{:S(2)}) collective-permute-start(f32[224,128]{1,0:T(8,128)S(1)} %get-tuple-element.40), channel_id=1, source_target_pairs={{0,24},{2,26},{4,28},{6,30},{8,16},{10,18},{12,20},{14,22},{16,8},... | collective-permute-start | bytes 344072 | tf_op jit(solution)/shard_map/ppermute | solution.py:329
  36.8 19.8 %all-to-all-start.1 = ((f32[16,48,128]{2,1,0:T(8,128)}), f32[16,48,128]{2,1,0:T(8,128)S(1)}, u32[]{:S(2)}, u32[]{:S(2)}) async-start(f32[16,48,128]{2,1,0:T(8,128)} %mix.1), calls=%async_computation.1 | async-start | bytes 786432 | tf_op jit(solution)/shard_map/all_to_all | solution.py:420
  46.9 9.7 %copy-start.1 = (bf16[128,512]{1,0:T(8,128)(2,1)S(1)}, bf16[128,512]{1,0:T(8,128)(2,1)}, u32[]{:S(2)}) copy-start(bf16[128,512]{1,0:T(8,128)(2,1)} %query.1) | copy-start | bytes 393220
  46.9 9.7 %copy-start.2 = (bf16[128,512]{1,0:T(8,128)(2,1)S(1)}, bf16[128,512]{1,0:T(8,128)(2,1)}, u32[]{:S(2)}) copy-start(bf16[128,512]{1,0:T(8,128)(2,1)} %key.1) | copy-start | bytes 393220
  46.9 9.7 %copy-start.3 = (bf16[128,512]{1,0:T(8,128)(2,1)S(1)}, bf16[128,512]{1,0:T(8,128)(2,1)}, u32[]{:S(2)}) copy-start(bf16[128,512]{1,0:T(8,128)(2,1)} %value.1) | copy-start | bytes 393220
  46.9 9.8 %copy-start.5 = (bf16[128,512]{1,0:T(8,128)(2,1)S(1)}, bf16[128,512]{1,0:T(8,128)(2,1)}, u32[]{:S(2)}) copy-start(bf16[128,512]{1,0:T(8,128)(2,1)} %grad.1) | copy-start | bytes 393220
  47.0 5.9 %collective-permute-start.9 = (f32[320,128]{1,0:T(8,128)S(1)}, f32[320,128]{1,0:T(8,128)S(1)}, u32[]{:S(2)}, u32[]{:S(2)}) collective-permute-start(f32[320,128]{1,0:T(8,128)S(1)} %get-tuple-element.41), channel_id=1, source_target_pairs={{0,2},{2,0},{4,6},{6,4},{8,10},{10,8},{12,14},{14,12},{16,18},{18,... | collective-permute-start | bytes 491528 | tf_op jit(solution)/shard_map/ppermute | solution.py:329
  49.6 7.1 %collective-permute-start.10 = (f32[320,128]{1,0:T(8,128)S(1)}, f32[320,128]{1,0:T(8,128)S(1)}, u32[]{:S(2)}, u32[]{:S(2)}) collective-permute-start(f32[320,128]{1,0:T(8,128)S(1)} %get-tuple-element.42), channel_id=1, source_target_pairs={{0,4},{2,6},{4,0},{6,2},{8,12},{10,14},{12,8},{14,10},{16,20},{18,... | collective-permute-start | bytes 491528 | tf_op jit(solution)/shard_map/ppermute | solution.py:329
  50.1 6.6 %collective-permute-start.11 = (f32[320,128]{1,0:T(8,128)S(1)}, f32[320,128]{1,0:T(8,128)S(1)}, u32[]{:S(2)}, u32[]{:S(2)}) collective-permute-start(f32[320,128]{1,0:T(8,128)S(1)} %get-tuple-element.43), channel_id=1, source_target_pairs={{0,6},{2,4},{4,2},{6,0},{8,14},{10,12},{12,10},{14,8},{16,22},{18,... | collective-permute-start | bytes 491528 | tf_op jit(solution)/shard_map/ppermute | solution.py:329

commit v13 on v12

--- a/solution.py
+++ b/solution.py
@@ -140,26 +140,26 @@
     return dot(values_high, high) + (dot(values_low, high) + dot(values_high, low))
 
 
-def pack_kernel(field, out):
-    blocks, share, rows = out.shape
-    out[...] = field[...].T.reshape(blocks, share, rows)
+def pack_kernel(product, mix_grad, out):
+    blocks, _, share, rows = out.shape
+    for a, field in enumerate((product, mix_grad)):
+        out[:, a] = field[...].T.reshape(blocks, share, rows)
 
 
 def chunk(sizes, count, field, at):
     return pl.ds(count * sum(sizes[:field]) + at * sizes[field], sizes[field])
 
 
-def split_kernel(*refs, near_count):
-    fields, outs, turned = refs[:2], refs[2:-1], refs[-1]
-    share = outs[0].shape[0] // (2 * near_count)
+def split_kernel(field, *rest, near_count):
+    outs, turned = rest[:-1], rest[-1]
+    share = outs[0].shape[0] // near_count
+    turned[...] = field[...].T
     me = lax.axis_index("ctx") if near_count > 1 else 0
-    for k, field in enumerate(fields):
-        turned[...] = field[...].T
-        for far, out in enumerate(outs):
-            for near in range(near_count):
-                start = (me ^ (far * near_count + near)) * share
-                start = start if near_count == 1 else pl.multiple_of(start, share)
-                out[chunk((share, share), near_count, k, near), :] = turned[pl.ds(start, share), :]
+    for far, out in enumerate(outs):
+        for near in range(near_count):
+            start = (me ^ (far * near_count + near)) * share
+            start = start if near_count == 1 else pl.multiple_of(start, share)
+            out[chunk((share,), near_count, 0, near), :] = turned[pl.ds(start, share), :]
 
 
 def gather_blocks(outs, sizes, far_parts, near_parts, me):
@@ -182,23 +182,25 @@
                 outs[len(sizes)][source] = rows
 
 
-def spectra_kernel(taps, skip, matrices, twists, mix_grads, *rest, near_count, early, grad_scale):
-    blocks, channels, rows = mix_grads.shape
+def spectra_kernel(taps, skip, matrices, twists, gates, *rest, near_count, early, grad_scale):
+    blocks, _, channels, rows = gates.shape
     far_count = blocks // near_count
     far_parts, rest = rest[:far_count], rest[far_count:]
     near_parts, rest = rest[: near_count - 1], rest[near_count - 1 :]
-    products, *outs, spectra, results, direct, lags, back, filters, gates = rest
+    products, *outs, spectra, results, direct, lags, back, filters = rest
     me = lax.axis_index("ctx") if near_count > 1 else 0
-    gather_blocks((filters, gates), (channels, channels), far_parts, near_parts, me)
+    gather_blocks((filters,), (channels,), far_parts, near_parts, me)
     row = lax.broadcasted_iota(jnp.int32, taps.shape, 0)
     direct[...] = (taps[...] + jnp.where(row == 0, skip[...], 0.0)).T
     own = 0 if direct.shape[0] == channels else pl.multiple_of(lax.axis_index("ctx") * channels, channels)
     for a in range(3):
         for low in range(0, channels, 8):
             part = pl.ds(low, 8)
-            values = [(gates, filters, mix_grads)[a][j, part, :] for j in range(blocks)]
             if a == 1:
+                values = [filters[j, part, :] for j in range(blocks)]
                 values[0] = values[0] + direct[pl.ds(own + low, 8), :]
+            else:
+                values = [gates[j, a // 2, part, :] for j in range(blocks)]
             bins = padded_bins(values)
             for p in range(blocks + 1):
                 real, imag = bins[p]
@@ -362,21 +364,22 @@
     split_parts = call(
         functools.partial(split_kernel, near_count=near_count),
         "split",
-        (shape((2 * near_count * share, rows)),) * far_count,
-        (pltpu.VMEM,) * 2,
+        (shape((near_count * share, rows)),) * far_count,
+        (pltpu.VMEM,),
         scratch=(pltpu.VMEM((channels, rows), f32),),
-        size=16 * rows * channels,
-    )(implicit_filter, product)
-    packed = call(pack_kernel, "pack", shape((blocks, share, rows)), (pltpu.VMEM,), size=8 * rows * channels)(mix_grad)
+        size=8 * rows * channels,
+    )(implicit_filter)
+    packed = call(
+        pack_kernel, "pack", shape((blocks, 2, share, rows)), (pltpu.VMEM,) * 2, size=16 * rows * channels
+    )(product, mix_grad)
     if near_count > 1:
-        far_parts, near_parts = send_parts(split_parts, "ctx", near_count, (share, share))
-        mix_grads = lax.all_to_all(packed, "ctx", 0, 0, tiled=True)
+        far_parts, near_parts = send_parts(split_parts, "ctx", near_count, (share,))
+        gates = lax.all_to_all(packed, "ctx", 0, 0, tiled=True)
     else:
-        together = jnp.concatenate([packed, jnp.stack(split_parts)], axis=1)
-        together = lax.all_to_all(together, "ctx", 0, 0, tiled=True).reshape(blocks, 3, share, rows)
+        together = jnp.concatenate([packed, jnp.stack(split_parts)[:, None]], axis=1)
+        together = lax.all_to_all(together, "ctx", 0, 0, tiled=True)
         together = jnp.pad(together, ((0, 0), (0, 0), (0, padded - share), (0, 0)))
-        mix_grads, near_parts = together[:, 0], []
-        far_parts = list(together[:, 1:].reshape(blocks, 2 * padded, rows))
+        gates, far_parts, near_parts = together[:, :2], list(together[:, 2]), []
         own = lax.axis_index("ctx") * share
         taps, skip = [
             jnp.pad(lax.dynamic_slice_in_dim(each, own, share, 1), ((0, 0), (0, padded - share)))
@@ -399,11 +402,10 @@
             block,
             pltpu.VMEM((blocks, max(early, 8), rows), f32),
             block,
-            block,
         ),
         flops=27 * height * (2 * rows) ** 2,
         size=24 * blocks * padded * rows,
-    )(taps, skip, matrices, twists, mix_grads, *far_parts, *near_parts)
+    )(taps, skip, matrices, twists, gates, *far_parts, *near_parts)
     if near_count > 1:
         sizes = (share, early) if early else (share,)
         far_parts, near_parts = send_parts(split_parts, "ctx", near_count, sizes, share)

time: 58.4 us -> 57.9 us (level)
  the two profiles are of different devices: /device:TPU:18 before, /device:TPU:0 now
where the time goes in v13:
time: 57.9 us; the launch traced here: 56.8 us
  starting transfers between devices  28.2 us (49%)
  waiting for transfers between devices  19.7 us (34%)
  Pallas kernels  5.89 us (10%)
  other arithmetic  1.16 us (2%)
  local copies, waits for them, and re-layouts  0.99 us (2%)
  between operations  0.82 us (1%)
    ppermute x12, starting transfers between devices, exchange(): lax.ppermute(value, axis, [(i, i ^ distance) for i in range(lax.axis_size...  17.2 us
    ppermute x12, waiting for transfers between devices, exchange(): lax.ppermute(value, axis, [(i, i ^ distance) for i in range(lax.axis_size...  14.7 us
    all_to_all x1, starting transfers between devices, body(): gates = lax.all_to_all(packed, 'ctx', 0, 0, tiled=True)  7.09 us
    all_to_all x1, waiting for transfers between devices, body(): gates = lax.all_to_all(packed, 'ctx', 0, 0, tiled=True)  4.99 us
    all_to_all x1, starting transfers between devices, body(): parts = lax.all_to_all(results, 'ctx', 0, 0, tiled=True)  3.85 us
    pallas_call x1, Pallas kernels, body(): call(functools.partial(spectra_kernel, near_count=near_count, early=early...  1.81 us
    pallas_call x1, Pallas kernels, body(): call(functools.partial(mix_kernel, channels=padded, early=early), 'mix',...  1.45 us
    pallas_call x1, Pallas kernels, body(): call(functools.partial(unpack_kernel, far_count=far_count, near_count=nea...  1.4 us
  transfers between devices with their start and end apart: 14, of which 8 were waited for; matrix products, arithmetic and copies ran while one was open for 2% of the time, Pallas kernels for 4%

profile of v13, /device:TPU:0, one launch (start us, length us, event | category | flops | bytes accessed | tf_op | source)
XLA Modules:
  0.0 56.8 jit_solution(1303094710903180666)
XLA Ops:
  0.6 0.0 copy-start.5
  0.6 0.9 %copy-done.5 = f32[128,512]{1,0:T(8,128)S(1)} copy-done((f32[128,512]{1,0:T(8,128)S(1)}, f32[128,512]{1,0:T(8,128)}, u32[]{:S(2)}) %copy-start.5) | copy-done | bytes 262168
  1.6 0.1 split.1
  1.7 3.1 %collective-permute-start = (f32[128,128]{1,0:T(8,128)S(1)}, f32[128,128]{1,0:T(8,128)S(1)}, u32[]{:S(2)}, u32[]{:S(2)}) collective-permute-start(f32[128,128]{1,0:T(8,128)S(1)} %get-tuple-element.30), channel_id=1, source_target_pairs={{0,8},{2,10},{4,12},{6,14},{8,0},{10,2},{12,4},{14,6},{16,24},{18,... | collective-permute-start | bytes 196616 | tf_op jit(solution)/shard_map/ppermute | solution.py:331
  4.8 2.6 %collective-permute-start.1 = (f32[128,128]{1,0:T(8,128)S(1)}, f32[128,128]{1,0:T(8,128)S(1)}, u32[]{:S(2)}, u32[]{:S(2)}) collective-permute-start(f32[128,128]{1,0:T(8,128)S(1)} %get-tuple-element.31), channel_id=1, source_target_pairs={{0,16},{2,18},{4,20},{6,22},{8,24},{10,26},{12,28},{14,30},{16,0},... | collective-permute-start | bytes 196616 | tf_op jit(solution)/shard_map/ppermute | solution.py:331
  7.4 0.0 collective-permute-start.2
  7.4 1.2 %convert_multiply_fusion = (f32[128,512]{1,0:T(8,128)S(1)}, f32[128,512]{1,0:T(8,128)S(1)}) fusion(bf16[128,512]{1,0:T(8,128)(2,1)} %query.1, bf16[128,512]{1,0:T(8,128)(2,1)} %grad.1, bf16[128,512]{1,0:T(8,128)(2,1)} %value.1, bf16[128,512]{1,0:T(8,128)(2,1)} %key.1), kind=kLoop, calls=%fused_computation | loop fusion | flops 393216 | bytes 1048576 | tf_op jit(solution)/shard_map/mul | solution.py:363
  8.6 1.0 %pack.1 = f32[16,2,32,128]{3,2,1,0:T(8,128)} custom-call(f32[128,512]{1,0:T(8,128)S(1)} %get-tuple-element.52.product, f32[128,512]{1,0:T(8,128)S(1)} %get-tuple-element.51.mix_grad), custom_call_target="tpu_custom_call" | custom-call | bytes 1048576 | tf_op jit(solution)/shard_map/pack/pallas_call | solution.py:372
  9.6 7.1 %all-to-all-start = ((f32[16,2,32,128]{3,2,1,0:T(8,128)}), f32[16,2,32,128]{3,2,1,0:T(8,128)S(1)}, u32[]{:S(2)}, u32[]{:S(2)}) async-start(f32[16,2,32,128]{3,2,1,0:T(8,128)} %pack.1), calls=%async_computation | async-start | bytes 1048576 | tf_op jit(solution)/shard_map/all_to_all | solution.py:377
  16.7 0.0 collective-permute-done.refs_3_.rest_1_
  16.7 0.0 collective-permute-done.1.refs_2_.rest_2_
  16.7 0.0 collective-permute-done.2.refs_1_.rest_3_
  16.7 0.0 copy-start.4
  16.8 0.0 copy-start.6
  16.8 0.0 copy-start.7
  16.8 0.0 copy-start.8
  16.8 2.0 %collective-permute-start.3 = (f32[128,128]{1,0:T(8,128)S(1)}, f32[128,128]{1,0:T(8,128)S(1)}, u32[]{:S(2)}, u32[]{:S(2)}) collective-permute-start(f32[128,128]{1,0:T(8,128)S(1)} %get-tuple-element.33), channel_id=1, source_target_pairs={{0,2},{2,0},{4,6},{6,4},{8,10},{10,8},{12,14},{14,12},{16,18},{18,... | collective-permute-start | bytes 196616 | tf_op jit(solution)/shard_map/ppermute | solution.py:331
  18.8 1.5 %collective-permute-start.4 = (f32[128,128]{1,0:T(8,128)S(1)}, f32[128,128]{1,0:T(8,128)S(1)}, u32[]{:S(2)}, u32[]{:S(2)}) collective-permute-start(f32[128,128]{1,0:T(8,128)S(1)} %get-tuple-element.34), channel_id=1, source_target_pairs={{0,4},{2,6},{4,0},{6,2},{8,12},{10,14},{12,8},{14,10},{16,20},{18,... | collective-permute-start | bytes 196616 | tf_op jit(solution)/shard_map/ppermute | solution.py:331
  20.3 0.1 collective-permute-start.5
  20.4 2.7 %collective-permute-done.3.rest_4_ = f32[128,128]{1,0:T(8,128)S(1)} collective-permute-done((f32[128,128]{1,0:T(8,128)S(1)}, f32[128,128]{1,0:T(8,128)S(1)}, u32[]{:S(2)}, u32[]{:S(2)}) %collective-permute-start.3) | collective-permute-done | bytes 65568 | tf_op jit(solution)/shard_map/ppermute | solution.py:331
  23.1 1.5 %collective-permute-done.4.rest_5_ = f32[128,128]{1,0:T(8,128)S(1)} collective-permute-done((f32[128,128]{1,0:T(8,128)S(1)}, f32[128,128]{1,0:T(8,128)S(1)}, u32[]{:S(2)}, u32[]{:S(2)}) %collective-permute-start.4) | collective-permute-done | bytes 65568 | tf_op jit(solution)/shard_map/ppermute | solution.py:331
  24.6 1.5 %collective-permute-done.5.rest_6_ = f32[128,128]{1,0:T(8,128)S(1)} collective-permute-done((f32[128,128]{1,0:T(8,128)S(1)}, f32[128,128]{1,0:T(8,128)S(1)}, u32[]{:S(2)}, u32[]{:S(2)}) %collective-permute-start.5) | collective-permute-done | bytes 65568 | tf_op jit(solution)/shard_map/ppermute | solution.py:331
  26.1 5.0 %all-to-all-done.gates = f32[16,2,32,128]{3,2,1,0:T(8,128)S(1)} async-done(((f32[16,2,32,128]{3,2,1,0:T(8,128)}), f32[16,2,32,128]{3,2,1,0:T(8,128)S(1)}, u32[]{:S(2)}, u32[]{:S(2)}) %all-to-all-start) | async-done | bytes 524320 | tf_op jit(solution)/shard_map/all_to_all | solution.py:377
  31.1 0.0 copy-done.4
  31.1 0.0 copy-done.6
  31.1 0.0 copy-done.7
  31.1 0.0 copy-done.8
  31.1 1.8 %spectra.1 = (f32[2,544,256]{2,1,0:T(8,128)S(1)}, f32[224,128]{1,0:T(8,128)S(1)}, f32[224,128]{1,0:T(8,128)S(1)}, f32[224,128]{1,0:T(8,128)S(1)}, f32[224,128]{1,0:T(8,128)S(1)}) custom-call(f32[128,512]{1,0:T(8,128)S(1)} %copy-done.7, f32[1,512]{1,0:T(1,128)S(1)} %bitcast.2, bf16[4,256,256]{2,1,0:T(8,128)(2,1)S(1)} %copy-done.4, ...), custom_call_target="tpu_custom_call" | custom-call | flops 962592768 | bytes 1572864 | tf_op jit(solution)/shard_map/spectra/pallas_call | solution.py:393
  32.9 1.3 %collective-permute-start.6 = (f32[224,128]{1,0:T(8,128)S(1)}, f32[224,128]{1,0:T(8,128)S(1)}, u32[]{:S(2)}, u32[]{:S(2)}) collective-permute-start(f32[224,128]{1,0:T(8,128)S(1)} %get-tuple-element.38), channel_id=1, source_target_pairs={{0,8},{2,10},{4,12},{6,14},{8,0},{10,2},{12,4},{14,6},{16,24},{18,... | collective-permute-start | bytes 344072 | tf_op jit(solution)/shard_map/ppermute | solution.py:331
  34.2 1.1 %collective-permute-start.7 = (f32[224,128]{1,0:T(8,128)S(1)}, f32[224,128]{1,0:T(8,128)S(1)}, u32[]{:S(2)}, u32[]{:S(2)}) collective-permute-start(f32[224,128]{1,0:T(8,128)S(1)} %get-tuple-element.39), channel_id=1, source_target_pairs={{0,16},{2,18},{4,20},{6,22},{8,24},{10,26},{12,28},{14,30},{16,0},... | collective-permute-start | bytes 344072 | tf_op jit(solution)/shard_map/ppermute | solution.py:331
  35.3 2.0 %collective-permute-start.8 = (f32[224,128]{1,0:T(8,128)S(1)}, f32[224,128]{1,0:T(8,128)S(1)}, u32[]{:S(2)}, u32[]{:S(2)}) collective-permute-start(f32[224,128]{1,0:T(8,128)S(1)} %get-tuple-element.40), channel_id=1, source_target_pairs={{0,24},{2,26},{4,28},{6,30},{8,16},{10,18},{12,20},{14,22},{16,8},... | collective-permute-start | bytes 344072 | tf_op jit(solution)/shard_map/ppermute | solution.py:331
  37.4 1.5 %mix.1 = f32[16,48,128]{2,1,0:T(8,128)} custom-call(bf16[4,256,256]{2,1,0:T(8,128)(2,1)S(1)} %copy-done.4, f32[17,4,128]{2,1,0:T(4,128)S(1)} %copy-done.6, f32[2,544,256]{2,1,0:T(8,128)S(1)} %get-tuple-element.36.products), custom_call_target="tpu_custom_call" | custom-call | flops 320864256 | bytes 1572864 | tf_op jit(solution)/shard_map/mix/pallas_call | solution.py:412
  38.8 3.9 %all-to-all-start.1 = ((f32[16,48,128]{2,1,0:T(8,128)}), f32[16,48,128]{2,1,0:T(8,128)S(1)}, u32[]{:S(2)}, u32[]{:S(2)}) async-start(f32[16,48,128]{2,1,0:T(8,128)} %mix.1), calls=%async_computation.1 | async-start | bytes 786432 | tf_op jit(solution)/shard_map/all_to_all | solution.py:422
  42.7 0.0 collective-permute-done.6.refs_3_.rest_1_
  42.7 1.3 %collective-permute-done.7.refs_2_.rest_2_ = f32[224,128]{1,0:T(8,128)S(1)} collective-permute-done((f32[224,128]{1,0:T(8,128)S(1)}, f32[224,128]{1,0:T(8,128)S(1)}, u32[]{:S(2)}, u32[]{:S(2)}) %collective-permute-start.7) | collective-permute-done | bytes 114720 | tf_op jit(solution)/shard_map/ppermute | solution.py:331
  44.0 0.0 collective-permute-done.8.refs_1_.rest_3_
  44.0 0.0 copy-start
  44.0 0.0 copy-start.1
  44.0 0.0 copy-start.2
  44.0 0.0 copy-start.3
  44.1 0.8 %collective-permute-start.9 = (f32[320,128]{1,0:T(8,128)S(1)}, f32[320,128]{1,0:T(8,128)S(1)}, u32[]{:S(2)}, u32[]{:S(2)}) collective-permute-start(f32[320,128]{1,0:T(8,128)S(1)} %get-tuple-element.41), channel_id=1, source_target_pairs={{0,2},{2,0},{4,6},{6,4},{8,10},{10,8},{12,14},{14,12},{16,18},{18,... | collective-permute-start | bytes 491528 | tf_op jit(solution)/shard_map/ppermute | solution.py:331
  44.9 1.4 %collective-permute-start.10 = (f32[320,128]{1,0:T(8,128)S(1)}, f32[320,128]{1,0:T(8,128)S(1)}, u32[]{:S(2)}, u32[]{:S(2)}) collective-permute-start(f32[320,128]{1,0:T(8,128)S(1)} %get-tuple-element.42), channel_id=1, source_target_pairs={{0,4},{2,6},{4,0},{6,2},{8,12},{10,14},{12,8},{14,10},{16,20},{18,... | collective-permute-start | bytes 491528 | tf_op jit(solution)/shard_map/ppermute | solution.py:331
  46.3 1.3 %collective-permute-start.11 = (f32[320,128]{1,0:T(8,128)S(1)}, f32[320,128]{1,0:T(8,128)S(1)}, u32[]{:S(2)}, u32[]{:S(2)}) collective-permute-start(f32[320,128]{1,0:T(8,128)S(1)} %get-tuple-element.43), channel_id=1, source_target_pairs={{0,6},{2,4},{4,2},{6,0},{8,14},{10,12},{12,10},{14,8},{16,22},{18,... | collective-permute-start | bytes 491528 | tf_op jit(solution)/shard_map/ppermute | solution.py:331
  47.6 4.5 %collective-permute-done.9.rest_4_ = f32[320,128]{1,0:T(8,128)S(1)} collective-permute-done((f32[320,128]{1,0:T(8,128)S(1)}, f32[320,128]{1,0:T(8,128)S(1)}, u32[]{:S(2)}, u32[]{:S(2)}) %collective-permute-start.9) | collective-permute-done | bytes 163872 | tf_op jit(solution)/shard_map/ppermute | solution.py:331
  52.1 2.0 %collective-permute-done.10.rest_5_ = f32[320,128]{1,0:T(8,128)S(1)} collective-permute-done((f32[320,128]{1,0:T(8,128)S(1)}, f32[320,128]{1,0:T(8,128)S(1)}, u32[]{:S(2)}, u32[]{:S(2)}) %collective-permute-start.10) | collective-permute-done | bytes 163872 | tf_op jit(solution)/shard_map/ppermute | solution.py:331
  54.1 1.3 %collective-permute-done.11.rest_6_ = f32[320,128]{1,0:T(8,128)S(1)} collective-permute-done((f32[320,128]{1,0:T(8,128)S(1)}, f32[320,128]{1,0:T(8,128)S(1)}, u32[]{:S(2)}, u32[]{:S(2)}) %collective-permute-start.11) | collective-permute-done | bytes 163872 | tf_op jit(solution)/shard_map/ppermute | solution.py:331
  55.3 0.0 all-to-all-done.1.parts
  55.3 0.0 copy-done
  55.3 0.0 copy-done.1
  55.3 0.0 copy-done.2
  55.4 0.0 copy-done.3
  55.4 1.4 %unpack.1 = (f32[128,512]{1,0:T(8,128)}, f32[128,512]{1,0:T(8,128)}, f32[128,512]{1,0:T(8,128)}, f32[128,512]{1,0:T(8,128)}, f32[128,512]{1,0:T(8,128)}, /*index=5*/f32[128,512]{1,0:T(8,128)}, f32[1,512]{1,0:T(1,128)}) custom-call(bf16[128,512]{1,0:T(8,128)(2,1)S(1)} %copy-done, bf16[128,512]{1,0:T(8,128)(2,1)S(1)} %copy-done.1, ...), custom_call_target="tpu_custom_call" | custom-call | bytes 3145728 | tf_op jit(solution)/shard_map/unpack/pallas_call | solution.py:429
  (2 shorter events, 0.1 us)
Async XLA Ops:
  0.6 1.0 %copy-start.5 = (f32[128,512]{1,0:T(8,128)S(1)}, f32[128,512]{1,0:T(8,128)}, u32[]{:S(2)}) copy-start(f32[128,512]{1,0:T(8,128)} %field.1) | copy-start | bytes 786436
  1.7 15.0 %collective-permute-start = (f32[128,128]{1,0:T(8,128)S(1)}, f32[128,128]{1,0:T(8,128)S(1)}, u32[]{:S(2)}, u32[]{:S(2)}) collective-permute-start(f32[128,128]{1,0:T(8,128)S(1)} %get-tuple-element.30), channel_id=1, source_target_pairs={{0,8},{2,10},{4,12},{6,14},{8,0},{10,2},{12,4},{14,6},{16,24},{18,... | collective-permute-start | bytes 196616 | tf_op jit(solution)/shard_map/ppermute | solution.py:331
  4.8 11.9 %collective-permute-start.1 = (f32[128,128]{1,0:T(8,128)S(1)}, f32[128,128]{1,0:T(8,128)S(1)}, u32[]{:S(2)}, u32[]{:S(2)}) collective-permute-start(f32[128,128]{1,0:T(8,128)S(1)} %get-tuple-element.31), channel_id=1, source_target_pairs={{0,16},{2,18},{4,20},{6,22},{8,24},{10,26},{12,28},{14,30},{16,0},... | collective-permute-start | bytes 196616 | tf_op jit(solution)/shard_map/ppermute | solution.py:331
  7.4 9.3 %collective-permute-start.2 = (f32[128,128]{1,0:T(8,128)S(1)}, f32[128,128]{1,0:T(8,128)S(1)}, u32[]{:S(2)}, u32[]{:S(2)}) collective-permute-start(f32[128,128]{1,0:T(8,128)S(1)} %get-tuple-element.32), channel_id=1, source_target_pairs={{0,24},{2,26},{4,28},{6,30},{8,16},{10,18},{12,20},{14,22},{16,8},... | collective-permute-start | bytes 196616 | tf_op jit(solution)/shard_map/ppermute | solution.py:331
  9.6 21.4 %all-to-all-start = ((f32[16,2,32,128]{3,2,1,0:T(8,128)}), f32[16,2,32,128]{3,2,1,0:T(8,128)S(1)}, u32[]{:S(2)}, u32[]{:S(2)}) async-start(f32[16,2,32,128]{3,2,1,0:T(8,128)} %pack.1), calls=%async_computation | async-start | bytes 1048576 | tf_op jit(solution)/shard_map/all_to_all | solution.py:377
  16.7 14.3 %copy-start.4 = (bf16[4,256,256]{2,1,0:T(8,128)(2,1)S(1)}, bf16[4,256,256]{2,1,0:T(8,128)(2,1)}, u32[]{:S(2)}) copy-start(bf16[4,256,256]{2,1,0:T(8,128)(2,1)} %constant.4.clone.matrices) | copy-start | bytes 1572868
  16.8 14.3 %copy-start.6 = (f32[17,4,128]{2,1,0:T(4,128)S(1)}, f32[17,4,128]{2,1,0:T(4,128)}, u32[]{:S(2)}) copy-start(f32[17,4,128]{2,1,0:T(4,128)} %constant.5.clone.twists) | copy-start | bytes 104452
  16.8 14.3 %copy-start.7 = (f32[128,512]{1,0:T(8,128)S(1)}, f32[128,512]{1,0:T(8,128)}, u32[]{:S(2)}) copy-start(f32[128,512]{1,0:T(8,128)} %taps.1) | copy-start | bytes 786436
  16.8 14.3 %copy-start.8 = (f32[512]{0:T(512)S(1)}, f32[512]{0:T(512)}, u32[]{:S(2)}) copy-start(f32[512]{0:T(512)} %param.14) | copy-start | bytes 6148
  16.8 6.2 %collective-permute-start.3 = (f32[128,128]{1,0:T(8,128)S(1)}, f32[128,128]{1,0:T(8,128)S(1)}, u32[]{:S(2)}, u32[]{:S(2)}) collective-permute-start(f32[128,128]{1,0:T(8,128)S(1)} %get-tuple-element.33), channel_id=1, source_target_pairs={{0,2},{2,0},{4,6},{6,4},{8,10},{10,8},{12,14},{14,12},{16,18},{18,... | collective-permute-start | bytes 196616 | tf_op jit(solution)/shard_map/ppermute | solution.py:331
  18.8 5.8 %collective-permute-start.4 = (f32[128,128]{1,0:T(8,128)S(1)}, f32[128,128]{1,0:T(8,128)S(1)}, u32[]{:S(2)}, u32[]{:S(2)}) collective-permute-start(f32[128,128]{1,0:T(8,128)S(1)} %get-tuple-element.34), channel_id=1, source_target_pairs={{0,4},{2,6},{4,0},{6,2},{8,12},{10,14},{12,8},{14,10},{16,20},{18,... | collective-permute-start | bytes 196616 | tf_op jit(solution)/shard_map/ppermute | solution.py:331
  20.3 5.8 %collective-permute-start.5 = (f32[128,128]{1,0:T(8,128)S(1)}, f32[128,128]{1,0:T(8,128)S(1)}, u32[]{:S(2)}, u32[]{:S(2)}) collective-permute-start(f32[128,128]{1,0:T(8,128)S(1)} %get-tuple-element.35), channel_id=1, source_target_pairs={{0,6},{2,4},{4,2},{6,0},{8,14},{10,12},{12,10},{14,8},{16,22},{18,... | collective-permute-start | bytes 196616 | tf_op jit(solution)/shard_map/ppermute | solution.py:331
  32.9 9.8 %collective-permute-start.6 = (f32[224,128]{1,0:T(8,128)S(1)}, f32[224,128]{1,0:T(8,128)S(1)}, u32[]{:S(2)}, u32[]{:S(2)}) collective-permute-start(f32[224,128]{1,0:T(8,128)S(1)} %get-tuple-element.38), channel_id=1, source_target_pairs={{0,8},{2,10},{4,12},{6,14},{8,0},{10,2},{12,4},{14,6},{16,24},{18,... | collective-permute-start | bytes 344072 | tf_op jit(solution)/shard_map/ppermute | solution.py:331
  34.2 9.8 %collective-permute-start.7 = (f32[224,128]{1,0:T(8,128)S(1)}, f32[224,128]{1,0:T(8,128)S(1)}, u32[]{:S(2)}, u32[]{:S(2)}) collective-permute-start(f32[224,128]{1,0:T(8,128)S(1)} %get-tuple-element.39), channel_id=1, source_target_pairs={{0,16},{2,18},{4,20},{6,22},{8,24},{10,26},{12,28},{14,30},{16,0},... | collective-permute-start | bytes 344072 | tf_op jit(solution)/shard_map/ppermute | solution.py:331
  35.3 8.7 %collective-permute-start.8 = (f32[224,128]{1,0:T(8,128)S(1)}, f32[224,128]{1,0:T(8,128)S(1)}, u32[]{:S(2)}, u32[]{:S(2)}) collective-permute-start(f32[224,128]{1,0:T(8,128)S(1)} %get-tuple-element.40), channel_id=1, source_target_pairs={{0,24},{2,26},{4,28},{6,30},{8,16},{10,18},{12,20},{14,22},{16,8},... | collective-permute-start | bytes 344072 | tf_op jit(solution)/shard_map/ppermute | solution.py:331
  38.8 16.5 %all-to-all-start.1 = ((f32[16,48,128]{2,1,0:T(8,128)}), f32[16,48,128]{2,1,0:T(8,128)S(1)}, u32[]{:S(2)}, u32[]{:S(2)}) async-start(f32[16,48,128]{2,1,0:T(8,128)} %mix.1), calls=%async_computation.1 | async-start | bytes 786432 | tf_op jit(solution)/shard_map/all_to_all | solution.py:422
  44.0 11.3 %copy-start = (bf16[128,512]{1,0:T(8,128)(2,1)S(1)}, bf16[128,512]{1,0:T(8,128)(2,1)}, u32[]{:S(2)}) copy-start(bf16[128,512]{1,0:T(8,128)(2,1)} %query.1) | copy-start | bytes 393220
  44.0 11.3 %copy-start.1 = (bf16[128,512]{1,0:T(8,128)(2,1)S(1)}, bf16[128,512]{1,0:T(8,128)(2,1)}, u32[]{:S(2)}) copy-start(bf16[128,512]{1,0:T(8,128)(2,1)} %key.1) | copy-start | bytes 393220
  44.0 11.3 %copy-start.2 = (bf16[128,512]{1,0:T(8,128)(2,1)S(1)}, bf16[128,512]{1,0:T(8,128)(2,1)}, u32[]{:S(2)}) copy-start(bf16[128,512]{1,0:T(8,128)(2,1)} %value.1) | copy-start | bytes 393220
  44.0 11.3 %copy-start.3 = (bf16[128,512]{1,0:T(8,128)(2,1)S(1)}, bf16[128,512]{1,0:T(8,128)(2,1)}, u32[]{:S(2)}) copy-start(bf16[128,512]{1,0:T(8,128)(2,1)} %grad.1) | copy-start | bytes 393220
  44.1 8.0 %collective-permute-start.9 = (f32[320,128]{1,0:T(8,128)S(1)}, f32[320,128]{1,0:T(8,128)S(1)}, u32[]{:S(2)}, u32[]{:S(2)}) collective-permute-start(f32[320,128]{1,0:T(8,128)S(1)} %get-tuple-element.41), channel_id=1, source_target_pairs={{0,2},{2,0},{4,6},{6,4},{8,10},{10,8},{12,14},{14,12},{16,18},{18,... | collective-permute-start | bytes 491528 | tf_op jit(solution)/shard_map/ppermute | solution.py:331
  44.9 9.2 %collective-permute-start.10 = (f32[320,128]{1,0:T(8,128)S(1)}, f32[320,128]{1,0:T(8,128)S(1)}, u32[]{:S(2)}, u32[]{:S(2)}) collective-permute-start(f32[320,128]{1,0:T(8,128)S(1)} %get-tuple-element.42), channel_id=1, source_target_pairs={{0,4},{2,6},{4,0},{6,2},{8,12},{10,14},{12,8},{14,10},{16,20},{18,... | collective-permute-start | bytes 491528 | tf_op jit(solution)/shard_map/ppermute | solution.py:331
  46.3 9.0 %collective-permute-start.11 = (f32[320,128]{1,0:T(8,128)S(1)}, f32[320,128]{1,0:T(8,128)S(1)}, u32[]{:S(2)}, u32[]{:S(2)}) collective-permute-start(f32[320,128]{1,0:T(8,128)S(1)} %get-tuple-element.43), channel_id=1, source_target_pairs={{0,6},{2,4},{4,2},{6,0},{8,14},{10,12},{12,10},{14,8},{16,22},{18,... | collective-permute-start | bytes 491528 | tf_op jit(solution)/shard_map/ppermute | solution.py:331

commit v14 on v13

--- a/solution.py
+++ b/solution.py
@@ -146,6 +146,10 @@
         out[:, a] = field[...].T.reshape(blocks, share, rows)
 
 
+def farthest_first(far_count):
+    return [0, *range(far_count - 1, 0, -1)]
+
+
 def chunk(sizes, count, field, at):
     return pl.ds(count * sum(sizes[:field]) + at * sizes[field], sizes[field])
 
@@ -155,7 +159,7 @@
     share = outs[0].shape[0] // near_count
     turned[...] = field[...].T
     me = lax.axis_index("ctx") if near_count > 1 else 0
-    for far, out in enumerate(outs):
+    for far, out in zip(farthest_first(len(outs)), outs):
         for near in range(near_count):
             start = (me ^ (far * near_count + near)) * share
             start = start if near_count == 1 else pl.multiple_of(start, share)
@@ -164,7 +168,7 @@
 
 def gather_blocks(outs, sizes, far_parts, near_parts, me):
     far_count, near_count = len(far_parts), len(near_parts) + 1
-    for far, part in enumerate(far_parts):
+    for far, part in zip(farthest_first(far_count), far_parts):
         for near in range(near_count):
             source = me ^ (far * near_count + near)
             for k, size in enumerate(sizes):
@@ -229,7 +233,7 @@
         for j, value in enumerate(values):
             back[j, pl.ds(low, 8), :] = value
     sizes = (channels, early) if early else (channels,)
-    for far, out in enumerate(outs):
+    for far, out in zip(farthest_first(far_count), outs):
         for near in range(near_count):
             target = me ^ (far * near_count + near)
             for k, size in enumerate(sizes):
@@ -264,7 +268,7 @@
 
 
 def relay_kernel(*refs, far_count, sizes, extra):
-    parts = (refs[0], *refs[1:far_count][::-1])
+    parts = refs[:far_count]
     outs = refs[far_count:]
     near_count = len(outs) + 1
     for near, out in enumerate(outs, 1):
@@ -332,9 +336,10 @@
 
 
 def send_parts(parts, axis, near_count, sizes, extra=0):
-    far_parts, far_count = list(parts), len(parts)
-    for far in range(far_count - 1, 0, -1):
-        far_parts[far] = exchange(parts[far], axis, far * near_count)
+    far_count = len(parts)
+    far_parts = [parts[0]] * far_count
+    for far, part in zip(farthest_first(far_count)[1:], parts[1:]):
+        far_parts[far] = exchange(part, axis, far * near_count)
     payload = jax.ShapeDtypeStruct((far_count * (sum(sizes) + extra), parts[0].shape[1]), jnp.float32)
     relay = call(
         functools.partial(relay_kernel, far_count=far_count, sizes=sizes, extra=extra),
@@ -343,8 +348,8 @@
         (pltpu.VMEM,) * far_count,
         flops=RELAY_WEIGHT,
     )
-    near_parts = relay(far_parts[0], *far_parts[:0:-1])
-    return far_parts, [exchange(part, axis, near) for near, part in enumerate(near_parts, 1)]
+    near_parts = relay(*far_parts)
+    return [far_parts[far] for far in farthest_first(far_count)], [exchange(part, axis, near) for near, part in enumerate(near_parts, 1)]
 
 
 def body(query, key, value, implicit_filter, explicit_taps, skip_gain, out_grad):
@@ -376,10 +381,10 @@
         far_parts, near_parts = send_parts(split_parts, "ctx", near_count, (share,))
         gates = lax.all_to_all(packed, "ctx", 0, 0, tiled=True)
     else:
-        together = jnp.concatenate([packed, jnp.stack(split_parts)[:, None]], axis=1)
+        together = jnp.concatenate([packed, jnp.stack([split_parts[far] for far in farthest_first(blocks)])[:, None]], axis=1)
         together = lax.all_to_all(together, "ctx", 0, 0, tiled=True)
         together = jnp.pad(together, ((0, 0), (0, 0), (0, padded - share), (0, 0)))
-        gates, far_parts, near_parts = together[:, :2], list(together[:, 2]), []
+        gates, far_parts, near_parts = together[:, :2], [together[far, 2] for far in farthest_first(blocks)], []
         own = lax.axis_index("ctx") * share
         taps, skip = [
             jnp.pad(lax.dynamic_slice_in_dim(each, own, share, 1), ((0, 0), (0, padded - share)))
@@ -421,9 +426,12 @@
     if near_count > 1:
         parts = lax.all_to_all(results, "ctx", 0, 0, tiled=True)
     else:
-        together = jnp.concatenate([results, jnp.stack(split_parts)], axis=1).reshape(blocks, 4, padded, rows)
+        together = jnp.concatenate(
+            [results, jnp.stack([split_parts[far] for far in farthest_first(blocks)])], axis=1
+        ).reshape(blocks, 4, padded, rows)
         together = lax.all_to_all(together[:, :, :share], "ctx", 0, 0, tiled=True).reshape(blocks, 4 * share, rows)
-        parts, far_parts, near_parts = together[:, : 2 * share], list(together[:, 2 * share :]), []
+        parts, near_parts = together[:, : 2 * share], []
+        far_parts = [together[far, 2 * share :] for far in farthest_first(blocks)]
     full, one = shape((rows, channels)), shape((1, channels))
     block = pltpu.VMEM((blocks, share, rows), f32)
     outs = call(

time: 57.9 us -> 59.2 us (1.022); the launches traced: 56.8 us -> 58.9 us
  waiting for transfers between devices: 19.7 us -> 21.8 us
    ppermute x12, waiting for transfers between devices: 14.7 us -> 16.8 us  [exchange(): lax.ppermute(value, axis, [(i, i ^ distance) for i in range(lax.axis_size...]
where the time goes in v14:
time: 59.2 us; the launch traced here: 58.9 us
  starting transfers between devices  28.2 us (48%)
  waiting for transfers between devices  21.8 us (37%)
  Pallas kernels  5.89 us (10%)
  other arithmetic  1.16 us (2%)
  local copies, waits for them, and re-layouts  0.99 us (2%)
  between operations  0.82 us (1%)
    ppermute x12, starting transfers between devices, exchange(): lax.ppermute(value, axis, [(i, i ^ distance) for i in range(lax.axis_size...  17.3 us
    ppermute x12, waiting for transfers between devices, exchange(): lax.ppermute(value, axis, [(i, i ^ distance) for i in range(lax.axis_size...  16.8 us
    all_to_all x1, starting transfers between devices, body(): gates = lax.all_to_all(packed, 'ctx', 0, 0, tiled=True)  7.01 us
    all_to_all x1, waiting for transfers between devices, body(): gates = lax.all_to_all(packed, 'ctx', 0, 0, tiled=True)  4.99 us
    all_to_all x1, starting transfers between devices, body(): parts = lax.all_to_all(results, 'ctx', 0, 0, tiled=True)  3.85 us
    pallas_call x1, Pallas kernels, body(): call(functools.partial(spectra_kernel, near_count=near_count, early=early...  1.81 us
    pallas_call x1, Pallas kernels, body(): call(functools.partial(mix_kernel, channels=padded, early=early), 'mix',...  1.45 us
    pallas_call x1, Pallas kernels, body(): call(functools.partial(unpack_kernel, far_count=far_count, near_count=nea...  1.4 us
  transfers between devices with their start and end apart: 14, of which 8 were waited for; matrix products, arithmetic and copies ran while one was open for 2% of the time, Pallas kernels for 4%

profile of v14, /device:TPU:0, one launch (start us, length us, event | category | flops | bytes accessed | tf_op | source)
XLA Modules:
  0.0 58.9 jit_solution(7808587235018120363)
XLA Ops:
  0.6 0.0 copy-start.5
  0.6 0.9 %copy-done.5 = f32[128,512]{1,0:T(8,128)S(1)} copy-done((f32[128,512]{1,0:T(8,128)S(1)}, f32[128,512]{1,0:T(8,128)}, u32[]{:S(2)}) %copy-start.5) | copy-done | bytes 262168
  1.6 0.1 split.1
  1.7 5.1 %collective-permute-start = (f32[128,128]{1,0:T(8,128)S(1)}, f32[128,128]{1,0:T(8,128)S(1)}, u32[]{:S(2)}, u32[]{:S(2)}) collective-permute-start(f32[128,128]{1,0:T(8,128)S(1)} %get-tuple-element.30), channel_id=1, source_target_pairs={{0,24},{2,26},{4,28},{6,30},{8,16},{10,18},{12,20},{14,22},{16,8},... | collective-permute-start | bytes 196616 | tf_op jit(solution)/shard_map/ppermute | solution.py:335
  6.9 0.0 collective-permute-start.1
  6.9 0.6 %collective-permute-start.2 = (f32[128,128]{1,0:T(8,128)S(1)}, f32[128,128]{1,0:T(8,128)S(1)}, u32[]{:S(2)}, u32[]{:S(2)}) collective-permute-start(f32[128,128]{1,0:T(8,128)S(1)} %get-tuple-element.32), channel_id=1, source_target_pairs={{0,8},{2,10},{4,12},{6,14},{8,0},{10,2},{12,4},{14,6},{16,24},{18,... | collective-permute-start | bytes 196616 | tf_op jit(solution)/shard_map/ppermute | solution.py:335
  7.5 1.2 %convert_multiply_fusion = (f32[128,512]{1,0:T(8,128)S(1)}, f32[128,512]{1,0:T(8,128)S(1)}) fusion(bf16[128,512]{1,0:T(8,128)(2,1)} %query.1, bf16[128,512]{1,0:T(8,128)(2,1)} %grad.1, bf16[128,512]{1,0:T(8,128)(2,1)} %value.1, bf16[128,512]{1,0:T(8,128)(2,1)} %key.1), kind=kLoop, calls=%fused_computation | loop fusion | flops 393216 | bytes 1048576 | tf_op jit(solution)/shard_map/mul | solution.py:368
  8.7 1.0 %pack.1 = f32[16,2,32,128]{3,2,1,0:T(8,128)} custom-call(f32[128,512]{1,0:T(8,128)S(1)} %get-tuple-element.52.product, f32[128,512]{1,0:T(8,128)S(1)} %get-tuple-element.51.mix_grad), custom_call_target="tpu_custom_call" | custom-call | bytes 1048576 | tf_op jit(solution)/shard_map/pack/pallas_call | solution.py:377
  9.7 7.0 %all-to-all-start = ((f32[16,2,32,128]{3,2,1,0:T(8,128)}), f32[16,2,32,128]{3,2,1,0:T(8,128)S(1)}, u32[]{:S(2)}, u32[]{:S(2)}) async-start(f32[16,2,32,128]{3,2,1,0:T(8,128)} %pack.1), calls=%async_computation | async-start | bytes 1048576 | tf_op jit(solution)/shard_map/all_to_all | solution.py:382
  16.7 0.0 collective-permute-done.refs_3_.rest_1_
  16.7 0.0 collective-permute-done.1.refs_2_.rest_2_
  16.7 0.0 collective-permute-done.2.refs_1_.rest_3_
  16.7 0.0 copy-start.4
  16.8 0.0 copy-start.6
  16.8 0.0 copy-start.7
  16.8 0.0 copy-start.8
  16.8 2.0 %collective-permute-start.3 = (f32[128,128]{1,0:T(8,128)S(1)}, f32[128,128]{1,0:T(8,128)S(1)}, u32[]{:S(2)}, u32[]{:S(2)}) collective-permute-start(f32[128,128]{1,0:T(8,128)S(1)} %get-tuple-element.33), channel_id=1, source_target_pairs={{0,2},{2,0},{4,6},{6,4},{8,10},{10,8},{12,14},{14,12},{16,18},{18,... | collective-permute-start | bytes 196616 | tf_op jit(solution)/shard_map/ppermute | solution.py:335
  18.8 1.5 %collective-permute-start.4 = (f32[128,128]{1,0:T(8,128)S(1)}, f32[128,128]{1,0:T(8,128)S(1)}, u32[]{:S(2)}, u32[]{:S(2)}) collective-permute-start(f32[128,128]{1,0:T(8,128)S(1)} %get-tuple-element.34), channel_id=1, source_target_pairs={{0,4},{2,6},{4,0},{6,2},{8,12},{10,14},{12,8},{14,10},{16,20},{18,... | collective-permute-start | bytes 196616 | tf_op jit(solution)/shard_map/ppermute | solution.py:335
  20.3 0.1 collective-permute-start.5
  20.4 2.7 %collective-permute-done.3.rest_4_ = f32[128,128]{1,0:T(8,128)S(1)} collective-permute-done((f32[128,128]{1,0:T(8,128)S(1)}, f32[128,128]{1,0:T(8,128)S(1)}, u32[]{:S(2)}, u32[]{:S(2)}) %collective-permute-start.3) | collective-permute-done | bytes 65568 | tf_op jit(solution)/shard_map/ppermute | solution.py:335
  23.1 1.5 %collective-permute-done.4.rest_5_ = f32[128,128]{1,0:T(8,128)S(1)} collective-permute-done((f32[128,128]{1,0:T(8,128)S(1)}, f32[128,128]{1,0:T(8,128)S(1)}, u32[]{:S(2)}, u32[]{:S(2)}) %collective-permute-start.4) | collective-permute-done | bytes 65568 | tf_op jit(solution)/shard_map/ppermute | solution.py:335
  24.6 1.5 %collective-permute-done.5.rest_6_ = f32[128,128]{1,0:T(8,128)S(1)} collective-permute-done((f32[128,128]{1,0:T(8,128)S(1)}, f32[128,128]{1,0:T(8,128)S(1)}, u32[]{:S(2)}, u32[]{:S(2)}) %collective-permute-start.5) | collective-permute-done | bytes 65568 | tf_op jit(solution)/shard_map/ppermute | solution.py:335
  26.1 5.0 %all-to-all-done.gates = f32[16,2,32,128]{3,2,1,0:T(8,128)S(1)} async-done(((f32[16,2,32,128]{3,2,1,0:T(8,128)}), f32[16,2,32,128]{3,2,1,0:T(8,128)S(1)}, u32[]{:S(2)}, u32[]{:S(2)}) %all-to-all-start) | async-done | bytes 524320 | tf_op jit(solution)/shard_map/all_to_all | solution.py:382
  31.1 0.0 copy-done.4
  31.1 0.0 copy-done.6
  31.1 0.0 copy-done.7
  31.1 0.0 copy-done.8
  31.1 1.8 %spectra.1 = (f32[2,544,256]{2,1,0:T(8,128)S(1)}, f32[224,128]{1,0:T(8,128)S(1)}, f32[224,128]{1,0:T(8,128)S(1)}, f32[224,128]{1,0:T(8,128)S(1)}, f32[224,128]{1,0:T(8,128)S(1)}) custom-call(f32[128,512]{1,0:T(8,128)S(1)} %copy-done.7, f32[1,512]{1,0:T(1,128)S(1)} %bitcast.2, bf16[4,256,256]{2,1,0:T(8,128)(2,1)S(1)} %copy-done.4, ...), custom_call_target="tpu_custom_call" | custom-call | flops 962592768 | bytes 1572864 | tf_op jit(solution)/shard_map/spectra/pallas_call | solution.py:398
  32.9 1.9 %collective-permute-start.6 = (f32[224,128]{1,0:T(8,128)S(1)}, f32[224,128]{1,0:T(8,128)S(1)}, u32[]{:S(2)}, u32[]{:S(2)}) collective-permute-start(f32[224,128]{1,0:T(8,128)S(1)} %get-tuple-element.38), channel_id=1, source_target_pairs={{0,24},{2,26},{4,28},{6,30},{8,16},{10,18},{12,20},{14,22},{16,8},... | collective-permute-start | bytes 344072 | tf_op jit(solution)/shard_map/ppermute | solution.py:335
  34.8 0.9 %collective-permute-start.7 = (f32[224,128]{1,0:T(8,128)S(1)}, f32[224,128]{1,0:T(8,128)S(1)}, u32[]{:S(2)}, u32[]{:S(2)}) collective-permute-start(f32[224,128]{1,0:T(8,128)S(1)} %get-tuple-element.39), channel_id=1, source_target_pairs={{0,16},{2,18},{4,20},{6,22},{8,24},{10,26},{12,28},{14,30},{16,0},... | collective-permute-start | bytes 344072 | tf_op jit(solution)/shard_map/ppermute | solution.py:335
  35.7 1.7 %collective-permute-start.8 = (f32[224,128]{1,0:T(8,128)S(1)}, f32[224,128]{1,0:T(8,128)S(1)}, u32[]{:S(2)}, u32[]{:S(2)}) collective-permute-start(f32[224,128]{1,0:T(8,128)S(1)} %get-tuple-element.40), channel_id=1, source_target_pairs={{0,8},{2,10},{4,12},{6,14},{8,0},{10,2},{12,4},{14,6},{16,24},{18,... | collective-permute-start | bytes 344072 | tf_op jit(solution)/shard_map/ppermute | solution.py:335
  37.4 1.5 %mix.1 = f32[16,48,128]{2,1,0:T(8,128)} custom-call(bf16[4,256,256]{2,1,0:T(8,128)(2,1)S(1)} %copy-done.4, f32[17,4,128]{2,1,0:T(4,128)S(1)} %copy-done.6, f32[2,544,256]{2,1,0:T(8,128)S(1)} %get-tuple-element.36.products), custom_call_target="tpu_custom_call" | custom-call | flops 320864256 | bytes 1572864 | tf_op jit(solution)/shard_map/mix/pallas_call | solution.py:417
  38.8 3.9 %all-to-all-start.1 = ((f32[16,48,128]{2,1,0:T(8,128)}), f32[16,48,128]{2,1,0:T(8,128)S(1)}, u32[]{:S(2)}, u32[]{:S(2)}) async-start(f32[16,48,128]{2,1,0:T(8,128)} %mix.1), calls=%async_computation.1 | async-start | bytes 786432 | tf_op jit(solution)/shard_map/all_to_all | solution.py:427
  42.7 0.0 collective-permute-done.6.refs_3_.rest_1_
  42.7 1.1 %collective-permute-done.7.refs_2_.rest_2_ = f32[224,128]{1,0:T(8,128)S(1)} collective-permute-done((f32[224,128]{1,0:T(8,128)S(1)}, f32[224,128]{1,0:T(8,128)S(1)}, u32[]{:S(2)}, u32[]{:S(2)}) %collective-permute-start.7) | collective-permute-done | bytes 114720 | tf_op jit(solution)/shard_map/ppermute | solution.py:335
  43.8 0.0 collective-permute-done.8.refs_1_.rest_3_
  43.8 0.0 copy-start
  43.8 0.0 copy-start.1
  43.8 0.0 copy-start.2
  43.8 0.0 copy-start.3
  43.8 1.1 %collective-permute-start.9 = (f32[320,128]{1,0:T(8,128)S(1)}, f32[320,128]{1,0:T(8,128)S(1)}, u32[]{:S(2)}, u32[]{:S(2)}) collective-permute-start(f32[320,128]{1,0:T(8,128)S(1)} %get-tuple-element.41), channel_id=1, source_target_pairs={{0,2},{2,0},{4,6},{6,4},{8,10},{10,8},{12,14},{14,12},{16,18},{18,... | collective-permute-start | bytes 491528 | tf_op jit(solution)/shard_map/ppermute | solution.py:335
  44.9 1.4 %collective-permute-start.10 = (f32[320,128]{1,0:T(8,128)S(1)}, f32[320,128]{1,0:T(8,128)S(1)}, u32[]{:S(2)}, u32[]{:S(2)}) collective-permute-start(f32[320,128]{1,0:T(8,128)S(1)} %get-tuple-element.42), channel_id=1, source_target_pairs={{0,4},{2,6},{4,0},{6,2},{8,12},{10,14},{12,8},{14,10},{16,20},{18,... | collective-permute-start | bytes 491528 | tf_op jit(solution)/shard_map/ppermute | solution.py:335
  46.3 1.1 %collective-permute-start.11 = (f32[320,128]{1,0:T(8,128)S(1)}, f32[320,128]{1,0:T(8,128)S(1)}, u32[]{:S(2)}, u32[]{:S(2)}) collective-permute-start(f32[320,128]{1,0:T(8,128)S(1)} %get-tuple-element.43), channel_id=1, source_target_pairs={{0,6},{2,4},{4,2},{6,0},{8,14},{10,12},{12,10},{14,8},{16,22},{18,... | collective-permute-start | bytes 491528 | tf_op jit(solution)/shard_map/ppermute | solution.py:335
  47.4 6.1 %collective-permute-done.9.rest_4_ = f32[320,128]{1,0:T(8,128)S(1)} collective-permute-done((f32[320,128]{1,0:T(8,128)S(1)}, f32[320,128]{1,0:T(8,128)S(1)}, u32[]{:S(2)}, u32[]{:S(2)}) %collective-permute-start.9) | collective-permute-done | bytes 163872 | tf_op jit(solution)/shard_map/ppermute | solution.py:335
  53.5 1.8 %collective-permute-done.10.rest_5_ = f32[320,128]{1,0:T(8,128)S(1)} collective-permute-done((f32[320,128]{1,0:T(8,128)S(1)}, f32[320,128]{1,0:T(8,128)S(1)}, u32[]{:S(2)}, u32[]{:S(2)}) %collective-permute-start.10) | collective-permute-done | bytes 163872 | tf_op jit(solution)/shard_map/ppermute | solution.py:335
  55.3 2.1 %collective-permute-done.11.rest_6_ = f32[320,128]{1,0:T(8,128)S(1)} collective-permute-done((f32[320,128]{1,0:T(8,128)S(1)}, f32[320,128]{1,0:T(8,128)S(1)}, u32[]{:S(2)}, u32[]{:S(2)}) %collective-permute-start.11) | collective-permute-done | bytes 163872 | tf_op jit(solution)/shard_map/ppermute | solution.py:335
  57.4 0.0 all-to-all-done.1.parts
  57.4 0.0 copy-done
  57.4 0.0 copy-done.1
  57.4 0.0 copy-done.2
  57.4 0.0 copy-done.3
  57.5 1.4 %unpack.1 = (f32[128,512]{1,0:T(8,128)}, f32[128,512]{1,0:T(8,128)}, f32[128,512]{1,0:T(8,128)}, f32[128,512]{1,0:T(8,128)}, f32[128,512]{1,0:T(8,128)}, /*index=5*/f32[128,512]{1,0:T(8,128)}, f32[1,512]{1,0:T(1,128)}) custom-call(bf16[128,512]{1,0:T(8,128)(2,1)S(1)} %copy-done, bf16[128,512]{1,0:T(8,128)(2,1)S(1)} %copy-done.1, ...), custom_call_target="tpu_custom_call" | custom-call | bytes 3145728 | tf_op jit(solution)/shard_map/unpack/pallas_call | solution.py:437
  (2 shorter events, 0.1 us)
Async XLA Ops:
  0.6 1.0 %copy-start.5 = (f32[128,512]{1,0:T(8,128)S(1)}, f32[128,512]{1,0:T(8,128)}, u32[]{:S(2)}) copy-start(f32[128,512]{1,0:T(8,128)} %field.1) | copy-start | bytes 786436
  1.7 15.0 %collective-permute-start = (f32[128,128]{1,0:T(8,128)S(1)}, f32[128,128]{1,0:T(8,128)S(1)}, u32[]{:S(2)}, u32[]{:S(2)}) collective-permute-start(f32[128,128]{1,0:T(8,128)S(1)} %get-tuple-element.30), channel_id=1, source_target_pairs={{0,24},{2,26},{4,28},{6,30},{8,16},{10,18},{12,20},{14,22},{16,8},... | collective-permute-start | bytes 196616 | tf_op jit(solution)/shard_map/ppermute | solution.py:335
  6.9 9.9 %collective-permute-start.1 = (f32[128,128]{1,0:T(8,128)S(1)}, f32[128,128]{1,0:T(8,128)S(1)}, u32[]{:S(2)}, u32[]{:S(2)}) collective-permute-start(f32[128,128]{1,0:T(8,128)S(1)} %get-tuple-element.31), channel_id=1, source_target_pairs={{0,16},{2,18},{4,20},{6,22},{8,24},{10,26},{12,28},{14,30},{16,0},... | collective-permute-start | bytes 196616 | tf_op jit(solution)/shard_map/ppermute | solution.py:335
  6.9 9.9 %collective-permute-start.2 = (f32[128,128]{1,0:T(8,128)S(1)}, f32[128,128]{1,0:T(8,128)S(1)}, u32[]{:S(2)}, u32[]{:S(2)}) collective-permute-start(f32[128,128]{1,0:T(8,128)S(1)} %get-tuple-element.32), channel_id=1, source_target_pairs={{0,8},{2,10},{4,12},{6,14},{8,0},{10,2},{12,4},{14,6},{16,24},{18,... | collective-permute-start | bytes 196616 | tf_op jit(solution)/shard_map/ppermute | solution.py:335
  9.7 21.4 %all-to-all-start = ((f32[16,2,32,128]{3,2,1,0:T(8,128)}), f32[16,2,32,128]{3,2,1,0:T(8,128)S(1)}, u32[]{:S(2)}, u32[]{:S(2)}) async-start(f32[16,2,32,128]{3,2,1,0:T(8,128)} %pack.1), calls=%async_computation | async-start | bytes 1048576 | tf_op jit(solution)/shard_map/all_to_all | solution.py:382
  16.7 14.3 %copy-start.4 = (bf16[4,256,256]{2,1,0:T(8,128)(2,1)S(1)}, bf16[4,256,256]{2,1,0:T(8,128)(2,1)}, u32[]{:S(2)}) copy-start(bf16[4,256,256]{2,1,0:T(8,128)(2,1)} %constant.4.clone.matrices) | copy-start | bytes 1572868
  16.8 14.3 %copy-start.6 = (f32[17,4,128]{2,1,0:T(4,128)S(1)}, f32[17,4,128]{2,1,0:T(4,128)}, u32[]{:S(2)}) copy-start(f32[17,4,128]{2,1,0:T(4,128)} %constant.5.clone.twists) | copy-start | bytes 104452
  16.8 14.3 %copy-start.7 = (f32[128,512]{1,0:T(8,128)S(1)}, f32[128,512]{1,0:T(8,128)}, u32[]{:S(2)}) copy-start(f32[128,512]{1,0:T(8,128)} %taps.1) | copy-start | bytes 786436
  16.8 14.3 %copy-start.8 = (f32[512]{0:T(512)S(1)}, f32[512]{0:T(512)}, u32[]{:S(2)}) copy-start(f32[512]{0:T(512)} %param.14) | copy-start | bytes 6148
  16.8 6.2 %collective-permute-start.3 = (f32[128,128]{1,0:T(8,128)S(1)}, f32[128,128]{1,0:T(8,128)S(1)}, u32[]{:S(2)}, u32[]{:S(2)}) collective-permute-start(f32[128,128]{1,0:T(8,128)S(1)} %get-tuple-element.33), channel_id=1, source_target_pairs={{0,2},{2,0},{4,6},{6,4},{8,10},{10,8},{12,14},{14,12},{16,18},{18,... | collective-permute-start | bytes 196616 | tf_op jit(solution)/shard_map/ppermute | solution.py:335
  18.8 5.8 %collective-permute-start.4 = (f32[128,128]{1,0:T(8,128)S(1)}, f32[128,128]{1,0:T(8,128)S(1)}, u32[]{:S(2)}, u32[]{:S(2)}) collective-permute-start(f32[128,128]{1,0:T(8,128)S(1)} %get-tuple-element.34), channel_id=1, source_target_pairs={{0,4},{2,6},{4,0},{6,2},{8,12},{10,14},{12,8},{14,10},{16,20},{18,... | collective-permute-start | bytes 196616 | tf_op jit(solution)/shard_map/ppermute | solution.py:335
  20.3 5.8 %collective-permute-start.5 = (f32[128,128]{1,0:T(8,128)S(1)}, f32[128,128]{1,0:T(8,128)S(1)}, u32[]{:S(2)}, u32[]{:S(2)}) collective-permute-start(f32[128,128]{1,0:T(8,128)S(1)} %get-tuple-element.35), channel_id=1, source_target_pairs={{0,6},{2,4},{4,2},{6,0},{8,14},{10,12},{12,10},{14,8},{16,22},{18,... | collective-permute-start | bytes 196616 | tf_op jit(solution)/shard_map/ppermute | solution.py:335
  32.9 9.8 %collective-permute-start.6 = (f32[224,128]{1,0:T(8,128)S(1)}, f32[224,128]{1,0:T(8,128)S(1)}, u32[]{:S(2)}, u32[]{:S(2)}) collective-permute-start(f32[224,128]{1,0:T(8,128)S(1)} %get-tuple-element.38), channel_id=1, source_target_pairs={{0,24},{2,26},{4,28},{6,30},{8,16},{10,18},{12,20},{14,22},{16,8},... | collective-permute-start | bytes 344072 | tf_op jit(solution)/shard_map/ppermute | solution.py:335
  34.8 9.0 %collective-permute-start.7 = (f32[224,128]{1,0:T(8,128)S(1)}, f32[224,128]{1,0:T(8,128)S(1)}, u32[]{:S(2)}, u32[]{:S(2)}) collective-permute-start(f32[224,128]{1,0:T(8,128)S(1)} %get-tuple-element.39), channel_id=1, source_target_pairs={{0,16},{2,18},{4,20},{6,22},{8,24},{10,26},{12,28},{14,30},{16,0},... | collective-permute-start | bytes 344072 | tf_op jit(solution)/shard_map/ppermute | solution.py:335
  35.7 8.1 %collective-permute-start.8 = (f32[224,128]{1,0:T(8,128)S(1)}, f32[224,128]{1,0:T(8,128)S(1)}, u32[]{:S(2)}, u32[]{:S(2)}) collective-permute-start(f32[224,128]{1,0:T(8,128)S(1)} %get-tuple-element.40), channel_id=1, source_target_pairs={{0,8},{2,10},{4,12},{6,14},{8,0},{10,2},{12,4},{14,6},{16,24},{18,... | collective-permute-start | bytes 344072 | tf_op jit(solution)/shard_map/ppermute | solution.py:335
  38.8 18.6 %all-to-all-start.1 = ((f32[16,48,128]{2,1,0:T(8,128)}), f32[16,48,128]{2,1,0:T(8,128)S(1)}, u32[]{:S(2)}, u32[]{:S(2)}) async-start(f32[16,48,128]{2,1,0:T(8,128)} %mix.1), calls=%async_computation.1 | async-start | bytes 786432 | tf_op jit(solution)/shard_map/all_to_all | solution.py:427
  43.8 13.7 %copy-start = (bf16[128,512]{1,0:T(8,128)(2,1)S(1)}, bf16[128,512]{1,0:T(8,128)(2,1)}, u32[]{:S(2)}) copy-start(bf16[128,512]{1,0:T(8,128)(2,1)} %query.1) | copy-start | bytes 393220
  43.8 13.7 %copy-start.1 = (bf16[128,512]{1,0:T(8,128)(2,1)S(1)}, bf16[128,512]{1,0:T(8,128)(2,1)}, u32[]{:S(2)}) copy-start(bf16[128,512]{1,0:T(8,128)(2,1)} %key.1) | copy-start | bytes 393220
  43.8 13.7 %copy-start.2 = (bf16[128,512]{1,0:T(8,128)(2,1)S(1)}, bf16[128,512]{1,0:T(8,128)(2,1)}, u32[]{:S(2)}) copy-start(bf16[128,512]{1,0:T(8,128)(2,1)} %value.1) | copy-start | bytes 393220
  43.8 13.7 %copy-start.3 = (bf16[128,512]{1,0:T(8,128)(2,1)S(1)}, bf16[128,512]{1,0:T(8,128)(2,1)}, u32[]{:S(2)}) copy-start(bf16[128,512]{1,0:T(8,128)(2,1)} %grad.1) | copy-start | bytes 393220
  43.8 9.7 %collective-permute-start.9 = (f32[320,128]{1,0:T(8,128)S(1)}, f32[320,128]{1,0:T(8,128)S(1)}, u32[]{:S(2)}, u32[]{:S(2)}) collective-permute-start(f32[320,128]{1,0:T(8,128)S(1)} %get-tuple-element.41), channel_id=1, source_target_pairs={{0,2},{2,0},{4,6},{6,4},{8,10},{10,8},{12,14},{14,12},{16,18},{18,... | collective-permute-start | bytes 491528 | tf_op jit(solution)/shard_map/ppermute | solution.py:335
  44.9 10.4 %collective-permute-start.10 = (f32[320,128]{1,0:T(8,128)S(1)}, f32[320,128]{1,0:T(8,128)S(1)}, u32[]{:S(2)}, u32[]{:S(2)}) collective-permute-start(f32[320,128]{1,0:T(8,128)S(1)} %get-tuple-element.42), channel_id=1, source_target_pairs={{0,4},{2,6},{4,0},{6,2},{8,12},{10,14},{12,8},{14,10},{16,20},{18,... | collective-permute-start | bytes 491528 | tf_op jit(solution)/shard_map/ppermute | solution.py:335
  46.3 11.1 %collective-permute-start.11 = (f32[320,128]{1,0:T(8,128)S(1)}, f32[320,128]{1,0:T(8,128)S(1)}, u32[]{:S(2)}, u32[]{:S(2)}) collective-permute-start(f32[320,128]{1,0:T(8,128)S(1)} %get-tuple-element.43), channel_id=1, source_target_pairs={{0,6},{2,4},{4,2},{6,0},{8,14},{10,12},{12,10},{14,8},{16,22},{18,... | collective-permute-start | bytes 491528 | tf_op jit(solution)/shard_map/ppermute | solution.py:335

commit v15 on v13

--- a/solution.py
+++ b/solution.py
@@ -140,10 +140,14 @@
     return dot(values_high, high) + (dot(values_low, high) + dot(values_high, low))
 
 
-def pack_kernel(product, mix_grad, out):
+def pack_kernel(product, mix_grad, out, held, sent):
     blocks, _, share, rows = out.shape
+    copies = [pltpu.make_async_copy(held.at[:, a], out.at[:, a], sent.at[a]) for a in range(2)]
     for a, field in enumerate((product, mix_grad)):
-        out[:, a] = field[...].T.reshape(blocks, share, rows)
+        held[:, a] = field[...].T.reshape(blocks, share, rows)
+        copies[a].start()
+    for copy in copies:
+        copy.wait()
 
 
 def chunk(sizes, count, field, at):
@@ -256,11 +260,18 @@
         yield low, padded_bins_back(bins, blocks)
 
 
-def mix_kernel(matrices, twists, products, out, results, *, channels, early):
+def mix_kernel(matrices, twists, products, out, results, held, sent, *, channels, early):
+    places = [pl.ds(0, channels), pl.ds(channels, channels - early)]
+    copies = [
+        pltpu.make_async_copy(held.at[:, place], out.at[:, place], sent.at[a]) for a, place in enumerate(places)
+    ]
     for a, first in enumerate((0, early)):
         for low, values in blocks_back(products.at[a], results.at[a], matrices, twists, channels, first, channels):
             for j, value in enumerate(values):
-                out[j, pl.ds(a * channels + low, 8), :] = value
+                held[j, pl.ds(a * channels + low, 8), :] = value
+        copies[a].start()
+    for copy in copies:
+        copy.wait()
 
 
 def relay_kernel(*refs, far_count, sizes, extra):
@@ -369,8 +380,15 @@
         scratch=(pltpu.VMEM((channels, rows), f32),),
         size=8 * rows * channels,
     )(implicit_filter)
+    both = shape((blocks, 2, share, rows))
     packed = call(
-        pack_kernel, "pack", shape((blocks, 2, share, rows)), (pltpu.VMEM,) * 2, size=16 * rows * channels
+        pack_kernel,
+        "pack",
+        both,
+        (pltpu.VMEM,) * 2,
+        scratch=(pltpu.VMEM(both.shape, f32), pltpu.SemaphoreType.DMA((2,))),
+        to=pltpu.HBM,
+        size=16 * rows * channels,
     )(product, mix_grad)
     if near_count > 1:
         far_parts, near_parts = send_parts(split_parts, "ctx", near_count, (share,))
@@ -388,7 +406,7 @@
     matrices, twists = tables(blocks, rows)
     height = (blocks + 1) * padded
     matrices, twists = jnp.asarray(matrices), jnp.asarray(twists)
-    early = padded // 16 * 8 if near_count > 1 else 0
+    early = padded // 32 * 8 if near_count > 1 else 0
     block = pltpu.VMEM((blocks, padded, rows), f32)
     products, *split_parts = call(
         functools.partial(spectra_kernel, near_count=near_count, early=early, grad_scale=grad_scale),
@@ -409,12 +427,14 @@
     if near_count > 1:
         sizes = (share, early) if early else (share,)
         far_parts, near_parts = send_parts(split_parts, "ctx", near_count, sizes, share)
+    late = shape((blocks, 2 * padded - early, rows))
     results = call(
         functools.partial(mix_kernel, channels=padded, early=early),
         "mix",
-        shape((blocks, 2 * padded - early, rows)),
+        late,
         (pltpu.VMEM,) * 3,
-        scratch=(pltpu.VMEM((2, height, 2 * rows), f32),),
+        scratch=(pltpu.VMEM((2, height, 2 * rows), f32), pltpu.VMEM(late.shape, f32), pltpu.SemaphoreType.DMA((2,))),
+        to=pltpu.HBM,
         flops=9 * height * (2 * rows) ** 2,
         size=24 * blocks * padded * rows,
     )(matrices, twists, products)

time: 57.9 us -> 57.4 us (level); the launches traced: 56.8 us -> 57.1 us
  transfers between devices with their start and end apart: 14 -> 14, of which waited for: 8 -> 7; matrix products, arithmetic and copies ran while one was open for 2% -> 2% of each run, Pallas kernels for 4% -> 5%
where the time goes in v15:
time: 57.4 us; the launch traced here: 57.1 us
  starting transfers between devices  28.2 us (49%)
  waiting for transfers between devices  19.9 us (35%)
  Pallas kernels  5.95 us (10%)
  other arithmetic  1.16 us (2%)
  local copies, waits for them, and re-layouts  0.99 us (2%)
  between operations  0.86 us (1%)
    ppermute x12, starting transfers between devices, exchange(): lax.ppermute(value, axis, [(i, i ^ distance) for i in range(lax.axis_size...  17.2 us
    ppermute x12, waiting for transfers between devices, exchange(): lax.ppermute(value, axis, [(i, i ^ distance) for i in range(lax.axis_size...  14.9 us
    all_to_all x1, starting transfers between devices, body(): gates = lax.all_to_all(packed, 'ctx', 0, 0, tiled=True)  7.1 us
    all_to_all x1, waiting for transfers between devices, body(): gates = lax.all_to_all(packed, 'ctx', 0, 0, tiled=True)  4.99 us
    all_to_all x1, starting transfers between devices, body(): parts = lax.all_to_all(results, 'ctx', 0, 0, tiled=True)  3.87 us
    pallas_call x1, Pallas kernels, body(): call(functools.partial(spectra_kernel, near_count=near_count, early=early...  1.81 us
    pallas_call x1, Pallas kernels, body(): call(functools.partial(mix_kernel, channels=padded, early=early), 'mix',...  1.58 us
    pallas_call x1, Pallas kernels, body(): call(functools.partial(unpack_kernel, far_count=far_count, near_count=nea...  1.4 us
  transfers between devices with their start and end apart: 14, of which 7 were waited for; matrix products, arithmetic and copies ran while one was open for 2% of the time, Pallas kernels for 5%

profile of v15, /device:TPU:0, one launch (start us, length us, event | category | flops | bytes accessed | tf_op | source)
XLA Modules:
  0.0 57.1 jit_solution(10807685580368582661)
XLA Ops:
  0.6 0.0 copy-start.5
  0.6 0.9 %copy-done.5 = f32[128,512]{1,0:T(8,128)S(1)} copy-done((f32[128,512]{1,0:T(8,128)S(1)}, f32[128,512]{1,0:T(8,128)}, u32[]{:S(2)}) %copy-start.5) | copy-done | bytes 262168
  1.6 0.1 split.1
  1.7 3.1 %collective-permute-start = (f32[128,128]{1,0:T(8,128)S(1)}, f32[128,128]{1,0:T(8,128)S(1)}, u32[]{:S(2)}, u32[]{:S(2)}) collective-permute-start(f32[128,128]{1,0:T(8,128)S(1)} %get-tuple-element.30), channel_id=1, source_target_pairs={{0,8},{2,10},{4,12},{6,14},{8,0},{10,2},{12,4},{14,6},{16,24},{18,... | collective-permute-start | bytes 196616 | tf_op jit(solution)/shard_map/ppermute | solution.py:342
  4.8 2.6 %collective-permute-start.1 = (f32[128,128]{1,0:T(8,128)S(1)}, f32[128,128]{1,0:T(8,128)S(1)}, u32[]{:S(2)}, u32[]{:S(2)}) collective-permute-start(f32[128,128]{1,0:T(8,128)S(1)} %get-tuple-element.31), channel_id=1, source_target_pairs={{0,16},{2,18},{4,20},{6,22},{8,24},{10,26},{12,28},{14,30},{16,0},... | collective-permute-start | bytes 196616 | tf_op jit(solution)/shard_map/ppermute | solution.py:342
  7.4 0.0 collective-permute-start.2
  7.4 1.2 %convert_multiply_fusion = (f32[128,512]{1,0:T(8,128)S(1)}, f32[128,512]{1,0:T(8,128)S(1)}) fusion(bf16[128,512]{1,0:T(8,128)(2,1)} %query.1, bf16[128,512]{1,0:T(8,128)(2,1)} %grad.1, bf16[128,512]{1,0:T(8,128)(2,1)} %value.1, bf16[128,512]{1,0:T(8,128)(2,1)} %key.1), kind=kLoop, calls=%fused_computation | loop fusion | flops 393216 | bytes 1048576 | tf_op jit(solution)/shard_map/mul | solution.py:374
  8.6 1.0 %pack.1 = f32[16,2,32,128]{3,2,1,0:T(8,128)} custom-call(f32[128,512]{1,0:T(8,128)S(1)} %get-tuple-element.52.product, f32[128,512]{1,0:T(8,128)S(1)} %get-tuple-element.51.mix_grad), custom_call_target="tpu_custom_call" | custom-call | bytes 1048576 | tf_op jit(solution)/shard_map/pack/pallas_call | solution.py:384
  9.6 7.1 %all-to-all-start = ((f32[16,2,32,128]{3,2,1,0:T(8,128)}), f32[16,2,32,128]{3,2,1,0:T(8,128)S(1)}, u32[]{:S(2)}, u32[]{:S(2)}) async-start(f32[16,2,32,128]{3,2,1,0:T(8,128)} %pack.1), calls=%async_computation | async-start | bytes 1048576 | tf_op jit(solution)/shard_map/all_to_all | solution.py:395
  16.7 0.0 collective-permute-done.refs_3_.rest_1_
  16.7 0.0 collective-permute-done.1.refs_2_.rest_2_
  16.7 0.0 collective-permute-done.2.refs_1_.rest_3_
  16.7 0.0 copy-start
  16.7 0.0 copy-start.6
  16.7 0.0 copy-start.7
  16.8 0.0 copy-start.8
  16.8 2.0 %collective-permute-start.3 = (f32[128,128]{1,0:T(8,128)S(1)}, f32[128,128]{1,0:T(8,128)S(1)}, u32[]{:S(2)}, u32[]{:S(2)}) collective-permute-start(f32[128,128]{1,0:T(8,128)S(1)} %get-tuple-element.33), channel_id=1, source_target_pairs={{0,2},{2,0},{4,6},{6,4},{8,10},{10,8},{12,14},{14,12},{16,18},{18,... | collective-permute-start | bytes 196616 | tf_op jit(solution)/shard_map/ppermute | solution.py:342
  18.8 1.5 %collective-permute-start.4 = (f32[128,128]{1,0:T(8,128)S(1)}, f32[128,128]{1,0:T(8,128)S(1)}, u32[]{:S(2)}, u32[]{:S(2)}) collective-permute-start(f32[128,128]{1,0:T(8,128)S(1)} %get-tuple-element.34), channel_id=1, source_target_pairs={{0,4},{2,6},{4,0},{6,2},{8,12},{10,14},{12,8},{14,10},{16,20},{18,... | collective-permute-start | bytes 196616 | tf_op jit(solution)/shard_map/ppermute | solution.py:342
  20.2 0.1 collective-permute-start.5
  20.3 2.7 %collective-permute-done.3.rest_4_ = f32[128,128]{1,0:T(8,128)S(1)} collective-permute-done((f32[128,128]{1,0:T(8,128)S(1)}, f32[128,128]{1,0:T(8,128)S(1)}, u32[]{:S(2)}, u32[]{:S(2)}) %collective-permute-start.3) | collective-permute-done | bytes 65568 | tf_op jit(solution)/shard_map/ppermute | solution.py:342
  23.0 1.5 %collective-permute-done.4.rest_5_ = f32[128,128]{1,0:T(8,128)S(1)} collective-permute-done((f32[128,128]{1,0:T(8,128)S(1)}, f32[128,128]{1,0:T(8,128)S(1)}, u32[]{:S(2)}, u32[]{:S(2)}) %collective-permute-start.4) | collective-permute-done | bytes 65568 | tf_op jit(solution)/shard_map/ppermute | solution.py:342
  24.6 1.5 %collective-permute-done.5.rest_6_ = f32[128,128]{1,0:T(8,128)S(1)} collective-permute-done((f32[128,128]{1,0:T(8,128)S(1)}, f32[128,128]{1,0:T(8,128)S(1)}, u32[]{:S(2)}, u32[]{:S(2)}) %collective-permute-start.5) | collective-permute-done | bytes 65568 | tf_op jit(solution)/shard_map/ppermute | solution.py:342
  26.0 5.0 %all-to-all-done.gates = f32[16,2,32,128]{3,2,1,0:T(8,128)S(1)} async-done(((f32[16,2,32,128]{3,2,1,0:T(8,128)}), f32[16,2,32,128]{3,2,1,0:T(8,128)S(1)}, u32[]{:S(2)}, u32[]{:S(2)}) %all-to-all-start) | async-done | bytes 524320 | tf_op jit(solution)/shard_map/all_to_all | solution.py:395
  31.0 0.0 copy-done
  31.0 0.0 copy-done.6
  31.0 0.0 copy-done.7
  31.0 0.0 copy-done.8
  31.0 1.8 %spectra.1 = (f32[2,544,256]{2,1,0:T(8,128)S(1)}, f32[192,128]{1,0:T(8,128)S(1)}, f32[192,128]{1,0:T(8,128)S(1)}, f32[192,128]{1,0:T(8,128)S(1)}, f32[192,128]{1,0:T(8,128)S(1)}) custom-call(f32[128,512]{1,0:T(8,128)S(1)} %copy-done.7, f32[1,512]{1,0:T(1,128)S(1)} %bitcast.2, bf16[4,256,256]{2,1,0:T(8,128)(2,1)S(1)} %copy-done, f32[17,4,128]{2,1,0:T(4,128)S(1)} %copy-done.6, ...), custom_call_target="tpu_custom_call" | custom-call | flops 962592768 | bytes 1572864 | tf_op jit(solution)/shard_map/spectra/pallas_call | solution.py:411
  32.9 1.3 %collective-permute-start.6 = (f32[192,128]{1,0:T(8,128)S(1)}, f32[192,128]{1,0:T(8,128)S(1)}, u32[]{:S(2)}, u32[]{:S(2)}) collective-permute-start(f32[192,128]{1,0:T(8,128)S(1)} %get-tuple-element.38), channel_id=1, source_target_pairs={{0,8},{2,10},{4,12},{6,14},{8,0},{10,2},{12,4},{14,6},{16,24},{18,... | collective-permute-start | bytes 294920 | tf_op jit(solution)/shard_map/ppermute | solution.py:342
  34.2 1.1 %collective-permute-start.7 = (f32[192,128]{1,0:T(8,128)S(1)}, f32[192,128]{1,0:T(8,128)S(1)}, u32[]{:S(2)}, u32[]{:S(2)}) collective-permute-start(f32[192,128]{1,0:T(8,128)S(1)} %get-tuple-element.39), channel_id=1, source_target_pairs={{0,16},{2,18},{4,20},{6,22},{8,24},{10,26},{12,28},{14,30},{16,0},... | collective-permute-start | bytes 294920 | tf_op jit(solution)/shard_map/ppermute | solution.py:342
  35.3 2.0 %collective-permute-start.8 = (f32[192,128]{1,0:T(8,128)S(1)}, f32[192,128]{1,0:T(8,128)S(1)}, u32[]{:S(2)}, u32[]{:S(2)}) collective-permute-start(f32[192,128]{1,0:T(8,128)S(1)} %get-tuple-element.40), channel_id=1, source_target_pairs={{0,24},{2,26},{4,28},{6,30},{8,16},{10,18},{12,20},{14,22},{16,8},... | collective-permute-start | bytes 294920 | tf_op jit(solution)/shard_map/ppermute | solution.py:342
  37.3 1.6 %mix.1 = f32[16,56,128]{2,1,0:T(8,128)} custom-call(bf16[4,256,256]{2,1,0:T(8,128)(2,1)S(1)} %copy-done, f32[17,4,128]{2,1,0:T(4,128)S(1)} %copy-done.6, f32[2,544,256]{2,1,0:T(8,128)S(1)} %get-tuple-element.36.products), custom_call_target="tpu_custom_call" | custom-call | flops 320864256 | bytes 1572864 | tf_op jit(solution)/shard_map/mix/pallas_call | solution.py:431
  38.9 3.9 %all-to-all-start.1 = ((f32[16,56,128]{2,1,0:T(8,128)}), f32[16,56,128]{2,1,0:T(8,128)S(1)}, u32[]{:S(2)}, u32[]{:S(2)}) async-start(f32[16,56,128]{2,1,0:T(8,128)} %mix.1), calls=%async_computation.1 | async-start | bytes 917504 | tf_op jit(solution)/shard_map/all_to_all | solution.py:442
  42.8 0.0 collective-permute-done.6.refs_3_.rest_1_
  42.8 0.0 collective-permute-done.7.refs_2_.rest_2_
  42.8 0.0 collective-permute-done.8.refs_1_.rest_3_
  42.8 0.0 copy-start.1
  42.8 0.0 copy-start.2
  42.8 0.0 copy-start.3
  42.8 0.0 copy-start.4
  42.9 2.0 %collective-permute-start.9 = (f32[288,128]{1,0:T(8,128)S(1)}, f32[288,128]{1,0:T(8,128)S(1)}, u32[]{:S(2)}, u32[]{:S(2)}) collective-permute-start(f32[288,128]{1,0:T(8,128)S(1)} %get-tuple-element.41), channel_id=1, source_target_pairs={{0,2},{2,0},{4,6},{6,4},{8,10},{10,8},{12,14},{14,12},{16,18},{18,... | collective-permute-start | bytes 442376 | tf_op jit(solution)/shard_map/ppermute | solution.py:342
  44.9 1.5 %collective-permute-start.10 = (f32[288,128]{1,0:T(8,128)S(1)}, f32[288,128]{1,0:T(8,128)S(1)}, u32[]{:S(2)}, u32[]{:S(2)}) collective-permute-start(f32[288,128]{1,0:T(8,128)S(1)} %get-tuple-element.42), channel_id=1, source_target_pairs={{0,4},{2,6},{4,0},{6,2},{8,12},{10,14},{12,8},{14,10},{16,20},{18,... | collective-permute-start | bytes 442376 | tf_op jit(solution)/shard_map/ppermute | solution.py:342
  46.4 0.1 collective-permute-start.11
  46.5 5.2 %collective-permute-done.9.rest_4_ = f32[288,128]{1,0:T(8,128)S(1)} collective-permute-done((f32[288,128]{1,0:T(8,128)S(1)}, f32[288,128]{1,0:T(8,128)S(1)}, u32[]{:S(2)}, u32[]{:S(2)}) %collective-permute-start.9) | collective-permute-done | bytes 147488 | tf_op jit(solution)/shard_map/ppermute | solution.py:342
  51.7 2.2 %collective-permute-done.10.rest_5_ = f32[288,128]{1,0:T(8,128)S(1)} collective-permute-done((f32[288,128]{1,0:T(8,128)S(1)}, f32[288,128]{1,0:T(8,128)S(1)}, u32[]{:S(2)}, u32[]{:S(2)}) %collective-permute-start.10) | collective-permute-done | bytes 147488 | tf_op jit(solution)/shard_map/ppermute | solution.py:342
  53.9 1.7 %collective-permute-done.11.rest_6_ = f32[288,128]{1,0:T(8,128)S(1)} collective-permute-done((f32[288,128]{1,0:T(8,128)S(1)}, f32[288,128]{1,0:T(8,128)S(1)}, u32[]{:S(2)}, u32[]{:S(2)}) %collective-permute-start.11) | collective-permute-done | bytes 147488 | tf_op jit(solution)/shard_map/ppermute | solution.py:342
  55.6 0.0 all-to-all-done.1.parts
  55.6 0.0 copy-done.1
  55.6 0.0 copy-done.2
  55.6 0.0 copy-done.3
  55.7 0.0 copy-done.4
  55.7 1.4 %unpack.1 = (f32[128,512]{1,0:T(8,128)}, f32[128,512]{1,0:T(8,128)}, f32[128,512]{1,0:T(8,128)}, f32[128,512]{1,0:T(8,128)}, f32[128,512]{1,0:T(8,128)}, /*index=5*/f32[128,512]{1,0:T(8,128)}, f32[1,512]{1,0:T(1,128)}) custom-call(bf16[128,512]{1,0:T(8,128)(2,1)S(1)} %copy-done.1, bf16[128,512]{1,0:T(8,128)(2,1)S(1)} %copy-done.2, ...), custom_call_target="tpu_custom_call" | custom-call | bytes 3145728 | tf_op jit(solution)/shard_map/unpack/pallas_call | solution.py:449
  (2 shorter events, 0.1 us)
Async XLA Ops:
  0.6 1.0 %copy-start.5 = (f32[128,512]{1,0:T(8,128)S(1)}, f32[128,512]{1,0:T(8,128)}, u32[]{:S(2)}) copy-start(f32[128,512]{1,0:T(8,128)} %field.1) | copy-start | bytes 786436
  1.7 14.9 %collective-permute-start = (f32[128,128]{1,0:T(8,128)S(1)}, f32[128,128]{1,0:T(8,128)S(1)}, u32[]{:S(2)}, u32[]{:S(2)}) collective-permute-start(f32[128,128]{1,0:T(8,128)S(1)} %get-tuple-element.30), channel_id=1, source_target_pairs={{0,8},{2,10},{4,12},{6,14},{8,0},{10,2},{12,4},{14,6},{16,24},{18,... | collective-permute-start | bytes 196616 | tf_op jit(solution)/shard_map/ppermute | solution.py:342
  4.8 11.9 %collective-permute-start.1 = (f32[128,128]{1,0:T(8,128)S(1)}, f32[128,128]{1,0:T(8,128)S(1)}, u32[]{:S(2)}, u32[]{:S(2)}) collective-permute-start(f32[128,128]{1,0:T(8,128)S(1)} %get-tuple-element.31), channel_id=1, source_target_pairs={{0,16},{2,18},{4,20},{6,22},{8,24},{10,26},{12,28},{14,30},{16,0},... | collective-permute-start | bytes 196616 | tf_op jit(solution)/shard_map/ppermute | solution.py:342
  7.4 9.3 %collective-permute-start.2 = (f32[128,128]{1,0:T(8,128)S(1)}, f32[128,128]{1,0:T(8,128)S(1)}, u32[]{:S(2)}, u32[]{:S(2)}) collective-permute-start(f32[128,128]{1,0:T(8,128)S(1)} %get-tuple-element.32), channel_id=1, source_target_pairs={{0,24},{2,26},{4,28},{6,30},{8,16},{10,18},{12,20},{14,22},{16,8},... | collective-permute-start | bytes 196616 | tf_op jit(solution)/shard_map/ppermute | solution.py:342
  9.6 21.5 %all-to-all-start = ((f32[16,2,32,128]{3,2,1,0:T(8,128)}), f32[16,2,32,128]{3,2,1,0:T(8,128)S(1)}, u32[]{:S(2)}, u32[]{:S(2)}) async-start(f32[16,2,32,128]{3,2,1,0:T(8,128)} %pack.1), calls=%async_computation | async-start | bytes 1048576 | tf_op jit(solution)/shard_map/all_to_all | solution.py:395
  16.7 14.3 %copy-start = (bf16[4,256,256]{2,1,0:T(8,128)(2,1)S(1)}, bf16[4,256,256]{2,1,0:T(8,128)(2,1)}, u32[]{:S(2)}) copy-start(bf16[4,256,256]{2,1,0:T(8,128)(2,1)} %constant.4.clone.matrices) | copy-start | bytes 1572868
  16.7 14.3 %copy-start.6 = (f32[17,4,128]{2,1,0:T(4,128)S(1)}, f32[17,4,128]{2,1,0:T(4,128)}, u32[]{:S(2)}) copy-start(f32[17,4,128]{2,1,0:T(4,128)} %constant.5.clone.twists) | copy-start | bytes 104452
  16.7 14.3 %copy-start.7 = (f32[128,512]{1,0:T(8,128)S(1)}, f32[128,512]{1,0:T(8,128)}, u32[]{:S(2)}) copy-start(f32[128,512]{1,0:T(8,128)} %taps.1) | copy-start | bytes 786436
  16.8 14.3 %copy-start.8 = (f32[512]{0:T(512)S(1)}, f32[512]{0:T(512)}, u32[]{:S(2)}) copy-start(f32[512]{0:T(512)} %param.14) | copy-start | bytes 6148
  16.8 6.2 %collective-permute-start.3 = (f32[128,128]{1,0:T(8,128)S(1)}, f32[128,128]{1,0:T(8,128)S(1)}, u32[]{:S(2)}, u32[]{:S(2)}) collective-permute-start(f32[128,128]{1,0:T(8,128)S(1)} %get-tuple-element.33), channel_id=1, source_target_pairs={{0,2},{2,0},{4,6},{6,4},{8,10},{10,8},{12,14},{14,12},{16,18},{18,... | collective-permute-start | bytes 196616 | tf_op jit(solution)/shard_map/ppermute | solution.py:342
  18.8 5.8 %collective-permute-start.4 = (f32[128,128]{1,0:T(8,128)S(1)}, f32[128,128]{1,0:T(8,128)S(1)}, u32[]{:S(2)}, u32[]{:S(2)}) collective-permute-start(f32[128,128]{1,0:T(8,128)S(1)} %get-tuple-element.34), channel_id=1, source_target_pairs={{0,4},{2,6},{4,0},{6,2},{8,12},{10,14},{12,8},{14,10},{16,20},{18,... | collective-permute-start | bytes 196616 | tf_op jit(solution)/shard_map/ppermute | solution.py:342
  20.2 5.8 %collective-permute-start.5 = (f32[128,128]{1,0:T(8,128)S(1)}, f32[128,128]{1,0:T(8,128)S(1)}, u32[]{:S(2)}, u32[]{:S(2)}) collective-permute-start(f32[128,128]{1,0:T(8,128)S(1)} %get-tuple-element.35), channel_id=1, source_target_pairs={{0,6},{2,4},{4,2},{6,0},{8,14},{10,12},{12,10},{14,8},{16,22},{18,... | collective-permute-start | bytes 196616 | tf_op jit(solution)/shard_map/ppermute | solution.py:342
  32.9 9.9 %collective-permute-start.6 = (f32[192,128]{1,0:T(8,128)S(1)}, f32[192,128]{1,0:T(8,128)S(1)}, u32[]{:S(2)}, u32[]{:S(2)}) collective-permute-start(f32[192,128]{1,0:T(8,128)S(1)} %get-tuple-element.38), channel_id=1, source_target_pairs={{0,8},{2,10},{4,12},{6,14},{8,0},{10,2},{12,4},{14,6},{16,24},{18,... | collective-permute-start | bytes 294920 | tf_op jit(solution)/shard_map/ppermute | solution.py:342
  34.2 8.6 %collective-permute-start.7 = (f32[192,128]{1,0:T(8,128)S(1)}, f32[192,128]{1,0:T(8,128)S(1)}, u32[]{:S(2)}, u32[]{:S(2)}) collective-permute-start(f32[192,128]{1,0:T(8,128)S(1)} %get-tuple-element.39), channel_id=1, source_target_pairs={{0,16},{2,18},{4,20},{6,22},{8,24},{10,26},{12,28},{14,30},{16,0},... | collective-permute-start | bytes 294920 | tf_op jit(solution)/shard_map/ppermute | solution.py:342
  35.3 7.5 %collective-permute-start.8 = (f32[192,128]{1,0:T(8,128)S(1)}, f32[192,128]{1,0:T(8,128)S(1)}, u32[]{:S(2)}, u32[]{:S(2)}) collective-permute-start(f32[192,128]{1,0:T(8,128)S(1)} %get-tuple-element.40), channel_id=1, source_target_pairs={{0,24},{2,26},{4,28},{6,30},{8,16},{10,18},{12,20},{14,22},{16,8},... | collective-permute-start | bytes 294920 | tf_op jit(solution)/shard_map/ppermute | solution.py:342
  38.9 16.7 %all-to-all-start.1 = ((f32[16,56,128]{2,1,0:T(8,128)}), f32[16,56,128]{2,1,0:T(8,128)S(1)}, u32[]{:S(2)}, u32[]{:S(2)}) async-start(f32[16,56,128]{2,1,0:T(8,128)} %mix.1), calls=%async_computation.1 | async-start | bytes 917504 | tf_op jit(solution)/shard_map/all_to_all | solution.py:442
  42.8 12.8 %copy-start.1 = (bf16[128,512]{1,0:T(8,128)(2,1)S(1)}, bf16[128,512]{1,0:T(8,128)(2,1)}, u32[]{:S(2)}) copy-start(bf16[128,512]{1,0:T(8,128)(2,1)} %query.1) | copy-start | bytes 393220
  42.8 12.8 %copy-start.2 = (bf16[128,512]{1,0:T(8,128)(2,1)S(1)}, bf16[128,512]{1,0:T(8,128)(2,1)}, u32[]{:S(2)}) copy-start(bf16[128,512]{1,0:T(8,128)(2,1)} %key.1) | copy-start | bytes 393220
  42.8 12.8 %copy-start.3 = (bf16[128,512]{1,0:T(8,128)(2,1)S(1)}, bf16[128,512]{1,0:T(8,128)(2,1)}, u32[]{:S(2)}) copy-start(bf16[128,512]{1,0:T(8,128)(2,1)} %value.1) | copy-start | bytes 393220
  42.8 12.8 %copy-start.4 = (bf16[128,512]{1,0:T(8,128)(2,1)S(1)}, bf16[128,512]{1,0:T(8,128)(2,1)}, u32[]{:S(2)}) copy-start(bf16[128,512]{1,0:T(8,128)(2,1)} %grad.1) | copy-start | bytes 393220
  42.9 8.8 %collective-permute-start.9 = (f32[288,128]{1,0:T(8,128)S(1)}, f32[288,128]{1,0:T(8,128)S(1)}, u32[]{:S(2)}, u32[]{:S(2)}) collective-permute-start(f32[288,128]{1,0:T(8,128)S(1)} %get-tuple-element.41), channel_id=1, source_target_pairs={{0,2},{2,0},{4,6},{6,4},{8,10},{10,8},{12,14},{14,12},{16,18},{18,... | collective-permute-start | bytes 442376 | tf_op jit(solution)/shard_map/ppermute | solution.py:342
  44.9 9.0 %collective-permute-start.10 = (f32[288,128]{1,0:T(8,128)S(1)}, f32[288,128]{1,0:T(8,128)S(1)}, u32[]{:S(2)}, u32[]{:S(2)}) collective-permute-start(f32[288,128]{1,0:T(8,128)S(1)} %get-tuple-element.42), channel_id=1, source_target_pairs={{0,4},{2,6},{4,0},{6,2},{8,12},{10,14},{12,8},{14,10},{16,20},{18,... | collective-permute-start | bytes 442376 | tf_op jit(solution)/shard_map/ppermute | solution.py:342
  46.4 9.3 %collective-permute-start.11 = (f32[288,128]{1,0:T(8,128)S(1)}, f32[288,128]{1,0:T(8,128)S(1)}, u32[]{:S(2)}, u32[]{:S(2)}) collective-permute-start(f32[288,128]{1,0:T(8,128)S(1)} %get-tuple-element.43), channel_id=1, source_target_pairs={{0,6},{2,4},{4,2},{6,0},{8,14},{10,12},{12,10},{14,8},{16,22},{18,... | collective-permute-start | bytes 442376 | tf_op jit(solution)/shard_map/ppermute | solution.py:342

commit v16 on v15

--- a/solution.py
+++ b/solution.py
@@ -140,12 +140,17 @@
     return dot(values_high, high) + (dot(values_low, high) + dot(values_high, low))
 
 
-def pack_kernel(product, mix_grad, out, held, sent):
-    blocks, _, share, rows = out.shape
-    copies = [pltpu.make_async_copy(held.at[:, a], out.at[:, a], sent.at[a]) for a in range(2)]
-    for a, field in enumerate((product, mix_grad)):
-        held[:, a] = field[...].T.reshape(blocks, share, rows)
-        copies[a].start()
+def pack_kernel(product, mix_grad, out, held, sent, *, early):
+    blocks, _, rows = out.shape
+    share = product.shape[1] // blocks
+    places = [pl.ds(0, share), pl.ds(share, share - early)]
+    copies = [
+        pltpu.make_async_copy(held.at[:, place], out.at[:, place], sent.at[a]) for a, place in enumerate(places)
+    ]
+    held[:, places[0], :] = mix_grad[...].T.reshape(blocks, share, rows)
+    copies[0].start()
+    held[:, places[1], :] = product[...].T.reshape(blocks, share, rows)[:, early:]
+    copies[1].start()
     for copy in copies:
         copy.wait()
 
@@ -154,16 +159,17 @@
     return pl.ds(count * sum(sizes[:field]) + at * sizes[field], sizes[field])
 
 
-def split_kernel(field, *rest, near_count):
-    outs, turned = rest[:-1], rest[-1]
-    share = outs[0].shape[0] // near_count
-    turned[...] = field[...].T
+def split_kernel(*refs, near_count, sizes):
+    fields, outs, turned = refs[: len(sizes)], refs[len(sizes) : -1], refs[-1]
+    share = turned.shape[0] // (near_count * len(outs))
     me = lax.axis_index("ctx") if near_count > 1 else 0
-    for far, out in enumerate(outs):
-        for near in range(near_count):
-            start = (me ^ (far * near_count + near)) * share
-            start = start if near_count == 1 else pl.multiple_of(start, share)
-            out[chunk((share,), near_count, 0, near), :] = turned[pl.ds(start, share), :]
+    for k, field in enumerate(fields):
+        turned[...] = field[...].T
+        for far, out in enumerate(outs):
+            for near in range(near_count):
+                start = (me ^ (far * near_count + near)) * share
+                start = start if near_count == 1 else pl.multiple_of(start, share)
+                out[chunk(sizes, near_count, k, near), :] = turned[pl.ds(start, sizes[k]), :]
 
 
 def gather_blocks(outs, sizes, far_parts, near_parts, me):
@@ -186,14 +192,19 @@
                 outs[len(sizes)][source] = rows
 
 
-def spectra_kernel(taps, skip, matrices, twists, gates, *rest, near_count, early, grad_scale):
-    blocks, _, channels, rows = gates.shape
+def spectra_kernel(taps, skip, matrices, twists, gates, *rest, near_count, first_early, early, grad_scale):
+    blocks, rows = gates.shape[0], gates.shape[2]
+    channels = (gates.shape[1] + first_early) // 2
     far_count = blocks // near_count
     far_parts, rest = rest[:far_count], rest[far_count:]
     near_parts, rest = rest[: near_count - 1], rest[near_count - 1 :]
-    products, *outs, spectra, results, direct, lags, back, filters = rest
+    products, *outs, spectra, results, direct, lags, back, filters, factors = rest
     me = lax.axis_index("ctx") if near_count > 1 else 0
-    gather_blocks((filters,), (channels,), far_parts, near_parts, me)
+    if first_early:
+        gather_blocks((filters, factors), (channels, first_early), far_parts, near_parts, me)
+    else:
+        gather_blocks((filters,), (channels,), far_parts, near_parts, me)
+    factors[:, first_early:, :] = gates[:, channels:, :]
     row = lax.broadcasted_iota(jnp.int32, taps.shape, 0)
     direct[...] = (taps[...] + jnp.where(row == 0, skip[...], 0.0)).T
     own = 0 if direct.shape[0] == channels else pl.multiple_of(lax.axis_index("ctx") * channels, channels)
@@ -204,7 +215,7 @@
                 values = [filters[j, part, :] for j in range(blocks)]
                 values[0] = values[0] + direct[pl.ds(own + low, 8), :]
             else:
-                values = [gates[j, a // 2, part, :] for j in range(blocks)]
+                values = [(factors, None, gates)[a][j, part, :] for j in range(blocks)]
             bins = padded_bins(values)
             for p in range(blocks + 1):
                 real, imag = bins[p]
@@ -372,17 +383,19 @@
     far_count = blocks // near_count
     product = key.astype(f32) * value.astype(f32)
     mix_grad = out_grad.astype(f32) * query.astype(f32)
+    first_early = share // 32 * 8 if near_count > 1 else 0
+    sizes = (share, first_early) if first_early else (share,)
     split_parts = call(
-        functools.partial(split_kernel, near_count=near_count),
+        functools.partial(split_kernel, near_count=near_count, sizes=sizes),
         "split",
-        (shape((near_count * share, rows)),) * far_count,
-        (pltpu.VMEM,),
+        (shape((near_count * sum(sizes), rows)),) * far_count,
+        (pltpu.VMEM,) * len(sizes),
         scratch=(pltpu.VMEM((channels, rows), f32),),
-        size=8 * rows * channels,
-    )(implicit_filter)
-    both = shape((blocks, 2, share, rows))
+        size=16 * rows * channels,
+    )(*(implicit_filter, product)[: len(sizes)])
+    both = shape((blocks, 2 * share - first_early, rows))
     packed = call(
-        pack_kernel,
+        functools.partial(pack_kernel, early=first_early),
         "pack",
         both,
         (pltpu.VMEM,) * 2,
@@ -391,13 +404,14 @@
         size=16 * rows * channels,
     )(product, mix_grad)
     if near_count > 1:
-        far_parts, near_parts = send_parts(split_parts, "ctx", near_count, (share,))
+        far_parts, near_parts = send_parts(split_parts, "ctx", near_count, sizes)
         gates = lax.all_to_all(packed, "ctx", 0, 0, tiled=True)
     else:
-        together = jnp.concatenate([packed, jnp.stack(split_parts)[:, None]], axis=1)
+        together = jnp.concatenate([packed, jnp.stack(split_parts)], axis=1).reshape(blocks, 3, share, rows)
         together = lax.all_to_all(together, "ctx", 0, 0, tiled=True)
         together = jnp.pad(together, ((0, 0), (0, 0), (0, padded - share), (0, 0)))
-        gates, far_parts, near_parts = together[:, :2], list(together[:, 2]), []
+        gates, near_parts = together[:, :2].reshape(blocks, 2 * padded, rows), []
+        far_parts = list(together[:, 2])
         own = lax.axis_index("ctx") * share
         taps, skip = [
             jnp.pad(lax.dynamic_slice_in_dim(each, own, share, 1), ((0, 0), (0, padded - share)))
@@ -409,7 +423,9 @@
     early = padded // 32 * 8 if near_count > 1 else 0
     block = pltpu.VMEM((blocks, padded, rows), f32)
     products, *split_parts = call(
-        functools.partial(spectra_kernel, near_count=near_count, early=early, grad_scale=grad_scale),
+        functools.partial(
+            spectra_kernel, near_count=near_count, first_early=first_early, early=early, grad_scale=grad_scale
+        ),
         "spectra",
         (shape((2, height, 2 * rows)),) + (shape((near_count * (padded + early) + padded, rows)),) * far_count,
         (pltpu.VMEM,) * (4 + far_count + near_count),
@@ -419,6 +435,7 @@
             pltpu.VMEM(taps.shape[::-1], f32),
             block,
             pltpu.VMEM((blocks, max(early, 8), rows), f32),
+            block,
             block,
         ),
         flops=27 * height * (2 * rows) ** 2,

time: 57.4 us -> 55 us (0.958)
  waiting for transfers between devices: 19.9 us -> 18.5 us
  local copies, waits for them, and re-layouts: 0.99 us -> 0.06 us
    all_to_all x1, waiting for transfers between devices: 4.99 us -> 3.18 us  [body(): gates = lax.all_to_all(packed, 'ctx', 0, 0, tiled=True)]
    unnamed x18, local copies, waits for them, and re-layouts: 0.99 us -> 0.06 us
  transfers between devices with their start and end apart: 14 -> 14, of which waited for: 7 -> 7; matrix products, arithmetic and copies ran while one was open for 2% -> 0% of each run, Pallas kernels for 5% -> 5%
where the time goes in v16:
time: 55 us; the launch traced here: 54.7 us
  starting transfers between devices  28.1 us (51%)
  waiting for transfers between devices  18.5 us (34%)
  Pallas kernels  6.01 us (11%)
  other arithmetic  1.21 us (2%)
  between operations  0.87 us (2%)
    ppermute x12, starting transfers between devices, exchange(): lax.ppermute(value, axis, [(i, i ^ distance) for i in range(lax.axis_size...  17.2 us
    ppermute x12, waiting for transfers between devices, exchange(): lax.ppermute(value, axis, [(i, i ^ distance) for i in range(lax.axis_size...  15.3 us
    all_to_all x1, starting transfers between devices, body(): gates = lax.all_to_all(packed, 'ctx', 0, 0, tiled=True)  7.1 us
    all_to_all x1, starting transfers between devices, body(): parts = lax.all_to_all(results, 'ctx', 0, 0, tiled=True)  3.73 us
    all_to_all x1, waiting for transfers between devices, body(): gates = lax.all_to_all(packed, 'ctx', 0, 0, tiled=True)  3.18 us
    pallas_call x1, Pallas kernels, body(): call(functools.partial(spectra_kernel, near_count=near_count, first_early...  1.82 us
    pallas_call x1, Pallas kernels, body(): call(functools.partial(mix_kernel, channels=padded, early=early), 'mix',...  1.59 us
    pallas_call x1, Pallas kernels, body(): call(functools.partial(unpack_kernel, far_count=far_count, near_count=nea...  1.4 us
  transfers between devices with their start and end apart: 14, of which 7 were waited for; matrix products, arithmetic and copies ran while one was open for 0% of the time, Pallas kernels for 5%

profile of v16, /device:TPU:0, one launch (start us, length us, event | category | flops | bytes accessed | tf_op | source)
XLA Modules:
  0.0 54.7 jit_solution(13725467566436488603)
XLA Ops:
  0.6 0.0 copy-start.5
  0.6 1.2 %convert_multiply_fusion = (f32[128,512]{1,0:T(8,128)S(1)}, f32[128,512]{1,0:T(8,128)S(1)}) fusion(bf16[128,512]{1,0:T(8,128)(2,1)} %query.1, bf16[128,512]{1,0:T(8,128)(2,1)} %grad.1, bf16[128,512]{1,0:T(8,128)(2,1)} %value.1, bf16[128,512]{1,0:T(8,128)(2,1)} %key.1), kind=kLoop, calls=%fused_computation | loop fusion | flops 393216 | bytes 1048576 | tf_op jit(solution)/shard_map/mul | solution.py:385
  1.9 0.0 copy-done.5
  1.9 0.2 split.1
  2.1 3.1 %collective-permute-start = (f32[160,128]{1,0:T(8,128)S(1)}, f32[160,128]{1,0:T(8,128)S(1)}, u32[]{:S(2)}, u32[]{:S(2)}) collective-permute-start(f32[160,128]{1,0:T(8,128)S(1)} %get-tuple-element.30), channel_id=1, source_target_pairs={{0,8},{2,10},{4,12},{6,14},{8,0},{10,2},{12,4},{14,6},{16,24},{18,... | collective-permute-start | bytes 245768 | tf_op jit(solution)/shard_map/ppermute | solution.py:353
  5.2 2.6 %collective-permute-start.1 = (f32[160,128]{1,0:T(8,128)S(1)}, f32[160,128]{1,0:T(8,128)S(1)}, u32[]{:S(2)}, u32[]{:S(2)}) collective-permute-start(f32[160,128]{1,0:T(8,128)S(1)} %get-tuple-element.31), channel_id=1, source_target_pairs={{0,16},{2,18},{4,20},{6,22},{8,24},{10,26},{12,28},{14,30},{16,0},... | collective-permute-start | bytes 245768 | tf_op jit(solution)/shard_map/ppermute | solution.py:353
  7.8 0.0 collective-permute-start.2
  7.8 0.9 %pack.1 = f32[16,56,128]{2,1,0:T(8,128)} custom-call(f32[128,512]{1,0:T(8,128)S(1)} %get-tuple-element.52.product.refs_1_, f32[128,512]{1,0:T(8,128)S(1)} %get-tuple-element.51.mix_grad), custom_call_target="tpu_custom_call" | custom-call | bytes 1048576 | tf_op jit(solution)/shard_map/pack/pallas_call | solution.py:397
  8.7 7.1 %all-to-all-start = ((f32[16,56,128]{2,1,0:T(8,128)}), f32[16,56,128]{2,1,0:T(8,128)S(1)}, u32[]{:S(2)}, u32[]{:S(2)}) async-start(f32[16,56,128]{2,1,0:T(8,128)} %pack.1), calls=%async_computation | async-start | bytes 917504 | tf_op jit(solution)/shard_map/all_to_all | solution.py:408
  15.8 0.0 collective-permute-done.refs_3_.rest_1_
  15.8 0.0 collective-permute-done.1.refs_2_.rest_2_
  15.8 0.0 collective-permute-done.2.refs_1_.rest_3_
  15.9 0.0 copy-start
  15.9 0.0 copy-start.6
  15.9 0.0 copy-start.7
  15.9 0.0 copy-start.8
  15.9 2.0 %collective-permute-start.3 = (f32[160,128]{1,0:T(8,128)S(1)}, f32[160,128]{1,0:T(8,128)S(1)}, u32[]{:S(2)}, u32[]{:S(2)}) collective-permute-start(f32[160,128]{1,0:T(8,128)S(1)} %get-tuple-element.33), channel_id=1, source_target_pairs={{0,2},{2,0},{4,6},{6,4},{8,10},{10,8},{12,14},{14,12},{16,18},{18,... | collective-permute-start | bytes 245768 | tf_op jit(solution)/shard_map/ppermute | solution.py:353
  17.9 1.5 %collective-permute-start.4 = (f32[160,128]{1,0:T(8,128)S(1)}, f32[160,128]{1,0:T(8,128)S(1)}, u32[]{:S(2)}, u32[]{:S(2)}) collective-permute-start(f32[160,128]{1,0:T(8,128)S(1)} %get-tuple-element.34), channel_id=1, source_target_pairs={{0,4},{2,6},{4,0},{6,2},{8,12},{10,14},{12,8},{14,10},{16,20},{18,... | collective-permute-start | bytes 245768 | tf_op jit(solution)/shard_map/ppermute | solution.py:353
  19.4 0.1 collective-permute-start.5
  19.5 4.0 %collective-permute-done.3.rest_4_ = f32[160,128]{1,0:T(8,128)S(1)} collective-permute-done((f32[160,128]{1,0:T(8,128)S(1)}, f32[160,128]{1,0:T(8,128)S(1)}, u32[]{:S(2)}, u32[]{:S(2)}) %collective-permute-start.3) | collective-permute-done | bytes 81952 | tf_op jit(solution)/shard_map/ppermute | solution.py:353
  23.5 0.6 %collective-permute-done.4.rest_5_ = f32[160,128]{1,0:T(8,128)S(1)} collective-permute-done((f32[160,128]{1,0:T(8,128)S(1)}, f32[160,128]{1,0:T(8,128)S(1)}, u32[]{:S(2)}, u32[]{:S(2)}) %collective-permute-start.4) | collective-permute-done | bytes 81952 | tf_op jit(solution)/shard_map/ppermute | solution.py:353
  24.1 1.6 %collective-permute-done.5.rest_6_ = f32[160,128]{1,0:T(8,128)S(1)} collective-permute-done((f32[160,128]{1,0:T(8,128)S(1)}, f32[160,128]{1,0:T(8,128)S(1)}, u32[]{:S(2)}, u32[]{:S(2)}) %collective-permute-start.5) | collective-permute-done | bytes 81952 | tf_op jit(solution)/shard_map/ppermute | solution.py:353
  25.7 3.2 %all-to-all-done.gates = f32[16,56,128]{2,1,0:T(8,128)S(1)} async-done(((f32[16,56,128]{2,1,0:T(8,128)}), f32[16,56,128]{2,1,0:T(8,128)S(1)}, u32[]{:S(2)}, u32[]{:S(2)}) %all-to-all-start) | async-done | bytes 458784 | tf_op jit(solution)/shard_map/all_to_all | solution.py:408
  28.9 0.0 copy-done
  28.9 0.0 copy-done.6
  28.9 0.0 copy-done.7
  28.9 0.0 copy-done.8
  28.9 1.8 %spectra.1 = (f32[2,544,256]{2,1,0:T(8,128)S(1)}, f32[192,128]{1,0:T(8,128)S(1)}, f32[192,128]{1,0:T(8,128)S(1)}, f32[192,128]{1,0:T(8,128)S(1)}, f32[192,128]{1,0:T(8,128)S(1)}) custom-call(f32[128,512]{1,0:T(8,128)S(1)} %copy-done.7, f32[1,512]{1,0:T(1,128)S(1)} %bitcast.2, bf16[4,256,256]{2,1,0:T(8,128)(2,1)S(1)} %copy-done, f32[17,4,128]{2,1,0:T(4,128)S(1)} %copy-done.6, ...), custom_call_target="tpu_custom_call" | custom-call | flops 962592768 | bytes 1572864 | tf_op jit(solution)/shard_map/spectra/pallas_call | solution.py:425
  30.7 1.2 %collective-permute-start.6 = (f32[192,128]{1,0:T(8,128)S(1)}, f32[192,128]{1,0:T(8,128)S(1)}, u32[]{:S(2)}, u32[]{:S(2)}) collective-permute-start(f32[192,128]{1,0:T(8,128)S(1)} %get-tuple-element.38), channel_id=1, source_target_pairs={{0,8},{2,10},{4,12},{6,14},{8,0},{10,2},{12,4},{14,6},{16,24},{18,... | collective-permute-start | bytes 294920 | tf_op jit(solution)/shard_map/ppermute | solution.py:353
  32.0 1.2 %collective-permute-start.7 = (f32[192,128]{1,0:T(8,128)S(1)}, f32[192,128]{1,0:T(8,128)S(1)}, u32[]{:S(2)}, u32[]{:S(2)}) collective-permute-start(f32[192,128]{1,0:T(8,128)S(1)} %get-tuple-element.39), channel_id=1, source_target_pairs={{0,16},{2,18},{4,20},{6,22},{8,24},{10,26},{12,28},{14,30},{16,0},... | collective-permute-start | bytes 294920 | tf_op jit(solution)/shard_map/ppermute | solution.py:353
  33.1 2.0 %collective-permute-start.8 = (f32[192,128]{1,0:T(8,128)S(1)}, f32[192,128]{1,0:T(8,128)S(1)}, u32[]{:S(2)}, u32[]{:S(2)}) collective-permute-start(f32[192,128]{1,0:T(8,128)S(1)} %get-tuple-element.40), channel_id=1, source_target_pairs={{0,24},{2,26},{4,28},{6,30},{8,16},{10,18},{12,20},{14,22},{16,8},... | collective-permute-start | bytes 294920 | tf_op jit(solution)/shard_map/ppermute | solution.py:353
  35.2 1.6 %mix.1 = f32[16,56,128]{2,1,0:T(8,128)} custom-call(bf16[4,256,256]{2,1,0:T(8,128)(2,1)S(1)} %copy-done, f32[17,4,128]{2,1,0:T(4,128)S(1)} %copy-done.6, f32[2,544,256]{2,1,0:T(8,128)S(1)} %get-tuple-element.36.products), custom_call_target="tpu_custom_call" | custom-call | flops 320864256 | bytes 1572864 | tf_op jit(solution)/shard_map/mix/pallas_call | solution.py:448
  36.8 3.7 %all-to-all-start.1 = ((f32[16,56,128]{2,1,0:T(8,128)}), f32[16,56,128]{2,1,0:T(8,128)S(1)}, u32[]{:S(2)}, u32[]{:S(2)}) async-start(f32[16,56,128]{2,1,0:T(8,128)} %mix.1), calls=%async_computation.1 | async-start | bytes 917504 | tf_op jit(solution)/shard_map/all_to_all | solution.py:459
  40.5 0.0 collective-permute-done.6.refs_3_.rest_1_
  40.5 0.0 collective-permute-done.7.refs_2_.rest_2_
  40.6 0.0 collective-permute-done.8.refs_1_.rest_3_
  40.6 0.0 copy-start.1
  40.6 0.0 copy-start.2
  40.6 0.0 copy-start.3
  40.6 0.0 copy-start.4
  40.7 2.0 %collective-permute-start.9 = (f32[288,128]{1,0:T(8,128)S(1)}, f32[288,128]{1,0:T(8,128)S(1)}, u32[]{:S(2)}, u32[]{:S(2)}) collective-permute-start(f32[288,128]{1,0:T(8,128)S(1)} %get-tuple-element.41), channel_id=1, source_target_pairs={{0,2},{2,0},{4,6},{6,4},{8,10},{10,8},{12,14},{14,12},{16,18},{18,... | collective-permute-start | bytes 442376 | tf_op jit(solution)/shard_map/ppermute | solution.py:353
  42.6 1.5 %collective-permute-start.10 = (f32[288,128]{1,0:T(8,128)S(1)}, f32[288,128]{1,0:T(8,128)S(1)}, u32[]{:S(2)}, u32[]{:S(2)}) collective-permute-start(f32[288,128]{1,0:T(8,128)S(1)} %get-tuple-element.42), channel_id=1, source_target_pairs={{0,4},{2,6},{4,0},{6,2},{8,12},{10,14},{12,8},{14,10},{16,20},{18,... | collective-permute-start | bytes 442376 | tf_op jit(solution)/shard_map/ppermute | solution.py:353
  44.1 0.1 collective-permute-start.11
  44.2 5.1 %collective-permute-done.9.rest_4_ = f32[288,128]{1,0:T(8,128)S(1)} collective-permute-done((f32[288,128]{1,0:T(8,128)S(1)}, f32[288,128]{1,0:T(8,128)S(1)}, u32[]{:S(2)}, u32[]{:S(2)}) %collective-permute-start.9) | collective-permute-done | bytes 147488 | tf_op jit(solution)/shard_map/ppermute | solution.py:353
  49.3 2.2 %collective-permute-done.10.rest_5_ = f32[288,128]{1,0:T(8,128)S(1)} collective-permute-done((f32[288,128]{1,0:T(8,128)S(1)}, f32[288,128]{1,0:T(8,128)S(1)}, u32[]{:S(2)}, u32[]{:S(2)}) %collective-permute-start.10) | collective-permute-done | bytes 147488 | tf_op jit(solution)/shard_map/ppermute | solution.py:353
  51.5 1.8 %collective-permute-done.11.rest_6_ = f32[288,128]{1,0:T(8,128)S(1)} collective-permute-done((f32[288,128]{1,0:T(8,128)S(1)}, f32[288,128]{1,0:T(8,128)S(1)}, u32[]{:S(2)}, u32[]{:S(2)}) %collective-permute-start.11) | collective-permute-done | bytes 147488 | tf_op jit(solution)/shard_map/ppermute | solution.py:353
  53.3 0.0 all-to-all-done.1.parts
  53.3 0.0 copy-done.1
  53.3 0.0 copy-done.2
  53.3 0.0 copy-done.3
  53.3 0.0 copy-done.4
  53.3 1.4 %unpack.1 = (f32[128,512]{1,0:T(8,128)}, f32[128,512]{1,0:T(8,128)}, f32[128,512]{1,0:T(8,128)}, f32[128,512]{1,0:T(8,128)}, f32[128,512]{1,0:T(8,128)}, /*index=5*/f32[128,512]{1,0:T(8,128)}, f32[1,512]{1,0:T(1,128)}) custom-call(bf16[128,512]{1,0:T(8,128)(2,1)S(1)} %copy-done.1, bf16[128,512]{1,0:T(8,128)(2,1)S(1)} %copy-done.2, ...), custom_call_target="tpu_custom_call" | custom-call | bytes 3145728 | tf_op jit(solution)/shard_map/unpack/pallas_call | solution.py:466
  (2 shorter events, 0.1 us)
Async XLA Ops:
  0.6 1.2 %copy-start.5 = (f32[128,512]{1,0:T(8,128)S(1)}, f32[128,512]{1,0:T(8,128)}, u32[]{:S(2)}) copy-start(f32[128,512]{1,0:T(8,128)} %refs_0_.1) | copy-start | bytes 786436
  2.1 13.7 %collective-permute-start = (f32[160,128]{1,0:T(8,128)S(1)}, f32[160,128]{1,0:T(8,128)S(1)}, u32[]{:S(2)}, u32[]{:S(2)}) collective-permute-start(f32[160,128]{1,0:T(8,128)S(1)} %get-tuple-element.30), channel_id=1, source_target_pairs={{0,8},{2,10},{4,12},{6,14},{8,0},{10,2},{12,4},{14,6},{16,24},{18,... | collective-permute-start | bytes 245768 | tf_op jit(solution)/shard_map/ppermute | solution.py:353
  5.2 10.7 %collective-permute-start.1 = (f32[160,128]{1,0:T(8,128)S(1)}, f32[160,128]{1,0:T(8,128)S(1)}, u32[]{:S(2)}, u32[]{:S(2)}) collective-permute-start(f32[160,128]{1,0:T(8,128)S(1)} %get-tuple-element.31), channel_id=1, source_target_pairs={{0,16},{2,18},{4,20},{6,22},{8,24},{10,26},{12,28},{14,30},{16,0},... | collective-permute-start | bytes 245768 | tf_op jit(solution)/shard_map/ppermute | solution.py:353
  7.8 8.1 %collective-permute-start.2 = (f32[160,128]{1,0:T(8,128)S(1)}, f32[160,128]{1,0:T(8,128)S(1)}, u32[]{:S(2)}, u32[]{:S(2)}) collective-permute-start(f32[160,128]{1,0:T(8,128)S(1)} %get-tuple-element.32), channel_id=1, source_target_pairs={{0,24},{2,26},{4,28},{6,30},{8,16},{10,18},{12,20},{14,22},{16,8},... | collective-permute-start | bytes 245768 | tf_op jit(solution)/shard_map/ppermute | solution.py:353
  8.7 20.2 %all-to-all-start = ((f32[16,56,128]{2,1,0:T(8,128)}), f32[16,56,128]{2,1,0:T(8,128)S(1)}, u32[]{:S(2)}, u32[]{:S(2)}) async-start(f32[16,56,128]{2,1,0:T(8,128)} %pack.1), calls=%async_computation | async-start | bytes 917504 | tf_op jit(solution)/shard_map/all_to_all | solution.py:408
  15.9 13.0 %copy-start = (bf16[4,256,256]{2,1,0:T(8,128)(2,1)S(1)}, bf16[4,256,256]{2,1,0:T(8,128)(2,1)}, u32[]{:S(2)}) copy-start(bf16[4,256,256]{2,1,0:T(8,128)(2,1)} %constant.4.clone.matrices) | copy-start | bytes 1572868
  15.9 13.0 %copy-start.6 = (f32[17,4,128]{2,1,0:T(4,128)S(1)}, f32[17,4,128]{2,1,0:T(4,128)}, u32[]{:S(2)}) copy-start(f32[17,4,128]{2,1,0:T(4,128)} %constant.5.clone.twists) | copy-start | bytes 104452
  15.9 13.0 %copy-start.7 = (f32[128,512]{1,0:T(8,128)S(1)}, f32[128,512]{1,0:T(8,128)}, u32[]{:S(2)}) copy-start(f32[128,512]{1,0:T(8,128)} %taps.1) | copy-start | bytes 786436
  15.9 13.0 %copy-start.8 = (f32[512]{0:T(512)S(1)}, f32[512]{0:T(512)}, u32[]{:S(2)}) copy-start(f32[512]{0:T(512)} %param.14) | copy-start | bytes 6148
  15.9 7.5 %collective-permute-start.3 = (f32[160,128]{1,0:T(8,128)S(1)}, f32[160,128]{1,0:T(8,128)S(1)}, u32[]{:S(2)}, u32[]{:S(2)}) collective-permute-start(f32[160,128]{1,0:T(8,128)S(1)} %get-tuple-element.33), channel_id=1, source_target_pairs={{0,2},{2,0},{4,6},{6,4},{8,10},{10,8},{12,14},{14,12},{16,18},{18,... | collective-permute-start | bytes 245768 | tf_op jit(solution)/shard_map/ppermute | solution.py:353
  17.9 6.1 %collective-permute-start.4 = (f32[160,128]{1,0:T(8,128)S(1)}, f32[160,128]{1,0:T(8,128)S(1)}, u32[]{:S(2)}, u32[]{:S(2)}) collective-permute-start(f32[160,128]{1,0:T(8,128)S(1)} %get-tuple-element.34), channel_id=1, source_target_pairs={{0,4},{2,6},{4,0},{6,2},{8,12},{10,14},{12,8},{14,10},{16,20},{18,... | collective-permute-start | bytes 245768 | tf_op jit(solution)/shard_map/ppermute | solution.py:353
  19.4 6.3 %collective-permute-start.5 = (f32[160,128]{1,0:T(8,128)S(1)}, f32[160,128]{1,0:T(8,128)S(1)}, u32[]{:S(2)}, u32[]{:S(2)}) collective-permute-start(f32[160,128]{1,0:T(8,128)S(1)} %get-tuple-element.35), channel_id=1, source_target_pairs={{0,6},{2,4},{4,2},{6,0},{8,14},{10,12},{12,10},{14,8},{16,22},{18,... | collective-permute-start | bytes 245768 | tf_op jit(solution)/shard_map/ppermute | solution.py:353
  30.7 9.8 %collective-permute-start.6 = (f32[192,128]{1,0:T(8,128)S(1)}, f32[192,128]{1,0:T(8,128)S(1)}, u32[]{:S(2)}, u32[]{:S(2)}) collective-permute-start(f32[192,128]{1,0:T(8,128)S(1)} %get-tuple-element.38), channel_id=1, source_target_pairs={{0,8},{2,10},{4,12},{6,14},{8,0},{10,2},{12,4},{14,6},{16,24},{18,... | collective-permute-start | bytes 294920 | tf_op jit(solution)/shard_map/ppermute | solution.py:353
  32.0 8.6 %collective-permute-start.7 = (f32[192,128]{1,0:T(8,128)S(1)}, f32[192,128]{1,0:T(8,128)S(1)}, u32[]{:S(2)}, u32[]{:S(2)}) collective-permute-start(f32[192,128]{1,0:T(8,128)S(1)} %get-tuple-element.39), channel_id=1, source_target_pairs={{0,16},{2,18},{4,20},{6,22},{8,24},{10,26},{12,28},{14,30},{16,0},... | collective-permute-start | bytes 294920 | tf_op jit(solution)/shard_map/ppermute | solution.py:353
  33.1 7.4 %collective-permute-start.8 = (f32[192,128]{1,0:T(8,128)S(1)}, f32[192,128]{1,0:T(8,128)S(1)}, u32[]{:S(2)}, u32[]{:S(2)}) collective-permute-start(f32[192,128]{1,0:T(8,128)S(1)} %get-tuple-element.40), channel_id=1, source_target_pairs={{0,24},{2,26},{4,28},{6,30},{8,16},{10,18},{12,20},{14,22},{16,8},... | collective-permute-start | bytes 294920 | tf_op jit(solution)/shard_map/ppermute | solution.py:353
  36.8 16.5 %all-to-all-start.1 = ((f32[16,56,128]{2,1,0:T(8,128)}), f32[16,56,128]{2,1,0:T(8,128)S(1)}, u32[]{:S(2)}, u32[]{:S(2)}) async-start(f32[16,56,128]{2,1,0:T(8,128)} %mix.1), calls=%async_computation.1 | async-start | bytes 917504 | tf_op jit(solution)/shard_map/all_to_all | solution.py:459
  40.6 12.7 %copy-start.1 = (bf16[128,512]{1,0:T(8,128)(2,1)S(1)}, bf16[128,512]{1,0:T(8,128)(2,1)}, u32[]{:S(2)}) copy-start(bf16[128,512]{1,0:T(8,128)(2,1)} %query.1) | copy-start | bytes 393220
  40.6 12.7 %copy-start.2 = (bf16[128,512]{1,0:T(8,128)(2,1)S(1)}, bf16[128,512]{1,0:T(8,128)(2,1)}, u32[]{:S(2)}) copy-start(bf16[128,512]{1,0:T(8,128)(2,1)} %key.1) | copy-start | bytes 393220
  40.6 12.7 %copy-start.3 = (bf16[128,512]{1,0:T(8,128)(2,1)S(1)}, bf16[128,512]{1,0:T(8,128)(2,1)}, u32[]{:S(2)}) copy-start(bf16[128,512]{1,0:T(8,128)(2,1)} %value.1) | copy-start | bytes 393220
  40.6 12.7 %copy-start.4 = (bf16[128,512]{1,0:T(8,128)(2,1)S(1)}, bf16[128,512]{1,0:T(8,128)(2,1)}, u32[]{:S(2)}) copy-start(bf16[128,512]{1,0:T(8,128)(2,1)} %grad.1) | copy-start | bytes 393220
  40.7 8.6 %collective-permute-start.9 = (f32[288,128]{1,0:T(8,128)S(1)}, f32[288,128]{1,0:T(8,128)S(1)}, u32[]{:S(2)}, u32[]{:S(2)}) collective-permute-start(f32[288,128]{1,0:T(8,128)S(1)} %get-tuple-element.41), channel_id=1, source_target_pairs={{0,2},{2,0},{4,6},{6,4},{8,10},{10,8},{12,14},{14,12},{16,18},{18,... | collective-permute-start | bytes 442376 | tf_op jit(solution)/shard_map/ppermute | solution.py:353
  42.6 8.8 %collective-permute-start.10 = (f32[288,128]{1,0:T(8,128)S(1)}, f32[288,128]{1,0:T(8,128)S(1)}, u32[]{:S(2)}, u32[]{:S(2)}) collective-permute-start(f32[288,128]{1,0:T(8,128)S(1)} %get-tuple-element.42), channel_id=1, source_target_pairs={{0,4},{2,6},{4,0},{6,2},{8,12},{10,14},{12,8},{14,10},{16,20},{18,... | collective-permute-start | bytes 442376 | tf_op jit(solution)/shard_map/ppermute | solution.py:353
  44.1 9.2 %collective-permute-start.11 = (f32[288,128]{1,0:T(8,128)S(1)}, f32[288,128]{1,0:T(8,128)S(1)}, u32[]{:S(2)}, u32[]{:S(2)}) collective-permute-start(f32[288,128]{1,0:T(8,128)S(1)} %get-tuple-element.43), channel_id=1, source_target_pairs={{0,6},{2,4},{4,2},{6,0},{8,14},{10,12},{12,10},{14,8},{16,22},{18,... | collective-permute-start | bytes 442376 | tf_op jit(solution)/shard_map/ppermute | solution.py:353

commit v17 on v16

--- a/solution.py
+++ b/solution.py
@@ -383,7 +383,7 @@
     far_count = blocks // near_count
     product = key.astype(f32) * value.astype(f32)
     mix_grad = out_grad.astype(f32) * query.astype(f32)
-    first_early = share // 32 * 8 if near_count > 1 else 0
+    first_early = share // 32 * 16 if near_count > 1 else 0
     sizes = (share, first_early) if first_early else (share,)
     split_parts = call(
         functools.partial(split_kernel, near_count=near_count, sizes=sizes),

time: 55 us -> 53.8 us (0.978)
  waiting for transfers between devices: 18.5 us -> 16.9 us
    all_to_all x1, waiting for transfers between devices: 3.18 us -> 1.19 us  [body(): gates = lax.all_to_all(packed, 'ctx', 0, 0, tiled=True)]
where the time goes in v17:
time: 53.8 us; the launch traced here: 53.4 us
  starting transfers between devices  28.5 us (53%)
  waiting for transfers between devices  16.9 us (31%)
  Pallas kernels  6 us (11%)
  other arithmetic  1.21 us (2%)
  between operations  0.87 us (2%)
    ppermute x12, starting transfers between devices, exchange(): lax.ppermute(value, axis, [(i, i ^ distance) for i in range(lax.axis_size...  17.2 us
    ppermute x12, waiting for transfers between devices, exchange(): lax.ppermute(value, axis, [(i, i ^ distance) for i in range(lax.axis_size...  15.7 us
    all_to_all x1, starting transfers between devices, body(): gates = lax.all_to_all(packed, 'ctx', 0, 0, tiled=True)  7.1 us
    all_to_all x1, starting transfers between devices, body(): parts = lax.all_to_all(results, 'ctx', 0, 0, tiled=True)  4.12 us
    pallas_call x1, Pallas kernels, body(): call(functools.partial(spectra_kernel, near_count=near_count, first_early...  1.83 us
    pallas_call x1, Pallas kernels, body(): call(functools.partial(mix_kernel, channels=padded, early=early), 'mix',...  1.58 us
    pallas_call x1, Pallas kernels, body(): call(functools.partial(unpack_kernel, far_count=far_count, near_count=nea...  1.4 us
    mul x1, other arithmetic, body(): mix_grad = out_grad.astype(f32) * query.astype(f32)  1.21 us
  transfers between devices with their start and end apart: 14, of which 7 were waited for; matrix products, arithmetic and copies ran while one was open for 0% of the time, Pallas kernels for 5%

profile of v17, /device:TPU:0, one launch (start us, length us, event | category | flops | bytes accessed | tf_op | source)
XLA Modules:
  0.0 53.4 jit_solution(10083114507916201242)
XLA Ops:
  0.6 0.0 copy-start.5
  0.6 1.2 %convert_multiply_fusion = (f32[128,512]{1,0:T(8,128)S(1)}, f32[128,512]{1,0:T(8,128)S(1)}) fusion(bf16[128,512]{1,0:T(8,128)(2,1)} %query.1, bf16[128,512]{1,0:T(8,128)(2,1)} %grad.1, bf16[128,512]{1,0:T(8,128)(2,1)} %value.1, bf16[128,512]{1,0:T(8,128)(2,1)} %key.1), kind=kLoop, calls=%fused_computation | loop fusion | flops 393216 | bytes 1048576 | tf_op jit(solution)/shard_map/mul | solution.py:385
  1.9 0.0 copy-done.5
  1.9 0.2 split.1
  2.1 3.1 %collective-permute-start = (f32[192,128]{1,0:T(8,128)S(1)}, f32[192,128]{1,0:T(8,128)S(1)}, u32[]{:S(2)}, u32[]{:S(2)}) collective-permute-start(f32[192,128]{1,0:T(8,128)S(1)} %get-tuple-element.30), channel_id=1, source_target_pairs={{0,8},{2,10},{4,12},{6,14},{8,0},{10,2},{12,4},{14,6},{16,24},{18,... | collective-permute-start | bytes 294920 | tf_op jit(solution)/shard_map/ppermute | solution.py:353
  5.2 2.6 %collective-permute-start.1 = (f32[192,128]{1,0:T(8,128)S(1)}, f32[192,128]{1,0:T(8,128)S(1)}, u32[]{:S(2)}, u32[]{:S(2)}) collective-permute-start(f32[192,128]{1,0:T(8,128)S(1)} %get-tuple-element.31), channel_id=1, source_target_pairs={{0,16},{2,18},{4,20},{6,22},{8,24},{10,26},{12,28},{14,30},{16,0},... | collective-permute-start | bytes 294920 | tf_op jit(solution)/shard_map/ppermute | solution.py:353
  7.8 0.0 collective-permute-start.2
  7.8 0.9 %pack.1 = f32[16,48,128]{2,1,0:T(8,128)} custom-call(f32[128,512]{1,0:T(8,128)S(1)} %get-tuple-element.52.product.refs_1_, f32[128,512]{1,0:T(8,128)S(1)} %get-tuple-element.51.mix_grad), custom_call_target="tpu_custom_call" | custom-call | bytes 1048576 | tf_op jit(solution)/shard_map/pack/pallas_call | solution.py:397
  8.7 7.1 %all-to-all-start = ((f32[16,48,128]{2,1,0:T(8,128)}), f32[16,48,128]{2,1,0:T(8,128)S(1)}, u32[]{:S(2)}, u32[]{:S(2)}) async-start(f32[16,48,128]{2,1,0:T(8,128)} %pack.1), calls=%async_computation | async-start | bytes 786432 | tf_op jit(solution)/shard_map/all_to_all | solution.py:408
  15.8 0.0 collective-permute-done.refs_3_.rest_1_
  15.8 0.0 collective-permute-done.1.refs_2_.rest_2_
  15.8 0.0 collective-permute-done.2.refs_1_.rest_3_
  15.8 0.0 copy-start
  15.9 0.0 copy-start.6
  15.9 0.0 copy-start.7
  15.9 0.0 copy-start.8
  15.9 2.0 %collective-permute-start.3 = (f32[192,128]{1,0:T(8,128)S(1)}, f32[192,128]{1,0:T(8,128)S(1)}, u32[]{:S(2)}, u32[]{:S(2)}) collective-permute-start(f32[192,128]{1,0:T(8,128)S(1)} %get-tuple-element.33), channel_id=1, source_target_pairs={{0,2},{2,0},{4,6},{6,4},{8,10},{10,8},{12,14},{14,12},{16,18},{18,... | collective-permute-start | bytes 294920 | tf_op jit(solution)/shard_map/ppermute | solution.py:353
  17.9 1.5 %collective-permute-start.4 = (f32[192,128]{1,0:T(8,128)S(1)}, f32[192,128]{1,0:T(8,128)S(1)}, u32[]{:S(2)}, u32[]{:S(2)}) collective-permute-start(f32[192,128]{1,0:T(8,128)S(1)} %get-tuple-element.34), channel_id=1, source_target_pairs={{0,4},{2,6},{4,0},{6,2},{8,12},{10,14},{12,8},{14,10},{16,20},{18,... | collective-permute-start | bytes 294920 | tf_op jit(solution)/shard_map/ppermute | solution.py:353
  19.4 0.1 collective-permute-start.5
  19.5 4.2 %collective-permute-done.3.rest_4_ = f32[192,128]{1,0:T(8,128)S(1)} collective-permute-done((f32[192,128]{1,0:T(8,128)S(1)}, f32[192,128]{1,0:T(8,128)S(1)}, u32[]{:S(2)}, u32[]{:S(2)}) %collective-permute-start.3) | collective-permute-done | bytes 98336 | tf_op jit(solution)/shard_map/ppermute | solution.py:353
  23.7 0.8 %collective-permute-done.4.rest_5_ = f32[192,128]{1,0:T(8,128)S(1)} collective-permute-done((f32[192,128]{1,0:T(8,128)S(1)}, f32[192,128]{1,0:T(8,128)S(1)}, u32[]{:S(2)}, u32[]{:S(2)}) %collective-permute-start.4) | collective-permute-done | bytes 98336 | tf_op jit(solution)/shard_map/ppermute | solution.py:353
  24.5 1.8 %collective-permute-done.5.rest_6_ = f32[192,128]{1,0:T(8,128)S(1)} collective-permute-done((f32[192,128]{1,0:T(8,128)S(1)}, f32[192,128]{1,0:T(8,128)S(1)}, u32[]{:S(2)}, u32[]{:S(2)}) %collective-permute-start.5) | collective-permute-done | bytes 98336 | tf_op jit(solution)/shard_map/ppermute | solution.py:353
  26.4 1.2 %all-to-all-done.gates = f32[16,48,128]{2,1,0:T(8,128)S(1)} async-done(((f32[16,48,128]{2,1,0:T(8,128)}), f32[16,48,128]{2,1,0:T(8,128)S(1)}, u32[]{:S(2)}, u32[]{:S(2)}) %all-to-all-start) | async-done | bytes 393248 | tf_op jit(solution)/shard_map/all_to_all | solution.py:408
  27.6 0.0 copy-done
  27.6 0.0 copy-done.6
  27.6 0.0 copy-done.7
  27.6 0.0 copy-done.8
  27.6 1.8 %spectra.1 = (f32[2,544,256]{2,1,0:T(8,128)S(1)}, f32[192,128]{1,0:T(8,128)S(1)}, f32[192,128]{1,0:T(8,128)S(1)}, f32[192,128]{1,0:T(8,128)S(1)}, f32[192,128]{1,0:T(8,128)S(1)}) custom-call(f32[128,512]{1,0:T(8,128)S(1)} %copy-done.7, f32[1,512]{1,0:T(1,128)S(1)} %bitcast.2, bf16[4,256,256]{2,1,0:T(8,128)(2,1)S(1)} %copy-done, f32[17,4,128]{2,1,0:T(4,128)S(1)} %copy-done.6, ...), custom_call_target="tpu_custom_call" | custom-call | flops 962592768 | bytes 1572864 | tf_op jit(solution)/shard_map/spectra/pallas_call | solution.py:425
  29.4 1.2 %collective-permute-start.6 = (f32[192,128]{1,0:T(8,128)S(1)}, f32[192,128]{1,0:T(8,128)S(1)}, u32[]{:S(2)}, u32[]{:S(2)}) collective-permute-start(f32[192,128]{1,0:T(8,128)S(1)} %get-tuple-element.38), channel_id=1, source_target_pairs={{0,8},{2,10},{4,12},{6,14},{8,0},{10,2},{12,4},{14,6},{16,24},{18,... | collective-permute-start | bytes 294920 | tf_op jit(solution)/shard_map/ppermute | solution.py:353
  30.6 1.9 %collective-permute-start.7 = (f32[192,128]{1,0:T(8,128)S(1)}, f32[192,128]{1,0:T(8,128)S(1)}, u32[]{:S(2)}, u32[]{:S(2)}) collective-permute-start(f32[192,128]{1,0:T(8,128)S(1)} %get-tuple-element.39), channel_id=1, source_target_pairs={{0,16},{2,18},{4,20},{6,22},{8,24},{10,26},{12,28},{14,30},{16,0},... | collective-permute-start | bytes 294920 | tf_op jit(solution)/shard_map/ppermute | solution.py:353
  32.5 1.4 %collective-permute-start.8 = (f32[192,128]{1,0:T(8,128)S(1)}, f32[192,128]{1,0:T(8,128)S(1)}, u32[]{:S(2)}, u32[]{:S(2)}) collective-permute-start(f32[192,128]{1,0:T(8,128)S(1)} %get-tuple-element.40), channel_id=1, source_target_pairs={{0,24},{2,26},{4,28},{6,30},{8,16},{10,18},{12,20},{14,22},{16,8},... | collective-permute-start | bytes 294920 | tf_op jit(solution)/shard_map/ppermute | solution.py:353
  33.9 1.6 %mix.1 = f32[16,56,128]{2,1,0:T(8,128)} custom-call(bf16[4,256,256]{2,1,0:T(8,128)(2,1)S(1)} %copy-done, f32[17,4,128]{2,1,0:T(4,128)S(1)} %copy-done.6, f32[2,544,256]{2,1,0:T(8,128)S(1)} %get-tuple-element.36.products), custom_call_target="tpu_custom_call" | custom-call | flops 320864256 | bytes 1572864 | tf_op jit(solution)/shard_map/mix/pallas_call | solution.py:448
  35.5 4.1 %all-to-all-start.1 = ((f32[16,56,128]{2,1,0:T(8,128)}), f32[16,56,128]{2,1,0:T(8,128)S(1)}, u32[]{:S(2)}, u32[]{:S(2)}) async-start(f32[16,56,128]{2,1,0:T(8,128)} %mix.1), calls=%async_computation.1 | async-start | bytes 917504 | tf_op jit(solution)/shard_map/all_to_all | solution.py:459
  39.6 0.0 collective-permute-done.6.refs_3_.rest_1_
  39.6 0.0 collective-permute-done.7.refs_2_.rest_2_
  39.6 0.0 collective-permute-done.8.refs_1_.rest_3_
  39.6 0.0 copy-start.1
  39.6 0.0 copy-start.2
  39.6 0.0 copy-start.3
  39.6 0.0 copy-start.4
  39.7 2.0 %collective-permute-start.9 = (f32[288,128]{1,0:T(8,128)S(1)}, f32[288,128]{1,0:T(8,128)S(1)}, u32[]{:S(2)}, u32[]{:S(2)}) collective-permute-start(f32[288,128]{1,0:T(8,128)S(1)} %get-tuple-element.41), channel_id=1, source_target_pairs={{0,2},{2,0},{4,6},{6,4},{8,10},{10,8},{12,14},{14,12},{16,18},{18,... | collective-permute-start | bytes 442376 | tf_op jit(solution)/shard_map/ppermute | solution.py:353
  41.7 1.5 %collective-permute-start.10 = (f32[288,128]{1,0:T(8,128)S(1)}, f32[288,128]{1,0:T(8,128)S(1)}, u32[]{:S(2)}, u32[]{:S(2)}) collective-permute-start(f32[288,128]{1,0:T(8,128)S(1)} %get-tuple-element.42), channel_id=1, source_target_pairs={{0,4},{2,6},{4,0},{6,2},{8,12},{10,14},{12,8},{14,10},{16,20},{18,... | collective-permute-start | bytes 442376 | tf_op jit(solution)/shard_map/ppermute | solution.py:353
  43.2 0.1 collective-permute-start.11
  43.3 4.8 %collective-permute-done.9.rest_4_ = f32[288,128]{1,0:T(8,128)S(1)} collective-permute-done((f32[288,128]{1,0:T(8,128)S(1)}, f32[288,128]{1,0:T(8,128)S(1)}, u32[]{:S(2)}, u32[]{:S(2)}) %collective-permute-start.9) | collective-permute-done | bytes 147488 | tf_op jit(solution)/shard_map/ppermute | solution.py:353
  48.0 2.2 %collective-permute-done.10.rest_5_ = f32[288,128]{1,0:T(8,128)S(1)} collective-permute-done((f32[288,128]{1,0:T(8,128)S(1)}, f32[288,128]{1,0:T(8,128)S(1)}, u32[]{:S(2)}, u32[]{:S(2)}) %collective-permute-start.10) | collective-permute-done | bytes 147488 | tf_op jit(solution)/shard_map/ppermute | solution.py:353
  50.2 1.8 %collective-permute-done.11.rest_6_ = f32[288,128]{1,0:T(8,128)S(1)} collective-permute-done((f32[288,128]{1,0:T(8,128)S(1)}, f32[288,128]{1,0:T(8,128)S(1)}, u32[]{:S(2)}, u32[]{:S(2)}) %collective-permute-start.11) | collective-permute-done | bytes 147488 | tf_op jit(solution)/shard_map/ppermute | solution.py:353
  52.0 0.0 all-to-all-done.1.parts
  52.0 0.0 copy-done.1
  52.0 0.0 copy-done.2
  52.0 0.0 copy-done.3
  52.0 0.0 copy-done.4
  52.0 1.4 %unpack.1 = (f32[128,512]{1,0:T(8,128)}, f32[128,512]{1,0:T(8,128)}, f32[128,512]{1,0:T(8,128)}, f32[128,512]{1,0:T(8,128)}, f32[128,512]{1,0:T(8,128)}, /*index=5*/f32[128,512]{1,0:T(8,128)}, f32[1,512]{1,0:T(1,128)}) custom-call(bf16[128,512]{1,0:T(8,128)(2,1)S(1)} %copy-done.1, bf16[128,512]{1,0:T(8,128)(2,1)S(1)} %copy-done.2, ...), custom_call_target="tpu_custom_call" | custom-call | bytes 3145728 | tf_op jit(solution)/shard_map/unpack/pallas_call | solution.py:466
  (2 shorter events, 0.1 us)
Async XLA Ops:
  0.6 1.2 %copy-start.5 = (f32[128,512]{1,0:T(8,128)S(1)}, f32[128,512]{1,0:T(8,128)}, u32[]{:S(2)}) copy-start(f32[128,512]{1,0:T(8,128)} %refs_0_.1) | copy-start | bytes 786436
  2.1 13.7 %collective-permute-start = (f32[192,128]{1,0:T(8,128)S(1)}, f32[192,128]{1,0:T(8,128)S(1)}, u32[]{:S(2)}, u32[]{:S(2)}) collective-permute-start(f32[192,128]{1,0:T(8,128)S(1)} %get-tuple-element.30), channel_id=1, source_target_pairs={{0,8},{2,10},{4,12},{6,14},{8,0},{10,2},{12,4},{14,6},{16,24},{18,... | collective-permute-start | bytes 294920 | tf_op jit(solution)/shard_map/ppermute | solution.py:353
  5.2 10.6 %collective-permute-start.1 = (f32[192,128]{1,0:T(8,128)S(1)}, f32[192,128]{1,0:T(8,128)S(1)}, u32[]{:S(2)}, u32[]{:S(2)}) collective-permute-start(f32[192,128]{1,0:T(8,128)S(1)} %get-tuple-element.31), channel_id=1, source_target_pairs={{0,16},{2,18},{4,20},{6,22},{8,24},{10,26},{12,28},{14,30},{16,0},... | collective-permute-start | bytes 294920 | tf_op jit(solution)/shard_map/ppermute | solution.py:353
  7.8 8.1 %collective-permute-start.2 = (f32[192,128]{1,0:T(8,128)S(1)}, f32[192,128]{1,0:T(8,128)S(1)}, u32[]{:S(2)}, u32[]{:S(2)}) collective-permute-start(f32[192,128]{1,0:T(8,128)S(1)} %get-tuple-element.32), channel_id=1, source_target_pairs={{0,24},{2,26},{4,28},{6,30},{8,16},{10,18},{12,20},{14,22},{16,8},... | collective-permute-start | bytes 294920 | tf_op jit(solution)/shard_map/ppermute | solution.py:353
  8.7 18.9 %all-to-all-start = ((f32[16,48,128]{2,1,0:T(8,128)}), f32[16,48,128]{2,1,0:T(8,128)S(1)}, u32[]{:S(2)}, u32[]{:S(2)}) async-start(f32[16,48,128]{2,1,0:T(8,128)} %pack.1), calls=%async_computation | async-start | bytes 786432 | tf_op jit(solution)/shard_map/all_to_all | solution.py:408
  15.8 11.7 %copy-start = (bf16[4,256,256]{2,1,0:T(8,128)(2,1)S(1)}, bf16[4,256,256]{2,1,0:T(8,128)(2,1)}, u32[]{:S(2)}) copy-start(bf16[4,256,256]{2,1,0:T(8,128)(2,1)} %constant.4.clone.matrices) | copy-start | bytes 1572868
  15.9 11.7 %copy-start.6 = (f32[17,4,128]{2,1,0:T(4,128)S(1)}, f32[17,4,128]{2,1,0:T(4,128)}, u32[]{:S(2)}) copy-start(f32[17,4,128]{2,1,0:T(4,128)} %constant.5.clone.twists) | copy-start | bytes 104452
  15.9 11.7 %copy-start.7 = (f32[128,512]{1,0:T(8,128)S(1)}, f32[128,512]{1,0:T(8,128)}, u32[]{:S(2)}) copy-start(f32[128,512]{1,0:T(8,128)} %taps.1) | copy-start | bytes 786436
  15.9 11.7 %copy-start.8 = (f32[512]{0:T(512)S(1)}, f32[512]{0:T(512)}, u32[]{:S(2)}) copy-start(f32[512]{0:T(512)} %param.14) | copy-start | bytes 6148
  15.9 7.8 %collective-permute-start.3 = (f32[192,128]{1,0:T(8,128)S(1)}, f32[192,128]{1,0:T(8,128)S(1)}, u32[]{:S(2)}, u32[]{:S(2)}) collective-permute-start(f32[192,128]{1,0:T(8,128)S(1)} %get-tuple-element.33), channel_id=1, source_target_pairs={{0,2},{2,0},{4,6},{6,4},{8,10},{10,8},{12,14},{14,12},{16,18},{18,... | collective-permute-start | bytes 294920 | tf_op jit(solution)/shard_map/ppermute | solution.py:353
  17.9 6.6 %collective-permute-start.4 = (f32[192,128]{1,0:T(8,128)S(1)}, f32[192,128]{1,0:T(8,128)S(1)}, u32[]{:S(2)}, u32[]{:S(2)}) collective-permute-start(f32[192,128]{1,0:T(8,128)S(1)} %get-tuple-element.34), channel_id=1, source_target_pairs={{0,4},{2,6},{4,0},{6,2},{8,12},{10,14},{12,8},{14,10},{16,20},{18,... | collective-permute-start | bytes 294920 | tf_op jit(solution)/shard_map/ppermute | solution.py:353
  19.4 7.0 %collective-permute-start.5 = (f32[192,128]{1,0:T(8,128)S(1)}, f32[192,128]{1,0:T(8,128)S(1)}, u32[]{:S(2)}, u32[]{:S(2)}) collective-permute-start(f32[192,128]{1,0:T(8,128)S(1)} %get-tuple-element.35), channel_id=1, source_target_pairs={{0,6},{2,4},{4,2},{6,0},{8,14},{10,12},{12,10},{14,8},{16,22},{18,... | collective-permute-start | bytes 294920 | tf_op jit(solution)/shard_map/ppermute | solution.py:353
  29.4 10.2 %collective-permute-start.6 = (f32[192,128]{1,0:T(8,128)S(1)}, f32[192,128]{1,0:T(8,128)S(1)}, u32[]{:S(2)}, u32[]{:S(2)}) collective-permute-start(f32[192,128]{1,0:T(8,128)S(1)} %get-tuple-element.38), channel_id=1, source_target_pairs={{0,8},{2,10},{4,12},{6,14},{8,0},{10,2},{12,4},{14,6},{16,24},{18,... | collective-permute-start | bytes 294920 | tf_op jit(solution)/shard_map/ppermute | solution.py:353
  30.6 9.0 %collective-permute-start.7 = (f32[192,128]{1,0:T(8,128)S(1)}, f32[192,128]{1,0:T(8,128)S(1)}, u32[]{:S(2)}, u32[]{:S(2)}) collective-permute-start(f32[192,128]{1,0:T(8,128)S(1)} %get-tuple-element.39), channel_id=1, source_target_pairs={{0,16},{2,18},{4,20},{6,22},{8,24},{10,26},{12,28},{14,30},{16,0},... | collective-permute-start | bytes 294920 | tf_op jit(solution)/shard_map/ppermute | solution.py:353
  32.5 7.1 %collective-permute-start.8 = (f32[192,128]{1,0:T(8,128)S(1)}, f32[192,128]{1,0:T(8,128)S(1)}, u32[]{:S(2)}, u32[]{:S(2)}) collective-permute-start(f32[192,128]{1,0:T(8,128)S(1)} %get-tuple-element.40), channel_id=1, source_target_pairs={{0,24},{2,26},{4,28},{6,30},{8,16},{10,18},{12,20},{14,22},{16,8},... | collective-permute-start | bytes 294920 | tf_op jit(solution)/shard_map/ppermute | solution.py:353
  35.5 16.6 %all-to-all-start.1 = ((f32[16,56,128]{2,1,0:T(8,128)}), f32[16,56,128]{2,1,0:T(8,128)S(1)}, u32[]{:S(2)}, u32[]{:S(2)}) async-start(f32[16,56,128]{2,1,0:T(8,128)} %mix.1), calls=%async_computation.1 | async-start | bytes 917504 | tf_op jit(solution)/shard_map/all_to_all | solution.py:459
  39.6 12.4 %copy-start.1 = (bf16[128,512]{1,0:T(8,128)(2,1)S(1)}, bf16[128,512]{1,0:T(8,128)(2,1)}, u32[]{:S(2)}) copy-start(bf16[128,512]{1,0:T(8,128)(2,1)} %query.1) | copy-start | bytes 393220
  39.6 12.4 %copy-start.2 = (bf16[128,512]{1,0:T(8,128)(2,1)S(1)}, bf16[128,512]{1,0:T(8,128)(2,1)}, u32[]{:S(2)}) copy-start(bf16[128,512]{1,0:T(8,128)(2,1)} %key.1) | copy-start | bytes 393220
  39.6 12.4 %copy-start.3 = (bf16[128,512]{1,0:T(8,128)(2,1)S(1)}, bf16[128,512]{1,0:T(8,128)(2,1)}, u32[]{:S(2)}) copy-start(bf16[128,512]{1,0:T(8,128)(2,1)} %value.1) | copy-start | bytes 393220
  39.6 12.4 %copy-start.4 = (bf16[128,512]{1,0:T(8,128)(2,1)S(1)}, bf16[128,512]{1,0:T(8,128)(2,1)}, u32[]{:S(2)}) copy-start(bf16[128,512]{1,0:T(8,128)(2,1)} %grad.1) | copy-start | bytes 393220
  39.7 8.3 %collective-permute-start.9 = (f32[288,128]{1,0:T(8,128)S(1)}, f32[288,128]{1,0:T(8,128)S(1)}, u32[]{:S(2)}, u32[]{:S(2)}) collective-permute-start(f32[288,128]{1,0:T(8,128)S(1)} %get-tuple-element.41), channel_id=1, source_target_pairs={{0,2},{2,0},{4,6},{6,4},{8,10},{10,8},{12,14},{14,12},{16,18},{18,... | collective-permute-start | bytes 442376 | tf_op jit(solution)/shard_map/ppermute | solution.py:353
  41.7 8.5 %collective-permute-start.10 = (f32[288,128]{1,0:T(8,128)S(1)}, f32[288,128]{1,0:T(8,128)S(1)}, u32[]{:S(2)}, u32[]{:S(2)}) collective-permute-start(f32[288,128]{1,0:T(8,128)S(1)} %get-tuple-element.42), channel_id=1, source_target_pairs={{0,4},{2,6},{4,0},{6,2},{8,12},{10,14},{12,8},{14,10},{16,20},{18,... | collective-permute-start | bytes 442376 | tf_op jit(solution)/shard_map/ppermute | solution.py:353
  43.2 8.9 %collective-permute-start.11 = (f32[288,128]{1,0:T(8,128)S(1)}, f32[288,128]{1,0:T(8,128)S(1)}, u32[]{:S(2)}, u32[]{:S(2)}) collective-permute-start(f32[288,128]{1,0:T(8,128)S(1)} %get-tuple-element.43), channel_id=1, source_target_pairs={{0,6},{2,4},{4,2},{6,0},{8,14},{10,12},{12,10},{14,8},{16,22},{18,... | collective-permute-start | bytes 442376 | tf_op jit(solution)/shard_map/ppermute | solution.py:353

commit v18 on v17

--- a/solution.py
+++ b/solution.py
@@ -383,7 +383,7 @@
     far_count = blocks // near_count
     product = key.astype(f32) * value.astype(f32)
     mix_grad = out_grad.astype(f32) * query.astype(f32)
-    first_early = share // 32 * 16 if near_count > 1 else 0
+    first_early = share // 32 * 24 if near_count > 1 else 0
     sizes = (share, first_early) if first_early else (share,)
     split_parts = call(
         functools.partial(split_kernel, near_count=near_count, sizes=sizes),

time: 53.8 us -> 55.7 us (1.035)
  the two profiles are of different devices: /device:TPU:0 before, /device:TPU:18 now
where the time goes in v18:
time: 55.7 us; the launch traced here: 55.4 us
  starting transfers between devices  30 us (54%)
  waiting for transfers between devices  17.4 us (31%)
  Pallas kernels  5.97 us (11%)
  other arithmetic  1.21 us (2%)
  between operations  0.8 us (1%)
    ppermute x12, waiting for transfers between devices, exchange(): lax.ppermute(value, axis, [(i, i ^ distance) for i in range(lax.axis_size...  17.4 us
    ppermute x12, starting transfers between devices, exchange(): lax.ppermute(value, axis, [(i, i ^ distance) for i in range(lax.axis_size...  16.4 us
    all_to_all x1, starting transfers between devices, body(): gates = lax.all_to_all(packed, 'ctx', 0, 0, tiled=True)  8 us
    all_to_all x1, starting transfers between devices, body(): parts = lax.all_to_all(results, 'ctx', 0, 0, tiled=True)  5.59 us
    pallas_call x1, Pallas kernels, body(): call(functools.partial(spectra_kernel, near_count=near_count, first_early...  1.83 us
    pallas_call x1, Pallas kernels, body(): call(functools.partial(mix_kernel, channels=padded, early=early), 'mix',...  1.59 us
    pallas_call x1, Pallas kernels, body(): call(functools.partial(unpack_kernel, far_count=far_count, near_count=nea...  1.4 us
    mul x1, other arithmetic, body(): mix_grad = out_grad.astype(f32) * query.astype(f32)  1.21 us
  transfers between devices with their start and end apart: 14, of which 7 were waited for; matrix products, arithmetic and copies ran while one was open for 0% of the time, Pallas kernels for 5%

profile of v18, /device:TPU:18, one launch (start us, length us, event | category | flops | bytes accessed | tf_op | source)
XLA Modules:
  0.0 55.4 jit_solution(2916783784548606525)
XLA Ops:
  0.6 0.0 copy-start.5
  0.6 1.2 %convert_multiply_fusion = (f32[128,512]{1,0:T(8,128)S(1)}, f32[128,512]{1,0:T(8,128)S(1)}) fusion(bf16[128,512]{1,0:T(8,128)(2,1)} %query.1, bf16[128,512]{1,0:T(8,128)(2,1)} %grad.1, bf16[128,512]{1,0:T(8,128)(2,1)} %value.1, bf16[128,512]{1,0:T(8,128)(2,1)} %key.1), kind=kLoop, calls=%fused_computation | loop fusion | flops 393216 | bytes 1048576 | tf_op jit(solution)/shard_map/mul | solution.py:385
  1.9 0.0 copy-done.5
  1.9 0.2 split.1
  2.1 1.6 %collective-permute-start = (f32[224,128]{1,0:T(8,128)S(1)}, f32[224,128]{1,0:T(8,128)S(1)}, u32[]{:S(2)}, u32[]{:S(2)}) collective-permute-start(f32[224,128]{1,0:T(8,128)S(1)} %get-tuple-element.30), channel_id=1, source_target_pairs={{0,8},{2,10},{4,12},{6,14},{8,0},{10,2},{12,4},{14,6},{16,24},{18,... | collective-permute-start | bytes 344072 | tf_op jit(solution)/shard_map/ppermute | solution.py:353
  3.7 0.3 collective-permute-start.1
  4.1 1.6 %collective-permute-start.2 = (f32[224,128]{1,0:T(8,128)S(1)}, f32[224,128]{1,0:T(8,128)S(1)}, u32[]{:S(2)}, u32[]{:S(2)}) collective-permute-start(f32[224,128]{1,0:T(8,128)S(1)} %get-tuple-element.32), channel_id=1, source_target_pairs={{0,24},{2,26},{4,28},{6,30},{8,16},{10,18},{12,20},{14,22},{16,8},... | collective-permute-start | bytes 344072 | tf_op jit(solution)/shard_map/ppermute | solution.py:353
  5.7 0.9 %pack.1 = f32[16,40,128]{2,1,0:T(8,128)} custom-call(f32[128,512]{1,0:T(8,128)S(1)} %get-tuple-element.52.product.refs_1_, f32[128,512]{1,0:T(8,128)S(1)} %get-tuple-element.51.mix_grad), custom_call_target="tpu_custom_call" | custom-call | bytes 1048576 | tf_op jit(solution)/shard_map/pack/pallas_call | solution.py:397
  6.5 8.0 %all-to-all-start = ((f32[16,40,128]{2,1,0:T(8,128)}), f32[16,40,128]{2,1,0:T(8,128)S(1)}, u32[]{:S(2)}, u32[]{:S(2)}) async-start(f32[16,40,128]{2,1,0:T(8,128)} %pack.1), calls=%async_computation | async-start | bytes 655360 | tf_op jit(solution)/shard_map/all_to_all | solution.py:408
  14.5 0.0 collective-permute-done.refs_3_.rest_1_
  14.5 0.0 collective-permute-done.1.refs_2_.rest_2_
  14.6 5.6 %collective-permute-done.2.refs_1_.rest_3_ = f32[224,128]{1,0:T(8,128)S(1)} collective-permute-done((f32[224,128]{1,0:T(8,128)S(1)}, f32[224,128]{1,0:T(8,128)S(1)}, u32[]{:S(2)}, u32[]{:S(2)}) %collective-permute-start.2) | collective-permute-done | bytes 114720 | tf_op jit(solution)/shard_map/ppermute | solution.py:353
  20.2 0.0 copy-start
  20.2 0.0 copy-start.6
  20.2 0.0 copy-start.7
  20.2 0.0 copy-start.8
  20.2 0.6 %collective-permute-start.3 = (f32[224,128]{1,0:T(8,128)S(1)}, f32[224,128]{1,0:T(8,128)S(1)}, u32[]{:S(2)}, u32[]{:S(2)}) collective-permute-start(f32[224,128]{1,0:T(8,128)S(1)} %get-tuple-element.33), channel_id=1, source_target_pairs={{0,2},{2,0},{4,6},{6,4},{8,10},{10,8},{12,14},{14,12},{16,18},{18,... | collective-permute-start | bytes 344072 | tf_op jit(solution)/shard_map/ppermute | solution.py:353
  20.8 1.6 %collective-permute-start.4 = (f32[224,128]{1,0:T(8,128)S(1)}, f32[224,128]{1,0:T(8,128)S(1)}, u32[]{:S(2)}, u32[]{:S(2)}) collective-permute-start(f32[224,128]{1,0:T(8,128)S(1)} %get-tuple-element.34), channel_id=1, source_target_pairs={{0,4},{2,6},{4,0},{6,2},{8,12},{10,14},{12,8},{14,10},{16,20},{18,... | collective-permute-start | bytes 344072 | tf_op jit(solution)/shard_map/ppermute | solution.py:353
  22.4 1.4 %collective-permute-start.5 = (f32[224,128]{1,0:T(8,128)S(1)}, f32[224,128]{1,0:T(8,128)S(1)}, u32[]{:S(2)}, u32[]{:S(2)}) collective-permute-start(f32[224,128]{1,0:T(8,128)S(1)} %get-tuple-element.35), channel_id=1, source_target_pairs={{0,6},{2,4},{4,2},{6,0},{8,14},{10,12},{12,10},{14,8},{16,22},{18,... | collective-permute-start | bytes 344072 | tf_op jit(solution)/shard_map/ppermute | solution.py:353
  23.8 1.3 %collective-permute-done.3.rest_4_ = f32[224,128]{1,0:T(8,128)S(1)} collective-permute-done((f32[224,128]{1,0:T(8,128)S(1)}, f32[224,128]{1,0:T(8,128)S(1)}, u32[]{:S(2)}, u32[]{:S(2)}) %collective-permute-start.3) | collective-permute-done | bytes 114720 | tf_op jit(solution)/shard_map/ppermute | solution.py:353
  25.1 0.5 collective-permute-done.4.rest_5_
  25.6 2.5 %collective-permute-done.5.rest_6_ = f32[224,128]{1,0:T(8,128)S(1)} collective-permute-done((f32[224,128]{1,0:T(8,128)S(1)}, f32[224,128]{1,0:T(8,128)S(1)}, u32[]{:S(2)}, u32[]{:S(2)}) %collective-permute-start.5) | collective-permute-done | bytes 114720 | tf_op jit(solution)/shard_map/ppermute | solution.py:353
  28.0 0.0 all-to-all-done.gates
  28.0 0.0 copy-done
  28.1 0.0 copy-done.6
  28.1 0.0 copy-done.7
  28.1 0.0 copy-done.8
  28.1 1.8 %spectra.1 = (f32[2,544,256]{2,1,0:T(8,128)S(1)}, f32[192,128]{1,0:T(8,128)S(1)}, f32[192,128]{1,0:T(8,128)S(1)}, f32[192,128]{1,0:T(8,128)S(1)}, f32[192,128]{1,0:T(8,128)S(1)}) custom-call(f32[128,512]{1,0:T(8,128)S(1)} %copy-done.7, f32[1,512]{1,0:T(1,128)S(1)} %bitcast.2, bf16[4,256,256]{2,1,0:T(8,128)(2,1)S(1)} %copy-done, f32[17,4,128]{2,1,0:T(4,128)S(1)} %copy-done.6, ...), custom_call_target="tpu_custom_call" | custom-call | flops 962592768 | bytes 1572864 | tf_op jit(solution)/shard_map/spectra/pallas_call | solution.py:425
  29.9 0.1 collective-permute-start.6
  30.0 0.8 %collective-permute-start.7 = (f32[192,128]{1,0:T(8,128)S(1)}, f32[192,128]{1,0:T(8,128)S(1)}, u32[]{:S(2)}, u32[]{:S(2)}) collective-permute-start(f32[192,128]{1,0:T(8,128)S(1)} %get-tuple-element.39), channel_id=1, source_target_pairs={{0,16},{2,18},{4,20},{6,22},{8,24},{10,26},{12,28},{14,30},{16,0},... | collective-permute-start | bytes 294920 | tf_op jit(solution)/shard_map/ppermute | solution.py:353
  30.8 2.6 %collective-permute-start.8 = (f32[192,128]{1,0:T(8,128)S(1)}, f32[192,128]{1,0:T(8,128)S(1)}, u32[]{:S(2)}, u32[]{:S(2)}) collective-permute-start(f32[192,128]{1,0:T(8,128)S(1)} %get-tuple-element.40), channel_id=1, source_target_pairs={{0,24},{2,26},{4,28},{6,30},{8,16},{10,18},{12,20},{14,22},{16,8},... | collective-permute-start | bytes 294920 | tf_op jit(solution)/shard_map/ppermute | solution.py:353
  33.5 1.6 %mix.1 = f32[16,56,128]{2,1,0:T(8,128)} custom-call(bf16[4,256,256]{2,1,0:T(8,128)(2,1)S(1)} %copy-done, f32[17,4,128]{2,1,0:T(4,128)S(1)} %copy-done.6, f32[2,544,256]{2,1,0:T(8,128)S(1)} %get-tuple-element.36.products), custom_call_target="tpu_custom_call" | custom-call | flops 320864256 | bytes 1572864 | tf_op jit(solution)/shard_map/mix/pallas_call | solution.py:448
  35.1 5.6 %all-to-all-start.1 = ((f32[16,56,128]{2,1,0:T(8,128)}), f32[16,56,128]{2,1,0:T(8,128)S(1)}, u32[]{:S(2)}, u32[]{:S(2)}) async-start(f32[16,56,128]{2,1,0:T(8,128)} %mix.1), calls=%async_computation.1 | async-start | bytes 917504 | tf_op jit(solution)/shard_map/all_to_all | solution.py:459
  40.7 0.0 collective-permute-done.6.refs_3_.rest_1_
  40.7 0.0 collective-permute-done.7.refs_2_.rest_2_
  40.7 2.3 %collective-permute-done.8.refs_1_.rest_3_ = f32[192,128]{1,0:T(8,128)S(1)} collective-permute-done((f32[192,128]{1,0:T(8,128)S(1)}, f32[192,128]{1,0:T(8,128)S(1)}, u32[]{:S(2)}, u32[]{:S(2)}) %collective-permute-start.8) | collective-permute-done | bytes 98336 | tf_op jit(solution)/shard_map/ppermute | solution.py:353
  43.0 0.0 copy-start.1
  43.0 0.0 copy-start.2
  43.0 0.0 copy-start.3
  43.0 0.0 copy-start.4
  43.0 4.2 %collective-permute-start.9 = (f32[288,128]{1,0:T(8,128)S(1)}, f32[288,128]{1,0:T(8,128)S(1)}, u32[]{:S(2)}, u32[]{:S(2)}) collective-permute-start(f32[288,128]{1,0:T(8,128)S(1)} %get-tuple-element.41), channel_id=1, source_target_pairs={{0,2},{2,0},{4,6},{6,4},{8,10},{10,8},{12,14},{14,12},{16,18},{18,... | collective-permute-start | bytes 442376 | tf_op jit(solution)/shard_map/ppermute | solution.py:353
  47.2 0.0 collective-permute-start.10
  47.2 1.5 %collective-permute-start.11 = (f32[288,128]{1,0:T(8,128)S(1)}, f32[288,128]{1,0:T(8,128)S(1)}, u32[]{:S(2)}, u32[]{:S(2)}) collective-permute-start(f32[288,128]{1,0:T(8,128)S(1)} %get-tuple-element.43), channel_id=1, source_target_pairs={{0,6},{2,4},{4,2},{6,0},{8,14},{10,12},{12,10},{14,8},{16,22},{18,... | collective-permute-start | bytes 442376 | tf_op jit(solution)/shard_map/ppermute | solution.py:353
  48.8 1.7 %collective-permute-done.9.rest_4_ = f32[288,128]{1,0:T(8,128)S(1)} collective-permute-done((f32[288,128]{1,0:T(8,128)S(1)}, f32[288,128]{1,0:T(8,128)S(1)}, u32[]{:S(2)}, u32[]{:S(2)}) %collective-permute-start.9) | collective-permute-done | bytes 147488 | tf_op jit(solution)/shard_map/ppermute | solution.py:353
  50.5 3.5 %collective-permute-done.10.rest_5_ = f32[288,128]{1,0:T(8,128)S(1)} collective-permute-done((f32[288,128]{1,0:T(8,128)S(1)}, f32[288,128]{1,0:T(8,128)S(1)}, u32[]{:S(2)}, u32[]{:S(2)}) %collective-permute-start.10) | collective-permute-done | bytes 147488 | tf_op jit(solution)/shard_map/ppermute | solution.py:353
  54.0 0.0 collective-permute-done.11.rest_6_
  54.0 0.0 all-to-all-done.1.parts
  54.0 0.0 copy-done.1
  54.0 0.0 copy-done.2
  54.0 0.0 copy-done.3
  54.0 0.0 copy-done.4
  54.0 1.4 %unpack.1 = (f32[128,512]{1,0:T(8,128)}, f32[128,512]{1,0:T(8,128)}, f32[128,512]{1,0:T(8,128)}, f32[128,512]{1,0:T(8,128)}, f32[128,512]{1,0:T(8,128)}, /*index=5*/f32[128,512]{1,0:T(8,128)}, f32[1,512]{1,0:T(1,128)}) custom-call(bf16[128,512]{1,0:T(8,128)(2,1)S(1)} %copy-done.1, bf16[128,512]{1,0:T(8,128)(2,1)S(1)} %copy-done.2, ...), custom_call_target="tpu_custom_call" | custom-call | bytes 3145728 | tf_op jit(solution)/shard_map/unpack/pallas_call | solution.py:466
  (2 shorter events, 0.1 us)
Async XLA Ops:
  0.6 1.2 %copy-start.5 = (f32[128,512]{1,0:T(8,128)S(1)}, f32[128,512]{1,0:T(8,128)}, u32[]{:S(2)}) copy-start(f32[128,512]{1,0:T(8,128)} %refs_0_.1) | copy-start | bytes 786436
  2.1 12.4 %collective-permute-start = (f32[224,128]{1,0:T(8,128)S(1)}, f32[224,128]{1,0:T(8,128)S(1)}, u32[]{:S(2)}, u32[]{:S(2)}) collective-permute-start(f32[224,128]{1,0:T(8,128)S(1)} %get-tuple-element.30), channel_id=1, source_target_pairs={{0,8},{2,10},{4,12},{6,14},{8,0},{10,2},{12,4},{14,6},{16,24},{18,... | collective-permute-start | bytes 344072 | tf_op jit(solution)/shard_map/ppermute | solution.py:353
  3.7 10.8 %collective-permute-start.1 = (f32[224,128]{1,0:T(8,128)S(1)}, f32[224,128]{1,0:T(8,128)S(1)}, u32[]{:S(2)}, u32[]{:S(2)}) collective-permute-start(f32[224,128]{1,0:T(8,128)S(1)} %get-tuple-element.31), channel_id=1, source_target_pairs={{0,16},{2,18},{4,20},{6,22},{8,24},{10,26},{12,28},{14,30},{16,0},... | collective-permute-start | bytes 344072 | tf_op jit(solution)/shard_map/ppermute | solution.py:353
  4.1 16.1 %collective-permute-start.2 = (f32[224,128]{1,0:T(8,128)S(1)}, f32[224,128]{1,0:T(8,128)S(1)}, u32[]{:S(2)}, u32[]{:S(2)}) collective-permute-start(f32[224,128]{1,0:T(8,128)S(1)} %get-tuple-element.32), channel_id=1, source_target_pairs={{0,24},{2,26},{4,28},{6,30},{8,16},{10,18},{12,20},{14,22},{16,8},... | collective-permute-start | bytes 344072 | tf_op jit(solution)/shard_map/ppermute | solution.py:353
  6.5 21.5 %all-to-all-start = ((f32[16,40,128]{2,1,0:T(8,128)}), f32[16,40,128]{2,1,0:T(8,128)S(1)}, u32[]{:S(2)}, u32[]{:S(2)}) async-start(f32[16,40,128]{2,1,0:T(8,128)} %pack.1), calls=%async_computation | async-start | bytes 655360 | tf_op jit(solution)/shard_map/all_to_all | solution.py:408
  20.2 7.9 %copy-start = (bf16[4,256,256]{2,1,0:T(8,128)(2,1)S(1)}, bf16[4,256,256]{2,1,0:T(8,128)(2,1)}, u32[]{:S(2)}) copy-start(bf16[4,256,256]{2,1,0:T(8,128)(2,1)} %constant.4.clone.matrices) | copy-start | bytes 1572868
  20.2 7.9 %copy-start.6 = (f32[17,4,128]{2,1,0:T(4,128)S(1)}, f32[17,4,128]{2,1,0:T(4,128)}, u32[]{:S(2)}) copy-start(f32[17,4,128]{2,1,0:T(4,128)} %constant.5.clone.twists) | copy-start | bytes 104452
  20.2 7.9 %copy-start.7 = (f32[128,512]{1,0:T(8,128)S(1)}, f32[128,512]{1,0:T(8,128)}, u32[]{:S(2)}) copy-start(f32[128,512]{1,0:T(8,128)} %taps.1) | copy-start | bytes 786436
  20.2 7.9 %copy-start.8 = (f32[512]{0:T(512)S(1)}, f32[512]{0:T(512)}, u32[]{:S(2)}) copy-start(f32[512]{0:T(512)} %param.14) | copy-start | bytes 6148
  20.2 4.9 %collective-permute-start.3 = (f32[224,128]{1,0:T(8,128)S(1)}, f32[224,128]{1,0:T(8,128)S(1)}, u32[]{:S(2)}, u32[]{:S(2)}) collective-permute-start(f32[224,128]{1,0:T(8,128)S(1)} %get-tuple-element.33), channel_id=1, source_target_pairs={{0,2},{2,0},{4,6},{6,4},{8,10},{10,8},{12,14},{14,12},{16,18},{18,... | collective-permute-start | bytes 344072 | tf_op jit(solution)/shard_map/ppermute | solution.py:353
  20.8 4.8 %collective-permute-start.4 = (f32[224,128]{1,0:T(8,128)S(1)}, f32[224,128]{1,0:T(8,128)S(1)}, u32[]{:S(2)}, u32[]{:S(2)}) collective-permute-start(f32[224,128]{1,0:T(8,128)S(1)} %get-tuple-element.34), channel_id=1, source_target_pairs={{0,4},{2,6},{4,0},{6,2},{8,12},{10,14},{12,8},{14,10},{16,20},{18,... | collective-permute-start | bytes 344072 | tf_op jit(solution)/shard_map/ppermute | solution.py:353
  22.4 5.7 %collective-permute-start.5 = (f32[224,128]{1,0:T(8,128)S(1)}, f32[224,128]{1,0:T(8,128)S(1)}, u32[]{:S(2)}, u32[]{:S(2)}) collective-permute-start(f32[224,128]{1,0:T(8,128)S(1)} %get-tuple-element.35), channel_id=1, source_target_pairs={{0,6},{2,4},{4,2},{6,0},{8,14},{10,12},{12,10},{14,8},{16,22},{18,... | collective-permute-start | bytes 344072 | tf_op jit(solution)/shard_map/ppermute | solution.py:353
  29.9 10.7 %collective-permute-start.6 = (f32[192,128]{1,0:T(8,128)S(1)}, f32[192,128]{1,0:T(8,128)S(1)}, u32[]{:S(2)}, u32[]{:S(2)}) collective-permute-start(f32[192,128]{1,0:T(8,128)S(1)} %get-tuple-element.38), channel_id=1, source_target_pairs={{0,8},{2,10},{4,12},{6,14},{8,0},{10,2},{12,4},{14,6},{16,24},{18,... | collective-permute-start | bytes 294920 | tf_op jit(solution)/shard_map/ppermute | solution.py:353
  30.0 10.7 %collective-permute-start.7 = (f32[192,128]{1,0:T(8,128)S(1)}, f32[192,128]{1,0:T(8,128)S(1)}, u32[]{:S(2)}, u32[]{:S(2)}) collective-permute-start(f32[192,128]{1,0:T(8,128)S(1)} %get-tuple-element.39), channel_id=1, source_target_pairs={{0,16},{2,18},{4,20},{6,22},{8,24},{10,26},{12,28},{14,30},{16,0},... | collective-permute-start | bytes 294920 | tf_op jit(solution)/shard_map/ppermute | solution.py:353
  30.8 12.1 %collective-permute-start.8 = (f32[192,128]{1,0:T(8,128)S(1)}, f32[192,128]{1,0:T(8,128)S(1)}, u32[]{:S(2)}, u32[]{:S(2)}) collective-permute-start(f32[192,128]{1,0:T(8,128)S(1)} %get-tuple-element.40), channel_id=1, source_target_pairs={{0,24},{2,26},{4,28},{6,30},{8,16},{10,18},{12,20},{14,22},{16,8},... | collective-permute-start | bytes 294920 | tf_op jit(solution)/shard_map/ppermute | solution.py:353
  35.1 18.9 %all-to-all-start.1 = ((f32[16,56,128]{2,1,0:T(8,128)}), f32[16,56,128]{2,1,0:T(8,128)S(1)}, u32[]{:S(2)}, u32[]{:S(2)}) async-start(f32[16,56,128]{2,1,0:T(8,128)} %mix.1), calls=%async_computation.1 | async-start | bytes 917504 | tf_op jit(solution)/shard_map/all_to_all | solution.py:459
  43.0 11.0 %copy-start.1 = (bf16[128,512]{1,0:T(8,128)(2,1)S(1)}, bf16[128,512]{1,0:T(8,128)(2,1)}, u32[]{:S(2)}) copy-start(bf16[128,512]{1,0:T(8,128)(2,1)} %query.1) | copy-start | bytes 393220
  43.0 11.0 %copy-start.2 = (bf16[128,512]{1,0:T(8,128)(2,1)S(1)}, bf16[128,512]{1,0:T(8,128)(2,1)}, u32[]{:S(2)}) copy-start(bf16[128,512]{1,0:T(8,128)(2,1)} %key.1) | copy-start | bytes 393220
  43.0 11.0 %copy-start.3 = (bf16[128,512]{1,0:T(8,128)(2,1)S(1)}, bf16[128,512]{1,0:T(8,128)(2,1)}, u32[]{:S(2)}) copy-start(bf16[128,512]{1,0:T(8,128)(2,1)} %value.1) | copy-start | bytes 393220
  43.0 11.0 %copy-start.4 = (bf16[128,512]{1,0:T(8,128)(2,1)S(1)}, bf16[128,512]{1,0:T(8,128)(2,1)}, u32[]{:S(2)}) copy-start(bf16[128,512]{1,0:T(8,128)(2,1)} %grad.1) | copy-start | bytes 393220
  43.0 7.5 %collective-permute-start.9 = (f32[288,128]{1,0:T(8,128)S(1)}, f32[288,128]{1,0:T(8,128)S(1)}, u32[]{:S(2)}, u32[]{:S(2)}) collective-permute-start(f32[288,128]{1,0:T(8,128)S(1)} %get-tuple-element.41), channel_id=1, source_target_pairs={{0,2},{2,0},{4,6},{6,4},{8,10},{10,8},{12,14},{14,12},{16,18},{18,... | collective-permute-start | bytes 442376 | tf_op jit(solution)/shard_map/ppermute | solution.py:353
  47.2 6.7 %collective-permute-start.10 = (f32[288,128]{1,0:T(8,128)S(1)}, f32[288,128]{1,0:T(8,128)S(1)}, u32[]{:S(2)}, u32[]{:S(2)}) collective-permute-start(f32[288,128]{1,0:T(8,128)S(1)} %get-tuple-element.42), channel_id=1, source_target_pairs={{0,4},{2,6},{4,0},{6,2},{8,12},{10,14},{12,8},{14,10},{16,20},{18,... | collective-permute-start | bytes 442376 | tf_op jit(solution)/shard_map/ppermute | solution.py:353
  47.2 6.7 %collective-permute-start.11 = (f32[288,128]{1,0:T(8,128)S(1)}, f32[288,128]{1,0:T(8,128)S(1)}, u32[]{:S(2)}, u32[]{:S(2)}) collective-permute-start(f32[288,128]{1,0:T(8,128)S(1)} %get-tuple-element.43), channel_id=1, source_target_pairs={{0,6},{2,4},{4,2},{6,0},{8,14},{10,12},{12,10},{14,8},{16,22},{18,... | collective-permute-start | bytes 442376 | tf_op jit(solution)/shard_map/ppermute | solution.py:353
